TPU v7x, 32 devices: a whole 2x2x4 slice. The times are simulated.
32 devices in a mesh: dp: 8 (over y, x, core), expert: 4 (over z).
Axes of the slice: x: 2, y: 2, z: 4, core: 2. Of those that a mesh axis runs over, the one named last changes fastest.
Arguments:
- tokens: bfloat16 [4096, 1536], P(('dp', 'expert')), may hold values from -6 to 6
- cotangent: float32 [4096, 1536], P(('dp', 'expert')), may hold values from -6 to 6
- segments: int32 [32, 128], P(('dp', 'expert')), may hold values from 0 to 3, never falling along the last dimension, each value on 1 to 64 neighbouring positions
- expert_ids: int32 [4096, 8], P(('dp', 'expert')), may hold values from 0 to 39, all different within a row; in each aligned block of 128 rows (0 to 127, 128 to 255, ...) at most 32 rows name the same one
- route_weights: float32 [4096, 8], P(('dp', 'expert')), may hold values from 0.2 to 1
- w_qkv: float32 [1536, 2560], P(('dp', 'expert')), may hold values from -0.15625 to 0.15625
- w_out: float32 [1536, 1536], P(('dp', 'expert')), may hold values from -0.625 to 0.625
- gains: float32 [2, 1536], P(None, ('dp', 'expert')), may hold values from 0.5 to 1.5
- w_gate_up: float32 [40, 1536, 1024], P('expert', 'dp'), may hold values from -0.15625 to 0.15625
- w_down: float32 [40, 512, 1536], P('expert', 'dp'), may hold values from -0.25 to 0.25
- first_moment_projection: float32 [1536, 2560], P(('dp', 'expert')), may hold values from -96 to 96
- first_out: float32 [1536, 1536], P(('dp', 'expert')), may hold values from -19.2 to 19.2
- first_gains: float32 [2, 1536], P(None, ('dp', 'expert')), may hold values from -76.8 to 76.8
- first_gate_up: float32 [40, 1536, 1024], P('expert', 'dp'), may hold values from -12.021101 to 12.021101
- first_down: float32 [40, 512, 1536], P('expert', 'dp'), may hold values from -6.8692008 to 6.8692008
- second_moment_projection: float32 [1536, 2560], P(('dp', 'expert')), may hold values from 1310.72 to 5406.72
- second_out: float32 [1536, 1536], P(('dp', 'expert')), may hold values from 53.248 to 217.088
- second_gains: float32 [2, 1536], P(None, ('dp', 'expert')), may hold values from 860.16 to 3481.6
- second_gate_up: float32 [40, 1536, 1024], P('expert', 'dp'), may hold values from 20.48 to 85.1968
- second_down: float32 [40, 512, 1536], P('expert', 'dp'), may hold values from 6.88128 to 27.8528
Outputs:
- out_tokens: float32 [4096, 1536], P(('dp', 'expert'))
- grad_tokens: float32 [4096, 1536], P(('dp', 'expert'))
- grad_qkv: float32 [1536, 2560], P(('dp', 'expert'))
- grad_out: float32 [1536, 1536], P(('dp', 'expert'))
- grad_gains: float32 [2, 1536], P(None, ('dp', 'expert'))
- grad_gate_up: float32 [40, 1536, 1024], P('expert', 'dp')
- grad_down: float32 [40, 512, 1536], P('expert', 'dp')
- new_qkv: float32 [1536, 2560], P(('dp', 'expert'))
- new_out: float32 [1536, 1536], P(('dp', 'expert'))
- new_gains: float32 [2, 1536], P(None, ('dp', 'expert'))
- new_gate_up: float32 [40, 1536, 1024], P('expert', 'dp')
- new_down: float32 [40, 512, 1536], P('expert', 'dp')
- new_first_qkv: float32 [1536, 2560], P(('dp', 'expert'))
- new_first_out: float32 [1536, 1536], P(('dp', 'expert'))
- new_first_gains: float32 [2, 1536], P(None, ('dp', 'expert'))
- new_first_gate_up: float32 [40, 1536, 1024], P('expert', 'dp')
- new_first_down: float32 [40, 512, 1536], P('expert', 'dp')
- new_second_qkv: float32 [1536, 2560], P(('dp', 'expert'))
- new_second_out: float32 [1536, 1536], P(('dp', 'expert'))
- new_second_gains: float32 [2, 1536], P(None, ('dp', 'expert'))
- new_second_gate_up: float32 [40, 1536, 1024], P('expert', 'dp')
- new_second_down: float32 [40, 512, 1536], P('expert', 'dp')
Inputs may be any that keep to these rules, and one draw needn't show every extreme that they name: `segments`: segment numbers never fall along a sequence; each segment spans at most half of 128 positions. `expert_ids`: each row names 8 different experts; within the rows of one device no expert is named more than 32 times, and in every draw some device names some expert exactly 32 times.
All inputs are finite; a program needn't handle non-finite values.
Results may differ from a plain program's by a relative error of at most 0.014.
The roundings to bfloat16 on the way count: a program that leaves them out, or rounds other values in their place, can miss the bound.
Values may be sent and summed in bfloat16 or wider, within the bound.
No kernel may reach another device: no remote copies, remote signals or barrier semaphores. Data moves between devices by JAX's collectives and lax.ppermute only.
A program may use at most 448 MiB of HBM per device.

v0:
```python
import jax
import jax.numpy as jnp
from jax import lax
from jax.sharding import PartitionSpec as P

MODEL_WIDTH = 1536
QUERY_HEADS = 24
KEY_VALUE_HEADS = 8
HEAD_SIZE = 64
FF = 512
EXPERTS = 40
TOP = 8
CAP = 32


eps_norm = 1e-05
beta_one = 0.9
beta_two = 0.95
adam_eps = 1e-08
learn_rate = 0.01
out_rate = 0.04
gain_rate = 0.2
weight_decay = 0.1
correct_one = 1.0 - beta_one**3
correct_two = 1.0 - beta_two**3


def norm_scale(rows):
    return lax.rsqrt(jnp.mean(rows * rows, -1, keepdims=True) + eps_norm)


def rotary_tables(sequence_length, half_dim):
    position = jnp.arange(sequence_length, dtype=jnp.float32)[:, None]
    frequency = 10000.0 ** (-jnp.arange(half_dim, dtype=jnp.float32) / half_dim)
    angles = position * frequency[None, :]
    return (jnp.cos(angles), jnp.sin(angles))


def apply_rotary(value_rows, cosine_table, sine_table, middle):
    half_dim = value_rows.shape[-1] // 2
    shape = (cosine_table.shape[0],) + (1,) * middle + (half_dim,)
    cosine_table = cosine_table.reshape(shape)
    sine_table = sine_table.reshape(shape)
    first = value_rows[..., :half_dim]
    second = value_rows[..., half_dim:]
    return jnp.concatenate(
        [first * cosine_table - second * sine_table, second * cosine_table + first * sine_table], -1
    )


def split_heads(projected_rows, sequence_count, sequence_length, cosine_table, sine_table):
    query_total_width = QUERY_HEADS * HEAD_SIZE
    key_columns_width = KEY_VALUE_HEADS * HEAD_SIZE
    reshaped_rows = projected_rows.reshape(sequence_count, sequence_length, -1)
    query_block = apply_rotary(
        reshaped_rows[..., :query_total_width].reshape(
            sequence_count,
            sequence_length,
            KEY_VALUE_HEADS,
            QUERY_HEADS // KEY_VALUE_HEADS,
            HEAD_SIZE,
        ),
        cosine_table,
        sine_table,
        2,
    )
    key_rows = apply_rotary(
        reshaped_rows[..., query_total_width : query_total_width + key_columns_width].reshape(
            sequence_count, sequence_length, KEY_VALUE_HEADS, HEAD_SIZE
        ),
        cosine_table,
        sine_table,
        1,
    )
    value_rows = reshaped_rows[..., query_total_width + key_columns_width :].reshape(
        sequence_count, sequence_length, KEY_VALUE_HEADS, HEAD_SIZE
    )
    return (
        query_block.astype(jnp.bfloat16),
        key_rows.astype(jnp.bfloat16),
        value_rows.astype(jnp.bfloat16),
    )


def allowed_mask(segment):
    spots = jnp.arange(segment.shape[0])
    return (spots[:, None] >= spots[None, :]) & (segment[:, None] == segment[None, :])


def score_block(query_block, key_rows, segment):
    scores = jnp.einsum(
        "qhgd,khd->hgqk", query_block, key_rows, preferred_element_type=jnp.float32
    ) * query_block.shape[-1] ** (-0.5)
    return jnp.where(allowed_mask(segment)[None, None], scores, -1e30)


def attend(query_block, key_rows, value_rows, segment):
    scores = score_block(query_block, key_rows, segment)
    highest = jnp.max(scores, -1, keepdims=True)
    logsum = highest + jnp.log(jnp.sum(jnp.exp(scores - highest), -1, keepdims=True))
    probs = jnp.exp(scores - logsum).astype(jnp.bfloat16)
    attended = jnp.einsum("hgqk,khd->qhgd", probs, value_rows, preferred_element_type=jnp.float32)
    return (attended.astype(jnp.bfloat16), logsum)


def attend_back(query_block, key_rows, value_rows, segment, logsum, attended_gradient):
    factor = query_block.shape[-1] ** (-0.5)
    probs = jnp.exp(score_block(query_block, key_rows, segment) - logsum)
    grad_probs = jnp.einsum(
        "qhgd,khd->hgqk", attended_gradient, value_rows, preferred_element_type=jnp.float32
    )
    inner_sum = jnp.sum(probs * grad_probs, -1, keepdims=True)
    grad_scores = (probs * (grad_probs - inner_sum) * factor).astype(jnp.bfloat16)
    grad_values = jnp.einsum(
        "hgqk,qhgd->khd",
        probs.astype(jnp.bfloat16),
        attended_gradient,
        preferred_element_type=jnp.float32,
    )
    grad_query = jnp.einsum(
        "hgqk,khd->qhgd", grad_scores, key_rows, preferred_element_type=jnp.float32
    )
    grad_keys = jnp.einsum(
        "hgqk,qhgd->khd", grad_scores, query_block, preferred_element_type=jnp.float32
    )
    return (grad_query, grad_keys, grad_values)


def join_grads(grad_query, grad_keys, grad_values, cosine_table, sine_table):
    sequence_length = grad_query.shape[0]
    grad_query = apply_rotary(grad_query, cosine_table, -sine_table, 2).reshape(sequence_length, -1)
    grad_keys = apply_rotary(grad_keys, cosine_table, -sine_table, 1).reshape(sequence_length, -1)
    return jnp.concatenate(
        [grad_query, grad_keys, grad_values.reshape(sequence_length, -1)], -1
    ).astype(jnp.bfloat16)


def adam_step(weight, grad, first, second, step_rate, shrink):
    first = beta_one * first + (1.0 - beta_one) * grad
    second = beta_two * second + (1.0 - beta_two) * grad * grad
    update = first / correct_one / (jnp.sqrt(second / correct_two) + adam_eps)
    return (weight - step_rate * (update + shrink * weight), first, second)


def shards(
    tokens,
    cotangent,
    segments,
    expert_ids,
    route_weights,
    w_qkv,
    w_out,
    gains,
    w_gate_up,
    w_down,
    first_moment_projection,
    first_out,
    first_gains,
    first_gate_up,
    first_down,
    second_moment_projection,
    second_out,
    second_gains,
    second_gate_up,
    second_down,
):
    sequence_count = segments.shape[0]
    sequence_length = segments.shape[1]
    groups_expert = lax.axis_size("expert")
    local_experts = EXPERTS // groups_expert
    slot_rows = groups_expert * CAP
    qkv_full, out_full, gain_full = (
        lax.all_gather(w_qkv.astype(jnp.bfloat16), ("dp", "expert"), axis=0, tiled=True),
        lax.all_gather(w_out.astype(jnp.bfloat16), ("dp", "expert"), axis=0, tiled=True),
        lax.all_gather(gains.astype(jnp.bfloat16), ("dp", "expert"), axis=1, tiled=True),
    )
    gate_up_full, down_full = (
        lax.all_gather(w_gate_up.astype(jnp.bfloat16), "dp", axis=1, tiled=True),
        lax.all_gather(w_down.astype(jnp.bfloat16), "dp", axis=1, tiled=True),
    )
    gain_attn = gain_full[0].astype(jnp.float32)
    gain_moe = gain_full[1].astype(jnp.float32)
    cosine_table, sine_table = rotary_tables(sequence_length, HEAD_SIZE // 2)
    inputs = tokens.astype(jnp.float32)
    scale_one = norm_scale(inputs)
    normed_one = (inputs * scale_one * gain_attn).astype(jnp.bfloat16)
    projected_rows = jnp.dot(normed_one, qkv_full, preferred_element_type=jnp.float32)
    query_block, key_rows, value_rows = split_heads(
        projected_rows, sequence_count, sequence_length, cosine_table, sine_table
    )
    index = 0
    attended_seq, logsum = attend(
        query_block[index], key_rows[index], value_rows[index], segments[index]
    )
    pieces = attended_seq.reshape(sequence_length, QUERY_HEADS * HEAD_SIZE)
    logsums = [logsum]
    resid = inputs + jnp.dot(pieces, out_full, preferred_element_type=jnp.float32)
    scale_two = norm_scale(resid)
    normed_two = (resid * scale_two * gain_moe).astype(jnp.bfloat16)
    flat_ids = expert_ids.reshape(-1)
    pair_count = flat_ids.shape[0]
    one_hot = (flat_ids[:, None] == jnp.arange(EXPERTS, dtype=jnp.int32)[None, :]).astype(jnp.int32)
    ranking = jnp.sum(jnp.cumsum(one_hot, 0) * one_hot, 1) - 1
    target = flat_ids * CAP + ranking
    owners = (
        jnp.full((EXPERTS * CAP,), -1, jnp.int32)
        .at[target]
        .set(jnp.arange(pair_count, dtype=jnp.int32))
    )
    filled = (owners >= 0)[:, None]
    safe_owner = jnp.maximum(owners, 0)
    send_rows = jnp.where(filled, normed_two[safe_owner // TOP], jnp.zeros((), jnp.bfloat16))
    received = lax.all_to_all(
        send_rows.reshape(groups_expert, local_experts, CAP, MODEL_WIDTH),
        "expert",
        split_axis=0,
        concat_axis=2,
        tiled=True,
    )
    received = received.reshape(local_experts, slot_rows, MODEL_WIDTH)
    mixed = jnp.einsum("erd,edf->erf", received, gate_up_full, preferred_element_type=jnp.float32)
    gate = mixed[..., :FF]
    upper = mixed[..., FF:]
    hidden = (jax.nn.silu(gate) * upper).astype(jnp.bfloat16)
    expert_out = jnp.einsum(
        "erf,efd->erd", hidden, down_full, preferred_element_type=jnp.float32
    ).astype(jnp.bfloat16)
    returned = lax.all_to_all(
        expert_out.reshape(1, local_experts, slot_rows, MODEL_WIDTH),
        "expert",
        split_axis=2,
        concat_axis=0,
        tiled=True,
    )
    picked = returned.reshape(EXPERTS * CAP, MODEL_WIDTH)[target].reshape(-1, TOP, MODEL_WIDTH)
    out_tokens = resid + jnp.sum(route_weights[..., None] * picked.astype(jnp.float32), 1)
    gate_up_back, down_back = (
        lax.all_gather(w_gate_up.astype(jnp.bfloat16), "dp", axis=1, tiled=True),
        lax.all_gather(w_down.astype(jnp.bfloat16), "dp", axis=1, tiled=True),
    )
    grad_routed = (
        (route_weights[..., None] * cotangent[:, None, :])
        .astype(jnp.bfloat16)
        .reshape(pair_count, MODEL_WIDTH)
    )
    send_grads = jnp.where(filled, grad_routed[safe_owner], jnp.zeros((), jnp.bfloat16))
    grad_expert = lax.all_to_all(
        send_grads.reshape(groups_expert, local_experts, CAP, MODEL_WIDTH),
        "expert",
        split_axis=0,
        concat_axis=2,
        tiled=True,
    )
    grad_expert = grad_expert.reshape(local_experts, slot_rows, MODEL_WIDTH)
    grad_hidden = jnp.einsum(
        "erd,efd->erf", grad_expert, down_back, preferred_element_type=jnp.float32
    )
    grad_down = jnp.einsum("erf,erd->efd", hidden, grad_expert, preferred_element_type=jnp.float32)
    sigma = jax.nn.sigmoid(gate)
    grad_mixed = jnp.concatenate(
        [grad_hidden * upper * sigma * (1.0 + gate * (1.0 - sigma)), grad_hidden * gate * sigma], -1
    ).astype(jnp.bfloat16)
    grad_gate_up = jnp.einsum(
        "erd,erf->edf", received, grad_mixed, preferred_element_type=jnp.float32
    )
    grad_received = jnp.einsum(
        "erf,edf->erd", grad_mixed, gate_up_back, preferred_element_type=jnp.float32
    ).astype(jnp.bfloat16)
    grad_back = lax.all_to_all(
        grad_received.reshape(1, local_experts, slot_rows, MODEL_WIDTH),
        "expert",
        split_axis=2,
        concat_axis=0,
        tiled=True,
    )
    grad_normed_two = jnp.sum(
        grad_back.reshape(EXPERTS * CAP, MODEL_WIDTH)[target]
        .reshape(-1, TOP, MODEL_WIDTH)
        .astype(jnp.float32),
        1,
    )
    hat_two = grad_normed_two * gain_moe
    grad_gain_moe = jnp.sum(grad_normed_two * resid * scale_two, 0)
    grad_resid = cotangent + scale_two * (
        hat_two - resid * scale_two**2 * jnp.mean(hat_two * resid, -1, keepdims=True)
    )
    grad_resid_half = grad_resid.astype(jnp.bfloat16)
    qkv_back, out_back = (
        lax.all_gather(w_qkv.astype(jnp.bfloat16), ("dp", "expert"), axis=0, tiled=True),
        lax.all_gather(w_out.astype(jnp.bfloat16), ("dp", "expert"), axis=0, tiled=True),
    )
    grad_out = jnp.dot(pieces.T, grad_resid_half, preferred_element_type=jnp.float32)
    attended_gradient = jnp.dot(
        grad_resid_half, out_back.T, preferred_element_type=jnp.float32
    ).astype(jnp.bfloat16)
    attended_gradient = attended_gradient.reshape(
        sequence_count, sequence_length, KEY_VALUE_HEADS, QUERY_HEADS // KEY_VALUE_HEADS, HEAD_SIZE
    )
    index = 0
    grad_query, grad_keys, grad_values = attend_back(
        query_block[index],
        key_rows[index],
        value_rows[index],
        segments[index],
        logsums[index],
        attended_gradient[index],
    )
    joined = join_grads(grad_query, grad_keys, grad_values, cosine_table, sine_table)
    grad_qkv = jnp.dot(normed_one.T, joined, preferred_element_type=jnp.float32)
    grad_normed_one = jnp.dot(joined, qkv_back.T, preferred_element_type=jnp.float32)
    hat_one = grad_normed_one * gain_attn
    grad_gain_attn = jnp.sum(grad_normed_one * inputs * scale_one, 0)
    grad_tokens = grad_resid + scale_one * (
        hat_one - inputs * scale_one**2 * jnp.mean(hat_one * inputs, -1, keepdims=True)
    )
    grad_gains = jnp.stack([grad_gain_attn, grad_gain_moe])
    part_qkv, part_out, part_gains = (
        lax.psum_scatter(grad_qkv, ("dp", "expert"), scatter_dimension=0, tiled=True),
        lax.psum_scatter(grad_out, ("dp", "expert"), scatter_dimension=0, tiled=True),
        lax.psum_scatter(grad_gains, ("dp", "expert"), scatter_dimension=1, tiled=True),
    )
    part_gate_up, part_down = (
        lax.psum_scatter(grad_gate_up, "dp", scatter_dimension=1, tiled=True),
        lax.psum_scatter(grad_down, "dp", scatter_dimension=1, tiled=True),
    )
    new_qkv, new_first_qkv, new_second_qkv = adam_step(
        w_qkv, part_qkv, first_moment_projection, second_moment_projection, learn_rate, weight_decay
    )
    new_out, new_first_out, new_second_out = adam_step(
        w_out, part_out, first_out, second_out, out_rate, weight_decay
    )
    new_gains, new_first_gains, new_second_gains = adam_step(
        gains, part_gains, first_gains, second_gains, gain_rate, 0.0
    )
    new_gate_up, new_first_gate_up, new_second_gate_up = adam_step(
        w_gate_up, part_gate_up, first_gate_up, second_gate_up, learn_rate, weight_decay
    )
    new_down, new_first_down, new_second_down = adam_step(
        w_down, part_down, first_down, second_down, learn_rate, weight_decay
    )
    return (
        out_tokens,
        grad_tokens,
        part_qkv,
        part_out,
        part_gains,
        part_gate_up,
        part_down,
        new_qkv,
        new_out,
        new_gains,
        new_gate_up,
        new_down,
        new_first_qkv,
        new_first_out,
        new_first_gains,
        new_first_gate_up,
        new_first_down,
        new_second_qkv,
        new_second_out,
        new_second_gains,
        new_second_gate_up,
        new_second_down,
    )


def solution(mesh):
    return jax.shard_map(
        shards,
        mesh=mesh,
        in_specs=(
            P(("dp", "expert"), None),
            P(("dp", "expert"), None),
            P(("dp", "expert"), None),
            P(("dp", "expert"), None),
            P(("dp", "expert"), None),
            P(("dp", "expert"), None),
            P(("dp", "expert"), None),
            P(None, ("dp", "expert")),
            P("expert", "dp", None),
            P("expert", "dp", None),
            P(("dp", "expert"), None),
            P(("dp", "expert"), None),
            P(None, ("dp", "expert")),
            P("expert", "dp", None),
            P("expert", "dp", None),
            P(("dp", "expert"), None),
            P(("dp", "expert"), None),
            P(None, ("dp", "expert")),
            P("expert", "dp", None),
            P("expert", "dp", None),
        ),
        out_specs=(
            P(("dp", "expert"), None),
            P(("dp", "expert"), None),
            P(("dp", "expert"), None),
            P(("dp", "expert"), None),
            P(None, ("dp", "expert")),
            P("expert", "dp", None),
            P("expert", "dp", None),
            P(("dp", "expert"), None),
            P(("dp", "expert"), None),
            P(None, ("dp", "expert")),
            P("expert", "dp", None),
            P("expert", "dp", None),
            P(("dp", "expert"), None),
            P(("dp", "expert"), None),
            P(None, ("dp", "expert")),
            P("expert", "dp", None),
            P("expert", "dp", None),
            P(("dp", "expert"), None),
            P(("dp", "expert"), None),
            P(None, ("dp", "expert")),
            P("expert", "dp", None),
            P("expert", "dp", None),
        ),
        check_vma=False,
    )
```

profile of v0, /device:TPU:0, one launch (start us, length us, event | category | flops | bytes accessed | tf_op | source)
XLA Modules:
  0.0 1754.2 jit_solution(7300954198123969958)
XLA Ops:
  10.8 5.8 convert_element_type.109
  16.7 3.6 convert_element_type.111
  20.6 69.7 %all-gather = bf16[32,48,2]{1,2,0:T(2,128)(2,1)S(1)} all-gather(bf16[1,48,2]{1,2,0:T(2,128)(2,1)S(1)} %convert_bitcast_fusion), channel_id=1, replica_groups=mesh['dp'=8,'expert'=4] {'dp','expert'}, dimensions={0}, use_global_device_ids=true | all-gather | bytes 6336 | tf_op jit(solution)/shard_map/all_gather | solution.py:175
  91.2 11.3 reduce-window.6
  103.0 4.3 scatter_custom_fusion
  110.3 5.4 gather_fusion.2
  118.6 4.5 convolution_bitcast_fusion
  125.2 30.1 %all-gather.8.cloned.1.call-done = bf16[1536,1536]{1,0:T(8,128)(2,1)} async-done(((bf16[48,1536]{1,0:T(8,128)(2,1)}), bf16[1536,1536]{1,0:T(8,128)(2,1)}) %all-gather.8.cloned.1.call-update) | async-done | bytes 4718608 | tf_op jit(solution)/shard_map/all_gather | solution.py:174
  155.3 3.2 multiply_reduce_fusion.2
  160.4 5.6 gather_fusion
  166.0 6.5 broadcast_select_fusion
  172.5 91.9 %all_to_all.60 = bf16[4,10,32,1536]{3,2,1,0:T(8,128)(2,1)} all-to-all(bf16[4,10,32,1536]{3,2,1,0:T(8,128)(2,1)S(1)} %get-tuple-element.57), channel_id=1, replica_groups=mesh['dp'=8,'expert'=4] {'expert'}, dimensions={0} | all-to-all | bytes 7864320 | tf_op jit(solution)/shard_map/all_to_all | solution.py:213
  264.4 5.3 all-to-all-start.2
  269.6 4.5 copy.95
  274.1 82.7 %all-to-all-done.2 = bf16[4,10,32,1536]{3,2,1,0:T(8,128)(2,1)} async-done(((bf16[4,10,32,1536]{3,2,1,0:T(8,128)(2,1)}), bf16[4,10,32,1536]{3,2,1,0:T(8,128)(2,1)}, u32[]{:S(2)}, u32[]{:S(2)}) %all-to-all-start.2) | async-done | bytes 3932192 | tf_op jit(solution)/shard_map/all_to_all | solution.py:247
  356.8 4.6 copy.99
  361.4 18.1 %fusion.79 = f32[10,128,1024]{2,1,0:T(8,128)} fusion(bf16[10,128,1536]{2,1,0:T(8,128)(2,1)} %bitcast.152, bf16[10,1536,1024]{2,1,0:T(8,128)(2,1)} %all-gather.10.cloned.1.call-done), kind=kOutput, calls=%fused_computation.163 | convolution fusion | flops 4026531840 | bytes 40632320 | tf_op jit(solution)/shard_map/erd,edf->erf/dot_general | solution.py:221
  379.4 16.9 all-gather.12.cloned.1.call-done
  396.4 12.1 multiply_convert_fusion.1
  408.5 17.5 fusion.5
  426.0 7.2 copy.100
  433.2 5.5 all-to-all-start.3
  438.7 8.1 fusion.6
  446.8 5.1 copy.96
  452.0 125.5 %all-to-all-done.3 = bf16[1,10,128,1536]{3,1,0,2:T(8,128)(2,1)} async-done(((bf16[1,10,128,1536]{3,1,0,2:T(8,128)(2,1)}), bf16[1,10,128,1536]{3,1,0,2:T(8,128)(2,1)}, u32[]{:S(2)}, u32[]{:S(2)}) %all-to-all-start.3) | async-done | bytes 3932192 | tf_op jit(solution)/shard_map/all_to_all | solution.py:269
  577.5 5.2 all-to-all-start.1
  582.8 6.9 copy.101
  589.7 9.9 gather_fusion.3
  599.6 4.0 convert_reduce_fusion
  605.3 115.5 %all-to-all-done.1 = bf16[1,10,128,1536]{3,1,0,2:T(8,128)(2,1)} async-done(((bf16[1,10,128,1536]{3,1,0,2:T(8,128)(2,1)}), bf16[1,10,128,1536]{3,1,0,2:T(8,128)(2,1)}, u32[]{:S(2)}, u32[]{:S(2)}) %all-to-all-start.1) | async-done | bytes 3932192 | tf_op jit(solution)/shard_map/all_to_all | solution.py:228
  720.8 6.9 copy.97
  727.6 10.3 gather_fusion.1
  738.0 4.8 fusion.2
  744.8 4.0 convolution_convert_fusion.2
  751.8 2.6 fusion.14
  754.4 2.7 convolution_bitcast_fusion.1
  757.4 6.9 fusion.25
  765.6 5.0 fusion.40
  771.5 7.9 fusion.34
  780.7 14.8 fusion.81
  796.8 24.9 %fusion.7 = f32[10,1536,1024]{2,1,0:T(8,128)} fusion(bf16[10,128,1536]{2,1,0:T(8,128)(2,1)} %bitcast.153, bf16[10,128,512]{2,1,0:T(8,128)(2,1)} %get-tuple-element.44, bf16[10,128,512]{2,1,0:T(8,128)(2,1)S(1)} %copy-done.6), kind=kOutput, calls=%fused_computation.38 | convolution fusion | flops 4031774720 | bytes 69468160 | tf_op jit(solution)/shard_map/erd,erf->edf/dot_general | solution.py:263
  824.2 35.2 %reduce-scatter.16.cloned.1.call-done = f32[48,2]{1,0:T(8,128)} async-done(((f32[1536,2]{1,0:T(8,128)}), f32[48,2]{1,0:T(8,128)}) %reduce-scatter.16.cloned.1.call-update) | async-done | bytes 400
  860.9 139.4 %reduce-scatter.10.cloned.1.call-done = f32[48,1536]{1,0:T(8,128)} async-done(((f32[1536,1536]{1,0:T(8,128)}), f32[48,1536]{1,0:T(8,128)}) %reduce-scatter.10.cloned.1.call-update) | async-done | bytes 294928 | tf_op jit(solution)/shard_map/reduce_scatter | solution.py:319
  1002.5 175.3 %reduce-scatter.8.cloned.1.call-done = f32[48,2560]{1,0:T(8,128)} async-done(((f32[1536,2560]{1,0:T(8,128)}), f32[48,2560]{1,0:T(8,128)}) %reduce-scatter.8.cloned.1.call-update) | async-done | bytes 491536 | tf_op jit(solution)/shard_map/reduce_scatter | solution.py:318
  1180.3 190.9 %reduce-scatter.14.cloned.1.call-done = f32[10,64,1536]{2,1,0:T(8,128)} async-done(((f32[10,512,1536]{2,1,0:T(8,128)}), f32[10,64,1536]{2,1,0:T(8,128)}) %reduce-scatter.14.cloned.1.call-update) | async-done | bytes 3932176 | tf_op jit(solution)/shard_map/reduce_scatter | solution.py:324
  1371.2 10.2 multiply_subtract_fusion.1
  1381.3 345.6 %reduce-scatter.12.cloned.1.call-done = f32[10,192,1024]{2,1,0:T(8,128)} async-done(((f32[10,1536,1024]{2,1,0:T(8,128)}), f32[10,192,1024]{2,1,0:T(8,128)}) %reduce-scatter.12.cloned.1.call-update) | async-done | bytes 7864336 | tf_op jit(solution)/shard_map/reduce_scatter | solution.py:323
  1726.9 20.6 %multiply_subtract_fusion = (f32[10,192,1024]{2,1,0:T(8,128)}, f32[10,192,1024]{2,1,0:T(8,128)}, f32[10,192,1024]{2,1,0:T(8,128)}) fusion(f32[10,192,1024]{2,1,0:T(8,128)} %param.28, f32[10,192,1024]{2,1,0:T(8,128)} %reduce-scatter.12.cloned.1.call-done, f32[10,192,1024]{2,1,0:T(8,128)} %param.33, f32[10,192,1024]{2,1,0:T(8,128)} %param.38), kind=kLoop, calls=%fused_computation.8 | loop fusion | flops 29491200 | bytes 55050240 | tf_op jit(solution)/shard_map/sub | solution.py:142
  (180 shorter events, 35.0 us)
Async XLA Ops:
  7.2 111.4 %all-gather.6.cloned.1.call-start = ((), (), s32[]{:S(2)}) async-start(), calls=%async_computation.9 | async-start | bytes 8110080 | tf_op jit(solution)/shard_map/all_gather | solution.py:173
  9.0 146.3 %all-gather.8.cloned.1.call-start = ((), (), s32[]{:S(2)}) async-start(), calls=%async_computation.10 | async-start | bytes 4866048 | tf_op jit(solution)/shard_map/all_gather | solution.py:174
  10.7 350.6 %all-gather.10.cloned.1.call-start = ((), (), s32[]{:S(2)}) async-start(), calls=%async_computation.11 | async-start | bytes 35389440 | tf_op jit(solution)/shard_map/all_gather | solution.py:178
  16.6 3.7 copy-start.30
  16.6 4.0 copy-start.39
  16.6 73.8 %copy-start.37 = (f32[128,8]{0,1:T(8,128)S(1)}, f32[128,8]{0,1:T(8,128)}, u32[]{:S(2)}) copy-start(f32[128,8]{0,1:T(8,128)} %param.24) | copy-start | bytes 12292
  16.6 379.7 %all-gather.12.cloned.1.call-start = ((), (), s32[]{:S(2)}) async-start(), calls=%async_computation.12 | async-start | bytes 17694720 | tf_op jit(solution)/shard_map/all_gather | solution.py:179
  103.0 7.2 copy-start.31
  110.3 6.1 copy-start
  116.3 6.8 copy-start.17
  117.0 6.1 copy-start.33
  123.4 1.8 copy-start.9
  123.8 31.5 %copy-start.28 = (bf16[128,8,32]{0,2,1:T(8,128)(2,1)}, bf16[128,8,32]{0,2,1:T(8,128)(2,1)S(1)}, u32[]{:S(2)}) copy-start(bf16[128,8,32]{0,2,1:T(8,128)(2,1)S(1)} %get-tuple-element.55) | copy-start | bytes 196612
  124.0 31.3 %copy-start.19 = (bf16[128,8,3,32]{0,3,2,1:T(8,128)(2,1)}, bf16[128,8,3,32]{0,3,2,1:T(8,128)(2,1)S(1)}, u32[]{:S(2)}) copy-start(bf16[128,8,3,32]{0,3,2,1:T(8,128)(2,1)S(1)} %get-tuple-element.48) | copy-start | bytes 589828
  124.0 31.3 %copy-start.21 = (bf16[128,8,3,32]{0,3,2,1:T(8,128)(2,1)}, bf16[128,8,3,32]{0,3,2,1:T(8,128)(2,1)S(1)}, u32[]{:S(2)}) copy-start(bf16[128,8,3,32]{0,3,2,1:T(8,128)(2,1)S(1)} %get-tuple-element.49) | copy-start | bytes 589828
  124.8 30.5 %copy-start.23 = (f32[8,3,128]{2,1,0:T(4,128)}, f32[8,3,128]{2,1,0:T(4,128)S(1)}, u32[]{:S(2)}) copy-start(f32[8,3,128]{2,1,0:T(4,128)S(1)} %log_add_fusion) | copy-start | bytes 36868
  264.4 92.4 %all-to-all-start.2 = ((bf16[4,10,32,1536]{3,2,1,0:T(8,128)(2,1)}), bf16[4,10,32,1536]{3,2,1,0:T(8,128)(2,1)}, u32[]{:S(2)}, u32[]{:S(2)}) async-start(bf16[4,10,32,1536]{3,2,1,0:T(8,128)(2,1)} %get-tuple-element.56), calls=%async_computation.2 | async-start | bytes 7864320 | tf_op jit(solution)/shard_map/all_to_all | solution.py:247
  433.2 144.3 %all-to-all-start.3 = ((bf16[1,10,128,1536]{3,1,0,2:T(8,128)(2,1)}), bf16[1,10,128,1536]{3,1,0,2:T(8,128)(2,1)}, u32[]{:S(2)}, u32[]{:S(2)}) async-start(bf16[1,10,128,1536]{3,1,0,2:T(8,128)(2,1)} %copy.100), calls=%async_computation.3 | async-start | bytes 12582912 | tf_op jit(solution)/shard_map/all_to_all | solution.py:269
  452.0 130.8 %copy-start.32 = (s32[1024,1]{0,1:T(1,128)S(1)}, s32[1024,1]{0,1:T(1,128)}, u32[]{:S(2)}) copy-start(s32[1024,1]{0,1:T(1,128)} %copy-done.31) | copy-start | bytes 12292
  577.5 143.3 %all-to-all-start.1 = ((bf16[1,10,128,1536]{3,1,0,2:T(8,128)(2,1)}), bf16[1,10,128,1536]{3,1,0,2:T(8,128)(2,1)}, u32[]{:S(2)}, u32[]{:S(2)}) async-start(bf16[1,10,128,1536]{3,1,0,2:T(8,128)(2,1)} %copy.96), calls=%async_computation.1 | async-start | bytes 12582912 | tf_op jit(solution)/shard_map/all_to_all | solution.py:228
  582.8 276.7 %reduce-scatter.16.cloned.1.call-start = ((), (), s32[]{:S(2)}) async-start(), calls=%async_computation.17 | async-start | bytes 811008
  599.6 4.9 copy-start.26
  599.6 4.9 copy-start.36
  727.6 10.3 copy-start.14
  738.0 4.9 copy-start.5
  738.0 4.9 copy-start.7
  738.0 4.9 copy-start.43
  743.9 5.1 copy-start.24
  744.8 5.4 copy-start.10
  748.8 3.0 copy-start.20
  749.1 2.7 copy-start.22
  751.8 5.4 copy-start.25
  751.8 5.5 copy-start.29
  757.4 8.2 copy-start.2
  765.6 234.7 %reduce-scatter.10.cloned.1.call-start = ((), (), s32[]{:S(2)}) async-start(), calls=%async_computation.14 | async-start | bytes 9732096 | tf_op jit(solution)/shard_map/reduce_scatter | solution.py:319
  770.7 407.1 %reduce-scatter.8.cloned.1.call-start = ((), (), s32[]{:S(2)}) async-start(), calls=%async_computation.13 | async-start | bytes 16220160 | tf_op jit(solution)/shard_map/reduce_scatter | solution.py:318
  779.4 1.3 copy-start.3
  779.4 591.7 %reduce-scatter.14.cloned.1.call-start = ((), (), s32[]{:S(2)}) async-start(), calls=%async_computation.16 | async-start | bytes 35389440 | tf_op jit(solution)/shard_map/reduce_scatter | solution.py:324
  795.5 1.3 copy-start.6
  795.5 931.4 %reduce-scatter.12.cloned.1.call-start = ((), (), s32[]{:S(2)}) async-start(), calls=%async_computation.15 | async-start | bytes 70778880 | tf_op jit(solution)/shard_map/reduce_scatter | solution.py:323
  821.8 1.1 copy-start.44
  821.8 38.5 %copy-start.40 = (f32[2,48]{1,0:T(2,128)S(1)}, f32[2,48]{1,0:T(2,128)}, u32[]{:S(2)}) copy-start(f32[2,48]{1,0:T(2,128)} %param.27) | copy-start | bytes 1156
  821.8 38.5 %copy-start.41 = (f32[2,48]{1,0:T(2,128)S(1)}, f32[2,48]{1,0:T(2,128)}, u32[]{:S(2)}) copy-start(f32[2,48]{1,0:T(2,128)} %param.32) | copy-start | bytes 1156
  821.8 38.5 %copy-start.42 = (f32[2,48]{1,0:T(2,128)S(1)}, f32[2,48]{1,0:T(2,128)}, u32[]{:S(2)}) copy-start(f32[2,48]{1,0:T(2,128)} %param.37) | copy-start | bytes 1156
  821.8 178.5 %copy-start.11 = (f32[48,1536]{1,0:T(8,128)S(1)}, f32[48,1536]{1,0:T(8,128)}, u32[]{:S(2)}) copy-start(f32[48,1536]{1,0:T(8,128)} %param.26) | copy-start | bytes 884740
  821.8 355.9 %copy-start.8 = (f32[48,2560]{1,0:T(8,128)S(1)}, f32[48,2560]{1,0:T(8,128)}, u32[]{:S(2)}) copy-start(f32[48,2560]{1,0:T(8,128)} %param.25) | copy-start | bytes 1474564
  821.8 355.9 %copy-start.16 = (f32[48,2560]{1,0:T(8,128)S(1)}, f32[48,2560]{1,0:T(8,128)}, u32[]{:S(2)}) copy-start(f32[48,2560]{1,0:T(8,128)} %param.30) | copy-start | bytes 1474564
  860.3 521.1 %copy-start.38 = (f32[2,48]{1,0:T(2,128)}, f32[2,48]{1,0:T(2,128)S(1)}, u32[]{:S(2)}) copy-start(f32[2,48]{1,0:T(2,128)S(1)} %copy.119) | copy-start | bytes 1156
  (9 other events, 7.4 us)
Sparse Core Ops, SparseCore 0:
  11.4 78.1 all-gather.5
  93.0 62.3 all-gather.7
  157.8 150.7 all-gather.9
  310.9 85.4 all-gather.11
  765.7 93.6 reduce-scatter.15
  865.8 134.4 reduce-scatter.9
  1007.9 169.8 reduce-scatter.7
  1182.4 188.7 reduce-scatter.13
  1375.8 351.0 reduce-scatter.11
where the time goes:
time: 1760 us; the launch traced here: 1750 us
  waiting for transfers between devices  1260 us (72%)
  blocking collectives  162 us (9%)
  matrix products  136 us (8%)
  other arithmetic  85.9 us (5%)
  local copies, waits for them, and re-layouts  82.2 us (5%)
    reduce_scatter x1, waiting for transfers between devices, shards(): lax.psum_scatter(grad_gate_up, 'dp', scatter_dimension=1, tiled=True)  346 us
    reduce_scatter x1, waiting for transfers between devices, shards(): lax.psum_scatter(grad_down, 'dp', scatter_dimension=1, tiled=True)  191 us
    reduce_scatter x1, waiting for transfers between devices, shards(): lax.psum_scatter(grad_qkv, ('dp', 'expert'), scatter_dimension=0, tiled=T...  175 us
    reduce_scatter x1, waiting for transfers between devices, shards(): lax.psum_scatter(grad_out, ('dp', 'expert'), scatter_dimension=0, tiled=T...  139 us
    all_to_all x1, waiting for transfers between devices, shards(): lax.all_to_all(grad_received.reshape(1, local_experts, slot_rows, MODEL_W...  126 us
    all_to_all x1, waiting for transfers between devices, shards(): lax.all_to_all(expert_out.reshape(1, local_experts, slot_rows, MODEL_WIDT...  115 us
    all_to_all x1, blocking collectives, shards(): lax.all_to_all(send_rows.reshape(groups_expert, local_experts, CAP, MODEL...  91.9 us
    all_to_all x1, waiting for transfers between devices, shards(): lax.all_to_all(send_grads.reshape(groups_expert, local_experts, CAP, MODE...  82.7 us
  transfers between devices with their start and end apart: 12, of which 10 were waited for; matrix products, arithmetic and copies ran while one was open for 11% of the time, Pallas kernels for 0%

commit v1 on v0

--- a/solution.py
+++ b/solution.py
@@ -1,6 +1,11 @@
+import functools
+
 import jax
 import jax.numpy as jnp
+import numpy as np
 from jax import lax
+from jax.experimental import pallas as pl
+from jax.experimental.pallas import tpu as pltpu
 from jax.sharding import PartitionSpec as P
 
 MODEL_WIDTH = 1536
@@ -142,7 +147,614 @@
     return (weight - step_rate * (update + shrink * weight), first, second)
 
 
-def shards(
+NARROW = jnp.bfloat16
+WIDE = jnp.float32
+DISTANCE = (0, 1, -1, 2)
+HOP_CORE, HOP_X, HOP_Y = 1, 2, 4
+
+
+def swap(rows, pick):
+    count = lax.axis_size("dp")
+    return lax.ppermute(rows, "dp", [(i, i ^ pick(i)) for i in range(count)])
+
+
+def first_hop(i):
+    return HOP_X if i & 1 else HOP_Y
+
+
+def second_hop(i):
+    return HOP_Y if i & 1 else HOP_X
+
+
+def swap_core(rows):
+    return swap(rows, lambda i: HOP_CORE)
+
+
+def swap_first(rows):
+    return swap(rows, first_hop)
+
+
+def swap_second(rows):
+    return swap(rows, second_hop)
+
+
+def turn(rows, step):
+    count = lax.axis_size("expert")
+    return lax.ppermute(rows, "expert", [(i, (i + step) % count) for i in range(count)])
+
+
+def gather_plane_last(block):
+    ahead, behind = turn(block, 1), turn(block, -1)
+    found = []
+    for part in (block, ahead, behind, turn(ahead, 1)):
+        pair = jnp.concatenate([part, swap_first(part)], 0)
+        found.append((pair, swap_second(pair)))
+    return found
+
+
+def gather_ring_middle(block):
+    pair = jnp.concatenate([block, swap_first(block)], 0)
+    ahead, behind = turn(pair, 1), turn(pair, -1)
+    return [(part, swap_second(part)) for part in (pair, ahead, behind, turn(ahead, 1))]
+
+
+def ring_sum(parts):
+    far = turn(parts[3].astype(NARROW), -1)
+    ahead = turn((parts[1] + far.astype(WIDE)).astype(NARROW), -1)
+    behind = turn(parts[2].astype(NARROW), 1)
+    return parts[0] + ahead.astype(WIDE) + behind.astype(WIDE)
+
+
+def scatter_plane_first(parts):
+    found = [None] * 4
+    for spot in (3, 1, 2, 0):
+        near, away = parts[spot]
+        near = near + swap_second(away).astype(WIDE)
+        half = near.shape[0] // 2
+        found[spot] = near[:half] + swap_first(near[half:].astype(NARROW)).astype(WIDE)
+    return ring_sum(found)
+
+
+def scatter_ring_middle(parts):
+    found = [None] * 4
+    for spot in (3, 1, 2, 0):
+        near, away = parts[spot]
+        found[spot] = near + swap_second(away).astype(WIDE)
+    total = ring_sum(found)
+    half = total.shape[0] // 2
+    return total[:half] + swap_first(total[half:].astype(NARROW)).astype(WIDE)
+
+
+def gathered_sources(count_dp, count_expert):
+    table = np.zeros((count_dp, count_expert, 4, 2, 2, 2), np.int32)
+    for i in range(count_dp):
+        for z in range(count_expert):
+            for spot, distance in enumerate(DISTANCE):
+                for second in range(2):
+                    for first in range(2):
+                        plane = i ^ (first_hop(i) * first) ^ (second_hop(i) * second)
+                        table[i, z, spot, second, first] = plane, (z - distance) % count_expert
+    return table.reshape(count_dp, count_expert, 16, 2)
+
+
+def split_three(values):
+    high = values.astype(NARROW)
+    left = values - high.astype(WIDE)
+    middle = left.astype(NARROW)
+    return [high, middle, (left - middle.astype(WIDE)).astype(NARROW)]
+
+
+def select_columns(values, chosen):
+    rows = values.shape[0]
+    parts = jnp.dot(
+        jnp.concatenate(split_three(values), 0), chosen, preferred_element_type=jnp.float32
+    )
+    return parts[:rows] + parts[rows : 2 * rows] + parts[2 * rows :]
+
+
+def parity_columns(rows, parity):
+    count = rows.shape[0]
+    query_total_width = QUERY_HEADS * HEAD_SIZE
+    key_columns_width = KEY_VALUE_HEADS * HEAD_SIZE
+    bounds = (
+        (0, query_total_width),
+        (query_total_width, query_total_width + key_columns_width),
+        (query_total_width + key_columns_width, query_total_width + 2 * key_columns_width),
+    )
+    return jnp.concatenate(
+        [
+            rows[:, low:high].reshape(count, KEY_VALUE_HEADS // 2, 2, -1)[:, :, parity]
+            .reshape(count, -1)
+            for low, high in bounds
+        ],
+        1,
+    )
+
+
+def join_parities(even, odd):
+    count = even.shape[0]
+    query_half = QUERY_HEADS * HEAD_SIZE // 2
+    key_half = KEY_VALUE_HEADS * HEAD_SIZE // 2
+    bounds = (
+        (0, query_half),
+        (query_half, query_half + key_half),
+        (query_half + key_half, query_half + 2 * key_half),
+    )
+    heads = KEY_VALUE_HEADS // 2
+    return jnp.concatenate(
+        [
+            jnp.stack(
+                [
+                    even[:, low:high].reshape(count, heads, -1),
+                    odd[:, low:high].reshape(count, heads, -1),
+                ],
+                2,
+            ).reshape(count, -1)
+            for low, high in bounds
+        ],
+        1,
+    )
+
+
+def split_head_group(projected_rows, cosine_table, sine_table):
+    sequences, length = projected_rows.shape[:2]
+    heads = KEY_VALUE_HEADS // 2
+    group = QUERY_HEADS // KEY_VALUE_HEADS
+    query_width = heads * group * HEAD_SIZE
+    key_width = heads * HEAD_SIZE
+    query_block = projected_rows[..., :query_width].reshape(
+        sequences, length, heads, group, HEAD_SIZE
+    )
+    key_rows = projected_rows[..., query_width : query_width + key_width].reshape(
+        sequences, length, heads, HEAD_SIZE
+    )
+    value_rows = projected_rows[..., query_width + key_width :].reshape(
+        sequences, length, heads, HEAD_SIZE
+    )
+    query_block = jax.vmap(lambda a: apply_rotary(a, cosine_table, sine_table, 2))(query_block)
+    key_rows = jax.vmap(lambda a: apply_rotary(a, cosine_table, sine_table, 1))(key_rows)
+    return (
+        query_block.astype(jnp.bfloat16),
+        key_rows.astype(jnp.bfloat16),
+        value_rows.astype(jnp.bfloat16),
+    )
+
+
+def expert_kernel(
+    near_ref,
+    away_ref,
+    near_grad_ref,
+    away_grad_ref,
+    route_ref,
+    gate_ref,
+    upper_ref,
+    down_ref,
+    near_out_ref,
+    away_out_ref,
+    near_back_ref,
+    away_back_ref,
+    hidden_ref,
+    grad_gate_ref,
+    grad_upper_ref,
+    rows_ref,
+    grads_ref,
+    out_ref,
+    back_ref,
+    *,
+    per_step,
+):
+    step = pl.program_id(0)
+    half = near_ref.shape[0]
+    width = near_ref.shape[1]
+
+    @pl.when(step == 0)
+    def _():
+        rows_ref[:half, :] = near_ref[...]
+        rows_ref[half:, :] = away_ref[...]
+        grads_ref[:half, :] = near_grad_ref[:, :width]
+        grads_ref[half:, :] = away_grad_ref[:, :width]
+        out_ref[...] = jnp.zeros_like(out_ref)
+        back_ref[...] = jnp.zeros_like(back_ref)
+
+    rows = rows_ref[...]
+    grads = grads_ref[...]
+    contract_last = (((1,), (1,)), ((), ()))
+    gate = jnp.dot(rows, gate_ref[...], preferred_element_type=jnp.float32)
+    upper = jnp.dot(rows, upper_ref[...], preferred_element_type=jnp.float32)
+    grad_hidden = lax.dot_general(
+        grads, down_ref[...], contract_last, preferred_element_type=jnp.float32
+    )
+    route = route_ref[...]
+    lanes = lax.broadcasted_iota(jnp.int32, route.shape, 1)
+    columns = gate.shape[1] // per_step
+    spread = []
+    for i in range(per_step):
+        one = jnp.sum(jnp.where(lanes == step * per_step + i, route, 0.0), 1, keepdims=True)
+        spread.append(jnp.broadcast_to(one, (route.shape[0], columns)))
+    weight = jnp.concatenate(spread, 1)
+    sigma = 1.0 / (1.0 + jnp.exp(-gate))
+    active = gate * sigma
+    hidden = (weight * active * upper).astype(jnp.bfloat16)
+    weighted = weight * grad_hidden
+    grad_gate = (weighted * upper * sigma * (1.0 + gate * (1.0 - sigma))).astype(jnp.bfloat16)
+    grad_upper = (weighted * active).astype(jnp.bfloat16)
+    hidden_ref[...] = hidden
+    grad_gate_ref[...] = grad_gate
+    grad_upper_ref[...] = grad_upper
+    out_ref[...] += jnp.dot(hidden, down_ref[...], preferred_element_type=jnp.float32)
+    back_ref[...] += lax.dot_general(
+        grad_gate, gate_ref[...], contract_last, preferred_element_type=jnp.float32
+    ) + lax.dot_general(
+        grad_upper, upper_ref[...], contract_last, preferred_element_type=jnp.float32
+    )
+
+    @pl.when(step == pl.num_programs(0) - 1)
+    def _():
+        near_out_ref[...] = out_ref[:half, :]
+        away_out_ref[...] = out_ref[half:, :].astype(jnp.bfloat16)
+        near_back_ref[...] = back_ref[:half, :]
+        away_back_ref[...] = back_ref[half:, :].astype(jnp.bfloat16)
+
+
+def expert_block(near, away, near_grad, away_grad, route, gate_w, upper_w, down_w, experts):
+    half, width = near.shape
+    total = gate_w.shape[1]
+    per_step = 2
+    steps = experts // per_step
+    columns = total // steps
+    whole = lambda a: pl.BlockSpec(a.shape, lambda i: (0, 0))
+    rows = 2 * half
+    f32 = lambda r, c: jax.ShapeDtypeStruct((r, c), jnp.float32)
+    b16 = lambda r, c: jax.ShapeDtypeStruct((r, c), jnp.bfloat16)
+    fixed = pl.BlockSpec((half, width), lambda i: (0, 0))
+    part = pl.BlockSpec((rows, columns), lambda i: (0, i))
+    flops = 2 * rows * width * total * 6
+    return pl.pallas_call(
+        functools.partial(expert_kernel, per_step=per_step),
+        grid=(steps,),
+        in_specs=[
+            whole(near),
+            whole(away),
+            whole(near_grad),
+            whole(away_grad),
+            whole(route),
+            pl.BlockSpec((width, columns), lambda i: (0, i)),
+            pl.BlockSpec((width, columns), lambda i: (0, i)),
+            pl.BlockSpec((columns, width), lambda i: (i, 0)),
+        ],
+        out_specs=[fixed] * 4 + [part] * 3,
+        out_shape=[f32(half, width), b16(half, width)] * 2 + [b16(rows, total)] * 3,
+        scratch_shapes=[
+            pltpu.VMEM((rows, width), jnp.bfloat16),
+            pltpu.VMEM((rows, width), jnp.bfloat16),
+            pltpu.VMEM((rows, width), jnp.float32),
+            pltpu.VMEM((rows, width), jnp.float32),
+        ],
+        compiler_params=pltpu.CompilerParams(vmem_limit_bytes=44 * 1024 * 1024),
+        cost_estimate=pl.CostEstimate(
+            flops=flops,
+            bytes_accessed=2 * (3 * width * total + 3 * rows * total + 10 * rows * width),
+            transcendentals=rows * total,
+        ),
+    )(near, away, near_grad, away_grad, route, gate_w, upper_w, down_w)
+
+
+def shards_moved(
+    tokens,
+    cotangent,
+    segments,
+    expert_ids,
+    route_weights,
+    w_qkv,
+    w_out,
+    gains,
+    w_gate_up,
+    w_down,
+    first_moment_projection,
+    first_out,
+    first_gains,
+    first_gate_up,
+    first_down,
+    second_moment_projection,
+    second_out,
+    second_gains,
+    second_gate_up,
+    second_down,
+):
+    sequence_length = segments.shape[1]
+    count_dp, count_expert = lax.axis_size("dp"), lax.axis_size("expert")
+    place_dp, place_expert = lax.axis_index("dp"), lax.axis_index("expert")
+    core = place_dp % 2
+    chip = place_dp // 2
+    chips = count_dp // 2
+    local_experts = EXPERTS // count_expert
+    owned = w_qkv.shape[0]
+    half_columns = w_qkv.shape[1] // 2
+    half_width = MODEL_WIDTH // 2
+    lane_pad = 128
+
+    narrow_qkv = w_qkv.astype(NARROW)
+    even_columns, odd_columns = parity_columns(narrow_qkv, 0), parity_columns(narrow_qkv, 1)
+    gain_columns = jnp.pad(gains.astype(NARROW).T, ((0, 0), (0, lane_pad - 2)))
+    kept = jnp.where(core == 0, even_columns, odd_columns)
+    given = jnp.where(core == 0, odd_columns, even_columns)
+    taken = swap_core(jnp.concatenate([given, gain_columns], 1))
+    narrow_out = w_out.astype(NARROW)
+    block = jnp.concatenate(
+        [
+            jnp.concatenate([jnp.concatenate([kept, gain_columns], 1), taken], 0),
+            jnp.concatenate([narrow_out[:, :half_width], narrow_out[:, half_width:]], 0),
+        ],
+        1,
+    )
+    attention_blocks = gather_ring_middle(block)
+
+    sources = jnp.asarray(gathered_sources(count_dp, count_expert))[place_dp, place_expert]
+    from_dp, from_expert = sources[:, 0], sources[:, 1]
+    row_in = jnp.arange(owned, dtype=jnp.int32)
+    feature = (
+        ((from_dp[:, None] ^ jnp.arange(2, dtype=jnp.int32)[None, :]) * count_expert
+         + from_expert[:, None])[:, :, None] * owned + row_in
+    ).reshape(-1)
+    head_feature = (
+        ((from_dp // 2 * count_expert + from_expert) * owned)[:, None] + row_in
+    ).reshape(-1)
+    places = jnp.arange(MODEL_WIDTH, dtype=jnp.int32)
+    to_gathered = (places[:, None] == feature[None, :]).astype(NARROW)
+    from_gathered = (feature[:, None] == places[None, :]).astype(NARROW)
+    head_places = places[: half_width]
+    heads_to_gathered = (head_places[:, None] == head_feature[None, :]).astype(NARROW)
+    heads_from_gathered = (head_feature[:, None] == head_places[None, :]).astype(NARROW)
+
+    ff_columns = FF // chips
+
+    def columns_of(which):
+        gate = lax.dynamic_slice_in_dim(w_gate_up, which * ff_columns, ff_columns, 2)
+        upper = lax.dynamic_slice_in_dim(w_gate_up, FF + which * ff_columns, ff_columns, 2)
+        return jnp.stack(
+            [
+                jnp.concatenate([a[e] for e in range(local_experts)], 1).astype(NARROW)
+                for a in (gate, upper)
+            ]
+        )
+
+    plane_rows = w_gate_up.shape[1]
+    share = local_experts * ff_columns
+    mine = jnp.zeros((chips, 2, plane_rows, share), NARROW)
+    for other in range(chips):
+        piece = columns_of(chip ^ other)
+        if other:
+            piece = swap(piece, lambda i, other=other: 2 * other)
+        mine = lax.dynamic_update_slice(mine, piece[None], (chip ^ other, 0, 0, 0))
+    theirs = swap_core(mine)
+    both = jnp.where(
+        core == 0, jnp.stack([mine, theirs], 1), jnp.stack([theirs, mine], 1)
+    )
+    gate_w = both[:, :, 0].reshape(MODEL_WIDTH, share)
+    upper_w = both[:, :, 1].reshape(MODEL_WIDTH, share)
+    down_mine = w_down.astype(NARROW)
+    down_theirs = swap_core(down_mine)
+    down_w = jnp.where(
+        core == 0,
+        jnp.concatenate([down_mine, down_theirs], 1),
+        jnp.concatenate([down_theirs, down_mine], 1),
+    ).reshape(share, MODEL_WIDTH)
+
+    routes = jnp.concatenate([expert_ids.astype(NARROW)] + split_three(route_weights), 1)
+    cotangent_blocks = gather_plane_last(
+        jnp.concatenate(
+            [
+                cotangent.astype(NARROW),
+                jnp.pad(routes, ((0, 0), (0, lane_pad - routes.shape[1]))),
+            ],
+            1,
+        )
+    )
+
+    def dense_route(rows):
+        ids = rows[:, :TOP].astype(jnp.int32)
+        parts = rows[:, TOP : 4 * TOP].astype(WIDE)
+        weights = parts[:, :TOP] + parts[:, TOP : 2 * TOP] + parts[:, 2 * TOP :]
+        local = place_expert * local_experts + jnp.arange(lane_pad, dtype=jnp.int32)
+        match = (ids[:, :, None] == local) & (jnp.arange(lane_pad) < local_experts)
+        return jnp.sum(jnp.where(match, weights[:, :, None], 0.0), 1)
+
+    cosine_table, sine_table = rotary_tables(sequence_length, HEAD_SIZE // 2)
+    inputs = tokens.astype(WIDE)
+    pair_tokens = jnp.concatenate([tokens, swap_core(tokens)], 0)
+    pair_segments = jnp.concatenate([segments, swap_core(segments)], 0)
+    scale_pair = norm_scale(pair_tokens.astype(WIDE))
+    scale_one = scale_pair[:sequence_length]
+    pair_gathered = jnp.dot(pair_tokens, to_gathered, preferred_element_type=jnp.float32)
+    blocks = [half for pair in attention_blocks for half in pair]
+    qkv_here = jnp.concatenate([b[:, :half_columns] for b in blocks], 0)
+    gain_here = jnp.concatenate(
+        [b[:, half_columns : half_columns + 2] for b in blocks], 0
+    ).T
+    out_here = jnp.concatenate(
+        [
+            b[:, half_columns + lane_pad :]
+            .reshape(2, 2, owned, half_width)
+            .transpose(0, 2, 1, 3)
+            .reshape(2 * owned, MODEL_WIDTH)
+            for b in blocks
+        ],
+        0,
+    )
+    gain_attn = gain_here[0].astype(WIDE)
+    gains_placed = jnp.dot(gain_here, from_gathered, preferred_element_type=jnp.float32)
+    gain_moe = gains_placed[1]
+    normed_one = (pair_gathered * scale_pair * gain_attn).astype(NARROW)
+    projected = jnp.dot(normed_one, qkv_here, preferred_element_type=jnp.float32)
+    query_block, key_rows, value_rows = split_head_group(
+        projected.reshape(2, sequence_length, -1), cosine_table, sine_table
+    )
+    attended, logsums = jax.vmap(attend)(query_block, key_rows, value_rows, pair_segments)
+    attended = attended.reshape(2 * sequence_length, half_width)
+    attended = jnp.dot(attended, heads_to_gathered, preferred_element_type=jnp.float32).astype(
+        NARROW
+    )
+    resid_parts = jnp.dot(attended, out_here, preferred_element_type=jnp.float32)
+    resid = inputs + resid_parts[:sequence_length] + swap_core(resid_parts[sequence_length:])
+    scale_two = norm_scale(resid)
+    normed_two = (resid * scale_two * gain_moe).astype(NARROW)
+
+    normed_blocks = gather_plane_last(normed_two)
+    out_parts, back_parts, hidden, grad_gate, grad_upper = [], [], [], [], []
+    for (near, away), (near_grad, away_grad) in zip(normed_blocks, cotangent_blocks):
+        route = jnp.concatenate(
+            [dense_route(g[:, MODEL_WIDTH:]) for g in (near_grad, away_grad)], 0
+        )
+        done = expert_block(
+            near, away, near_grad, away_grad, route, gate_w, upper_w, down_w, local_experts
+        )
+        out_parts.append((done[0], done[1]))
+        back_parts.append((done[2], done[3]))
+        hidden.append(done[4])
+        grad_gate.append(done[5])
+        grad_upper.append(done[6])
+    grad_normed_two = scatter_plane_first(back_parts)
+    out_tokens = resid + scatter_plane_first(out_parts)
+
+    rows_all = jnp.concatenate([half for pair in normed_blocks for half in pair], 0)
+    grads_all = jnp.concatenate(
+        [half[:, :MODEL_WIDTH] for pair in cotangent_blocks for half in pair], 0
+    )
+    over_rows = (((0,), (0,)), ((), ()))
+    grad_down_parts = lax.dot_general(
+        jnp.concatenate(hidden, 0), grads_all, over_rows, preferred_element_type=jnp.float32
+    ).reshape(local_experts, 2, ff_columns // 2, MODEL_WIDTH)
+    part_down = lax.dynamic_index_in_dim(grad_down_parts, core, 1, False) + swap_core(
+        lax.dynamic_index_in_dim(grad_down_parts, 1 - core, 1, False)
+    )
+    sums = []
+    for grads in (grad_gate, grad_upper):
+        full = lax.dot_general(
+            rows_all, jnp.concatenate(grads, 0), over_rows, preferred_element_type=jnp.float32
+        ).reshape(chips, 2, plane_rows, share)
+        theirs = swap_core(lax.dynamic_index_in_dim(full, 1 - core, 1, False).astype(NARROW))
+        sums.append(lax.dynamic_index_in_dim(full, core, 1, False) + theirs.astype(WIDE))
+    sums = jnp.stack(sums, 1).astype(NARROW)
+    collected = jnp.zeros((chips, 2, plane_rows, share), NARROW)
+    for other in range(chips):
+        piece = lax.dynamic_index_in_dim(sums, chip ^ other, 0, False)
+        if other:
+            piece = swap(piece, lambda i, other=other: 2 * other)
+        collected = lax.dynamic_update_slice(collected, piece[None], (chip ^ other, 0, 0, 0))
+    part_gate_up = (
+        collected.reshape(chips, 2, plane_rows, local_experts, ff_columns)
+        .transpose(3, 2, 1, 0, 4)
+        .reshape(local_experts, plane_rows, 2 * FF)
+        .astype(WIDE)
+    )
+
+    hat_two = grad_normed_two * gain_moe
+    grad_gain_moe = jnp.sum(grad_normed_two * resid * scale_two, 0)
+    grad_resid = cotangent + scale_two * (
+        hat_two - resid * scale_two**2 * jnp.mean(hat_two * resid, -1, keepdims=True)
+    )
+    grad_resid_half = grad_resid.astype(NARROW)
+    pair_grads = jnp.concatenate([grad_resid_half, swap_core(grad_resid_half)], 0)
+    grad_out = lax.dot_general(attended, pair_grads, over_rows, preferred_element_type=jnp.float32)
+    attended_gradient = lax.dot_general(
+        pair_grads, out_here, (((1,), (1,)), ((), ())), preferred_element_type=jnp.float32
+    ).astype(NARROW)
+    attended_gradient = (
+        jnp.dot(attended_gradient, heads_from_gathered, preferred_element_type=jnp.float32)
+        .astype(NARROW)
+        .reshape(query_block.shape)
+    )
+    grad_query, grad_keys, grad_values = jax.vmap(attend_back)(
+        query_block, key_rows, value_rows, pair_segments, logsums, attended_gradient
+    )
+    joined = jax.vmap(lambda a, b, c: join_grads(a, b, c, cosine_table, sine_table))(
+        grad_query, grad_keys, grad_values
+    ).reshape(2 * sequence_length, -1)
+    grad_qkv = lax.dot_general(normed_one, joined, over_rows, preferred_element_type=jnp.float32)
+    grad_normed_parts = lax.dot_general(
+        joined, qkv_here, (((1,), (1,)), ((), ())), preferred_element_type=jnp.float32
+    )
+    grad_gain_attn = jnp.sum(grad_normed_parts * pair_gathered * scale_pair, 0)
+    gain_parts = jnp.stack(
+        [grad_gain_attn, select_columns(grad_gain_moe[None], to_gathered)[0]], 1
+    )
+    attention_parts = jnp.concatenate(
+        [
+            grad_qkv,
+            jnp.pad(gain_parts, ((0, 0), (0, lane_pad - 2))),
+            grad_out.reshape(-1, owned, 2, half_width)
+            .transpose(0, 2, 1, 3)
+            .reshape(MODEL_WIDTH, half_width),
+        ],
+        1,
+    ).reshape(4, 2, 4 * owned, -1)
+    summed = scatter_ring_middle(
+        [(attention_parts[i, 0], attention_parts[i, 1].astype(NARROW)) for i in range(4)]
+    )
+    here, there = summed[:owned], summed[owned:]
+    part_out = jnp.concatenate(
+        [here[:, half_columns + lane_pad :], there[:, half_columns + lane_pad :]], 1
+    )
+    there = swap_core(there[:, : half_columns + lane_pad])
+    part_gains = (
+        here[:, half_columns : half_columns + 2] + there[:, half_columns : half_columns + 2]
+    ).T
+    here, there = here[:, :half_columns], there[:, :half_columns]
+    part_qkv = join_parities(
+        jnp.where(core == 0, here, there), jnp.where(core == 0, there, here)
+    )
+
+    grad_normed_parts = select_columns(grad_normed_parts, from_gathered)
+    grad_normed_one = grad_normed_parts[:sequence_length] + swap_core(
+        grad_normed_parts[sequence_length:]
+    )
+    hat_one = grad_normed_one * gains_placed[0]
+    grad_tokens = grad_resid + scale_one * (
+        hat_one - inputs * scale_one**2 * jnp.mean(hat_one * inputs, -1, keepdims=True)
+    )
+
+    new_qkv, new_first_qkv, new_second_qkv = adam_step(
+        w_qkv, part_qkv, first_moment_projection, second_moment_projection, learn_rate, weight_decay
+    )
+    new_out, new_first_out, new_second_out = adam_step(
+        w_out, part_out, first_out, second_out, out_rate, weight_decay
+    )
+    new_gains, new_first_gains, new_second_gains = adam_step(
+        gains, part_gains, first_gains, second_gains, gain_rate, 0.0
+    )
+    new_gate_up, new_first_gate_up, new_second_gate_up = adam_step(
+        w_gate_up, part_gate_up, first_gate_up, second_gate_up, learn_rate, weight_decay
+    )
+    new_down, new_first_down, new_second_down = adam_step(
+        w_down, part_down, first_down, second_down, learn_rate, weight_decay
+    )
+    return (
+        out_tokens,
+        grad_tokens,
+        part_qkv,
+        part_out,
+        part_gains,
+        part_gate_up,
+        part_down,
+        new_qkv,
+        new_out,
+        new_gains,
+        new_gate_up,
+        new_down,
+        new_first_qkv,
+        new_first_out,
+        new_first_gains,
+        new_first_gate_up,
+        new_first_down,
+        new_second_qkv,
+        new_second_out,
+        new_second_gains,
+        new_second_gate_up,
+        new_second_down,
+    )
+
+
+def shards_plain(
     tokens,
     cotangent,
     segments,
@@ -365,8 +977,9 @@
 
 
 def solution(mesh):
+    by_heads = mesh.shape["dp"] == KEY_VALUE_HEADS and mesh.shape["expert"] == 4
     return jax.shard_map(
-        shards,
+        shards_moved if by_heads else shards_plain,
         mesh=mesh,
         in_specs=(
             P(("dp", "expert"), None),

time: 1760 us -> 865 us (0.49)
  waiting for transfers between devices: 1260 us -> 166 us
  local copies, waits for them, and re-layouts: 82.2 us -> 279 us
  blocking collectives: 162 us -> 0 us
  starting transfers between devices: 16.5 us -> 95.8 us
  Pallas kernels: 0 us -> 75.6 us
  other arithmetic: 85.9 us -> 146 us
  matrix products: 136 us -> 86.4 us
    reduce_scatter x4 -> x0, waiting for transfers between devices: 851 us -> none  [the longest x1 346 us: shards(): lax.psum_scatter(grad_gate_up, 'dp', scatter_dimension=1, tiled=True)]
    all_to_all x3 -> x0, waiting for transfers between devices: 324 us -> none  [the longest x1 126 us: shards(): lax.all_to_all(grad_received.reshape(1, local_experts, slot_rows, MODEL_W...]
    ppermute x0 -> x78, waiting for transfers between devices: none -> 166 us  [the longest x18 98 us: turn(): lax.ppermute(rows, 'expert', [(i, (i + step) % count) for i in range(coun...]
    ppermute x0 -> x78, starting transfers between devices: none -> 95.8 us  [the longest x60 54.9 us: swap(): return lax.ppermute(rows, 'dp', [(i, i ^ pick(i)) for i in range(count)])]
    all_to_all x1 -> x0, blocking collectives: 91.9 us -> none  [shards(): lax.all_to_all(send_rows.reshape(groups_expert, local_experts, CAP, MODEL...]
    unnamed x95 -> x372, local copies, waits for them, and re-layouts: 9.28 us -> 99.7 us
    pallas_call x0 -> x4, Pallas kernels: none -> 75.6 us  [expert_block(): pl.pallas_call(functools.partial(expert_kernel, per_step=per_step), grid=...]
    all_gather x1 -> x0, blocking collectives: 69.7 us -> none  [shards(): lax.all_gather(gains.astype(jnp.bfloat16), ('dp', 'expert'), axis=1, tile...]
  transfers between devices with their start and end apart: 12 -> 78, of which waited for: 10 -> 23; matrix products, arithmetic and copies ran while one was open for 11% -> 57% of each run, Pallas kernels for 0% -> 9%
where the time goes in v1:
time: 865 us; the launch traced here: 852 us
  local copies, waits for them, and re-layouts  279 us (32%)
  waiting for transfers between devices  166 us (19%)
  other arithmetic  146 us (17%)
  starting transfers between devices  95.8 us (11%)
  matrix products  86.4 us (10%)
  Pallas kernels  75.6 us (9%)
    unnamed x372, local copies, waits for them, and re-layouts  99.7 us
    ppermute x18, waiting for transfers between devices, turn(): lax.ppermute(rows, 'expert', [(i, (i + step) % count) for i in range(coun...  98 us
    pallas_call x4, Pallas kernels, expert_block(): pl.pallas_call(functools.partial(expert_kernel, per_step=per_step), grid=...  75.6 us
    ppermute x60, waiting for transfers between devices, swap(): return lax.ppermute(rows, 'dp', [(i, i ^ pick(i)) for i in range(count)])  68.4 us
    ppermute x60, starting transfers between devices, swap(): return lax.ppermute(rows, 'dp', [(i, i ^ pick(i)) for i in range(count)])  54.9 us
    ppermute x18, starting transfers between devices, turn(): lax.ppermute(rows, 'expert', [(i, (i + step) % count) for i in range(coun...  40.9 us
    sub x5, other arithmetic, adam_step(): return (weight - step_rate * (update + shrink * weight), first, second)  38.1 us
    convert_element_type x3, local copies, waits for them, and re-layouts, shards_moved(): part_gate_up = collected.reshape(chips, 2, plane_rows, local_experts, ff_...  29.7 us
  transfers between devices with their start and end apart: 78, of which 23 were waited for; matrix products, arithmetic and copies ran while one was open for 57% of the time, Pallas kernels for 9%

profile of v1, /device:TPU:0, one launch (start us, length us, event | category | flops | bytes accessed | tf_op | source)
XLA Modules:
  0.0 852.1 jit_solution(89053773557503381)
XLA Ops:
  24.0 4.1 dynamic-slice_convert_fusion.1
  107.0 35.5 %collective-permute-done.2 = bf16[96,2176]{1,0:T(8,128)(2,1)S(1)} collective-permute-done((bf16[96,2176]{1,0:T(8,128)(2,1)S(1)}, bf16[96,2176]{1,0:T(8,128)(2,1)S(1)}, u32[]{:S(2)}, u32[]{:S(2)}) %collective-permute-start.2) | collective-permute-done | bytes 417824 | tf_op jit(solution)/shard_map/ppermute | solution.py:158
  153.2 6.1 collective-permute-done.27
  160.9 9.4 %collective-permute-done.34 = bf16[128,1664]{1,0:T(8,128)(2,1)S(1)} collective-permute-done((bf16[128,1664]{1,0:T(8,128)(2,1)}, bf16[128,1664]{1,0:T(8,128)(2,1)S(1)}, u32[]{:S(2)}, u32[]{:S(2)}) %collective-permute-start.34) | collective-permute-done | bytes 426016 | tf_op jit(solution)/shard_map/ppermute | solution.py:183
  183.6 3.9 collective-permute-done.35
  194.5 13.1 %collective-permute-done.6 = bf16[192,2176]{1,0:T(8,128)(2,1)S(1)} collective-permute-done((bf16[192,2176]{1,0:T(8,128)(2,1)}, bf16[192,2176]{1,0:T(8,128)(2,1)S(1)}, u32[]{:S(2)}, u32[]{:S(2)}) %collective-permute-start.6) | collective-permute-done | bytes 835616 | tf_op jit(solution)/shard_map/ppermute | solution.py:183
  239.8 5.8 maximum_select_fusion.1
  247.7 5.7 select_reduce_fusion.3
  271.8 3.9 fusion.158
  305.4 3.9 collective-permute-start.41
  309.4 9.2 %collective-permute-done.23 = bf16[128,1536]{1,0:T(8,128)(2,1)S(1)} collective-permute-done((bf16[128,1536]{1,0:T(8,128)(2,1)S(1)}, bf16[128,1536]{1,0:T(8,128)(2,1)S(1)}, u32[]{:S(2)}, u32[]{:S(2)}) %collective-permute-start.23) | collective-permute-done | bytes 393248 | tf_op jit(solution)/shard_map/ppermute | solution.py:183
  320.6 5.0 collective-permute-done.41
  327.1 10.5 %collective-permute-done.31 = bf16[128,1536]{1,0:T(8,128)(2,1)} collective-permute-done((bf16[128,1536]{1,0:T(8,128)(2,1)S(1)}, bf16[128,1536]{1,0:T(8,128)(2,1)}, u32[]{:S(2)}, u32[]{:S(2)}) %collective-permute-start.31) | collective-permute-done | bytes 393248 | tf_op jit(solution)/shard_map/ppermute | solution.py:183
  338.3 7.8 maximum_select_fusion
  354.7 18.5 %shard_map.372 = (f32[256,1536]{1,0:T(8,128)}, bf16[256,1536]{1,0:T(8,128)(2,1)S(1)}, f32[256,1536]{1,0:T(8,128)}, bf16[256,1536]{1,0:T(8,128)(2,1)S(1)}, bf16[5...) custom-call(bf16[256,1536]{1,0:T(8,128)(2,1)S(1)} %pad_maximum_fusion.6.near_ref, ...), custom_call_target="tpu_custom_call" | custom-call | flops 12079595520 | bytes 31457280 | tf_op jit(solution)/shard_map/pallas_call | solution.py:412
  380.7 19.0 %shard_map.373 = (f32[256,1536]{1,0:T(8,128)}, bf16[256,1536]{1,0:T(8,128)(2,1)S(1)}, f32[256,1536]{1,0:T(8,128)}, bf16[256,1536]{1,0:T(8,128)(2,1)S(1)}, bf16[5...) custom-call(bf16[256,1536]{1,0:T(8,128)(2,1)S(1)} %get-tuple-element.323.near_ref, ...), custom_call_target="tpu_custom_call" | custom-call | flops 12079595520 | bytes 31457280 | tf_op jit(solution)/shard_map/pallas_call | solution.py:412
  412.7 19.2 %shard_map.375 = (f32[256,1536]{1,0:T(8,128)}, bf16[256,1536]{1,0:T(8,128)(2,1)S(1)}, f32[256,1536]{1,0:T(8,128)}, bf16[256,1536]{1,0:T(8,128)(2,1)S(1)}, bf16[5...) custom-call(bf16[256,1536]{1,0:T(8,128)(2,1)S(1)} %get-tuple-element.319.near_ref, ...), custom_call_target="tpu_custom_call" | custom-call | flops 12079595520 | bytes 31457280 | tf_op jit(solution)/shard_map/pallas_call | solution.py:412
  437.9 19.0 %shard_map.374 = (f32[256,1536]{1,0:T(8,128)}, bf16[256,1536]{1,0:T(8,128)(2,1)S(1)}, f32[256,1536]{1,0:T(8,128)}, bf16[256,1536]{1,0:T(8,128)(2,1)S(1)}, bf16[5...) custom-call(bf16[256,1536]{1,0:T(8,128)(2,1)S(1)} %get-tuple-element.315.near_ref, ...), custom_call_target="tpu_custom_call" | custom-call | flops 12079595520 | bytes 31457280 | tf_op jit(solution)/shard_map/pallas_call | solution.py:412
  457.8 13.2 %fusion.22 = f32[1280,1536]{1,0:T(8,128)} fusion(bf16[2048,1536]{1,0:T(8,128)(2,1)} %slice_dynamic-update-slice_fusion, bf16[512,1280]{1,0:T(8,128)(2,1)S(1)} %get-tuple-element.77, bf16[512,1280]{1,0:T(8,128)(2,1)S(1)} %get-tuple-element.76, bf16[512,1280]{1,0:T(8,128)(2,1)S(1)} %get-tuple-element.75, bf16[512,1280]{1,0:T(8,128)(2,1)S(1)} %get-tuple-element.74), kind=kOutput, calls=%fused_computation.38 | convolution fusion | flops 8074035200 | bytes 19398656 | tf_op jit(solution)/shard_map/dot_general | solution.py:624
  471.9 13.0 %fusion.6 = f32[1536,1280]{1,0:T(8,128)} fusion(bf16[2048,1536]{1,0:T(8,128)(2,1)} %constant_dynamic-update-slice_fusion.107, bf16[512,1280]{1,0:T(8,128)(2,1)} %copy-done.12, bf16[512,1280]{1,0:T(8,128)(2,1)S(1)} %copy-done.11, bf16[512,1280]{1,0:T(8,128)(2,1)S(1)} %copy-done.9, bf16[512,1280]{1,0:T(8,128)(2,1)S(1)} %copy-done.5), kind=kOutput, calls=%fused_computation.22 | convolution fusion | flops 8074035200 | bytes 19398656 | tf_op jit(solution)/shard_map/dot_general | solution.py:632
  484.9 12.7 %fusion.14 = f32[1536,1280]{1,0:T(8,128)} fusion(bf16[2048,1536]{1,0:T(8,128)(2,1)} %constant_dynamic-update-slice_fusion.107, bf16[512,1280]{1,0:T(8,128)(2,1)S(1)} %get-tuple-element.73, bf16[512,1280]{1,0:T(8,128)(2,1)S(1)} %get-tuple-element.72, bf16[512,1280]{1,0:T(8,128)(2,1)S(1)} %copy-done.7, bf16[512,1280]{1,0:T(8,128)(2,1)S(1)} %copy-done.3), kind=kOutput, calls=%fused_computation.30 | convolution fusion | flops 8074035200 | bytes 19398656 | tf_op jit(solution)/shard_map/dot_general | solution.py:632
  513.1 5.6 collective-permute-done.59
  522.0 6.1 collective-permute-done.38
  529.6 6.3 collective-permute-done.55
  539.2 6.0 collective-permute-done.39
  555.4 4.3 collective-permute-start.57
  562.4 7.1 collective-permute-done.60
  569.4 10.5 %collective-permute-start.40 = (bf16[128,1536]{1,0:T(8,128)(2,1)S(1)}, bf16[128,1536]{1,0:T(8,128)(2,1)S(1)}, u32[]{:S(2)}, u32[]{:S(2)}) collective-permute-start(bf16[128,1536]{1,0:T(8,128)(2,1)S(1)} %fusion.106), channel_id=1, source_target_pairs={{0,3},{1,0},{2,1},{3,2},{4,7},{5,4},{6,5},{7,6},{8,11},{9,8},{10,9... | collective-permute-start | bytes 1179656 | tf_op jit(solution)/shard_map/ppermute | solution.py:183
  587.7 4.6 collective-permute-done.40
  614.8 4.9 multiply_reduce_fusion
  619.7 4.5 fusion.157
  625.4 4.0 fusion.116
  629.4 7.0 reshape.1479
  636.4 5.1 copy.495
  641.5 6.2 copy.498
  647.7 10.5 %copy.496 = f32[4,2,192,1280]{2,3,1,0:T(8,128)} copy(f32[4,2,192,1280]{3,2,1,0:T(8,128)} %bitcast.280) | data formatting | bytes 15728640 | tf_op jit(solution)/shard_map/concatenate | solution.py:681
  658.2 7.8 fusion.159
  668.2 6.3 pad_maximum_fusion
  674.5 5.7 fusion.1
  701.7 8.2 copy.525
  709.9 11.4 %copy.526 = f32[10,192,2,4,128]{4,3,2,1,0:T(4,128)} copy(f32[10,192,2,4,128]{1,4,0,2,3:T(8,128)} %bitcast.281) | data formatting | bytes 15728640 | tf_op jit(solution)/shard_map/convert_element_type | solution.py:648
  721.3 10.1 %reshape.1487 = f32[10,192,1024]{2,1,0:T(8,128)} reshape(f32[10,192,2,4,128]{4,3,2,1,0:T(4,128)} %copy.526) | data formatting | bytes 15728640 | tf_op jit(solution)/shard_map/convert_element_type | solution.py:648
  738.2 5.4 collective-permute-start.66
  743.6 20.9 %multiply_subtract_fusion = (f32[10,192,1024]{2,1,0:T(8,128)}, f32[10,192,1024]{2,1,0:T(8,128)}, f32[10,192,1024]{2,1,0:T(8,128)}) fusion(f32[10,192,1024]{2,1,0:T(8,128)} %param.29, f32[10,192,1024]{2,1,0:T(8,128)} %reshape.1487, f32[10,192,1024]{2,1,0:T(8,128)} %param.34, f32[10,192,1024]{2,1,0:T(8,128)} %param.39), kind=kLoop, calls=%fused_computation.11 | loop fusion | flops 29491200 | bytes 55050240 | tf_op jit(solution)/shard_map/sub | solution.py:147
  771.9 4.9 fusion.52
  789.9 15.2 %collective-permute-done.69 = bf16[192,2176]{1,0:T(8,128)(2,1)} collective-permute-done((bf16[192,2176]{1,0:T(8,128)(2,1)}, bf16[192,2176]{1,0:T(8,128)(2,1)}, u32[]{:S(2)}, u32[]{:S(2)}) %collective-permute-start.69) | collective-permute-done | bytes 835616 | tf_op jit(solution)/shard_map/ppermute | solution.py:183
  807.4 11.4 %collective-permute-done.67 = bf16[192,2176]{1,0:T(8,128)(2,1)} collective-permute-done((bf16[192,2176]{1,0:T(8,128)(2,1)}, bf16[192,2176]{1,0:T(8,128)(2,1)}, u32[]{:S(2)}, u32[]{:S(2)}) %collective-permute-start.67) | collective-permute-done | bytes 835616 | tf_op jit(solution)/shard_map/ppermute | solution.py:183
  825.0 12.9 %multiply_subtract_fusion.1 = (f32[10,64,1536]{2,1,0:T(8,128)}, f32[10,64,1536]{2,1,0:T(8,128)}, f32[10,64,1536]{2,1,0:T(8,128)}, f32[10,64,1536]{2,1,0:T(8,128)}) fusion(f32[10,64,1536]{2,1,0:T(8,128)} %param.30, f32[10,64,1536]{2,1,0:T(8,128)} %param.35, f32[10,64,1536]{2,1,0:T(8,128)} %param.40, f32[10,64,1536]{2,1,0:T(8,128)} %collective-permute-done.77, ...), kind=kLoop, calls=%fused_computation.59 | loop fusion | flops 15728640 | bytes 35389444 | tf_op jit(solution)/shard_map/sub | solution.py:147
  (787 shorter events, 397.6 us)
Async XLA Ops:
  4.9 99.6 %collective-permute-start.26 = (bf16[128,1664]{1,0:T(8,128)(2,1)}, bf16[128,1664]{1,0:T(8,128)(2,1)}, u32[]{:S(2)}, u32[]{:S(2)}) collective-permute-start(bf16[128,1664]{1,0:T(8,128)(2,1)} %pad_maximum_fusion.12), channel_id=1, source_target_pairs={{0,1},{1,2},{2,3},{3,0},{4,5},{5,6},{6,7},{7,4},{8,9},{9,10},{10,1... | collective-permute-start | bytes 1277960 | tf_op jit(solution)/shard_map/ppermute | solution.py:183
  7.9 93.9 %collective-permute-start.44 = (bf16[128,1664]{1,0:T(8,128)(2,1)}, bf16[128,1664]{1,0:T(8,128)(2,1)}, u32[]{:S(2)}, u32[]{:S(2)}) collective-permute-start(bf16[128,1664]{1,0:T(8,128)(2,1)} %pad_maximum_fusion.12), channel_id=1, source_target_pairs={{0,3},{1,0},{2,1},{3,2},{4,7},{5,4},{6,5},{7,6},{8,11},{9,8},{10,9... | collective-permute-start | bytes 1277960 | tf_op jit(solution)/shard_map/ppermute | solution.py:183
  10.0 88.8 %collective-permute-start.14 = (bf16[128,1664]{1,0:T(8,128)(2,1)}, bf16[128,1664]{1,0:T(8,128)(2,1)}, u32[]{:S(2)}, u32[]{:S(2)}) collective-permute-start(bf16[128,1664]{1,0:T(8,128)(2,1)} %pad_maximum_fusion.12), channel_id=1, source_target_pairs={{0,16},{4,12},{8,24},{12,4},{16,0},{20,28},{24,8},{28,20},{1,17},{... | collective-permute-start | bytes 1277960 | tf_op jit(solution)/shard_map/ppermute | solution.py:158
  11.7 78.5 %collective-permute-start.10 = (s32[1,128]{1,0:T(1,128)}, s32[1,128]{1,0:T(1,128)S(1)}, u32[]{:S(2)}, u32[]{:S(2)}) collective-permute-start(s32[1,128]{1,0:T(1,128)} %param.23), channel_id=1, source_target_pairs={{0,4},{4,0},{8,12},{12,8},{16,20},{20,16},{24,28},{28,24},{1,5},{5... | collective-permute-start | bytes 1544 | tf_op jit(solution)/shard_map/ppermute | solution.py:158
  11.7 80.0 %collective-permute-start = (bf16[128,1536]{1,0:T(8,128)(2,1)}, bf16[128,1536]{1,0:T(8,128)(2,1)}, u32[]{:S(2)}, u32[]{:S(2)}) collective-permute-start(bf16[128,1536]{1,0:T(8,128)(2,1)} %param.21), channel_id=1, source_target_pairs={{0,4},{4,0},{8,12},{12,8},{16,20},{20,16},{24,28},{28,24},{1,5},{5... | collective-permute-start | bytes 1179656 | tf_op jit(solution)/shard_map/ppermute | solution.py:158
  91.5 147.3 %collective-permute-start.20 = (bf16[10,64,1536]{2,1,0:T(8,128)(2,1)}, bf16[10,64,1536]{2,1,0:T(8,128)(2,1)}, u32[]{:S(2)}, u32[]{:S(2)}) collective-permute-start(bf16[10,64,1536]{2,1,0:T(8,128)(2,1)} %convert_element_type.484), channel_id=1, source_target_pairs={{0,4},{4,0},{8,12},{12,8},{16,20},{20,16},{24,28},{28,24},{1,5},{5... | collective-permute-start | bytes 5898248 | tf_op jit(solution)/shard_map/ppermute | solution.py:158
  91.7 87.1 %collective-permute-start.18 = (bf16[2,192,1280]{2,1,0:T(8,128)(2,1)}, bf16[2,192,1280]{2,1,0:T(8,128)(2,1)}, u32[]{:S(2)}, u32[]{:S(2)}) collective-permute-start(bf16[2,192,1280]{2,1,0:T(8,128)(2,1)} %pad_maximum_fusion.3), channel_id=1, source_target_pairs={{0,24},{4,28},{8,16},{12,20},{16,8},{20,12},{24,0},{28,4},{1,25},{... | collective-permute-start | bytes 2949128 | tf_op jit(solution)/shard_map/ppermute | solution.py:158
  98.8 73.3 %collective-permute-start.16 = (bf16[2,192,1280]{2,1,0:T(8,128)(2,1)}, bf16[2,192,1280]{2,1,0:T(8,128)(2,1)}, u32[]{:S(2)}, u32[]{:S(2)}) collective-permute-start(bf16[2,192,1280]{2,1,0:T(8,128)(2,1)} %pad_maximum_fusion.1), channel_id=1, source_target_pairs={{0,8},{4,12},{8,0},{12,4},{16,24},{20,28},{24,16},{28,20},{1,9},{5... | collective-permute-start | bytes 2949128 | tf_op jit(solution)/shard_map/ppermute | solution.py:158
  101.9 72.5 %collective-permute-start.17 = (bf16[2,192,1280]{2,1,0:T(8,128)(2,1)}, bf16[2,192,1280]{2,1,0:T(8,128)(2,1)}, u32[]{:S(2)}, u32[]{:S(2)}) collective-permute-start(bf16[2,192,1280]{2,1,0:T(8,128)(2,1)} %pad_maximum_fusion.2), channel_id=1, source_target_pairs={{0,16},{4,20},{8,24},{12,28},{16,0},{20,4},{24,8},{28,12},{1,17},{... | collective-permute-start | bytes 2949128 | tf_op jit(solution)/shard_map/ppermute | solution.py:158
  104.5 37.9 %collective-permute-start.2 = (bf16[96,2176]{1,0:T(8,128)(2,1)S(1)}, bf16[96,2176]{1,0:T(8,128)(2,1)S(1)}, u32[]{:S(2)}, u32[]{:S(2)}) collective-permute-start(bf16[96,2176]{1,0:T(8,128)(2,1)S(1)} %maximum_maximum_fusion), channel_id=1, source_target_pairs={{0,16},{4,12},{8,24},{12,4},{16,0},{20,28},{24,8},{28,20},{1,17},{... | collective-permute-start | bytes 1253384 | tf_op jit(solution)/shard_map/ppermute | solution.py:158
  172.1 35.6 %collective-permute-start.6 = (bf16[192,2176]{1,0:T(8,128)(2,1)}, bf16[192,2176]{1,0:T(8,128)(2,1)S(1)}, u32[]{:S(2)}, u32[]{:S(2)}) collective-permute-start(bf16[192,2176]{1,0:T(8,128)(2,1)} %pad_maximum_fusion.5), channel_id=1, source_target_pairs={{0,3},{1,0},{2,1},{3,2},{4,7},{5,4},{6,5},{7,6},{8,11},{9,8},{10,9... | collective-permute-start | bytes 2506760 | tf_op jit(solution)/shard_map/ppermute | solution.py:183
  174.3 38.5 %collective-permute-start.4 = (bf16[192,2176]{1,0:T(8,128)(2,1)}, bf16[192,2176]{1,0:T(8,128)(2,1)}, u32[]{:S(2)}, u32[]{:S(2)}) collective-permute-start(bf16[192,2176]{1,0:T(8,128)(2,1)} %pad_maximum_fusion.5), channel_id=1, source_target_pairs={{0,1},{1,2},{2,3},{3,0},{4,5},{5,6},{6,7},{7,4},{8,9},{9,10},{10,1... | collective-permute-start | bytes 2506760 | tf_op jit(solution)/shard_map/ppermute | solution.py:183
  187.5 29.6 %collective-permute-start.3 = (bf16[192,2176]{1,0:T(8,128)(2,1)}, bf16[192,2176]{1,0:T(8,128)(2,1)}, u32[]{:S(2)}, u32[]{:S(2)}) collective-permute-start(bf16[192,2176]{1,0:T(8,128)(2,1)} %pad_maximum_fusion.5), channel_id=1, source_target_pairs={{0,8},{4,20},{8,0},{12,28},{16,24},{20,4},{24,16},{28,12},{1,9},{5... | collective-permute-start | bytes 2506760 | tf_op jit(solution)/shard_map/ppermute | solution.py:158
  189.2 38.5 %collective-permute-start.28 = (bf16[256,1664]{1,0:T(8,128)(2,1)S(1)}, bf16[256,1664]{1,0:T(8,128)(2,1)}, u32[]{:S(2)}, u32[]{:S(2)}) collective-permute-start(bf16[256,1664]{1,0:T(8,128)(2,1)S(1)} %constant_dynamic-update-slice_fusion.92.near_grad_ref), channel_id=1, source_target_pairs={{0,8},{4,20},{8,0},{12,28},{16,24},{20,4},{24,16},{28,12},{1,9},{5... | collective-permute-start | bytes 2555912 | tf_op jit(solution)/shard_map/ppermute | solution.py:158
  207.6 25.3 %collective-permute-start.46 = (bf16[256,1664]{1,0:T(8,128)(2,1)S(1)}, bf16[256,1664]{1,0:T(8,128)(2,1)}, u32[]{:S(2)}, u32[]{:S(2)}) collective-permute-start(bf16[256,1664]{1,0:T(8,128)(2,1)S(1)} %constant_dynamic-update-slice_fusion.100.near_grad_ref), channel_id=1, source_target_pairs={{0,8},{4,20},{8,0},{12,28},{16,24},{20,4},{24,16},{28,12},{1,9},{5... | collective-permute-start | bytes 2555912 | tf_op jit(solution)/shard_map/ppermute | solution.py:158
  212.8 125.5 %collective-permute-start.19 = (bf16[4,2,192,1280]{3,2,1,0:T(8,128)(2,1)}, bf16[4,2,192,1280]{3,2,1,0:T(8,128)(2,1)}, u32[]{:S(2)}, u32[]{:S(2)}) collective-permute-start(bf16[4,2,192,1280]{3,2,1,0:T(8,128)(2,1)} %bitcast_dynamic-update-slice_fusion.3), channel_id=1, source_target_pairs={{0,4},{4,0},{8,12},{12,8},{16,20},{20,16},{24,28},{28,24},{1,5},{5... | collective-permute-start | bytes 11796488 | tf_op jit(solution)/shard_map/ppermute | solution.py:158
  217.1 28.5 %collective-permute-start.36 = (bf16[256,1664]{1,0:T(8,128)(2,1)S(1)}, bf16[256,1664]{1,0:T(8,128)(2,1)}, u32[]{:S(2)}, u32[]{:S(2)}) collective-permute-start(bf16[256,1664]{1,0:T(8,128)(2,1)S(1)} %constant_dynamic-update-slice_fusion.96.near_grad_ref), channel_id=1, source_target_pairs={{0,8},{4,20},{8,0},{12,28},{16,24},{20,4},{24,16},{28,12},{1,9},{5... | collective-permute-start | bytes 2555912 | tf_op jit(solution)/shard_map/ppermute | solution.py:158
  227.8 25.6 %collective-permute-start.7 = (bf16[192,2176]{1,0:T(8,128)(2,1)S(1)}, bf16[192,2176]{1,0:T(8,128)(2,1)S(1)}, u32[]{:S(2)}, u32[]{:S(2)}) collective-permute-start(bf16[192,2176]{1,0:T(8,128)(2,1)S(1)} %copy-done.48), channel_id=1, source_target_pairs={{0,8},{4,20},{8,0},{12,28},{16,24},{20,4},{24,16},{28,12},{1,9},{5... | collective-permute-start | bytes 2506760 | tf_op jit(solution)/shard_map/ppermute | solution.py:158
  318.8 32.2 %collective-permute-start.13 = (bf16[256,1536]{1,0:T(8,128)(2,1)S(1)}, bf16[256,1536]{1,0:T(8,128)(2,1)S(1)}, u32[]{:S(2)}, u32[]{:S(2)}) collective-permute-start(bf16[256,1536]{1,0:T(8,128)(2,1)S(1)} %pad_maximum_fusion.6.near_ref), channel_id=1, source_target_pairs={{0,8},{4,20},{8,0},{12,28},{16,24},{20,4},{24,16},{28,12},{1,9},{5... | collective-permute-start | bytes 2359304 | tf_op jit(solution)/shard_map/ppermute | solution.py:158
  320.0 32.7 %collective-permute-start.24 = (bf16[128,1536]{1,0:T(8,128)(2,1)S(1)}, bf16[128,1536]{1,0:T(8,128)(2,1)S(1)}, u32[]{:S(2)}, u32[]{:S(2)}) collective-permute-start(bf16[128,1536]{1,0:T(8,128)(2,1)S(1)} %collective-permute-done.23), channel_id=1, source_target_pairs={{0,16},{4,12},{8,24},{12,4},{16,0},{20,28},{24,8},{28,20},{1,17},{... | collective-permute-start | bytes 1179656 | tf_op jit(solution)/shard_map/ppermute | solution.py:158
  325.7 53.3 %collective-permute-start.42 = (bf16[128,1536]{1,0:T(8,128)(2,1)}, bf16[128,1536]{1,0:T(8,128)(2,1)S(1)}, u32[]{:S(2)}, u32[]{:S(2)}) collective-permute-start(bf16[128,1536]{1,0:T(8,128)(2,1)} %collective-permute-done.41), channel_id=1, source_target_pairs={{0,16},{4,12},{8,24},{12,4},{16,0},{20,28},{24,8},{28,20},{1,17},{... | collective-permute-start | bytes 1179656 | tf_op jit(solution)/shard_map/ppermute | solution.py:158
  337.6 72.1 %collective-permute-start.32 = (bf16[128,1536]{1,0:T(8,128)(2,1)}, bf16[128,1536]{1,0:T(8,128)(2,1)}, u32[]{:S(2)}, u32[]{:S(2)}) collective-permute-start(bf16[128,1536]{1,0:T(8,128)(2,1)} %collective-permute-done.31), channel_id=1, source_target_pairs={{0,16},{4,12},{8,24},{12,4},{16,0},{20,28},{24,8},{28,20},{1,17},{... | collective-permute-start | bytes 1179656 | tf_op jit(solution)/shard_map/ppermute | solution.py:158
  374.3 26.7 %collective-permute-start.21 = (bf16[256,1536]{1,0:T(8,128)(2,1)S(1)}, bf16[256,1536]{1,0:T(8,128)(2,1)}, u32[]{:S(2)}, u32[]{:S(2)}) collective-permute-start(bf16[256,1536]{1,0:T(8,128)(2,1)S(1)} %get-tuple-element.51), channel_id=1, source_target_pairs={{0,8},{4,20},{8,0},{12,28},{16,24},{20,4},{24,16},{28,12},{1,9},{5... | collective-permute-start | bytes 2359304 | tf_op jit(solution)/shard_map/ppermute | solution.py:158
  375.2 29.3 %collective-permute-start.50 = (bf16[256,1536]{1,0:T(8,128)(2,1)S(1)}, bf16[256,1536]{1,0:T(8,128)(2,1)S(1)}, u32[]{:S(2)}, u32[]{:S(2)}) collective-permute-start(bf16[256,1536]{1,0:T(8,128)(2,1)S(1)} %get-tuple-element.59), channel_id=1, source_target_pairs={{0,8},{4,20},{8,0},{12,28},{16,24},{20,4},{24,16},{28,12},{1,9},{5... | collective-permute-start | bytes 2359304 | tf_op jit(solution)/shard_map/ppermute | solution.py:158
  379.8 27.2 %collective-permute-start.43 = (bf16[256,1536]{1,0:T(8,128)(2,1)S(1)}, bf16[256,1536]{1,0:T(8,128)(2,1)S(1)}, u32[]{:S(2)}, u32[]{:S(2)}) collective-permute-start(bf16[256,1536]{1,0:T(8,128)(2,1)S(1)} %get-tuple-element.319.near_ref), channel_id=1, source_target_pairs={{0,8},{4,20},{8,0},{12,28},{16,24},{20,4},{24,16},{28,12},{1,9},{5... | collective-permute-start | bytes 2359304 | tf_op jit(solution)/shard_map/ppermute | solution.py:158
  399.7 33.0 %collective-permute-start.29 = (bf16[256,1536]{1,0:T(8,128)(2,1)S(1)}, bf16[256,1536]{1,0:T(8,128)(2,1)S(1)}, u32[]{:S(2)}, u32[]{:S(2)}) collective-permute-start(bf16[256,1536]{1,0:T(8,128)(2,1)S(1)} %get-tuple-element.53), channel_id=1, source_target_pairs={{0,8},{4,20},{8,0},{12,28},{16,24},{20,4},{24,16},{28,12},{1,9},{5... | collective-permute-start | bytes 2359304 | tf_op jit(solution)/shard_map/ppermute | solution.py:158
  400.9 35.4 %collective-permute-start.52 = (bf16[256,1536]{1,0:T(8,128)(2,1)S(1)}, bf16[256,1536]{1,0:T(8,128)(2,1)S(1)}, u32[]{:S(2)}, u32[]{:S(2)}) collective-permute-start(bf16[256,1536]{1,0:T(8,128)(2,1)S(1)} %get-tuple-element.61), channel_id=1, source_target_pairs={{0,8},{4,20},{8,0},{12,28},{16,24},{20,4},{24,16},{28,12},{1,9},{5... | collective-permute-start | bytes 2359304 | tf_op jit(solution)/shard_map/ppermute | solution.py:158
  404.5 177.6 %collective-permute-start.22 = (bf16[128,1536]{1,0:T(8,128)(2,1)}, bf16[128,1536]{1,0:T(8,128)(2,1)}, u32[]{:S(2)}, u32[]{:S(2)}) collective-permute-start(bf16[128,1536]{1,0:T(8,128)(2,1)} %slice.1583), channel_id=1, source_target_pairs={{0,16},{4,12},{8,24},{12,4},{16,0},{20,28},{24,8},{28,20},{1,17},{... | collective-permute-start | bytes 1179656 | tf_op jit(solution)/shard_map/ppermute | solution.py:158
  411.5 26.4 %collective-permute-start.33 = (bf16[256,1536]{1,0:T(8,128)(2,1)S(1)}, bf16[256,1536]{1,0:T(8,128)(2,1)S(1)}, u32[]{:S(2)}, u32[]{:S(2)}) collective-permute-start(bf16[256,1536]{1,0:T(8,128)(2,1)S(1)} %get-tuple-element.315.near_ref), channel_id=1, source_target_pairs={{0,8},{4,20},{8,0},{12,28},{16,24},{20,4},{24,16},{28,12},{1,9},{5... | collective-permute-start | bytes 2359304 | tf_op jit(solution)/shard_map/ppermute | solution.py:158
  431.9 65.8 %collective-permute-start.47 = (bf16[256,1536]{1,0:T(8,128)(2,1)S(1)}, bf16[256,1536]{1,0:T(8,128)(2,1)}, u32[]{:S(2)}, u32[]{:S(2)}) collective-permute-start(bf16[256,1536]{1,0:T(8,128)(2,1)S(1)} %get-tuple-element.57), channel_id=1, source_target_pairs={{0,8},{4,20},{8,0},{12,28},{16,24},{20,4},{24,16},{28,12},{1,9},{5... | collective-permute-start | bytes 2359304 | tf_op jit(solution)/shard_map/ppermute | solution.py:158
  432.8 70.3 %collective-permute-start.58 = (bf16[256,1536]{1,0:T(8,128)(2,1)S(1)}, bf16[256,1536]{1,0:T(8,128)(2,1)}, u32[]{:S(2)}, u32[]{:S(2)}) collective-permute-start(bf16[256,1536]{1,0:T(8,128)(2,1)S(1)} %get-tuple-element.65), channel_id=1, source_target_pairs={{0,8},{4,20},{8,0},{12,28},{16,24},{20,4},{24,16},{28,12},{1,9},{5... | collective-permute-start | bytes 2359304 | tf_op jit(solution)/shard_map/ppermute | solution.py:158
  436.3 101.5 %collective-permute-start.30 = (bf16[128,1536]{1,0:T(8,128)(2,1)}, bf16[128,1536]{1,0:T(8,128)(2,1)}, u32[]{:S(2)}, u32[]{:S(2)}) collective-permute-start(bf16[128,1536]{1,0:T(8,128)(2,1)} %slice.1582), channel_id=1, source_target_pairs={{0,16},{4,12},{8,24},{12,4},{16,0},{20,28},{24,8},{28,20},{1,17},{... | collective-permute-start | bytes 1179656 | tf_op jit(solution)/shard_map/ppermute | solution.py:158
  456.9 62.6 %collective-permute-start.37 = (bf16[256,1536]{1,0:T(8,128)(2,1)S(1)}, bf16[256,1536]{1,0:T(8,128)(2,1)S(1)}, u32[]{:S(2)}, u32[]{:S(2)}) collective-permute-start(bf16[256,1536]{1,0:T(8,128)(2,1)S(1)} %get-tuple-element.55), channel_id=1, source_target_pairs={{0,8},{4,20},{8,0},{12,28},{16,24},{20,4},{24,16},{28,12},{1,9},{5... | collective-permute-start | bytes 2359304 | tf_op jit(solution)/shard_map/ppermute | solution.py:158
  518.7 36.2 %collective-permute-start.73 = (bf16[4,192,1280]{2,1,0:T(8,128)(2,1)S(1)}, bf16[4,192,1280]{2,1,0:T(8,128)(2,1)S(1)}, u32[]{:S(2)}, u32[]{:S(2)}) collective-permute-start(bf16[4,192,1280]{2,1,0:T(8,128)(2,1)S(1)} %fusion.59), channel_id=1, source_target_pairs={{0,4},{4,0},{8,12},{12,8},{16,20},{20,16},{24,28},{28,24},{1,5},{5... | collective-permute-start | bytes 5898248 | tf_op jit(solution)/shard_map/ppermute | solution.py:158
  519.5 35.9 %collective-permute-start.72 = (bf16[4,192,1280]{2,1,0:T(8,128)(2,1)S(1)}, bf16[4,192,1280]{2,1,0:T(8,128)(2,1)S(1)}, u32[]{:S(2)}, u32[]{:S(2)}) collective-permute-start(bf16[4,192,1280]{2,1,0:T(8,128)(2,1)S(1)} %fusion.58), channel_id=1, source_target_pairs={{0,4},{4,0},{8,12},{12,8},{16,20},{20,16},{24,28},{28,24},{1,5},{5... | collective-permute-start | bytes 5898248 | tf_op jit(solution)/shard_map/ppermute | solution.py:158
  554.7 270.3 %collective-permute-start.77 = (f32[10,64,1536]{2,1,0:T(8,128)}, f32[10,64,1536]{2,1,0:T(8,128)}, u32[]{:S(2)}, u32[]{:S(2)}) collective-permute-start(f32[10,64,1536]{2,1,0:T(8,128)} %dynamic-slice_bitcast_fusion), channel_id=1, source_target_pairs={{0,4},{4,0},{8,12},{12,8},{16,20},{20,16},{24,28},{28,24},{1,5},{5... | collective-permute-start | bytes 11796488 | tf_op jit(solution)/shard_map/ppermute | solution.py:158
  555.4 24.5 %collective-permute-start.57 = (bf16[128,1536]{1,0:T(8,128)(2,1)S(1)}, bf16[128,1536]{1,0:T(8,128)(2,1)S(1)}, u32[]{:S(2)}, u32[]{:S(2)}) collective-permute-start(bf16[128,1536]{1,0:T(8,128)(2,1)S(1)} %fusion.100), channel_id=1, source_target_pairs={{0,3},{1,0},{2,1},{3,2},{4,7},{5,4},{6,5},{7,6},{8,11},{9,8},{10,9... | collective-permute-start | bytes 1179656 | tf_op jit(solution)/shard_map/ppermute | solution.py:183
  562.3 24.0 %collective-permute-start.49 = (bf16[128,1536]{1,0:T(8,128)(2,1)S(1)}, bf16[128,1536]{1,0:T(8,128)(2,1)S(1)}, u32[]{:S(2)}, u32[]{:S(2)}) collective-permute-start(bf16[128,1536]{1,0:T(8,128)(2,1)S(1)} %copy-done.75), channel_id=1, source_target_pairs={{0,1},{1,2},{2,3},{3,0},{4,5},{5,6},{6,7},{7,4},{8,9},{9,10},{10,1... | collective-permute-start | bytes 1179656 | tf_op jit(solution)/shard_map/ppermute | solution.py:183
  580.0 118.6 %collective-permute-start.76 = (bf16[2,192,1280]{2,1,0:T(8,128)(2,1)}, bf16[2,192,1280]{2,1,0:T(8,128)(2,1)}, u32[]{:S(2)}, u32[]{:S(2)}) collective-permute-start(bf16[2,192,1280]{2,1,0:T(8,128)(2,1)} %get-tuple-element.291), channel_id=1, source_target_pairs={{0,24},{4,28},{8,16},{12,20},{16,8},{20,12},{24,0},{28,4},{1,25},{... | collective-permute-start | bytes 2949128 | tf_op jit(solution)/shard_map/ppermute | solution.py:158
  582.1 110.0 %collective-permute-start.74 = (bf16[2,192,1280]{2,1,0:T(8,128)(2,1)}, bf16[2,192,1280]{2,1,0:T(8,128)(2,1)}, u32[]{:S(2)}, u32[]{:S(2)}) collective-permute-start(bf16[2,192,1280]{2,1,0:T(8,128)(2,1)} %get-tuple-element.293), channel_id=1, source_target_pairs={{0,8},{4,12},{8,0},{12,4},{16,24},{20,28},{24,16},{28,20},{1,9},{5... | collective-permute-start | bytes 2949128 | tf_op jit(solution)/shard_map/ppermute | solution.py:158
  586.3 108.9 %collective-permute-start.75 = (bf16[2,192,1280]{2,1,0:T(8,128)(2,1)}, bf16[2,192,1280]{2,1,0:T(8,128)(2,1)}, u32[]{:S(2)}, u32[]{:S(2)}) collective-permute-start(bf16[2,192,1280]{2,1,0:T(8,128)(2,1)} %get-tuple-element.294), channel_id=1, source_target_pairs={{0,16},{4,20},{8,24},{12,28},{16,0},{20,4},{24,8},{28,12},{1,17},{... | collective-permute-start | bytes 2949128 | tf_op jit(solution)/shard_map/ppermute | solution.py:158
  681.6 103.7 %collective-permute-start.62 = (f32[128,1536]{1,0:T(8,128)}, f32[128,1536]{1,0:T(8,128)S(1)}, u32[]{:S(2)}, u32[]{:S(2)}) collective-permute-start(f32[128,1536]{1,0:T(8,128)} %slice.1257), channel_id=1, source_target_pairs={{0,4},{4,0},{8,12},{12,8},{16,20},{20,16},{24,28},{28,24},{1,5},{5... | collective-permute-start | bytes 2359304 | tf_op jit(solution)/shard_map/ppermute | solution.py:158
  692.1 72.3 %collective-permute-start.64 = (bf16[192,2176]{1,0:T(8,128)(2,1)}, bf16[192,2176]{1,0:T(8,128)(2,1)}, u32[]{:S(2)}, u32[]{:S(2)}) collective-permute-start(bf16[192,2176]{1,0:T(8,128)(2,1)} %copy.501), channel_id=1, source_target_pairs={{0,8},{4,20},{8,0},{12,28},{16,24},{20,4},{24,16},{28,12},{1,9},{5... | collective-permute-start | bytes 2506760 | tf_op jit(solution)/shard_map/ppermute | solution.py:158
  695.2 36.1 %collective-permute-start.65 = (bf16[192,2176]{1,0:T(8,128)(2,1)}, bf16[192,2176]{1,0:T(8,128)(2,1)}, u32[]{:S(2)}, u32[]{:S(2)}) collective-permute-start(bf16[192,2176]{1,0:T(8,128)(2,1)} %copy.503), channel_id=1, source_target_pairs={{0,8},{4,20},{8,0},{12,28},{16,24},{20,4},{24,16},{28,12},{1,9},{5... | collective-permute-start | bytes 2506760 | tf_op jit(solution)/shard_map/ppermute | solution.py:158
  698.6 68.7 %collective-permute-start.68 = (bf16[192,2176]{1,0:T(8,128)(2,1)}, bf16[192,2176]{1,0:T(8,128)(2,1)}, u32[]{:S(2)}, u32[]{:S(2)}) collective-permute-start(bf16[192,2176]{1,0:T(8,128)(2,1)} %copy.509), channel_id=1, source_target_pairs={{0,8},{4,20},{8,0},{12,28},{16,24},{20,4},{24,16},{28,12},{1,9},{5... | collective-permute-start | bytes 2506760 | tf_op jit(solution)/shard_map/ppermute | solution.py:158
  738.2 31.4 %collective-permute-start.66 = (bf16[192,2176]{1,0:T(8,128)(2,1)}, bf16[192,2176]{1,0:T(8,128)(2,1)}, u32[]{:S(2)}, u32[]{:S(2)}) collective-permute-start(bf16[192,2176]{1,0:T(8,128)(2,1)} %copy.505), channel_id=1, source_target_pairs={{0,3},{1,0},{2,1},{3,2},{4,7},{5,4},{6,5},{7,6},{8,11},{9,8},{10,9... | collective-permute-start | bytes 2506760 | tf_op jit(solution)/shard_map/ppermute | solution.py:183
  781.4 23.6 %collective-permute-start.69 = (bf16[192,2176]{1,0:T(8,128)(2,1)}, bf16[192,2176]{1,0:T(8,128)(2,1)}, u32[]{:S(2)}, u32[]{:S(2)}) collective-permute-start(bf16[192,2176]{1,0:T(8,128)(2,1)} %copy.511), channel_id=1, source_target_pairs={{0,1},{1,2},{2,3},{3,0},{4,5},{5,6},{6,7},{7,4},{8,9},{9,10},{10,1... | collective-permute-start | bytes 2506760 | tf_op jit(solution)/shard_map/ppermute | solution.py:183
  781.5 37.3 %collective-permute-start.67 = (bf16[192,2176]{1,0:T(8,128)(2,1)}, bf16[192,2176]{1,0:T(8,128)(2,1)}, u32[]{:S(2)}, u32[]{:S(2)}) collective-permute-start(bf16[192,2176]{1,0:T(8,128)(2,1)} %copy.507), channel_id=1, source_target_pairs={{0,3},{1,0},{2,1},{3,2},{4,7},{5,4},{6,5},{7,6},{8,11},{9,8},{10,9... | collective-permute-start | bytes 2506760 | tf_op jit(solution)/shard_map/ppermute | solution.py:183
  (156 other events, 1879.9 us)

commit v2 on v1

--- a/solution.py
+++ b/solution.py
@@ -320,6 +320,188 @@
     )
 
 
+def spread_columns_kernel(place_ref, weight_ref, *out_refs):
+    lanes = out_refs[0].shape[2]
+    for other, out_ref in enumerate(out_refs):
+        start = pl.multiple_of((place_ref[0] ^ other) * lanes, lanes)
+        for part in range(2):
+            out_ref[part] = weight_ref[0, :, pl.ds(part * FF + start, lanes)].astype(out_ref.dtype)
+
+
+def spread_columns(place, weight, chips):
+    experts, rows, both = weight.shape
+    lanes = both // 2 // chips
+    return pl.pallas_call(
+        spread_columns_kernel,
+        grid_spec=pltpu.PrefetchScalarGridSpec(
+            num_scalar_prefetch=1,
+            grid=(experts,),
+            in_specs=[pl.BlockSpec((1, rows, both), lambda e, place: (e, 0, 0))],
+            out_specs=[pl.BlockSpec((2, rows, lanes), lambda e, place: (0, 0, e))] * chips,
+        ),
+        out_shape=[jax.ShapeDtypeStruct((2, rows, experts * lanes), jnp.bfloat16)] * chips,
+        cost_estimate=pl.CostEstimate(
+            flops=0, bytes_accessed=6 * experts * rows * both, transcendentals=0
+        ),
+    )(place, weight)
+
+
+def stack_rows_kernel(place_ref, *refs):
+    pieces, (gate_ref, upper_ref, sems) = refs[:-3], refs[-3:]
+    chip, core = place_ref[0], place_ref[1]
+    chips = len(pieces) // 2
+    rows = pieces[0].shape[1]
+    copies = []
+    for other in range(chips):
+        for mate in range(2):
+            start = pl.multiple_of(((chip ^ other) * 2 + (core ^ mate)) * rows, rows)
+            for part, out_ref in enumerate((gate_ref, upper_ref)):
+                copies.append(
+                    pltpu.make_async_copy(
+                        pieces[mate * chips + other].at[part],
+                        out_ref.at[pl.ds(start, rows), :],
+                        sems.at[len(copies)],
+                    )
+                )
+    for copy in copies:
+        copy.start()
+    for copy in copies:
+        copy.wait()
+
+
+def stack_rows(place, pieces):
+    _, rows, columns = pieces[0].shape
+    shape = jax.ShapeDtypeStruct((rows * len(pieces), columns), jnp.bfloat16)
+    return pl.pallas_call(
+        stack_rows_kernel,
+        in_specs=[pl.BlockSpec(memory_space=pltpu.SMEM)]
+        + [pl.BlockSpec(memory_space=pl.ANY)] * len(pieces),
+        out_specs=[pl.BlockSpec(memory_space=pl.ANY)] * 2,
+        out_shape=[shape] * 2,
+        scratch_shapes=[pltpu.SemaphoreType.DMA((2 * len(pieces),))],
+        cost_estimate=pl.CostEstimate(
+            flops=0, bytes_accessed=8 * len(pieces) * rows * columns, transcendentals=0
+        ),
+    )(place, *pieces)
+
+
+def stack_attention_kernel(*refs):
+    blocks, (qkv_ref, gain_ref, out_ref, sems) = refs[:-4], refs[-4:]
+    wide, lanes = qkv_ref.shape[1], gain_ref.shape[1]
+    owned = out_ref.shape[0] // (2 * len(blocks))
+    copies = []
+    for i, block in enumerate(blocks):
+        for j in range(2):
+            top, spot = 3 * owned * j, 2 * i + j
+            pairs = (
+                (
+                    block.at[pl.ds(top, 2 * owned), pl.ds(0, wide)],
+                    qkv_ref.at[pl.ds(2 * owned * spot, 2 * owned), :],
+                ),
+                (
+                    block.at[pl.ds(top, 2 * owned), pl.ds(wide, lanes)],
+                    gain_ref.at[pl.ds(2 * owned * spot, 2 * owned), :],
+                ),
+                (
+                    block.at[pl.ds(top + 2 * owned, owned), :],
+                    out_ref.at[pl.ds(owned * spot, owned), :],
+                ),
+            )
+            for source, target in pairs:
+                copies.append(pltpu.make_async_copy(source, target, sems.at[len(copies)]))
+    for copy in copies:
+        copy.start()
+    for copy in copies:
+        copy.wait()
+
+
+def stack_attention(blocks, wide, lanes):
+    owned = blocks[0].shape[0] // 6
+    count = 2 * len(blocks)
+    b16 = lambda r, c: jax.ShapeDtypeStruct((r, c), jnp.bfloat16)
+    return pl.pallas_call(
+        stack_attention_kernel,
+        in_specs=[pl.BlockSpec(memory_space=pl.ANY)] * len(blocks),
+        out_specs=[pl.BlockSpec(memory_space=pl.ANY)] * 3,
+        out_shape=[
+            b16(2 * owned * count, wide),
+            b16(2 * owned * count, lanes),
+            b16(owned * count, blocks[0].shape[1]),
+        ],
+        scratch_shapes=[pltpu.SemaphoreType.DMA((3 * count,))],
+        cost_estimate=pl.CostEstimate(
+            flops=0, bytes_accessed=4 * 3 * owned * count * MODEL_WIDTH, transcendentals=0
+        ),
+    )(*blocks)
+
+
+def attention_grads_kernel(
+    normed_ref, joined_ref, attended_ref, grads_ref, gain_ref, near_ref, away_ref
+):
+    contract = (((0,), (0,)), ((), ()))
+    wide, lanes = joined_ref.shape[1], gain_ref.shape[1]
+    spots = near_ref.shape[0]
+    owned = near_ref.shape[1] // 6
+    joined, grads = joined_ref[...], grads_ref[...]
+
+    def place(spot, second, first, row, columns, values):
+        rows = pl.ds(3 * owned * first + row, values.shape[0])
+        if second:
+            away_ref[spot, rows, columns] = values.astype(away_ref.dtype)
+        else:
+            near_ref[spot, rows, columns] = values
+
+    for spot in range(spots):
+        rows = 8 * owned
+        qkv = lax.dot_general(
+            normed_ref[:, rows * spot : rows * (spot + 1)],
+            joined,
+            contract,
+            preferred_element_type=jnp.float32,
+        )
+        for i in range(4):
+            part = slice(2 * owned * i, 2 * owned * (i + 1))
+            place(spot, i // 2, i % 2, 0, pl.ds(0, wide), qkv[part])
+            gain = gain_ref[pl.ds(rows * spot + 2 * owned * i, 2 * owned), :]
+            place(spot, i // 2, i % 2, 0, pl.ds(wide, lanes), gain)
+            place(spot, i // 2, i % 2, 0, pl.ds(wide + lanes, lanes), jnp.zeros_like(gain))
+        if spot % 2 == 0:
+            out = lax.dot_general(
+                attended_ref[:, 4 * owned * spot : 4 * owned * (spot + 2)],
+                grads,
+                contract,
+                preferred_element_type=jnp.float32,
+            )
+            for i in range(8):
+                part = slice(owned * i, owned * (i + 1))
+                place(
+                    spot + i // 4,
+                    i // 2 % 2,
+                    i % 2,
+                    2 * owned,
+                    pl.ds(0, out.shape[1]),
+                    out[part],
+                )
+
+
+def attention_grads(normed, joined, attended, grads, gain, owned):
+    spots = len(DISTANCE)
+    shape = (spots, 6 * owned, grads.shape[1])
+    return pl.pallas_call(
+        attention_grads_kernel,
+        out_shape=[
+            jax.ShapeDtypeStruct(shape, jnp.float32),
+            jax.ShapeDtypeStruct(shape, jnp.bfloat16),
+        ],
+        compiler_params=pltpu.CompilerParams(vmem_limit_bytes=44 * 1024 * 1024),
+        cost_estimate=pl.CostEstimate(
+            flops=2 * normed.shape[0] * normed.shape[1] * (joined.shape[1] + grads.shape[1] // 2),
+            bytes_accessed=20 * 1024 * 1024,
+            transcendentals=0,
+        ),
+    )(normed, joined, attended, grads, gain)
+
+
 def expert_kernel(
     near_ref,
     away_ref,
@@ -329,20 +511,12 @@
     gate_ref,
     upper_ref,
     down_ref,
-    near_out_ref,
-    away_out_ref,
-    near_back_ref,
-    away_back_ref,
-    hidden_ref,
-    grad_gate_ref,
-    grad_upper_ref,
-    rows_ref,
-    grads_ref,
-    out_ref,
-    back_ref,
-    *,
+    *refs,
     per_step,
 ):
+    near_out_ref, away_out_ref, near_back_ref, away_back_ref = refs[-13:-9]
+    hidden_ref, grad_gate_ref, grad_upper_ref, rows_all_ref, grads_all_ref = refs[-9:-4]
+    rows_ref, grads_ref, out_ref, back_ref = refs[-4:]
     step = pl.program_id(0)
     half = near_ref.shape[0]
     width = near_ref.shape[1]
@@ -353,6 +527,8 @@
         rows_ref[half:, :] = away_ref[...]
         grads_ref[:half, :] = near_grad_ref[:, :width]
         grads_ref[half:, :] = away_grad_ref[:, :width]
+        rows_all_ref[...] = rows_ref[...]
+        grads_all_ref[...] = grads_ref[...]
         out_ref[...] = jnp.zeros_like(out_ref)
         back_ref[...] = jnp.zeros_like(back_ref)
 
@@ -396,7 +572,8 @@
         away_back_ref[...] = back_ref[half:, :].astype(jnp.bfloat16)
 
 
-def expert_block(near, away, near_grad, away_grad, route, gate_w, upper_w, down_w, experts):
+def expert_block(spot, near, away, near_grad, away_grad, route, weights, experts, filled):
+    gate_w, upper_w, down_w = weights
     half, width = near.shape
     total = gate_w.shape[1]
     per_step = 2
@@ -404,11 +581,14 @@
     columns = total // steps
     whole = lambda a: pl.BlockSpec(a.shape, lambda i: (0, 0))
     rows = 2 * half
+    every = rows * len(DISTANCE)
     f32 = lambda r, c: jax.ShapeDtypeStruct((r, c), jnp.float32)
     b16 = lambda r, c: jax.ShapeDtypeStruct((r, c), jnp.bfloat16)
     fixed = pl.BlockSpec((half, width), lambda i: (0, 0))
-    part = pl.BlockSpec((rows, columns), lambda i: (0, i))
+    part = pl.BlockSpec((rows, columns), lambda i: (spot, i))
+    kept = pl.BlockSpec((rows, width), lambda i: (spot, 0))
     flops = 2 * rows * width * total * 6
+    inputs = (near, away, near_grad, away_grad, route, gate_w, upper_w, down_w)
     return pl.pallas_call(
         functools.partial(expert_kernel, per_step=per_step),
         grid=(steps,),
@@ -421,22 +601,145 @@
             pl.BlockSpec((width, columns), lambda i: (0, i)),
             pl.BlockSpec((width, columns), lambda i: (0, i)),
             pl.BlockSpec((columns, width), lambda i: (i, 0)),
-        ],
-        out_specs=[fixed] * 4 + [part] * 3,
-        out_shape=[f32(half, width), b16(half, width)] * 2 + [b16(rows, total)] * 3,
+        ]
+        + [pl.BlockSpec(memory_space=pl.ANY)] * len(filled),
+        out_specs=[fixed] * 4 + [part] * 3 + [kept] * 2,
+        out_shape=[f32(half, width), b16(half, width)] * 2
+        + [b16(every, total)] * 3
+        + [b16(every, width)] * 2,
+        input_output_aliases={len(inputs) + i: 4 + i for i in range(len(filled))},
         scratch_shapes=[
             pltpu.VMEM((rows, width), jnp.bfloat16),
             pltpu.VMEM((rows, width), jnp.bfloat16),
             pltpu.VMEM((rows, width), jnp.float32),
             pltpu.VMEM((rows, width), jnp.float32),
         ],
-        compiler_params=pltpu.CompilerParams(vmem_limit_bytes=44 * 1024 * 1024),
+        compiler_params=pltpu.CompilerParams(vmem_limit_bytes=48 * 1024 * 1024),
         cost_estimate=pl.CostEstimate(
             flops=flops,
-            bytes_accessed=2 * (3 * width * total + 3 * rows * total + 10 * rows * width),
+            bytes_accessed=2 * (3 * width * total + 3 * rows * total + 12 * rows * width),
             transcendentals=rows * total,
         ),
-    )(near, away, near_grad, away_grad, route, gate_w, upper_w, down_w)
+    )(*inputs, *filled)
+
+
+def expert_grads_kernel(
+    place_ref,
+    rows_ref,
+    grads_ref,
+    hidden_ref,
+    grad_gate_ref,
+    grad_upper_ref,
+    keep_ref,
+    give_ref,
+    keep_down_ref,
+    give_down_ref,
+    full_ref,
+    full_down_ref,
+):
+    core = place_ref[1]
+    contract = (((0,), (0,)), ((), ()))
+    chips, _, plane_rows, _ = keep_ref.shape
+    for part, ref in enumerate((grad_gate_ref, grad_upper_ref)):
+        full_ref[...] = lax.dot_general(
+            rows_ref[...], ref[...], contract, preferred_element_type=jnp.float32
+        )
+        for chip in range(chips):
+            mine = pl.multiple_of((2 * chip + core) * plane_rows, plane_rows)
+            theirs = pl.multiple_of((2 * chip + 1 - core) * plane_rows, plane_rows)
+            keep_ref[chip, part] = full_ref[pl.ds(mine, plane_rows), :]
+            give_ref[chip, part] = full_ref[pl.ds(theirs, plane_rows), :].astype(give_ref.dtype)
+    full_down_ref[...] = lax.dot_general(
+        hidden_ref[...], grads_ref[...], contract, preferred_element_type=jnp.float32
+    )
+    experts, down_rows, _ = keep_down_ref.shape
+    for e in range(experts):
+        mine = pl.multiple_of((2 * e + core) * down_rows, down_rows)
+        theirs = pl.multiple_of((2 * e + 1 - core) * down_rows, down_rows)
+        keep_down_ref[e] = full_down_ref[pl.ds(mine, down_rows), :]
+        give_down_ref[e] = full_down_ref[pl.ds(theirs, down_rows), :]
+
+
+def expert_grads(place, rows_all, grads_all, hidden, grad_gate, grad_upper, experts, chips):
+    tokens, width = rows_all.shape
+    total = hidden.shape[1]
+    per_step = 2
+    steps = experts // per_step
+    columns = total // steps
+    plane_rows = width // (2 * chips)
+    down_rows = total // experts // 2
+    whole = pl.BlockSpec((tokens, width), lambda i, p: (0, 0), pipeline_mode=pl.Buffered(1))
+    part = pl.BlockSpec((tokens, columns), lambda i, p: (0, i))
+    wide = pl.BlockSpec((chips, 2, plane_rows, columns), lambda i, p: (0, 0, 0, i))
+    down = pl.BlockSpec((per_step, down_rows, width), lambda i, p: (i, 0, 0))
+    return pl.pallas_call(
+        expert_grads_kernel,
+        grid_spec=pltpu.PrefetchScalarGridSpec(
+            num_scalar_prefetch=1,
+            grid=(steps,),
+            in_specs=[whole, whole, part, part, part],
+            out_specs=[wide, wide, down, down],
+            scratch_shapes=[
+                pltpu.VMEM((width, columns), jnp.float32),
+                pltpu.VMEM((columns, width), jnp.float32),
+            ],
+        ),
+        out_shape=[
+            jax.ShapeDtypeStruct((chips, 2, plane_rows, total), jnp.float32),
+            jax.ShapeDtypeStruct((chips, 2, plane_rows, total), jnp.bfloat16),
+            jax.ShapeDtypeStruct((experts, down_rows, width), jnp.float32),
+            jax.ShapeDtypeStruct((experts, down_rows, width), jnp.float32),
+        ],
+        compiler_params=pltpu.CompilerParams(vmem_limit_bytes=52 * 1024 * 1024),
+        cost_estimate=pl.CostEstimate(
+            flops=6 * tokens * width * total,
+            bytes_accessed=2 * tokens * (2 * width + 3 * total) + 20 * width * total,
+            transcendentals=0,
+        ),
+    )(place, rows_all, grads_all, hidden, grad_gate, grad_upper)
+
+
+def adam_columns_kernel(place_ref, w_ref, first_ref, second_ref, *refs):
+    pieces, outs = refs[:-4], refs[-4:]
+    lanes = pieces[0].shape[2]
+    for other, piece in enumerate(pieces):
+        start = pl.multiple_of((place_ref[0] ^ other) * lanes, lanes)
+        for part in range(2):
+            columns = pl.ds(part * FF + start, lanes)
+            grad = piece[part].astype(jnp.float32)
+            found = adam_step(
+                w_ref[0, :, columns],
+                grad,
+                first_ref[0, :, columns],
+                second_ref[0, :, columns],
+                learn_rate,
+                weight_decay,
+            )
+            for out_ref, value in zip(outs, (grad,) + found):
+                out_ref[0, :, columns] = value
+
+
+def adam_columns(place, weight, first, second, pieces):
+    experts, rows, both = weight.shape
+    lanes = pieces[0].shape[2] // experts
+    block = pl.BlockSpec((1, rows, both), lambda e, p: (e, 0, 0))
+    return pl.pallas_call(
+        adam_columns_kernel,
+        grid_spec=pltpu.PrefetchScalarGridSpec(
+            num_scalar_prefetch=1,
+            grid=(experts,),
+            in_specs=[block] * 3
+            + [pl.BlockSpec((2, rows, lanes), lambda e, p: (0, 0, e))] * len(pieces),
+            out_specs=[block] * 4,
+        ),
+        out_shape=[jax.ShapeDtypeStruct(weight.shape, jnp.float32)] * 4,
+        compiler_params=pltpu.CompilerParams(vmem_limit_bytes=32 * 1024 * 1024),
+        cost_estimate=pl.CostEstimate(
+            flops=20 * experts * rows * both,
+            bytes_accessed=30 * experts * rows * both,
+            transcendentals=experts * rows * both,
+        ),
+    )(place, weight, first, second, *pieces)
 
 
 def shards_moved(
@@ -478,14 +781,15 @@
     gain_columns = jnp.pad(gains.astype(NARROW).T, ((0, 0), (0, lane_pad - 2)))
     kept = jnp.where(core == 0, even_columns, odd_columns)
     given = jnp.where(core == 0, odd_columns, even_columns)
+    rest = jnp.zeros((owned, MODEL_WIDTH - half_columns - lane_pad), NARROW)
     taken = swap_core(jnp.concatenate([given, gain_columns], 1))
-    narrow_out = w_out.astype(NARROW)
     block = jnp.concatenate(
         [
-            jnp.concatenate([jnp.concatenate([kept, gain_columns], 1), taken], 0),
-            jnp.concatenate([narrow_out[:, :half_width], narrow_out[:, half_width:]], 0),
+            jnp.concatenate([kept, gain_columns, rest], 1),
+            jnp.concatenate([taken, rest], 1),
+            w_out.astype(NARROW),
         ],
-        1,
+        0,
     )
     attention_blocks = gather_ring_middle(block)
 
@@ -508,30 +812,14 @@
 
     ff_columns = FF // chips
 
-    def columns_of(which):
-        gate = lax.dynamic_slice_in_dim(w_gate_up, which * ff_columns, ff_columns, 2)
-        upper = lax.dynamic_slice_in_dim(w_gate_up, FF + which * ff_columns, ff_columns, 2)
-        return jnp.stack(
-            [
-                jnp.concatenate([a[e] for e in range(local_experts)], 1).astype(NARROW)
-                for a in (gate, upper)
-            ]
-        )
-
-    plane_rows = w_gate_up.shape[1]
     share = local_experts * ff_columns
-    mine = jnp.zeros((chips, 2, plane_rows, share), NARROW)
-    for other in range(chips):
-        piece = columns_of(chip ^ other)
-        if other:
-            piece = swap(piece, lambda i, other=other: 2 * other)
-        mine = lax.dynamic_update_slice(mine, piece[None], (chip ^ other, 0, 0, 0))
-    theirs = swap_core(mine)
-    both = jnp.where(
-        core == 0, jnp.stack([mine, theirs], 1), jnp.stack([theirs, mine], 1)
-    )
-    gate_w = both[:, :, 0].reshape(MODEL_WIDTH, share)
-    upper_w = both[:, :, 1].reshape(MODEL_WIDTH, share)
+    place = jnp.stack([chip, core]).astype(jnp.int32)
+    pieces = spread_columns(place, w_gate_up, chips)
+    pieces = [
+        swap(piece, lambda i, other=other: 2 * other) if other else piece
+        for other, piece in enumerate(pieces)
+    ]
+    gate_w, upper_w = stack_rows(place, pieces + [swap_core(piece) for piece in pieces])
     down_mine = w_down.astype(NARROW)
     down_theirs = swap_core(down_mine)
     down_w = jnp.where(
@@ -567,20 +855,8 @@
     scale_one = scale_pair[:sequence_length]
     pair_gathered = jnp.dot(pair_tokens, to_gathered, preferred_element_type=jnp.float32)
     blocks = [half for pair in attention_blocks for half in pair]
-    qkv_here = jnp.concatenate([b[:, :half_columns] for b in blocks], 0)
-    gain_here = jnp.concatenate(
-        [b[:, half_columns : half_columns + 2] for b in blocks], 0
-    ).T
-    out_here = jnp.concatenate(
-        [
-            b[:, half_columns + lane_pad :]
-            .reshape(2, 2, owned, half_width)
-            .transpose(0, 2, 1, 3)
-            .reshape(2 * owned, MODEL_WIDTH)
-            for b in blocks
-        ],
-        0,
-    )
+    qkv_here, gain_here, out_here = stack_attention(blocks, half_columns, lane_pad)
+    gain_here = gain_here[:, :2].T
     gain_attn = gain_here[0].astype(WIDE)
     gains_placed = jnp.dot(gain_here, from_gathered, preferred_element_type=jnp.float32)
     gain_moe = gains_placed[1]
@@ -600,52 +876,47 @@
     normed_two = (resid * scale_two * gain_moe).astype(NARROW)
 
     normed_blocks = gather_plane_last(normed_two)
-    out_parts, back_parts, hidden, grad_gate, grad_upper = [], [], [], [], []
-    for (near, away), (near_grad, away_grad) in zip(normed_blocks, cotangent_blocks):
+    out_parts, back_parts, filled = [], [], []
+    for spot, ((near, away), (near_grad, away_grad)) in enumerate(
+        zip(normed_blocks, cotangent_blocks)
+    ):
         route = jnp.concatenate(
             [dense_route(g[:, MODEL_WIDTH:]) for g in (near_grad, away_grad)], 0
         )
         done = expert_block(
-            near, away, near_grad, away_grad, route, gate_w, upper_w, down_w, local_experts
+            spot,
+            near,
+            away,
+            near_grad,
+            away_grad,
+            route,
+            (gate_w, upper_w, down_w),
+            local_experts,
+            filled,
         )
         out_parts.append((done[0], done[1]))
         back_parts.append((done[2], done[3]))
-        hidden.append(done[4])
-        grad_gate.append(done[5])
-        grad_upper.append(done[6])
+        filled = done[4:]
     grad_normed_two = scatter_plane_first(back_parts)
     out_tokens = resid + scatter_plane_first(out_parts)
 
-    rows_all = jnp.concatenate([half for pair in normed_blocks for half in pair], 0)
-    grads_all = jnp.concatenate(
-        [half[:, :MODEL_WIDTH] for pair in cotangent_blocks for half in pair], 0
-    )
-    over_rows = (((0,), (0,)), ((), ()))
-    grad_down_parts = lax.dot_general(
-        jnp.concatenate(hidden, 0), grads_all, over_rows, preferred_element_type=jnp.float32
-    ).reshape(local_experts, 2, ff_columns // 2, MODEL_WIDTH)
-    part_down = lax.dynamic_index_in_dim(grad_down_parts, core, 1, False) + swap_core(
-        lax.dynamic_index_in_dim(grad_down_parts, 1 - core, 1, False)
-    )
-    sums = []
-    for grads in (grad_gate, grad_upper):
-        full = lax.dot_general(
-            rows_all, jnp.concatenate(grads, 0), over_rows, preferred_element_type=jnp.float32
-        ).reshape(chips, 2, plane_rows, share)
-        theirs = swap_core(lax.dynamic_index_in_dim(full, 1 - core, 1, False).astype(NARROW))
-        sums.append(lax.dynamic_index_in_dim(full, core, 1, False) + theirs.astype(WIDE))
-    sums = jnp.stack(sums, 1).astype(NARROW)
-    collected = jnp.zeros((chips, 2, plane_rows, share), NARROW)
+    hidden, grad_gate, grad_upper, rows_all, grads_all = filled
+    keep, give, keep_down, give_down = expert_grads(
+        place, rows_all, grads_all, hidden, grad_gate, grad_upper, local_experts, chips
+    )
+    part_down = keep_down + swap_core(give_down)
+    taken = swap_core(give)
+    collected = []
     for other in range(chips):
-        piece = lax.dynamic_index_in_dim(sums, chip ^ other, 0, False)
+        piece = (
+            lax.dynamic_index_in_dim(keep, chip ^ other, 0, False)
+            + lax.dynamic_index_in_dim(taken, chip ^ other, 0, False).astype(WIDE)
+        ).astype(NARROW)
         if other:
             piece = swap(piece, lambda i, other=other: 2 * other)
-        collected = lax.dynamic_update_slice(collected, piece[None], (chip ^ other, 0, 0, 0))
-    part_gate_up = (
-        collected.reshape(chips, 2, plane_rows, local_experts, ff_columns)
-        .transpose(3, 2, 1, 0, 4)
-        .reshape(local_experts, plane_rows, 2 * FF)
-        .astype(WIDE)
+        collected.append(piece)
+    part_gate_up, new_gate_up, new_first_gate_up, new_second_gate_up = adam_columns(
+        place, w_gate_up, first_gate_up, second_gate_up, collected
     )
 
     hat_two = grad_normed_two * gain_moe
@@ -655,7 +926,6 @@
     )
     grad_resid_half = grad_resid.astype(NARROW)
     pair_grads = jnp.concatenate([grad_resid_half, swap_core(grad_resid_half)], 0)
-    grad_out = lax.dot_general(attended, pair_grads, over_rows, preferred_element_type=jnp.float32)
     attended_gradient = lax.dot_general(
         pair_grads, out_here, (((1,), (1,)), ((), ())), preferred_element_type=jnp.float32
     ).astype(NARROW)
@@ -670,7 +940,6 @@
     joined = jax.vmap(lambda a, b, c: join_grads(a, b, c, cosine_table, sine_table))(
         grad_query, grad_keys, grad_values
     ).reshape(2 * sequence_length, -1)
-    grad_qkv = lax.dot_general(normed_one, joined, over_rows, preferred_element_type=jnp.float32)
     grad_normed_parts = lax.dot_general(
         joined, qkv_here, (((1,), (1,)), ((), ())), preferred_element_type=jnp.float32
     )
@@ -678,23 +947,16 @@
     gain_parts = jnp.stack(
         [grad_gain_attn, select_columns(grad_gain_moe[None], to_gathered)[0]], 1
     )
-    attention_parts = jnp.concatenate(
-        [
-            grad_qkv,
-            jnp.pad(gain_parts, ((0, 0), (0, lane_pad - 2))),
-            grad_out.reshape(-1, owned, 2, half_width)
-            .transpose(0, 2, 1, 3)
-            .reshape(MODEL_WIDTH, half_width),
-        ],
-        1,
-    ).reshape(4, 2, 4 * owned, -1)
-    summed = scatter_ring_middle(
-        [(attention_parts[i, 0], attention_parts[i, 1].astype(NARROW)) for i in range(4)]
-    )
-    here, there = summed[:owned], summed[owned:]
-    part_out = jnp.concatenate(
-        [here[:, half_columns + lane_pad :], there[:, half_columns + lane_pad :]], 1
-    )
+    near_parts, away_parts = attention_grads(
+        normed_one,
+        joined,
+        attended,
+        pair_grads,
+        jnp.pad(gain_parts, ((0, 0), (0, lane_pad - 2))),
+        owned,
+    )
+    summed = scatter_ring_middle([(near_parts[i], away_parts[i]) for i in range(len(DISTANCE))])
+    here, there, part_out = summed[:owned], summed[owned : 2 * owned], summed[2 * owned :]
     there = swap_core(there[:, : half_columns + lane_pad])
     part_gains = (
         here[:, half_columns : half_columns + 2] + there[:, half_columns : half_columns + 2]
@@ -721,9 +983,6 @@
     )
     new_gains, new_first_gains, new_second_gains = adam_step(
         gains, part_gains, first_gains, second_gains, gain_rate, 0.0
-    )
-    new_gate_up, new_first_gate_up, new_second_gate_up = adam_step(
-        w_gate_up, part_gate_up, first_gate_up, second_gate_up, learn_rate, weight_decay
     )
     new_down, new_first_down, new_second_down = adam_step(
         w_down, part_down, first_down, second_down, learn_rate, weight_decay

time: 865 us -> 1140 us (1.32)
  Pallas kernels: 75.6 us -> 591 us
  local copies, waits for them, and re-layouts: 279 us -> 48.1 us
  waiting for transfers between devices: 166 us -> 255 us
  other arithmetic: 146 us -> 90.2 us
  matrix products: 86.4 us -> 33.7 us
    pallas_call x0 -> x6, Pallas kernels: none -> 511 us  [the longest x1 240 us: stack_rows(): pl.pallas_call(stack_rows_kernel, in_specs=[pl.BlockSpec(memory_space=plt...]
    unnamed x372 -> x239, local copies, waits for them, and re-layouts: 99.7 us -> 23.1 us
    convert_element_type x13 -> x0, local copies, waits for them, and re-layouts: 51.7 us -> none  [the longest x3 29.7 us: shards_moved(): part_gate_up = collected.reshape(chips, 2, plane_rows, local_experts, ff_...]
    dot_general x5 -> x0, matrix products: 47.4 us -> none  [the longest x2 25.7 us: shards_moved(): lax.dot_general(rows_all, jnp.concatenate(grads, 0), over_rows, preferred...]
    ppermute x60 -> x62, waiting for transfers between devices: 68.4 us -> 115 us  [swap(): return lax.ppermute(rows, 'dp', [(i, i ^ pick(i)) for i in range(count)])]
    ppermute x18, waiting for transfers between devices: 98 us -> 139 us  [turn(): lax.ppermute(rows, 'expert', [(i, (i + step) % count) for i in range(coun...]
    concatenate x12 -> x1, local copies, waits for them, and re-layouts: 25.9 us -> 0.01 us  [shards_moved(): jnp.concatenate([taken, rest], 1)]
    sub x5 -> x4, other arithmetic: 38.1 us -> 14 us  [adam_step(): return (weight - step_rate * (update + shrink * weight), first, second)]
  transfers between devices with their start and end apart: 78 -> 80, of which waited for: 23 -> 33; matrix products, arithmetic and copies ran while one was open for 57% -> 11% of each run, Pallas kernels for 9% -> 35%
where the time goes in v2:
time: 1140 us; the launch traced here: 1120 us
  Pallas kernels  591 us (52%)
  waiting for transfers between devices  255 us (22%)
  starting transfers between devices  100 us (9%)
  other arithmetic  90.2 us (8%)
  local copies, waits for them, and re-layouts  48.1 us (4%)
  matrix products  33.7 us (3%)
    pallas_call x1, Pallas kernels, stack_rows(): pl.pallas_call(stack_rows_kernel, in_specs=[pl.BlockSpec(memory_space=plt...  240 us
    pallas_call x1, Pallas kernels, stack_attention(): pl.pallas_call(stack_attention_kernel, in_specs=[pl.BlockSpec(memory_spac...  204 us
    ppermute x18, waiting for transfers between devices, turn(): lax.ppermute(rows, 'expert', [(i, (i + step) % count) for i in range(coun...  139 us
    ppermute x62, waiting for transfers between devices, swap(): return lax.ppermute(rows, 'dp', [(i, i ^ pick(i)) for i in range(count)])  115 us
    pallas_call x4, Pallas kernels, expert_block(): pl.pallas_call(functools.partial(expert_kernel, per_step=per_step), grid=...  80.6 us
    ppermute x62, starting transfers between devices, swap(): return lax.ppermute(rows, 'dp', [(i, i ^ pick(i)) for i in range(count)])  67.8 us
    pallas_call x1, Pallas kernels, expert_grads(): pl.pallas_call(expert_grads_kernel, grid_spec=pltpu.PrefetchScalarGridSpe...  34.8 us
    ppermute x18, starting transfers between devices, turn(): lax.ppermute(rows, 'expert', [(i, (i + step) % count) for i in range(coun...  32.7 us
  transfers between devices with their start and end apart: 80, of which 33 were waited for; matrix products, arithmetic and copies ran while one was open for 11% of the time, Pallas kernels for 35%

profile of v2, /device:TPU:0, one launch (start us, length us, event | category | flops | bytes accessed | tf_op | source)
XLA Modules:
  0.0 1121.4 jit_solution(12269278958333561804)
XLA Ops:
  4.3 5.0 collective-permute-start.43
  30.9 3.6 convert_element_type.412
  34.5 9.3 shard_map.373
  58.3 38.6 %collective-permute-done.2 = bf16[144,1536]{1,0:T(8,128)(2,1)S(1)} collective-permute-done((bf16[144,1536]{1,0:T(8,128)(2,1)S(1)}, bf16[144,1536]{1,0:T(8,128)(2,1)S(1)}, u32[]{:S(2)}, u32[]{:S(2)}) %collective-permute-start.2) | collective-permute-done | bytes 442400 | tf_op jit(solution)/shard_map/ppermute | solution.py:158
  98.4 6.1 collective-permute-done.30
  106.0 9.1 collective-permute-done.44
  116.1 10.4 collective-permute-done.37
  128.4 6.9 collective-permute-done.38
  140.0 3.8 collective-permute-start.6
  150.7 13.9 %collective-permute-done.4.refs_2_ = bf16[288,1536]{1,0:T(8,128)(2,1)} collective-permute-done((bf16[288,1536]{1,0:T(8,128)(2,1)}, bf16[288,1536]{1,0:T(8,128)(2,1)}, u32[]{:S(2)}, u32[]{:S(2)}) %collective-permute-start.4) | collective-permute-done | bytes 884768 | tf_op jit(solution)/shard_map/ppermute | solution.py:183
  164.6 16.7 %collective-permute-done.6.refs_4_ = bf16[288,1536]{1,0:T(8,128)(2,1)} collective-permute-done((bf16[288,1536]{1,0:T(8,128)(2,1)}, bf16[288,1536]{1,0:T(8,128)(2,1)}, u32[]{:S(2)}, u32[]{:S(2)}) %collective-permute-start.6) | collective-permute-done | bytes 884768 | tf_op jit(solution)/shard_map/ppermute | solution.py:183
  191.3 16.0 %collective-permute-done.8.refs_6_ = bf16[288,1536]{1,0:T(8,128)(2,1)} collective-permute-done((bf16[288,1536]{1,0:T(8,128)(2,1)}, bf16[288,1536]{1,0:T(8,128)(2,1)}, u32[]{:S(2)}, u32[]{:S(2)}) %collective-permute-start.8) | collective-permute-done | bytes 884768 | tf_op jit(solution)/shard_map/ppermute | solution.py:183
  210.1 240.1 %shard_map.374 = (bf16[1536,1280]{1,0:T(8,128)(2,1)}, bf16[1536,1280]{1,0:T(8,128)(2,1)}) custom-call(s32[2]{0:T(128)} %pad_add_fusion.1.place_ref, bf16[2,192,1280]{2,1,0:T(8,128)(2,1)} %get-tuple-element.80.refs_0_, bf16[2,192,1280]{2,1,0:T(8,128)(2,1)} %copy-done.41, bf16[2,192,1280]{2,1,0:T(8,128)(2,1)} %copy-done.42, bf16[2,192,1280]{2,1,0:T(8,128)(2,1)} %copy-done.43, ...), custom_call_target="tpu_custom_call" | custom-call | bytes 15728640 | tf_op jit(solution)/shard_map/pallas_call | solution.py:375
  453.6 204.0 %shard_map.372 = (bf16[1536,1280]{1,0:T(8,128)(2,1)}, bf16[1536,128]{1,0:T(8,128)(2,1)}, bf16[768,1536]{1,0:T(8,128)(2,1)}) custom-call(bf16[288,1536]{1,0:T(8,128)(2,1)} %pad_maximum_fusion.refs_0_, bf16[288,1536]{1,0:T(8,128)(2,1)} %collective-permute-done.3.refs_1_, bf16[288,1536]{1,0:T(8,128)(2,1)} %collective-permute-done.4.refs_2_, ...), custom_call_target="tpu_custom_call" | custom-call | bytes 14155776 | tf_op jit(solution)/shard_map/pallas_call | solution.py:422
  658.9 4.5 multiply_convert_fusion
  677.7 4.7 select_reduce_fusion.3
  688.7 3.7 collective-permute-done.12
  694.3 3.9 collective-permute-done.40
  698.7 7.0 collective-permute-done.26
  707.1 9.4 collective-permute-start.42
  716.7 8.2 collective-permute-start.28
  727.5 19.9 %shard_map.375 = (f32[256,1536]{1,0:T(8,128)}, bf16[256,1536]{1,0:T(8,128)(2,1)S(1)}, f32[256,1536]{1,0:T(8,128)}, bf16[256,1536]{1,0:T(8,128)(2,1)S(1)}, bf16[2...) custom-call(bf16[256,1536]{1,0:T(8,128)(2,1)S(1)} %pad_maximum_fusio, ...), custom_call_target="tpu_custom_call" | custom-call | flops 12079595520 | bytes 34603008 | tf_op jit(solution)/shard_map/pallas_call | solution.py:592
  749.6 19.9 %shard_map.376 = (f32[256,1536]{1,0:T(8,128)}, bf16[256,1536]{1,0:T(8,128)(2,1)S(1)}, f32[256,1536]{1,0:T(8,128)}, bf16[256,1536]{1,0:T(8,128)(2,1)S(1)}, bf16[2...) custom-call(bf16[256,1536]{1,0:T(8,128)(2,1)S(1)} %constant_dynamic-, ...), custom_call_target="tpu_custom_call", output_to_operand_aliasing={{4}: (8, {}), {5}: (9, {}), {6}: (10, {}), {7}: (11, {}), {... | custom-call | flops 12079595520 | bytes 34603008 | tf_op jit(solution)/shard_map/pallas_call | solution.py:592
  769.6 20.1 %shard_map.377 = (f32[256,1536]{1,0:T(8,128)}, bf16[256,1536]{1,0:T(8,128)(2,1)S(1)}, f32[256,1536]{1,0:T(8,128)}, bf16[256,1536]{1,0:T(8,128)(2,1)S(1)}, bf16[2...) custom-call(bf16[256,1536]{1,0:T(8,128)(2,1)S(1)} %constant_dynamic-, ...), custom_call_target="tpu_custom_call", output_to_operand_aliasing={{4}: (8, {}), {5}: (9, {}), {6}: (10, {}), {7}: (11, {}), {... | custom-call | flops 12079595520 | bytes 34603008 | tf_op jit(solution)/shard_map/pallas_call | solution.py:592
  798.9 20.7 %shard_map.378 = (f32[256,1536]{1,0:T(8,128)}, bf16[256,1536]{1,0:T(8,128)(2,1)S(1)}, f32[256,1536]{1,0:T(8,128)}, bf16[256,1536]{1,0:T(8,128)(2,1)S(1)}, bf16[2...) custom-call(bf16[256,1536]{1,0:T(8,128)(2,1)S(1)} %constant_dynamic-, ...), custom_call_target="tpu_custom_call", output_to_operand_aliasing={{4}: (8, {}), {5}: (9, {}), {6}: (10, {}), {7}: (11, {}), {... | custom-call | flops 12079595520 | bytes 34603008 | tf_op jit(solution)/shard_map/pallas_call | solution.py:592
  819.6 34.8 %shard_map.380 = (f32[4,2,192,1280]{3,2,1,0:T(8,128)}, bf16[4,2,192,1280]{3,2,1,0:T(8,128)(2,1)}, f32[10,64,1536]{2,1,0:T(8,128)}, f32[10,64,1536]{2,1,0:T(8,128)}) custom-call(s32[2]{0:T(128)S(1)} %copy-done.7, bf16[2048,1536]{1,0:T(8,128)(2,1)} %get-tuple-element.119.rows_ref, bf16[2048,1536]{1,0:T(8,128)(2,1)} %get-tuple-element.120.grads_ref, ...), custom_call_target="tpu_custom_call" | custom-call | flops 24159191040 | bytes 67633152 | tf_op jit(solution)/shard_map/pallas_call | solution.py:675
  864.6 8.2 collective-permute-done.62
  874.5 6.0 collective-permute-done.51
  884.0 8.6 collective-permute-done.58
  894.4 6.0 collective-permute-done.47
  902.3 8.0 collective-permute-done.59
  912.6 13.8 %collective-permute-done.48 = bf16[128,1536]{1,0:T(8,128)(2,1)S(1)} collective-permute-done((bf16[128,1536]{1,0:T(8,128)(2,1)S(1)}, bf16[128,1536]{1,0:T(8,128)(2,1)S(1)}, u32[]{:S(2)}, u32[]{:S(2)}) %collective-permute-start.48) | collective-permute-done | bytes 393248 | tf_op jit(solution)/shard_map/ppermute | solution.py:183
  930.9 7.2 collective-permute-start.49
  938.0 8.8 collective-permute-done.60
  947.8 5.1 collective-permute-done.49
  974.2 5.4 multiply_reduce_fusion
  981.1 4.8 shard_map.379
  988.9 4.3 fusion.1
  995.7 4.9 collective-permute-done.68
  1004.7 4.2 collective-permute-start.69
  1011.5 8.1 collective-permute-done.71
  1019.6 8.3 collective-permute-done.69
  1031.4 4.3 collective-permute-start.70
  1037.1 6.2 fusion.49
  1045.0 11.2 %collective-permute-done.72 = bf16[288,1536]{1,0:T(8,128)(2,1)S(1)} collective-permute-done((bf16[288,1536]{1,0:T(8,128)(2,1)S(1)}, bf16[288,1536]{1,0:T(8,128)(2,1)S(1)}, u32[]{:S(2)}, u32[]{:S(2)}) %collective-permute-start.72) | collective-permute-done | bytes 884768 | tf_op jit(solution)/shard_map/ppermute | solution.py:183
  1057.4 13.4 %collective-permute-done.70 = bf16[288,1536]{1,0:T(8,128)(2,1)S(1)} collective-permute-done((bf16[288,1536]{1,0:T(8,128)(2,1)S(1)}, bf16[288,1536]{1,0:T(8,128)(2,1)S(1)}, u32[]{:S(2)}, u32[]{:S(2)}) %collective-permute-start.70) | collective-permute-done | bytes 884768 | tf_op jit(solution)/shard_map/ppermute | solution.py:183
  1073.5 11.6 %multiply_subtract_fusion = (f32[10,64,1536]{2,1,0:T(8,128)}, f32[10,64,1536]{2,1,0:T(8,128)}, f32[10,64,1536]{2,1,0:T(8,128)}, f32[10,64,1536]{2,1,0:T(8,128)}) fusion(f32[10,64,1536]{2,1,0:T(8,128)S(1)} %copy-done.10, f32[10,64,1536]{2,1,0:T(8,128)} %param.35, f32[10,64,1536]{2,1,0:T(8,128)} %param.40, f32[10,64,1536]{2,1,0:T(8,128)} %get-tuple-element.127, ...), kind=kLoop, calls=%fused_computation.14 | loop fusion | flops 15728640 | bytes 35389440 | tf_op jit(solution)/shard_map/sub | solution.py:147
  1092.3 17.8 %shard_map.381 = (f32[10,192,1024]{2,1,0:T(8,128)}, f32[10,192,1024]{2,1,0:T(8,128)}, f32[10,192,1024]{2,1,0:T(8,128)}, f32[10,192,1024]{2,1,0:T(8,128)}) custom-call(s32[2]{0:T(128)S(1)} %copy-done.7, f32[10,192,1024]{2,1,0:T(8,128)S(1)} %bitcast.141, f32[10,192,1024]{2,1,0:T(8,128)S(1)} %copy-done, f32[10,192,1024]{2,1,0:T(8,128)} %second_ref.1, ...), custom_call_target="tpu_custom_call" | custom-call | flops 39321600 | bytes 58982400 | tf_op jit(solution)/shard_map/pallas_call | solution.py:726
  (581 shorter events, 201.4 us)
Async XLA Ops:
  4.3 50.0 %collective-permute-start.43 = (bf16[128,1664]{1,0:T(8,128)(2,1)}, bf16[128,1664]{1,0:T(8,128)(2,1)}, u32[]{:S(2)}, u32[]{:S(2)}) collective-permute-start(bf16[128,1664]{1,0:T(8,128)(2,1)} %pad_maximum_fusion.6), channel_id=1, source_target_pairs={{0,3},{1,0},{2,1},{3,2},{4,7},{5,4},{6,5},{7,6},{8,11},{9,8},{10,9... | collective-permute-start | bytes 1277960 | tf_op jit(solution)/shard_map/ppermute | solution.py:183
  9.3 42.5 %collective-permute-start.29 = (bf16[128,1664]{1,0:T(8,128)(2,1)}, bf16[128,1664]{1,0:T(8,128)(2,1)S(1)}, u32[]{:S(2)}, u32[]{:S(2)}) collective-permute-start(bf16[128,1664]{1,0:T(8,128)(2,1)} %pad_maximum_fusion.6), channel_id=1, source_target_pairs={{0,1},{1,2},{2,3},{3,0},{4,5},{5,6},{6,7},{7,4},{8,9},{9,10},{10,1... | collective-permute-start | bytes 1277960 | tf_op jit(solution)/shard_map/ppermute | solution.py:183
  9.3 39.1 %collective-permute-start.14 = (bf16[128,1664]{1,0:T(8,128)(2,1)}, bf16[128,1664]{1,0:T(8,128)(2,1)S(1)}, u32[]{:S(2)}, u32[]{:S(2)}) collective-permute-start(bf16[128,1664]{1,0:T(8,128)(2,1)} %pad_maximum_fusion.6), channel_id=1, source_target_pairs={{0,16},{4,12},{8,24},{12,4},{16,0},{20,28},{24,8},{28,20},{1,17},{... | collective-permute-start | bytes 1277960 | tf_op jit(solution)/shard_map/ppermute | solution.py:158
  10.9 36.1 %collective-permute-start = (bf16[128,1536]{1,0:T(8,128)(2,1)S(1)}, bf16[128,1536]{1,0:T(8,128)(2,1)S(1)}, u32[]{:S(2)}, u32[]{:S(2)}) collective-permute-start(bf16[128,1536]{1,0:T(8,128)(2,1)S(1)} %copy-done.14), channel_id=1, source_target_pairs={{0,4},{4,0},{8,12},{12,8},{16,20},{20,16},{24,28},{28,24},{1,5},{5... | collective-permute-start | bytes 1179656 | tf_op jit(solution)/shard_map/ppermute | solution.py:158
  10.9 33.0 %collective-permute-start.10 = (s32[1,128]{1,0:T(1,128)}, s32[1,128]{1,0:T(1,128)}, u32[]{:S(2)}, u32[]{:S(2)}) collective-permute-start(s32[1,128]{1,0:T(1,128)} %param.23), channel_id=1, source_target_pairs={{0,4},{4,0},{8,12},{12,8},{16,20},{20,16},{24,28},{28,24},{1,5},{5... | collective-permute-start | bytes 1544 | tf_op jit(solution)/shard_map/ppermute | solution.py:158
  45.4 94.5 %collective-permute-start.16 = (bf16[2,192,1280]{2,1,0:T(8,128)(2,1)}, bf16[2,192,1280]{2,1,0:T(8,128)(2,1)S(1)}, u32[]{:S(2)}, u32[]{:S(2)}) collective-permute-start(bf16[2,192,1280]{2,1,0:T(8,128)(2,1)} %get-tuple-element.81), channel_id=1, source_target_pairs={{0,8},{4,12},{8,0},{12,4},{16,24},{20,28},{24,16},{28,20},{1,9},{5... | collective-permute-start | bytes 2949128 | tf_op jit(solution)/shard_map/ppermute | solution.py:158
  47.0 93.0 %collective-permute-start.17 = (bf16[2,192,1280]{2,1,0:T(8,128)(2,1)}, bf16[2,192,1280]{2,1,0:T(8,128)(2,1)S(1)}, u32[]{:S(2)}, u32[]{:S(2)}) collective-permute-start(bf16[2,192,1280]{2,1,0:T(8,128)(2,1)} %get-tuple-element.82), channel_id=1, source_target_pairs={{0,16},{4,20},{8,24},{12,28},{16,0},{20,4},{24,8},{28,12},{1,17},{... | collective-permute-start | bytes 2949128 | tf_op jit(solution)/shard_map/ppermute | solution.py:158
  49.2 90.9 %collective-permute-start.18 = (bf16[2,192,1280]{2,1,0:T(8,128)(2,1)S(1)}, bf16[2,192,1280]{2,1,0:T(8,128)(2,1)S(1)}, u32[]{:S(2)}, u32[]{:S(2)}) collective-permute-start(bf16[2,192,1280]{2,1,0:T(8,128)(2,1)S(1)} %copy-done.104), channel_id=1, source_target_pairs={{0,24},{4,28},{8,16},{12,20},{16,8},{20,12},{24,0},{28,4},{1,25},{... | collective-permute-start | bytes 2949128 | tf_op jit(solution)/shard_map/ppermute | solution.py:158
  52.6 44.3 %collective-permute-start.2 = (bf16[144,1536]{1,0:T(8,128)(2,1)S(1)}, bf16[144,1536]{1,0:T(8,128)(2,1)S(1)}, u32[]{:S(2)}, u32[]{:S(2)}) collective-permute-start(bf16[144,1536]{1,0:T(8,128)(2,1)S(1)} %pad_maximum_fusion.5), channel_id=1, source_target_pairs={{0,16},{4,12},{8,24},{12,4},{16,0},{20,28},{24,8},{28,20},{1,17},{... | collective-permute-start | bytes 1327112 | tf_op jit(solution)/shard_map/ppermute | solution.py:158
  54.3 50.2 %collective-permute-start.30 = (bf16[128,1664]{1,0:T(8,128)(2,1)}, bf16[128,1664]{1,0:T(8,128)(2,1)S(1)}, u32[]{:S(2)}, u32[]{:S(2)}) collective-permute-start(bf16[128,1664]{1,0:T(8,128)(2,1)} %copy-done.67), channel_id=1, source_target_pairs={{0,16},{4,12},{8,24},{12,4},{16,0},{20,28},{24,8},{28,20},{1,17},{... | collective-permute-start | bytes 1277960 | tf_op jit(solution)/shard_map/ppermute | solution.py:158
  96.9 40.3 %collective-permute-start.15 = (bf16[256,1664]{1,0:T(8,128)(2,1)S(1)}, bf16[256,1664]{1,0:T(8,128)(2,1)S(1)}, u32[]{:S(2)}, u32[]{:S(2)}) collective-permute-start(bf16[256,1664]{1,0:T(8,128)(2,1)S(1)} %pad_maximum_fusion.1.near_grad_ref), channel_id=1, source_target_pairs={{0,8},{4,20},{8,0},{12,28},{16,24},{20,4},{24,16},{28,12},{1,9},{5... | collective-permute-start | bytes 2555912 | tf_op jit(solution)/shard_map/ppermute | solution.py:158
  139.9 49.7 %collective-permute-start.23 = (bf16[10,64,1536]{2,1,0:T(8,128)(2,1)S(1)}, bf16[10,64,1536]{2,1,0:T(8,128)(2,1)S(1)}, u32[]{:S(2)}, u32[]{:S(2)}) collective-permute-start(bf16[10,64,1536]{2,1,0:T(8,128)(2,1)S(1)} %copy-done.13), channel_id=1, source_target_pairs={{0,4},{4,0},{8,12},{12,8},{16,20},{20,16},{24,28},{28,24},{1,5},{5... | collective-permute-start | bytes 5898248 | tf_op jit(solution)/shard_map/ppermute | solution.py:158
  140.0 24.7 %collective-permute-start.4 = (bf16[288,1536]{1,0:T(8,128)(2,1)}, bf16[288,1536]{1,0:T(8,128)(2,1)}, u32[]{:S(2)}, u32[]{:S(2)}) collective-permute-start(bf16[288,1536]{1,0:T(8,128)(2,1)} %pad_maximum_fusion.refs_0_), channel_id=1, source_target_pairs={{0,1},{1,2},{2,3},{3,0},{4,5},{5,6},{6,7},{7,4},{8,9},{9,10},{10,1... | collective-permute-start | bytes 2654216 | tf_op jit(solution)/shard_map/ppermute | solution.py:183
  140.0 41.3 %collective-permute-start.6 = (bf16[288,1536]{1,0:T(8,128)(2,1)}, bf16[288,1536]{1,0:T(8,128)(2,1)}, u32[]{:S(2)}, u32[]{:S(2)}) collective-permute-start(bf16[288,1536]{1,0:T(8,128)(2,1)} %pad_maximum_fusion.refs_0_), channel_id=1, source_target_pairs={{0,3},{1,0},{2,1},{3,2},{4,7},{5,4},{6,5},{7,6},{8,11},{9,8},{10,9... | collective-permute-start | bytes 2654216 | tf_op jit(solution)/shard_map/ppermute | solution.py:183
  144.6 38.3 %collective-permute-start.45 = (bf16[256,1664]{1,0:T(8,128)(2,1)S(1)}, bf16[256,1664]{1,0:T(8,128)(2,1)S(1)}, u32[]{:S(2)}, u32[]{:S(2)}) collective-permute-start(bf16[256,1664]{1,0:T(8,128)(2,1)S(1)} %constant_dynamic-update-slice_fusion.18.near_grad_ref), channel_id=1, source_target_pairs={{0,8},{4,20},{8,0},{12,28},{16,24},{20,4},{24,16},{28,12},{1,9},{5... | collective-permute-start | bytes 2555912 | tf_op jit(solution)/shard_map/ppermute | solution.py:158
  149.9 34.9 %collective-permute-start.20 = (bf16[2,192,1280]{2,1,0:T(8,128)(2,1)S(1)}, bf16[2,192,1280]{2,1,0:T(8,128)(2,1)S(1)}, u32[]{:S(2)}, u32[]{:S(2)}) collective-permute-start(bf16[2,192,1280]{2,1,0:T(8,128)(2,1)S(1)} %collective-permute-done.16.refs_1_), channel_id=1, source_target_pairs={{0,4},{4,0},{8,12},{12,8},{16,20},{20,16},{24,28},{28,24},{1,5},{5... | collective-permute-start | bytes 2949128 | tf_op jit(solution)/shard_map/ppermute | solution.py:158
  164.6 22.9 %collective-permute-start.21 = (bf16[2,192,1280]{2,1,0:T(8,128)(2,1)S(1)}, bf16[2,192,1280]{2,1,0:T(8,128)(2,1)S(1)}, u32[]{:S(2)}, u32[]{:S(2)}) collective-permute-start(bf16[2,192,1280]{2,1,0:T(8,128)(2,1)S(1)} %collective-permute-done.17.refs_2_), channel_id=1, source_target_pairs={{0,4},{4,0},{8,12},{12,8},{16,20},{20,16},{24,28},{28,24},{1,5},{5... | collective-permute-start | bytes 2949128 | tf_op jit(solution)/shard_map/ppermute | solution.py:158
  182.9 24.3 %collective-permute-start.8 = (bf16[288,1536]{1,0:T(8,128)(2,1)}, bf16[288,1536]{1,0:T(8,128)(2,1)}, u32[]{:S(2)}, u32[]{:S(2)}) collective-permute-start(bf16[288,1536]{1,0:T(8,128)(2,1)} %collective-permute-done.4.refs_2_), channel_id=1, source_target_pairs={{0,1},{1,2},{2,3},{3,0},{4,5},{5,6},{6,7},{7,4},{8,9},{9,10},{10,1... | collective-permute-start | bytes 2654216 | tf_op jit(solution)/shard_map/ppermute | solution.py:183
  184.8 265.5 %collective-permute-start.39 = (bf16[256,1664]{1,0:T(8,128)(2,1)}, bf16[256,1664]{1,0:T(8,128)(2,1)}, u32[]{:S(2)}, u32[]{:S(2)}) collective-permute-start(bf16[256,1664]{1,0:T(8,128)(2,1)} %constant_dynamic-update-slice_fusion.14.near_grad_ref), channel_id=1, source_target_pairs={{0,8},{4,20},{8,0},{12,28},{16,24},{20,4},{24,16},{28,12},{1,9},{5... | collective-permute-start | bytes 2555912 | tf_op jit(solution)/shard_map/ppermute | solution.py:158
  187.6 266.0 %collective-permute-start.3 = (bf16[288,1536]{1,0:T(8,128)(2,1)}, bf16[288,1536]{1,0:T(8,128)(2,1)}, u32[]{:S(2)}, u32[]{:S(2)}) collective-permute-start(bf16[288,1536]{1,0:T(8,128)(2,1)} %pad_maximum_fusion.refs_0_), channel_id=1, source_target_pairs={{0,8},{4,20},{8,0},{12,28},{16,24},{20,4},{24,16},{28,12},{1,9},{5... | collective-permute-start | bytes 2654216 | tf_op jit(solution)/shard_map/ppermute | solution.py:158
  189.3 264.3 %collective-permute-start.5 = (bf16[288,1536]{1,0:T(8,128)(2,1)}, bf16[288,1536]{1,0:T(8,128)(2,1)}, u32[]{:S(2)}, u32[]{:S(2)}) collective-permute-start(bf16[288,1536]{1,0:T(8,128)(2,1)} %collective-permute-done.4.refs_2_), channel_id=1, source_target_pairs={{0,8},{4,20},{8,0},{12,28},{16,24},{20,4},{24,16},{28,12},{1,9},{5... | collective-permute-start | bytes 2654216 | tf_op jit(solution)/shard_map/ppermute | solution.py:158
  189.6 264.0 %collective-permute-start.7 = (bf16[288,1536]{1,0:T(8,128)(2,1)}, bf16[288,1536]{1,0:T(8,128)(2,1)}, u32[]{:S(2)}, u32[]{:S(2)}) collective-permute-start(bf16[288,1536]{1,0:T(8,128)(2,1)} %collective-permute-done.6.refs_4_), channel_id=1, source_target_pairs={{0,8},{4,20},{8,0},{12,28},{16,24},{20,4},{24,16},{28,12},{1,9},{5... | collective-permute-start | bytes 2654216 | tf_op jit(solution)/shard_map/ppermute | solution.py:158
  207.3 246.3 %collective-permute-start.9 = (bf16[288,1536]{1,0:T(8,128)(2,1)}, bf16[288,1536]{1,0:T(8,128)(2,1)}, u32[]{:S(2)}, u32[]{:S(2)}) collective-permute-start(bf16[288,1536]{1,0:T(8,128)(2,1)} %collective-permute-done.8.refs_6_), channel_id=1, source_target_pairs={{0,8},{4,20},{8,0},{12,28},{16,24},{20,4},{24,16},{28,12},{1,9},{5... | collective-permute-start | bytes 2654216 | tf_op jit(solution)/shard_map/ppermute | solution.py:158
  692.5 35.0 %collective-permute-start.13 = (bf16[256,1536]{1,0:T(8,128)(2,1)S(1)}, bf16[256,1536]{1,0:T(8,128)(2,1)S(1)}, u32[]{:S(2)}, u32[]{:S(2)}) collective-permute-start(bf16[256,1536]{1,0:T(8,128)(2,1)S(1)} %pad_maximum_fusion.2.near_ref), channel_id=1, source_target_pairs={{0,8},{4,20},{8,0},{12,28},{16,24},{20,4},{24,16},{28,12},{1,9},{5... | collective-permute-start | bytes 2359304 | tf_op jit(solution)/shard_map/ppermute | solution.py:158
  707.1 62.4 %collective-permute-start.42 = (bf16[256,1536]{1,0:T(8,128)(2,1)S(1)}, bf16[256,1536]{1,0:T(8,128)(2,1)S(1)}, u32[]{:S(2)}, u32[]{:S(2)}) collective-permute-start(bf16[256,1536]{1,0:T(8,128)(2,1)S(1)} %constant_dynamic-update-slice_fusion.16.near_ref), channel_id=1, source_target_pairs={{0,8},{4,20},{8,0},{12,28},{16,24},{20,4},{24,16},{28,12},{1,9},{5... | collective-permute-start | bytes 2359304 | tf_op jit(solution)/shard_map/ppermute | solution.py:158
  716.7 33.0 %collective-permute-start.28 = (bf16[256,1536]{1,0:T(8,128)(2,1)S(1)}, bf16[256,1536]{1,0:T(8,128)(2,1)S(1)}, u32[]{:S(2)}, u32[]{:S(2)}) collective-permute-start(bf16[256,1536]{1,0:T(8,128)(2,1)S(1)} %constant_dynamic-update-slice_fusion.8.near_ref), channel_id=1, source_target_pairs={{0,8},{4,20},{8,0},{12,28},{16,24},{20,4},{24,16},{28,12},{1,9},{5... | collective-permute-start | bytes 2359304 | tf_op jit(solution)/shard_map/ppermute | solution.py:158
  724.9 24.5 %collective-permute-start.35 = (bf16[128,1536]{1,0:T(8,128)(2,1)S(1)}, bf16[128,1536]{1,0:T(8,128)(2,1)S(1)}, u32[]{:S(2)}, u32[]{:S(2)}) collective-permute-start(bf16[128,1536]{1,0:T(8,128)(2,1)S(1)} %collective-permute-done.34), channel_id=1, source_target_pairs={{0,16},{4,12},{8,24},{12,4},{16,0},{20,28},{24,8},{28,20},{1,17},{... | collective-permute-start | bytes 1179656 | tf_op jit(solution)/shard_map/ppermute | solution.py:158
  747.3 44.4 %collective-permute-start.53 = (bf16[256,1536]{1,0:T(8,128)(2,1)S(1)}, bf16[256,1536]{1,0:T(8,128)(2,1)}, u32[]{:S(2)}, u32[]{:S(2)}) collective-permute-start(bf16[256,1536]{1,0:T(8,128)(2,1)S(1)} %get-tuple-element.110), channel_id=1, source_target_pairs={{0,8},{4,20},{8,0},{12,28},{16,24},{20,4},{24,16},{28,12},{1,9},{5... | collective-permute-start | bytes 2359304 | tf_op jit(solution)/shard_map/ppermute | solution.py:158
  747.5 47.7 %collective-permute-start.24 = (bf16[256,1536]{1,0:T(8,128)(2,1)S(1)}, bf16[256,1536]{1,0:T(8,128)(2,1)S(1)}, u32[]{:S(2)}, u32[]{:S(2)}) collective-permute-start(bf16[256,1536]{1,0:T(8,128)(2,1)S(1)} %get-tuple-element.87), channel_id=1, source_target_pairs={{0,8},{4,20},{8,0},{12,28},{16,24},{20,4},{24,16},{28,12},{1,9},{5... | collective-permute-start | bytes 2359304 | tf_op jit(solution)/shard_map/ppermute | solution.py:158
  749.5 48.2 %collective-permute-start.36 = (bf16[256,1536]{1,0:T(8,128)(2,1)S(1)}, bf16[256,1536]{1,0:T(8,128)(2,1)S(1)}, u32[]{:S(2)}, u32[]{:S(2)}) collective-permute-start(bf16[256,1536]{1,0:T(8,128)(2,1)S(1)} %constant_dynamic-update-slice_fusion.12.near_ref), channel_id=1, source_target_pairs={{0,8},{4,20},{8,0},{12,28},{16,24},{20,4},{24,16},{28,12},{1,9},{5... | collective-permute-start | bytes 2359304 | tf_op jit(solution)/shard_map/ppermute | solution.py:158
  789.7 64.7 %collective-permute-start.61 = (bf16[256,1536]{1,0:T(8,128)(2,1)S(1)}, bf16[256,1536]{1,0:T(8,128)(2,1)}, u32[]{:S(2)}, u32[]{:S(2)}) collective-permute-start(bf16[256,1536]{1,0:T(8,128)(2,1)S(1)} %get-tuple-element.116), channel_id=1, source_target_pairs={{0,8},{4,20},{8,0},{12,28},{16,24},{20,4},{24,16},{28,12},{1,9},{5... | collective-permute-start | bytes 2359304 | tf_op jit(solution)/shard_map/ppermute | solution.py:158
  791.7 65.2 %collective-permute-start.55 = (bf16[256,1536]{1,0:T(8,128)(2,1)S(1)}, bf16[256,1536]{1,0:T(8,128)(2,1)}, u32[]{:S(2)}, u32[]{:S(2)}) collective-permute-start(bf16[256,1536]{1,0:T(8,128)(2,1)S(1)} %get-tuple-element.112), channel_id=1, source_target_pairs={{0,8},{4,20},{8,0},{12,28},{16,24},{20,4},{24,16},{28,12},{1,9},{5... | collective-permute-start | bytes 2359304 | tf_op jit(solution)/shard_map/ppermute | solution.py:158
  791.8 68.5 %collective-permute-start.50 = (bf16[256,1536]{1,0:T(8,128)(2,1)S(1)}, bf16[256,1536]{1,0:T(8,128)(2,1)}, u32[]{:S(2)}, u32[]{:S(2)}) collective-permute-start(bf16[256,1536]{1,0:T(8,128)(2,1)S(1)} %get-tuple-element.108), channel_id=1, source_target_pairs={{0,8},{4,20},{8,0},{12,28},{16,24},{20,4},{24,16},{28,12},{1,9},{5... | collective-permute-start | bytes 2359304 | tf_op jit(solution)/shard_map/ppermute | solution.py:158
  796.2 66.9 %collective-permute-start.32 = (bf16[256,1536]{1,0:T(8,128)(2,1)S(1)}, bf16[256,1536]{1,0:T(8,128)(2,1)S(1)}, u32[]{:S(2)}, u32[]{:S(2)}) collective-permute-start(bf16[256,1536]{1,0:T(8,128)(2,1)S(1)} %get-tuple-element.94), channel_id=1, source_target_pairs={{0,8},{4,20},{8,0},{12,28},{16,24},{20,4},{24,16},{28,12},{1,9},{5... | collective-permute-start | bytes 2359304 | tf_op jit(solution)/shard_map/ppermute | solution.py:158
  797.7 128.8 %collective-permute-start.54 = (bf16[128,1536]{1,0:T(8,128)(2,1)S(1)}, bf16[128,1536]{1,0:T(8,128)(2,1)S(1)}, u32[]{:S(2)}, u32[]{:S(2)}) collective-permute-start(bf16[128,1536]{1,0:T(8,128)(2,1)S(1)} %slice.792), channel_id=1, source_target_pairs={{0,16},{4,12},{8,24},{12,4},{16,0},{20,28},{24,8},{28,20},{1,17},{... | collective-permute-start | bytes 1179656 | tf_op jit(solution)/shard_map/ppermute | solution.py:158
  854.4 93.0 %collective-permute-start.25 = (bf16[128,1536]{1,0:T(8,128)(2,1)S(1)}, bf16[128,1536]{1,0:T(8,128)(2,1)S(1)}, u32[]{:S(2)}, u32[]{:S(2)}) collective-permute-start(bf16[128,1536]{1,0:T(8,128)(2,1)S(1)} %slice.796), channel_id=1, source_target_pairs={{0,16},{4,12},{8,24},{12,4},{16,0},{20,28},{24,8},{28,20},{1,17},{... | collective-permute-start | bytes 1179656 | tf_op jit(solution)/shard_map/ppermute | solution.py:158
  856.8 23.8 %collective-permute-start.57 = (bf16[256,1536]{1,0:T(8,128)(2,1)S(1)}, bf16[256,1536]{1,0:T(8,128)(2,1)S(1)}, u32[]{:S(2)}, u32[]{:S(2)}) collective-permute-start(bf16[256,1536]{1,0:T(8,128)(2,1)S(1)} %get-tuple-element.114), channel_id=1, source_target_pairs={{0,8},{4,20},{8,0},{12,28},{16,24},{20,4},{24,16},{28,12},{1,9},{5... | collective-permute-start | bytes 2359304 | tf_op jit(solution)/shard_map/ppermute | solution.py:158
  860.3 22.3 %collective-permute-start.46 = (bf16[256,1536]{1,0:T(8,128)(2,1)S(1)}, bf16[256,1536]{1,0:T(8,128)(2,1)S(1)}, u32[]{:S(2)}, u32[]{:S(2)}) collective-permute-start(bf16[256,1536]{1,0:T(8,128)(2,1)S(1)} %get-tuple-element.106), channel_id=1, source_target_pairs={{0,8},{4,20},{8,0},{12,28},{16,24},{20,4},{24,16},{28,12},{1,9},{5... | collective-permute-start | bytes 2359304 | tf_op jit(solution)/shard_map/ppermute | solution.py:158
  880.5 156.5 %collective-permute-start.75 = (bf16[4,2,192,1280]{3,2,1,0:T(8,128)(2,1)}, bf16[4,2,192,1280]{3,2,1,0:T(8,128)(2,1)}, u32[]{:S(2)}, u32[]{:S(2)}) collective-permute-start(bf16[4,2,192,1280]{3,2,1,0:T(8,128)(2,1)} %get-tuple-element.125), channel_id=1, source_target_pairs={{0,4},{4,0},{8,12},{12,8},{16,20},{20,16},{24,28},{28,24},{1,5},{5... | collective-permute-start | bytes 11796488 | tf_op jit(solution)/shard_map/ppermute | solution.py:158
  994.2 78.8 %collective-permute-start.79 = (f32[10,64,1536]{2,1,0:T(8,128)}, f32[10,64,1536]{2,1,0:T(8,128)}, u32[]{:S(2)}, u32[]{:S(2)}) collective-permute-start(f32[10,64,1536]{2,1,0:T(8,128)} %get-tuple-element.128), channel_id=1, source_target_pairs={{0,4},{4,0},{8,12},{12,8},{16,20},{20,16},{24,28},{28,24},{1,5},{5... | collective-permute-start | bytes 11796488 | tf_op jit(solution)/shard_map/ppermute | solution.py:158
  1004.7 23.3 %collective-permute-start.69 = (bf16[288,1536]{1,0:T(8,128)(2,1)}, bf16[288,1536]{1,0:T(8,128)(2,1)}, u32[]{:S(2)}, u32[]{:S(2)}) collective-permute-start(bf16[288,1536]{1,0:T(8,128)(2,1)} %fusion.20), channel_id=1, source_target_pairs={{0,3},{1,0},{2,1},{3,2},{4,7},{5,4},{6,5},{7,6},{8,11},{9,8},{10,9... | collective-permute-start | bytes 2654216 | tf_op jit(solution)/shard_map/ppermute | solution.py:183
  1010.4 34.3 %collective-permute-start.66 = (bf16[288,1536]{1,0:T(8,128)(2,1)S(1)}, bf16[288,1536]{1,0:T(8,128)(2,1)S(1)}, u32[]{:S(2)}, u32[]{:S(2)}) collective-permute-start(bf16[288,1536]{1,0:T(8,128)(2,1)S(1)} %copy-done.48), channel_id=1, source_target_pairs={{0,8},{4,20},{8,0},{12,28},{16,24},{20,4},{24,16},{28,12},{1,9},{5... | collective-permute-start | bytes 2654216 | tf_op jit(solution)/shard_map/ppermute | solution.py:158
  1031.3 24.9 %collective-permute-start.72 = (bf16[288,1536]{1,0:T(8,128)(2,1)S(1)}, bf16[288,1536]{1,0:T(8,128)(2,1)S(1)}, u32[]{:S(2)}, u32[]{:S(2)}) collective-permute-start(bf16[288,1536]{1,0:T(8,128)(2,1)S(1)} %get-tuple-element.286), channel_id=1, source_target_pairs={{0,1},{1,2},{2,3},{3,0},{4,5},{5,6},{6,7},{7,4},{8,9},{9,10},{10,1... | collective-permute-start | bytes 2654216 | tf_op jit(solution)/shard_map/ppermute | solution.py:183
  1031.4 39.4 %collective-permute-start.70 = (bf16[288,1536]{1,0:T(8,128)(2,1)S(1)}, bf16[288,1536]{1,0:T(8,128)(2,1)S(1)}, u32[]{:S(2)}, u32[]{:S(2)}) collective-permute-start(bf16[288,1536]{1,0:T(8,128)(2,1)S(1)} %get-tuple-element.285), channel_id=1, source_target_pairs={{0,3},{1,0},{2,1},{3,2},{4,7},{5,4},{6,5},{7,6},{8,11},{9,8},{10,9... | collective-permute-start | bytes 2654216 | tf_op jit(solution)/shard_map/ppermute | solution.py:183
  1043.3 41.8 %collective-permute-start.76 = (bf16[2,192,1280]{2,1,0:T(8,128)(2,1)}, bf16[2,192,1280]{2,1,0:T(8,128)(2,1)S(1)}, u32[]{:S(2)}, u32[]{:S(2)}) collective-permute-start(bf16[2,192,1280]{2,1,0:T(8,128)(2,1)} %get-tuple-element.283), channel_id=1, source_target_pairs={{0,8},{4,12},{8,0},{12,4},{16,24},{20,28},{24,16},{28,20},{1,9},{5... | collective-permute-start | bytes 2949128 | tf_op jit(solution)/shard_map/ppermute | solution.py:158
  1044.7 43.0 %collective-permute-start.77 = (bf16[2,192,1280]{2,1,0:T(8,128)(2,1)S(1)}, bf16[2,192,1280]{2,1,0:T(8,128)(2,1)S(1)}, u32[]{:S(2)}, u32[]{:S(2)}) collective-permute-start(bf16[2,192,1280]{2,1,0:T(8,128)(2,1)S(1)} %get-tuple-element.282), channel_id=1, source_target_pairs={{0,16},{4,20},{8,24},{12,28},{16,0},{20,4},{24,8},{28,12},{1,17},{... | collective-permute-start | bytes 2949128 | tf_op jit(solution)/shard_map/ppermute | solution.py:158
  1056.2 32.8 %collective-permute-start.78 = (bf16[2,192,1280]{2,1,0:T(8,128)(2,1)S(1)}, bf16[2,192,1280]{2,1,0:T(8,128)(2,1)S(1)}, u32[]{:S(2)}, u32[]{:S(2)}) collective-permute-start(bf16[2,192,1280]{2,1,0:T(8,128)(2,1)S(1)} %get-tuple-element.281), channel_id=1, source_target_pairs={{0,24},{4,28},{8,16},{12,20},{16,8},{20,12},{24,0},{28,4},{1,25},{... | collective-permute-start | bytes 2949128 | tf_op jit(solution)/shard_map/ppermute | solution.py:158
  1072.9 37.2 %collective-permute-start.73 = (bf16[144,1536]{1,0:T(8,128)(2,1)S(1)}, bf16[144,1536]{1,0:T(8,128)(2,1)}, u32[]{:S(2)}, u32[]{:S(2)}) collective-permute-start(bf16[144,1536]{1,0:T(8,128)(2,1)S(1)} %slice.788), channel_id=1, source_target_pairs={{0,16},{4,12},{8,24},{12,4},{16,0},{20,28},{24,8},{28,20},{1,17},{... | collective-permute-start | bytes 1327112 | tf_op jit(solution)/shard_map/ppermute | solution.py:158
  (142 other events, 2522.7 us)

commit v3 on v2

--- a/solution.py
+++ b/solution.py
@@ -183,46 +183,45 @@
     return lax.ppermute(rows, "expert", [(i, (i + step) % count) for i in range(count)])
 
 
+def after(values, *others):
+    return lax.optimization_barrier((values, others))[0]
+
+
+def along_first(part):
+    return jnp.concatenate([part, swap_first(part)], 0)
+
+
 def gather_plane_last(block):
     ahead, behind = turn(block, 1), turn(block, -1)
+    far = turn(ahead, 1)
     found = []
-    for part in (block, ahead, behind, turn(ahead, 1)):
+    for part in (block, ahead, behind, far):
         pair = jnp.concatenate([part, swap_first(part)], 0)
         found.append((pair, swap_second(pair)))
-    return found
-
-
-def gather_ring_middle(block):
+    return found, far
+
+
+def gather_ring(block):
     pair = jnp.concatenate([block, swap_first(block)], 0)
     ahead, behind = turn(pair, 1), turn(pair, -1)
-    return [(part, swap_second(part)) for part in (pair, ahead, behind, turn(ahead, 1))]
-
-
-def ring_sum(parts):
+    return pair, ahead, behind, turn(ahead, 1)
+
+
+def ring_sum(parts, gate=()):
+    behind = turn(parts[2].astype(NARROW), 1)
     far = turn(parts[3].astype(NARROW), -1)
     ahead = turn((parts[1] + far.astype(WIDE)).astype(NARROW), -1)
-    behind = turn(parts[2].astype(NARROW), 1)
-    return parts[0] + ahead.astype(WIDE) + behind.astype(WIDE)
-
-
-def scatter_plane_first(parts):
-    found = [None] * 4
-    for spot in (3, 1, 2, 0):
-        near, away = parts[spot]
-        near = near + swap_second(away).astype(WIDE)
-        half = near.shape[0] // 2
-        found[spot] = near[:half] + swap_first(near[half:].astype(NARROW)).astype(WIDE)
-    return ring_sum(found)
-
-
-def scatter_ring_middle(parts):
-    found = [None] * 4
-    for spot in (3, 1, 2, 0):
-        near, away = parts[spot]
-        found[spot] = near + swap_second(away).astype(WIDE)
-    total = ring_sum(found)
-    half = total.shape[0] // 2
-    return total[:half] + swap_first(total[half:].astype(NARROW)).astype(WIDE)
+    behind, ahead = after((behind, ahead), gate)
+    return parts[0] + behind.astype(WIDE) + ahead.astype(WIDE)
+
+
+def add_second(near, away, gate=()):
+    return near + after(swap_second(away.astype(NARROW)), gate).astype(WIDE)
+
+
+def add_first(rows, gate=()):
+    half = rows.shape[0] // 2
+    return rows[:half] + after(swap_first(rows[half:].astype(NARROW)), gate).astype(WIDE)
 
 
 def gathered_sources(count_dp, count_expert):
@@ -320,45 +319,40 @@
     )
 
 
-def spread_columns_kernel(place_ref, weight_ref, *out_refs):
-    lanes = out_refs[0].shape[2]
-    for other, out_ref in enumerate(out_refs):
-        start = pl.multiple_of((place_ref[0] ^ other) * lanes, lanes)
+def spread_columns_kernel(weight_ref, out_ref):
+    chips, _, _, lanes = out_ref.shape
+    for chip in range(chips):
         for part in range(2):
-            out_ref[part] = weight_ref[0, :, pl.ds(part * FF + start, lanes)].astype(out_ref.dtype)
-
-
-def spread_columns(place, weight, chips):
+            columns = slice(part * FF + chip * lanes, part * FF + (chip + 1) * lanes)
+            out_ref[chip, part] = weight_ref[0, :, columns].astype(out_ref.dtype)
+
+
+def spread_columns(weight, chips):
     experts, rows, both = weight.shape
     lanes = both // 2 // chips
     return pl.pallas_call(
         spread_columns_kernel,
-        grid_spec=pltpu.PrefetchScalarGridSpec(
-            num_scalar_prefetch=1,
-            grid=(experts,),
-            in_specs=[pl.BlockSpec((1, rows, both), lambda e, place: (e, 0, 0))],
-            out_specs=[pl.BlockSpec((2, rows, lanes), lambda e, place: (0, 0, e))] * chips,
-        ),
-        out_shape=[jax.ShapeDtypeStruct((2, rows, experts * lanes), jnp.bfloat16)] * chips,
+        grid=(experts,),
+        in_specs=[pl.BlockSpec((1, rows, both), lambda e: (e, 0, 0))],
+        out_specs=pl.BlockSpec((chips, 2, rows, lanes), lambda e: (0, 0, 0, e)),
+        out_shape=jax.ShapeDtypeStruct((chips, 2, rows, experts * lanes), jnp.bfloat16),
         cost_estimate=pl.CostEstimate(
             flops=0, bytes_accessed=6 * experts * rows * both, transcendentals=0
         ),
-    )(place, weight)
-
-
-def stack_rows_kernel(place_ref, *refs):
-    pieces, (gate_ref, upper_ref, sems) = refs[:-3], refs[-3:]
-    chip, core = place_ref[0], place_ref[1]
-    chips = len(pieces) // 2
-    rows = pieces[0].shape[1]
+    )(weight)
+
+
+def stack_rows_kernel(place_ref, mine_ref, theirs_ref, gate_ref, upper_ref, sems):
+    core = place_ref[1]
+    chips, _, rows, _ = mine_ref.shape
     copies = []
-    for other in range(chips):
-        for mate in range(2):
-            start = pl.multiple_of(((chip ^ other) * 2 + (core ^ mate)) * rows, rows)
+    for chip in range(chips):
+        for mate, ref in enumerate((mine_ref, theirs_ref)):
+            start = pl.multiple_of((chip * 2 + (core ^ mate)) * rows, rows)
             for part, out_ref in enumerate((gate_ref, upper_ref)):
                 copies.append(
                     pltpu.make_async_copy(
-                        pieces[mate * chips + other].at[part],
+                        ref.at[chip, part],
                         out_ref.at[pl.ds(start, rows), :],
                         sems.at[len(copies)],
                     )
@@ -369,20 +363,20 @@
         copy.wait()
 
 
-def stack_rows(place, pieces):
-    _, rows, columns = pieces[0].shape
-    shape = jax.ShapeDtypeStruct((rows * len(pieces), columns), jnp.bfloat16)
+def stack_rows(place, mine, theirs):
+    chips, _, rows, columns = mine.shape
+    shape = jax.ShapeDtypeStruct((2 * chips * rows, columns), jnp.bfloat16)
     return pl.pallas_call(
         stack_rows_kernel,
         in_specs=[pl.BlockSpec(memory_space=pltpu.SMEM)]
-        + [pl.BlockSpec(memory_space=pl.ANY)] * len(pieces),
+        + [pl.BlockSpec(memory_space=pltpu.VMEM)] * 2,
         out_specs=[pl.BlockSpec(memory_space=pl.ANY)] * 2,
         out_shape=[shape] * 2,
-        scratch_shapes=[pltpu.SemaphoreType.DMA((2 * len(pieces),))],
+        scratch_shapes=[pltpu.SemaphoreType.DMA((4 * chips,))],
         cost_estimate=pl.CostEstimate(
-            flops=0, bytes_accessed=8 * len(pieces) * rows * columns, transcendentals=0
-        ),
-    )(place, *pieces)
+            flops=0, bytes_accessed=16 * chips * rows * columns, transcendentals=0
+        ),
+    )(place, mine, theirs)
 
 
 def stack_attention_kernel(*refs):
@@ -421,7 +415,7 @@
     b16 = lambda r, c: jax.ShapeDtypeStruct((r, c), jnp.bfloat16)
     return pl.pallas_call(
         stack_attention_kernel,
-        in_specs=[pl.BlockSpec(memory_space=pl.ANY)] * len(blocks),
+        in_specs=[pl.BlockSpec(memory_space=pltpu.VMEM)] * len(blocks),
         out_specs=[pl.BlockSpec(memory_space=pl.ANY)] * 3,
         out_shape=[
             b16(2 * owned * count, wide),
@@ -502,33 +496,31 @@
     )(normed, joined, attended, grads, gain)
 
 
-def expert_kernel(
-    near_ref,
-    away_ref,
-    near_grad_ref,
-    away_grad_ref,
-    route_ref,
-    gate_ref,
-    upper_ref,
-    down_ref,
-    *refs,
-    per_step,
-):
-    near_out_ref, away_out_ref, near_back_ref, away_back_ref = refs[-13:-9]
-    hidden_ref, grad_gate_ref, grad_upper_ref, rows_all_ref, grads_all_ref = refs[-9:-4]
-    rows_ref, grads_ref, out_ref, back_ref = refs[-4:]
+def expert_kernel(place_ref, near_ref, away_ref, *refs, per_step, spot):
+    given_ref, gate_ref, upper_ref, down_ref = refs[:4]
+    near_back_ref, away_back_ref = refs[-11:-9]
+    hidden_ref, grad_gate_ref, grad_upper_ref, rows_ref, grads_ref, narrow_ref = refs[-9:-3]
+    route_ref, out_ref, back_ref = refs[-3:]
     step = pl.program_id(0)
-    half = near_ref.shape[0]
-    width = near_ref.shape[1]
+    half, width = near_ref.shape
 
     @pl.when(step == 0)
     def _():
         rows_ref[:half, :] = near_ref[...]
         rows_ref[half:, :] = away_ref[...]
-        grads_ref[:half, :] = near_grad_ref[:, :width]
-        grads_ref[half:, :] = away_grad_ref[:, :width]
-        rows_all_ref[...] = rows_ref[...]
-        grads_all_ref[...] = grads_ref[...]
+        grads_ref[...] = given_ref[:, :width]
+        lanes = lax.broadcasted_iota(jnp.int32, route_ref.shape, 1)
+        expert = (lanes + place_ref[2]).astype(jnp.float32)
+        routes = given_ref[:, width:].astype(jnp.float32)
+        weights = (
+            routes[:, TOP : 2 * TOP]
+            + routes[:, 2 * TOP : 3 * TOP]
+            + routes[:, 3 * TOP : 4 * TOP]
+        )
+        dense = jnp.zeros_like(expert)
+        for k in range(TOP):
+            dense += jnp.where(expert == routes[:, k : k + 1], weights[:, k : k + 1], 0.0)
+        route_ref[...] = dense
         out_ref[...] = jnp.zeros_like(out_ref)
         back_ref[...] = jnp.zeros_like(back_ref)
 
@@ -566,77 +558,74 @@
 
     @pl.when(step == pl.num_programs(0) - 1)
     def _():
-        near_out_ref[...] = out_ref[:half, :]
-        away_out_ref[...] = out_ref[half:, :].astype(jnp.bfloat16)
+        narrow_ref[...] = out_ref[...].astype(jnp.bfloat16)
         near_back_ref[...] = back_ref[:half, :]
         away_back_ref[...] = back_ref[half:, :].astype(jnp.bfloat16)
 
 
-def expert_block(spot, near, away, near_grad, away_grad, route, weights, experts, filled):
+def expert_block(place, spot, near, away, given, weights, experts, filled):
     gate_w, upper_w, down_w = weights
     half, width = near.shape
+    block = half // 2
     total = gate_w.shape[1]
     per_step = 2
     steps = experts // per_step
     columns = total // steps
-    whole = lambda a: pl.BlockSpec(a.shape, lambda i: (0, 0))
+    whole = lambda a: pl.BlockSpec(a.shape, lambda i, p: (0, 0))
     rows = 2 * half
     every = rows * len(DISTANCE)
-    f32 = lambda r, c: jax.ShapeDtypeStruct((r, c), jnp.float32)
     b16 = lambda r, c: jax.ShapeDtypeStruct((r, c), jnp.bfloat16)
-    fixed = pl.BlockSpec((half, width), lambda i: (0, 0))
-    part = pl.BlockSpec((rows, columns), lambda i: (spot, i))
-    kept = pl.BlockSpec((rows, width), lambda i: (spot, 0))
-    flops = 2 * rows * width * total * 6
-    inputs = (near, away, near_grad, away_grad, route, gate_w, upper_w, down_w)
+    fixed = pl.BlockSpec((half, width), lambda i, p: (0, 0))
+    part = pl.BlockSpec((rows, columns), lambda i, p: (spot, i))
+    kept = pl.BlockSpec((rows, width), lambda i, p: (spot, 0))
+    wide = given.shape[1]
+    inputs = (place, near, away, given, gate_w, upper_w, down_w)
     return pl.pallas_call(
-        functools.partial(expert_kernel, per_step=per_step),
-        grid=(steps,),
-        in_specs=[
-            whole(near),
-            whole(away),
-            whole(near_grad),
-            whole(away_grad),
-            whole(route),
-            pl.BlockSpec((width, columns), lambda i: (0, i)),
-            pl.BlockSpec((width, columns), lambda i: (0, i)),
-            pl.BlockSpec((columns, width), lambda i: (i, 0)),
+        functools.partial(expert_kernel, per_step=per_step, spot=spot),
+        grid_spec=pltpu.PrefetchScalarGridSpec(
+            num_scalar_prefetch=1,
+            grid=(steps,),
+            in_specs=[
+                whole(near),
+                whole(away),
+                pl.BlockSpec((rows, wide), lambda i, p: (p[3 + spot], 0)),
+            ]
+            + [
+                pl.BlockSpec((width, columns), lambda i, p: (0, i)),
+                pl.BlockSpec((width, columns), lambda i, p: (0, i)),
+                pl.BlockSpec((columns, width), lambda i, p: (i, 0)),
+            ]
+            + [pl.BlockSpec(memory_space=pl.ANY)] * len(filled),
+            out_specs=[fixed] * 2
+            + [part] * 3
+            + [kept] * 2
+            + [pl.BlockSpec((rows, width), lambda i, p: (p[3 + spot], 0))],
+            scratch_shapes=[
+                pltpu.VMEM((rows, wide - width), jnp.float32),
+                pltpu.VMEM((rows, width), jnp.float32),
+                pltpu.VMEM((rows, width), jnp.float32),
+            ],
+        ),
+        out_shape=[
+            jax.ShapeDtypeStruct((half, width), jnp.float32),
+            b16(half, width),
         ]
-        + [pl.BlockSpec(memory_space=pl.ANY)] * len(filled),
-        out_specs=[fixed] * 4 + [part] * 3 + [kept] * 2,
-        out_shape=[f32(half, width), b16(half, width)] * 2
         + [b16(every, total)] * 3
-        + [b16(every, width)] * 2,
-        input_output_aliases={len(inputs) + i: 4 + i for i in range(len(filled))},
-        scratch_shapes=[
-            pltpu.VMEM((rows, width), jnp.bfloat16),
-            pltpu.VMEM((rows, width), jnp.bfloat16),
-            pltpu.VMEM((rows, width), jnp.float32),
-            pltpu.VMEM((rows, width), jnp.float32),
-        ],
+        + [b16(every, width)] * 3,
+        input_output_aliases={len(inputs) + i: 2 + i for i in range(len(filled))},
         compiler_params=pltpu.CompilerParams(vmem_limit_bytes=48 * 1024 * 1024),
         cost_estimate=pl.CostEstimate(
-            flops=flops,
+            flops=2 * rows * width * total * 6,
             bytes_accessed=2 * (3 * width * total + 3 * rows * total + 12 * rows * width),
             transcendentals=rows * total,
         ),
     )(*inputs, *filled)
 
 
-def expert_grads_kernel(
-    place_ref,
-    rows_ref,
-    grads_ref,
-    hidden_ref,
-    grad_gate_ref,
-    grad_upper_ref,
-    keep_ref,
-    give_ref,
-    keep_down_ref,
-    give_down_ref,
-    full_ref,
-    full_down_ref,
+def column_grads_kernel(
+    place_ref, rows_ref, grad_gate_ref, grad_upper_ref, *refs
 ):
+    keep_ref, give_ref, full_ref = refs[-3:]
     core = place_ref[1]
     contract = (((0,), (0,)), ((), ()))
     chips, _, plane_rows, _ = keep_ref.shape
@@ -649,64 +638,91 @@
             theirs = pl.multiple_of((2 * chip + 1 - core) * plane_rows, plane_rows)
             keep_ref[chip, part] = full_ref[pl.ds(mine, plane_rows), :]
             give_ref[chip, part] = full_ref[pl.ds(theirs, plane_rows), :].astype(give_ref.dtype)
-    full_down_ref[...] = lax.dot_general(
-        hidden_ref[...], grads_ref[...], contract, preferred_element_type=jnp.float32
-    )
-    experts, down_rows, _ = keep_down_ref.shape
+
+
+def column_grads(place, step, steps, rows_all, grad_gate, grad_upper, chips, filled):
+    tokens, width = rows_all.shape
+    total = grad_gate.shape[1]
+    columns = total // steps
+    plane_rows = width // (2 * chips)
+    part = pl.BlockSpec((tokens, columns), lambda i, p: (0, step))
+    wide = pl.BlockSpec((chips, 2, plane_rows, columns), lambda i, p: (0, 0, 0, step))
+    shape = (chips, 2, plane_rows, total)
+    return pl.pallas_call(
+        column_grads_kernel,
+        grid_spec=pltpu.PrefetchScalarGridSpec(
+            num_scalar_prefetch=1,
+            grid=(1,),
+            in_specs=[pl.BlockSpec((tokens, width), lambda i, p: (0, 0)), part, part]
+            + [pl.BlockSpec(memory_space=pl.ANY)] * len(filled),
+            out_specs=[wide, wide],
+            scratch_shapes=[pltpu.VMEM((width, columns), jnp.float32)],
+        ),
+        out_shape=[
+            jax.ShapeDtypeStruct(shape, jnp.float32),
+            jax.ShapeDtypeStruct(shape, jnp.bfloat16),
+        ],
+        input_output_aliases={4 + i: i for i in range(len(filled))},
+        compiler_params=pltpu.CompilerParams(vmem_limit_bytes=36 * 1024 * 1024),
+        cost_estimate=pl.CostEstimate(
+            flops=4 * tokens * width * columns,
+            bytes_accessed=2 * tokens * (width + 2 * columns) + 6 * 2 * width * columns,
+            transcendentals=0,
+        ),
+    )(place, rows_all, grad_gate, grad_upper, *filled)
+
+
+def down_grads_kernel(place_ref, grads_ref, hidden_ref, keep_ref, give_ref, full_ref):
+    core = place_ref[1]
+    full_ref[...] = lax.dot_general(
+        hidden_ref[...],
+        grads_ref[...],
+        (((0,), (0,)), ((), ())),
+        preferred_element_type=jnp.float32,
+    )
+    experts, down_rows, _ = keep_ref.shape
     for e in range(experts):
         mine = pl.multiple_of((2 * e + core) * down_rows, down_rows)
         theirs = pl.multiple_of((2 * e + 1 - core) * down_rows, down_rows)
-        keep_down_ref[e] = full_down_ref[pl.ds(mine, down_rows), :]
-        give_down_ref[e] = full_down_ref[pl.ds(theirs, down_rows), :]
-
-
-def expert_grads(place, rows_all, grads_all, hidden, grad_gate, grad_upper, experts, chips):
-    tokens, width = rows_all.shape
+        keep_ref[e] = full_ref[pl.ds(mine, down_rows), :]
+        give_ref[e] = full_ref[pl.ds(theirs, down_rows), :]
+
+
+def down_grads(place, steps, grads_all, hidden, experts):
+    tokens, width = grads_all.shape
     total = hidden.shape[1]
-    per_step = 2
-    steps = experts // per_step
     columns = total // steps
-    plane_rows = width // (2 * chips)
+    per_step = experts // steps
     down_rows = total // experts // 2
-    whole = pl.BlockSpec((tokens, width), lambda i, p: (0, 0), pipeline_mode=pl.Buffered(1))
-    part = pl.BlockSpec((tokens, columns), lambda i, p: (0, i))
-    wide = pl.BlockSpec((chips, 2, plane_rows, columns), lambda i, p: (0, 0, 0, i))
     down = pl.BlockSpec((per_step, down_rows, width), lambda i, p: (i, 0, 0))
     return pl.pallas_call(
-        expert_grads_kernel,
+        down_grads_kernel,
         grid_spec=pltpu.PrefetchScalarGridSpec(
             num_scalar_prefetch=1,
             grid=(steps,),
-            in_specs=[whole, whole, part, part, part],
-            out_specs=[wide, wide, down, down],
-            scratch_shapes=[
-                pltpu.VMEM((width, columns), jnp.float32),
-                pltpu.VMEM((columns, width), jnp.float32),
+            in_specs=[
+                pl.BlockSpec((tokens, width), lambda i, p: (0, 0)),
+                pl.BlockSpec((tokens, columns), lambda i, p: (0, i)),
             ],
-        ),
-        out_shape=[
-            jax.ShapeDtypeStruct((chips, 2, plane_rows, total), jnp.float32),
-            jax.ShapeDtypeStruct((chips, 2, plane_rows, total), jnp.bfloat16),
-            jax.ShapeDtypeStruct((experts, down_rows, width), jnp.float32),
-            jax.ShapeDtypeStruct((experts, down_rows, width), jnp.float32),
-        ],
-        compiler_params=pltpu.CompilerParams(vmem_limit_bytes=52 * 1024 * 1024),
+            out_specs=[down, down],
+            scratch_shapes=[pltpu.VMEM((columns, width), jnp.float32)],
+        ),
+        out_shape=[jax.ShapeDtypeStruct((experts, down_rows, width), jnp.float32)] * 2,
+        compiler_params=pltpu.CompilerParams(vmem_limit_bytes=36 * 1024 * 1024),
         cost_estimate=pl.CostEstimate(
-            flops=6 * tokens * width * total,
-            bytes_accessed=2 * tokens * (2 * width + 3 * total) + 20 * width * total,
+            flops=2 * tokens * width * total,
+            bytes_accessed=2 * tokens * (width + total) + 4 * width * total,
             transcendentals=0,
         ),
-    )(place, rows_all, grads_all, hidden, grad_gate, grad_upper)
-
-
-def adam_columns_kernel(place_ref, w_ref, first_ref, second_ref, *refs):
-    pieces, outs = refs[:-4], refs[-4:]
-    lanes = pieces[0].shape[2]
-    for other, piece in enumerate(pieces):
-        start = pl.multiple_of((place_ref[0] ^ other) * lanes, lanes)
+    )(place, grads_all, hidden)
+
+
+def adam_columns_kernel(w_ref, first_ref, second_ref, grad_ref, *outs):
+    chips, _, _, lanes = grad_ref.shape
+    for chip in range(chips):
         for part in range(2):
-            columns = pl.ds(part * FF + start, lanes)
-            grad = piece[part].astype(jnp.float32)
+            columns = slice(part * FF + chip * lanes, part * FF + (chip + 1) * lanes)
+            grad = grad_ref[chip, part].astype(jnp.float32)
             found = adam_step(
                 w_ref[0, :, columns],
                 grad,
@@ -719,27 +735,24 @@
                 out_ref[0, :, columns] = value
 
 
-def adam_columns(place, weight, first, second, pieces):
+def adam_columns(weight, first, second, grads):
     experts, rows, both = weight.shape
-    lanes = pieces[0].shape[2] // experts
-    block = pl.BlockSpec((1, rows, both), lambda e, p: (e, 0, 0))
+    chips = grads.shape[0]
+    lanes = grads.shape[3] // experts
+    block = pl.BlockSpec((1, rows, both), lambda e: (e, 0, 0))
     return pl.pallas_call(
         adam_columns_kernel,
-        grid_spec=pltpu.PrefetchScalarGridSpec(
-            num_scalar_prefetch=1,
-            grid=(experts,),
-            in_specs=[block] * 3
-            + [pl.BlockSpec((2, rows, lanes), lambda e, p: (0, 0, e))] * len(pieces),
-            out_specs=[block] * 4,
-        ),
+        grid=(experts,),
+        in_specs=[block] * 3 + [pl.BlockSpec((chips, 2, rows, lanes), lambda e: (0, 0, 0, e))],
+        out_specs=[block] * 4,
         out_shape=[jax.ShapeDtypeStruct(weight.shape, jnp.float32)] * 4,
-        compiler_params=pltpu.CompilerParams(vmem_limit_bytes=32 * 1024 * 1024),
+        compiler_params=pltpu.CompilerParams(vmem_limit_bytes=56 * 1024 * 1024),
         cost_estimate=pl.CostEstimate(
             flops=20 * experts * rows * both,
             bytes_accessed=30 * experts * rows * both,
             transcendentals=experts * rows * both,
         ),
-    )(place, weight, first, second, *pieces)
+    )(weight, first, second, grads)
 
 
 def shards_moved(
@@ -791,7 +804,27 @@
         ],
         0,
     )
-    attention_blocks = gather_ring_middle(block)
+    share = local_experts * (FF // chips)
+    attention_ring = [block] + [turn(block, distance) for distance in DISTANCE[1:]]
+    attention_pairs = [along_first(part) for part in attention_ring[:2]]
+    pieces = spread_columns(after(w_gate_up, attention_pairs[0]), chips)
+    routes = jnp.concatenate([expert_ids.astype(NARROW)] + split_three(route_weights), 1)
+    cotangent_rows = jnp.concatenate(
+        [
+            cotangent.astype(NARROW),
+            jnp.pad(routes, ((0, 0), (0, lane_pad - routes.shape[1]))),
+        ],
+        1,
+    )
+    cotangent_pair = along_first(cotangent_rows)
+    cotangent_here = jnp.concatenate([cotangent_pair, swap_second(cotangent_pair)], 0)
+    cotangent_all = lax.all_gather(
+        after(cotangent_here, attention_ring), "expert", axis=0, tiled=True
+    )
+    attention_ring = attention_ring[:2] + after(attention_ring[2:], (pieces, cotangent_pair))
+    attention_pairs.append(along_first(attention_ring[2]))
+    attention_pairs.append(along_first(after(attention_ring[3], cotangent_here)))
+    attention_blocks = [(pair, swap_second(pair)) for pair in attention_pairs]
 
     sources = jnp.asarray(gathered_sources(count_dp, count_expert))[place_dp, place_expert]
     from_dp, from_expert = sources[:, 0], sources[:, 1]
@@ -810,42 +843,21 @@
     heads_to_gathered = (head_places[:, None] == head_feature[None, :]).astype(NARROW)
     heads_from_gathered = (head_feature[:, None] == head_places[None, :]).astype(NARROW)
 
-    ff_columns = FF // chips
-
-    share = local_experts * ff_columns
-    place = jnp.stack([chip, core]).astype(jnp.int32)
-    pieces = spread_columns(place, w_gate_up, chips)
-    pieces = [
-        swap(piece, lambda i, other=other: 2 * other) if other else piece
-        for other, piece in enumerate(pieces)
-    ]
-    gate_w, upper_w = stack_rows(place, pieces + [swap_core(piece) for piece in pieces])
-    down_mine = w_down.astype(NARROW)
+    found_at = (place_expert - jnp.asarray(DISTANCE, jnp.int32)) % count_expert
+    place = jnp.concatenate(
+        [jnp.stack([chip, core, place_expert * local_experts]).astype(jnp.int32), found_at]
+    )
+    parities = [list(range(i, count_dp, 2)) for i in range(2)]
+    pieces = lax.all_to_all(
+        after(pieces, attention_blocks[1][1]), "dp", 0, 0, axis_index_groups=parities, tiled=True
+    )
+    down_mine = after(w_down, attention_pairs[0]).astype(NARROW)
     down_theirs = swap_core(down_mine)
     down_w = jnp.where(
         core == 0,
         jnp.concatenate([down_mine, down_theirs], 1),
         jnp.concatenate([down_theirs, down_mine], 1),
     ).reshape(share, MODEL_WIDTH)
-
-    routes = jnp.concatenate([expert_ids.astype(NARROW)] + split_three(route_weights), 1)
-    cotangent_blocks = gather_plane_last(
-        jnp.concatenate(
-            [
-                cotangent.astype(NARROW),
-                jnp.pad(routes, ((0, 0), (0, lane_pad - routes.shape[1]))),
-            ],
-            1,
-        )
-    )
-
-    def dense_route(rows):
-        ids = rows[:, :TOP].astype(jnp.int32)
-        parts = rows[:, TOP : 4 * TOP].astype(WIDE)
-        weights = parts[:, :TOP] + parts[:, TOP : 2 * TOP] + parts[:, 2 * TOP :]
-        local = place_expert * local_experts + jnp.arange(lane_pad, dtype=jnp.int32)
-        match = (ids[:, :, None] == local) & (jnp.arange(lane_pad) < local_experts)
-        return jnp.sum(jnp.where(match, weights[:, :, None], 0.0), 1)
 
     cosine_table, sine_table = rotary_tables(sequence_length, HEAD_SIZE // 2)
     inputs = tokens.astype(WIDE)
@@ -874,49 +886,58 @@
     resid = inputs + resid_parts[:sequence_length] + swap_core(resid_parts[sequence_length:])
     scale_two = norm_scale(resid)
     normed_two = (resid * scale_two * gain_moe).astype(NARROW)
-
-    normed_blocks = gather_plane_last(normed_two)
-    out_parts, back_parts, filled = [], [], []
-    for spot, ((near, away), (near_grad, away_grad)) in enumerate(
-        zip(normed_blocks, cotangent_blocks)
-    ):
-        route = jnp.concatenate(
-            [dense_route(g[:, MODEL_WIDTH:]) for g in (near_grad, away_grad)], 0
-        )
+    normed_two = after(normed_two, pieces)
+
+    normed_blocks, _ = gather_plane_last(normed_two)
+    gate_w, upper_w = stack_rows(place, pieces, after(swap_core(pieces), normed_two))
+    back_parts, filled = [], []
+    second_parts = []
+    for spot, (near, away) in enumerate(normed_blocks):
+        if spot >= 2:
+            near = after(near, (second_parts[spot - 2], back_parts[: spot - 2]))
         done = expert_block(
+            place,
             spot,
             near,
             away,
-            near_grad,
-            away_grad,
-            route,
+            cotangent_all,
             (gate_w, upper_w, down_w),
             local_experts,
             filled,
         )
-        out_parts.append((done[0], done[1]))
-        back_parts.append((done[2], done[3]))
-        filled = done[4:]
-    grad_normed_two = scatter_plane_first(back_parts)
-    out_tokens = resid + scatter_plane_first(out_parts)
-
-    hidden, grad_gate, grad_upper, rows_all, grads_all = filled
-    keep, give, keep_down, give_down = expert_grads(
-        place, rows_all, grads_all, hidden, grad_gate, grad_upper, local_experts, chips
-    )
-    part_down = keep_down + swap_core(give_down)
+        filled = done[2:]
+        if spot < len(DISTANCE) - 1:
+            second_parts.append(add_second(done[0], done[1]))
+            back_parts.append(add_first(second_parts[-1]))
+    hidden, grad_gate, grad_upper, rows_all, grads_all, out_all = filled
+    steps = local_experts // 2
+    kept_grads = []
+    for step in range(steps):
+        kept_grads = column_grads(
+            place, step, steps, rows_all, grad_gate, grad_upper, chips, kept_grads
+        )
+        if step == 0:
+            last = add_second(done[0], done[1], kept_grads)
+        elif step == 1:
+            back_parts.append(add_first(last, kept_grads))
+        elif step == 2:
+            found = [
+                turn(part.astype(NARROW), -distance)
+                for part, distance in zip(back_parts[1:], DISTANCE[1:])
+            ]
+            grad_normed_two = back_parts[0] + sum(
+                part.astype(WIDE) for part in after(found, kept_grads)
+            )
+            rows_all = after(rows_all, grad_normed_two)
+    keep, give = kept_grads
     taken = swap_core(give)
-    collected = []
-    for other in range(chips):
-        piece = (
-            lax.dynamic_index_in_dim(keep, chip ^ other, 0, False)
-            + lax.dynamic_index_in_dim(taken, chip ^ other, 0, False).astype(WIDE)
-        ).astype(NARROW)
-        if other:
-            piece = swap(piece, lambda i, other=other: 2 * other)
-        collected.append(piece)
-    part_gate_up, new_gate_up, new_first_gate_up, new_second_gate_up = adam_columns(
-        place, w_gate_up, first_gate_up, second_gate_up, collected
+    expert_sums = (keep + taken.astype(WIDE)).astype(NARROW)
+    parities = [list(range(i, count_dp, 2)) for i in range(2)]
+    collected = lax.all_to_all(
+        expert_sums, "dp", 0, 0, axis_index_groups=parities, tiled=True
+    )
+    out_sums = lax.psum_scatter(
+        after(out_all, grad_normed_two), "expert", scatter_dimension=0, tiled=True
     )
 
     hat_two = grad_normed_two * gain_moe
@@ -940,6 +961,7 @@
     joined = jax.vmap(lambda a, b, c: join_grads(a, b, c, cosine_table, sine_table))(
         grad_query, grad_keys, grad_values
     ).reshape(2 * sequence_length, -1)
+    joined = after(joined, expert_sums)
     grad_normed_parts = lax.dot_general(
         joined, qkv_here, (((1,), (1,)), ((), ())), preferred_element_type=jnp.float32
     )
@@ -955,7 +977,26 @@
         jnp.pad(gain_parts, ((0, 0), (0, lane_pad - 2))),
         owned,
     )
-    summed = scatter_ring_middle([(near_parts[i], away_parts[i]) for i in range(len(DISTANCE))])
+    keep_down, give_down = down_grads(
+        place, steps, after(grads_all, near_parts), hidden, local_experts
+    )
+    part_down = keep_down + swap_core(give_down)
+    new_down, new_first_down, new_second_down = adam_step(
+        w_down, part_down, first_down, second_down, learn_rate, weight_decay
+    )
+    part_gate_up, new_gate_up, new_first_gate_up, new_second_gate_up = adam_columns(
+        w_gate_up, first_gate_up, second_gate_up, after(collected, near_parts)
+    )
+    in_plane = [None] * len(DISTANCE)
+    for i in (3, 1, 2, 0):
+        in_plane[i] = add_second(near_parts[i], away_parts[i], new_gate_up if i in (2, 0) else ())
+    for i in (3, 1, 2, 0):
+        in_plane[i] = add_first(in_plane[i])
+    out_sums = after(out_sums, in_plane[3]).astype(WIDE)
+    out_half = out_sums.shape[0] // 2
+    out_sums = add_second(out_sums[:out_half], out_sums[out_half:])
+    summed = ring_sum(in_plane, (new_down, out_sums))
+    out_tokens = resid + add_first(out_sums, summed)
     here, there, part_out = summed[:owned], summed[owned : 2 * owned], summed[2 * owned :]
     there = swap_core(there[:, : half_columns + lane_pad])
     part_gains = (
@@ -983,9 +1024,6 @@
     )
     new_gains, new_first_gains, new_second_gains = adam_step(
         gains, part_gains, first_gains, second_gains, gain_rate, 0.0
-    )
-    new_down, new_first_down, new_second_down = adam_step(
-        w_down, part_down, first_down, second_down, learn_rate, weight_decay
     )
     return (
         out_tokens,

time: 1140 us -> 639 us (0.56); the launches traced: 1120 us -> 632 us
  Pallas kernels: 591 us -> 194 us
  waiting for transfers between devices: 255 us -> 193 us
  starting transfers between devices: 100 us -> 67.7 us
  other arithmetic: 90.2 us -> 65.8 us
  between operations: 2.96 us -> 16.2 us
  local copies, waits for them, and re-layouts: 48.1 us -> 60.1 us
    pallas_call x1, Pallas kernels: 240 us -> 6.59 us  [stack_rows(): pl.pallas_call(stack_rows_kernel, in_specs=[pl.BlockSpec(memory_space=plt...]
    pallas_call x1, Pallas kernels: 204 us -> 6.19 us  [stack_attention(): pl.pallas_call(stack_attention_kernel, in_specs=[pl.BlockSpec(memory_spac...]
    ppermute x18 -> x12, waiting for transfers between devices: 139 us -> 56.5 us  [turn(): lax.ppermute(rows, 'expert', [(i, (i + step) % count) for i in range(coun...]
    pallas_call x7 -> x12, Pallas kernels: 142 us -> 177 us  [the longest x4 87.3 us: expert_block(): pl.pallas_call(functools.partial(expert_kernel, per_step=per_step, spot=s...]
    ppermute x62 -> x47, starting transfers between devices: 67.8 us -> 45 us  [swap(): return lax.ppermute(rows, 'dp', [(i, i ^ pick(i)) for i in range(count)])]
    ppermute x18 -> x12, starting transfers between devices: 32.7 us -> 12.5 us  [turn(): lax.ppermute(rows, 'expert', [(i, (i + step) % count) for i in range(coun...]
    all_to_all x0 -> x2, waiting for transfers between devices: none -> 14.4 us  [the longest x1 14.4 us: shards_moved(): lax.all_to_all(after(pieces, attention_blocks[1][1]), 'dp', 0, 0, axis_in...]
    convert_element_type x21 -> x5, other arithmetic: 21.5 us -> 7.61 us  [the longest x1 7.16 us: shards_moved(): expert_sums = (keep + taken.astype(WIDE)).astype(NARROW)]
  transfers between devices with their start and end apart: 80 -> 63, of which waited for: 33 -> 21; matrix products, arithmetic and copies ran while one was open for 11% -> 22% of each run, Pallas kernels for 35% -> 28%
where the time goes in v3:
time: 639 us; the launch traced here: 632 us
  Pallas kernels  194 us (30%)
  waiting for transfers between devices  193 us (30%)
  starting transfers between devices  67.7 us (11%)
  other arithmetic  65.8 us (10%)
  local copies, waits for them, and re-layouts  60.1 us (9%)
  matrix products  35.3 us (6%)
  between operations  16.2 us (3%)
    ppermute x47, waiting for transfers between devices, swap(): return lax.ppermute(rows, 'dp', [(i, i ^ pick(i)) for i in range(count)])  122 us
    pallas_call x4, Pallas kernels, expert_block(): pl.pallas_call(functools.partial(expert_kernel, per_step=per_step, spot=s...  87.3 us
    ppermute x12, waiting for transfers between devices, turn(): lax.ppermute(rows, 'expert', [(i, (i + step) % count) for i in range(coun...  56.5 us
    ppermute x47, starting transfers between devices, swap(): return lax.ppermute(rows, 'dp', [(i, i ^ pick(i)) for i in range(count)])  45 us
    pallas_call x5, Pallas kernels, column_grads(): pl.pallas_call(column_grads_kernel, grid_spec=pltpu.PrefetchScalarGridSpe...  42.2 us
    unnamed x176, local copies, waits for them, and re-layouts  24.7 us
    pallas_call x1, Pallas kernels, adam_columns(): pl.pallas_call(adam_columns_kernel, grid=(experts,), in_specs=[block] * 3...  24.4 us
    sub x4, other arithmetic, adam_step(): return (weight - step_rate * (update + shrink * weight), first, second)  16.8 us
  transfers between devices with their start and end apart: 63, of which 21 were waited for; matrix products, arithmetic and copies ran while one was open for 22% of the time, Pallas kernels for 28%

profile of v3, /device:TPU:0, one launch (start us, length us, event | category | flops | bytes accessed | tf_op | source)
XLA Modules:
  0.0 631.8 jit_solution(5667693393865908206)
XLA Ops:
  16.9 4.5 collective-permute-done.9
  26.9 3.6 collective-permute-start.7
  33.4 6.7 %collective-permute-done.12 = bf16[256,1664]{1,0:T(8,128)(2,1)} collective-permute-done((bf16[256,1664]{1,0:T(8,128)(2,1)}, bf16[256,1664]{1,0:T(8,128)(2,1)}, u32[]{:S(2)}, u32[]{:S(2)}) %collective-permute-start.12) | collective-permute-done | bytes 852000 | tf_op jit(solution)/shard_map/ppermute | solution.py:158
  43.1 24.7 %collective-permute-done.8 = bf16[144,1536]{1,0:T(8,128)(2,1)} collective-permute-done((bf16[144,1536]{1,0:T(8,128)(2,1)}, bf16[144,1536]{1,0:T(8,128)(2,1)}, u32[]{:S(2)}, u32[]{:S(2)}) %collective-permute-start.8) | collective-permute-done | bytes 442400 | tf_op jit(solution)/shard_map/ppermute | solution.py:183
  69.3 8.6 %shard_map.381 = bf16[4,2,192,1280]{3,2,1,0:T(8,128)(2,1)} custom-call(f32[10,192,1024]{2,1,0:T(8,128)} %w_ref.1), custom_call_target="tpu_custom_call" | custom-call | bytes 11796480 | tf_op jit(solution)/shard_map/pallas_call | solution.py:333
  82.8 3.6 collective-permute-done.10
  88.7 2.9 collective-permute-done.5
  94.3 10.7 %collective-permute-done.13 = bf16[144,1536]{1,0:T(8,128)(2,1)S(1)} collective-permute-done((bf16[144,1536]{1,0:T(8,128)(2,1)}, bf16[144,1536]{1,0:T(8,128)(2,1)S(1)}, u32[]{:S(2)}, u32[]{:S(2)}) %collective-permute-start.13) | collective-permute-done | bytes 442400 | tf_op jit(solution)/shard_map/ppermute | solution.py:158
  110.1 8.0 %collective-permute-done.6.refs_3_ = bf16[288,1536]{1,0:T(8,128)(2,1)} collective-permute-done((bf16[288,1536]{1,0:T(8,128)(2,1)S(1)}, bf16[288,1536]{1,0:T(8,128)(2,1)}, u32[]{:S(2)}, u32[]{:S(2)}) %collective-permute-start.6) | collective-permute-done | bytes 884768 | tf_op jit(solution)/shard_map/ppermute | solution.py:158
  118.1 4.8 all-to-all-start
  123.2 8.2 %collective-permute-done.14.refs_7_ = bf16[288,1536]{1,0:T(8,128)(2,1)} collective-permute-done((bf16[288,1536]{1,0:T(8,128)(2,1)}, bf16[288,1536]{1,0:T(8,128)(2,1)}, u32[]{:S(2)}, u32[]{:S(2)}) %collective-permute-start.14) | collective-permute-done | bytes 884768 | tf_op jit(solution)/shard_map/ppermute | solution.py:158
  131.4 6.2 shard_map.382
  138.8 3.3 multiply_convert_fusion
  155.4 14.4 %all-to-all-done.mine_ref = bf16[4,2,192,1280]{3,2,1,0:T(8,128)(2,1)} async-done(((bf16[4,2,192,1280]{3,2,1,0:T(8,128)(2,1)}), bf16[4,2,192,1280]{3,2,1,0:T(8,128)(2,1)}, u32[]{:S(2)}, u32[]{:S(2)}) %all-to-all-start) | async-done | bytes 3932192 | tf_op jit(solution)/shard_map/all_to_all | solution.py:851
  176.6 4.5 maximum_select_fusion
  184.7 2.9 collective-permute-start.25
  187.6 19.2 %collective-permute-done.17 = bf16[128,1536]{1,0:T(8,128)(2,1)S(1)} collective-permute-done((bf16[128,1536]{1,0:T(8,128)(2,1)S(1)}, bf16[128,1536]{1,0:T(8,128)(2,1)S(1)}, u32[]{:S(2)}, u32[]{:S(2)}) %collective-permute-start.17) | collective-permute-done | bytes 393248 | tf_op jit(solution)/shard_map/ppermute | solution.py:183
  209.4 5.2 collective-permute-done.20
  216.3 4.5 collective-permute-done.18
  223.5 9.4 %collective-permute-done.19 = bf16[128,1536]{1,0:T(8,128)(2,1)S(1)} collective-permute-done((bf16[128,1536]{1,0:T(8,128)(2,1)S(1)}, bf16[128,1536]{1,0:T(8,128)(2,1)S(1)}, u32[]{:S(2)}, u32[]{:S(2)}) %collective-permute-start.19) | collective-permute-done | bytes 393248 | tf_op jit(solution)/shard_map/ppermute | solution.py:158
  234.0 6.6 %shard_map.383 = (bf16[1536,1280]{1,0:T(8,128)(2,1)}, bf16[1536,1280]{1,0:T(8,128)(2,1)}) custom-call(s32[7]{0:T(128)} %pad_add_fusion.1.place_ref, bf16[4,2,192,1280]{3,2,1,0:T(8,128)(2,1)} %all-to-all-done.mine_ref, bf16[4,2,192,1280]{3,2,1,0:T(8,128)(2,1)} %collective-permute-done.22.theirs_ref), custom_call_target="tpu_custom_call" | custom-call | bytes 15728640 | tf_op jit(solution)/shard_map/pallas_call | solution.py:369
  240.7 22.1 %shard_map.384 = (f32[256,1536]{1,0:T(8,128)S(1)}, bf16[256,1536]{1,0:T(8,128)(2,1)S(1)}, bf16[2048,1280]{1,0:T(8,128)(2,1)}, bf16[2048,1280]{1,0:T(8,128)(2,1)}...) custom-call(s32[7]{0:T(128)S(1)} %copy-done.3, ...), custom_call_target="tpu_custom_call" | custom-call | flops 12079595520 | bytes 34603008 | tf_op jit(solution)/shard_map/pallas_call | solution.py:583
  263.8 21.8 %shard_map.385 = (f32[256,1536]{1,0:T(8,128)S(1)}, bf16[256,1536]{1,0:T(8,128)(2,1)S(1)}, bf16[2048,1280]{1,0:T(8,128)(2,1)}, bf16[2048,1280]{1,0:T(8,128)(2,1)}...) custom-call(s32[7]{0:T(128)S(1)} %copy-done.3, ...), custom_call_target="tpu_custom_call", output_to_operand_aliasing={{2}: (7, {}), {3}: (8, {}), {4}: (9, {}), {5}: (10, {}), {6... | custom-call | flops 12079595520 | bytes 34603008 | tf_op jit(solution)/shard_map/pallas_call | solution.py:583
  288.5 21.9 %shard_map.386 = (f32[256,1536]{1,0:T(8,128)S(1)}, bf16[256,1536]{1,0:T(8,128)(2,1)S(1)}, bf16[2048,1280]{1,0:T(8,128)(2,1)}, bf16[2048,1280]{1,0:T(8,128)(2,1)}...) custom-call(s32[7]{0:T(128)S(1)} %copy-done.3, ...), custom_call_target="tpu_custom_call", output_to_operand_aliasing={{2}: (7, {}), {3}: (8, {}), {4}: (9, {}), {5}: (10, {}), {6... | custom-call | flops 12079595520 | bytes 34603008 | tf_op jit(solution)/shard_map/pallas_call | solution.py:583
  312.4 21.6 %shard_map.387 = (f32[256,1536]{1,0:T(8,128)S(1)}, bf16[256,1536]{1,0:T(8,128)(2,1)S(1)}, bf16[2048,1280]{1,0:T(8,128)(2,1)}, bf16[2048,1280]{1,0:T(8,128)(2,1)}...) custom-call(s32[7]{0:T(128)S(1)} %copy-done.3, ...), custom_call_target="tpu_custom_call", output_to_operand_aliasing={{2}: (7, {}), {3}: (8, {}), {4}: (9, {}), {5}: (10, {}), {6... | custom-call | flops 12079595520 | bytes 34603008 | tf_op jit(solution)/shard_map/pallas_call | solution.py:583
  340.4 8.4 %shard_map.388 = (f32[4,2,192,1280]{3,2,1,0:T(8,128)}, bf16[4,2,192,1280]{3,2,1,0:T(8,128)(2,1)}) custom-call(s32[7]{0:T(128)S(1)} %copy-done.3, bf16[2048,1536]{1,0:T(8,128)(2,1)} %get-tuple-element.162.rows_ref, bf16[2048,1280]{1,0:T(8,128)(2,1)S(1)} %copy-done, bf16[2048,1280]{1,0:T(8,128)(2,1)S(1)} %copy-done.1), custom_call_target="tpu_custom_call" | custom-call | flops 3221225472 | bytes 13107200 | tf_op jit(solution)/shard_map/pallas_call | solution.py:651
  351.5 5.4 collective-permute-done.36
  359.3 8.4 %shard_map.389 = (f32[4,2,192,1280]{3,2,1,0:T(8,128)}, bf16[4,2,192,1280]{3,2,1,0:T(8,128)(2,1)}) custom-call(s32[7]{0:T(128)S(1)} %copy-done.3, bf16[2048,1536]{1,0:T(8,128)(2,1)} %get-tuple-element.162.rows_ref, bf16[2048,1280]{1,0:T(8,128)(2,1)S(1)} %copy-done, bf16[2048,1280]{1,0:T(8,128)(2,1)S(1)} %copy-done.1, ...), custom_call_target="tpu_custom_call", output_to_operand_aliasing={{0}: (4, {}), {1}: (5, {})} | custom-call | flops 3221225472 | bytes 13107200 | tf_op jit(solution)/shard_map/pallas_call | solution.py:651
  367.9 8.4 %shard_map.390 = (f32[4,2,192,1280]{3,2,1,0:T(8,128)}, bf16[4,2,192,1280]{3,2,1,0:T(8,128)(2,1)}) custom-call(s32[7]{0:T(128)S(1)} %copy-done.3, bf16[2048,1536]{1,0:T(8,128)(2,1)} %get-tuple-element.162.rows_ref, bf16[2048,1280]{1,0:T(8,128)(2,1)S(1)} %copy-done, bf16[2048,1280]{1,0:T(8,128)(2,1)S(1)} %copy-done.1, ...), custom_call_target="tpu_custom_call", output_to_operand_aliasing={{0}: (4, {}), {1}: (5, {})} | custom-call | flops 3221225472 | bytes 13107200 | tf_op jit(solution)/shard_map/pallas_call | solution.py:651
  376.3 8.1 %collective-permute-done.40 = bf16[128,1536]{1,0:T(8,128)(2,1)S(1)} collective-permute-done((bf16[128,1536]{1,0:T(8,128)(2,1)S(1)}, bf16[128,1536]{1,0:T(8,128)(2,1)S(1)}, u32[]{:S(2)}, u32[]{:S(2)}) %collective-permute-start.40) | collective-permute-done | bytes 393248 | tf_op jit(solution)/shard_map/ppermute | solution.py:183
  385.4 8.4 %shard_map.391 = (f32[4,2,192,1280]{3,2,1,0:T(8,128)}, bf16[4,2,192,1280]{3,2,1,0:T(8,128)(2,1)}) custom-call(s32[7]{0:T(128)S(1)} %copy-done.3, bf16[2048,1536]{1,0:T(8,128)(2,1)} %get-tuple-element.162.rows_ref, bf16[2048,1280]{1,0:T(8,128)(2,1)S(1)} %copy-done, bf16[2048,1280]{1,0:T(8,128)(2,1)S(1)} %copy-done.1, ...), custom_call_target="tpu_custom_call", output_to_operand_aliasing={{0}: (4, {}), {1}: (5, {})} | custom-call | flops 3221225472 | bytes 13107200 | tf_op jit(solution)/shard_map/pallas_call | solution.py:651
  393.9 8.4 %shard_map.392 = (f32[4,2,192,1280]{3,2,1,0:T(8,128)}, bf16[4,2,192,1280]{3,2,1,0:T(8,128)(2,1)}) custom-call(s32[7]{0:T(128)S(1)} %copy-done.3, bf16[2048,1536]{1,0:T(8,128)(2,1)} %get-tuple-element.162.rows_ref, bf16[2048,1280]{1,0:T(8,128)(2,1)S(1)} %copy-done, bf16[2048,1280]{1,0:T(8,128)(2,1)S(1)} %copy-done.1, ...), custom_call_target="tpu_custom_call", output_to_operand_aliasing={{0}: (4, {}), {1}: (5, {})} | custom-call | flops 3221225472 | bytes 13107200 | tf_op jit(solution)/shard_map/pallas_call | solution.py:651
  409.8 3.2 fusion.25
  416.9 3.5 convolution_bitcast_fusion
  423.1 3.0 fusion.36
  435.8 7.2 %add_convert_fusion = bf16[4,2,192,1280]{3,2,1,0:T(8,128)(2,1)} fusion(f32[4,2,192,1280]{3,2,1,0:T(8,128)} %get-tuple-element.165, bf16[4,2,192,1280]{3,2,1,0:T(8,128)(2,1)} %collective-permute-done.42), kind=kLoop, calls=%fused_computation.7 | loop fusion | flops 5898240 | bytes 15728640 | tf_op jit(solution)/shard_map/convert_element_type | solution.py:934
  443.0 5.1 all-to-all-start.1
  448.1 5.4 fusion.103
  456.0 4.7 shard_map.393
  460.7 4.1 fusion.1
  465.5 14.2 %shard_map.395 = (f32[10,64,1536]{2,1,0:T(8,128)S(1)}, f32[10,64,1536]{2,1,0:T(8,128)}) custom-call(s32[7]{0:T(128)S(1)} %copy-done.3, bf16[2048,1536]{1,0:T(8,128)(2,1)} %get-tuple-element.176.grads_ref, bf16[2048,1280]{1,0:T(8,128)(2,1)S(1)} %bitcast.123), custom_call_target="tpu_custom_call" | custom-call | flops 8053063680 | bytes 19398656 | tf_op jit(solution)/shard_map/pallas_call | solution.py:698
  491.4 30.3 %collective-permute-done.43 = bf16[288,1536]{1,0:T(8,128)(2,1)} collective-permute-done((bf16[288,1536]{1,0:T(8,128)(2,1)}, bf16[288,1536]{1,0:T(8,128)(2,1)}, u32[]{:S(2)}, u32[]{:S(2)}) %collective-permute-start.43) | collective-permute-done | bytes 884768 | tf_op jit(solution)/shard_map/ppermute | solution.py:158
  521.8 9.5 %collective-permute-done.52 = bf16[288,1536]{1,0:T(8,128)(2,1)} collective-permute-done((bf16[288,1536]{1,0:T(8,128)(2,1)}, bf16[288,1536]{1,0:T(8,128)(2,1)}, u32[]{:S(2)}, u32[]{:S(2)}) %collective-permute-start.52) | collective-permute-done | bytes 884768 | tf_op jit(solution)/shard_map/ppermute | solution.py:158
  531.2 24.4 %shard_map.394 = (f32[10,192,1024]{2,1,0:T(8,128)}, f32[10,192,1024]{2,1,0:T(8,128)}, f32[10,192,1024]{2,1,0:T(8,128)}, f32[10,192,1024]{2,1,0:T(8,128)}) custom-call(f32[10,192,1024]{2,1,0:T(8,128)} %w_ref.1, f32[10,192,1024]{2,1,0:T(8,128)} %first_ref.1, f32[10,192,1024]{2,1,0:T(8,128)} %second_ref.1, bf16[4,2,192,1280]{3,2,1,0:T(8,128)(2,1)} %all-to-all-done.1.grad_ref), custom_call_target="tpu_custom_call" | custom-call | flops 39321600 | bytes 58982400 | tf_op jit(solution)/shard_map/pallas_call | solution.py:743
  555.8 5.2 bitcast_add_fusion
  570.9 8.0 %collective-permute-done.50 = bf16[144,1536]{1,0:T(8,128)(2,1)S(1)} collective-permute-done((bf16[144,1536]{1,0:T(8,128)(2,1)S(1)}, bf16[144,1536]{1,0:T(8,128)(2,1)S(1)}, u32[]{:S(2)}, u32[]{:S(2)}) %collective-permute-start.50) | collective-permute-done | bytes 442400 | tf_op jit(solution)/shard_map/ppermute | solution.py:158
  579.0 4.6 collective-permute-done.48
  588.2 13.1 %multiply_subtract_fusion = (f32[10,64,1536]{2,1,0:T(8,128)}, f32[10,64,1536]{2,1,0:T(8,128)}, f32[10,64,1536]{2,1,0:T(8,128)}, f32[10,64,1536]{2,1,0:T(8,128)}) fusion(f32[10,64,1536]{2,1,0:T(8,128)} %param.31, f32[10,64,1536]{2,1,0:T(8,128)} %param.36, f32[10,64,1536]{2,1,0:T(8,128)} %param.41, f32[10,64,1536]{2,1,0:T(8,128)} %copy-done.2, ...), kind=kLoop, calls=%fused_computation.15 | loop fusion | flops 15728640 | bytes 35389440 | tf_op jit(solution)/shard_map/sub | solution.py:147
  (460 shorter events, 165.0 us)
Async XLA Ops:
  7.2 233.5 %all-gather.2.cloned.1.call-start = ((), (), s32[]{:S(2)}) async-start(), calls=%async_computation.3 | async-start | bytes 8519680 | tf_op jit(solution)/shard_map/all_gather | solution.py:821
  22.4 17.7 %collective-permute-start.12 = (bf16[256,1664]{1,0:T(8,128)(2,1)}, bf16[256,1664]{1,0:T(8,128)(2,1)}, u32[]{:S(2)}, u32[]{:S(2)}) collective-permute-start(bf16[256,1664]{1,0:T(8,128)(2,1)} %pad_maximum_fusion.2), channel_id=1, source_target_pairs={{0,8},{4,20},{8,0},{12,28},{16,24},{20,4},{24,16},{28,12},{1,9},{5... | collective-permute-start | bytes 2555912 | tf_op jit(solution)/shard_map/ppermute | solution.py:158
  25.4 42.5 %collective-permute-start.2 = (bf16[144,1536]{1,0:T(8,128)(2,1)}, bf16[144,1536]{1,0:T(8,128)(2,1)S(1)}, u32[]{:S(2)}, u32[]{:S(2)}) collective-permute-start(bf16[144,1536]{1,0:T(8,128)(2,1)} %pad_maximum_fusion.5), channel_id=1, source_target_pairs={{0,16},{4,12},{8,24},{12,4},{16,0},{20,28},{24,8},{28,20},{1,17},{... | collective-permute-start | bytes 1327112 | tf_op jit(solution)/shard_map/ppermute | solution.py:158
  26.9 15.7 %collective-permute-start.7 = (bf16[144,1536]{1,0:T(8,128)(2,1)}, bf16[144,1536]{1,0:T(8,128)(2,1)}, u32[]{:S(2)}, u32[]{:S(2)}) collective-permute-start(bf16[144,1536]{1,0:T(8,128)(2,1)} %pad_maximum_fusion.5), channel_id=1, source_target_pairs={{0,3},{1,0},{2,1},{3,2},{4,7},{5,4},{6,5},{7,6},{8,11},{9,8},{10,9... | collective-permute-start | bytes 1327112 | tf_op jit(solution)/shard_map/ppermute | solution.py:183
  30.5 37.3 %collective-permute-start.8 = (bf16[144,1536]{1,0:T(8,128)(2,1)}, bf16[144,1536]{1,0:T(8,128)(2,1)}, u32[]{:S(2)}, u32[]{:S(2)}) collective-permute-start(bf16[144,1536]{1,0:T(8,128)(2,1)} %pad_maximum_fusion.5), channel_id=1, source_target_pairs={{0,2},{1,3},{2,0},{3,1},{4,6},{5,7},{6,4},{7,5},{8,10},{9,11},{10,... | collective-permute-start | bytes 1327112 | tf_op jit(solution)/shard_map/ppermute | solution.py:183
  30.5 37.3 %collective-permute-start.4 = (bf16[144,1536]{1,0:T(8,128)(2,1)}, bf16[144,1536]{1,0:T(8,128)(2,1)}, u32[]{:S(2)}, u32[]{:S(2)}) collective-permute-start(bf16[144,1536]{1,0:T(8,128)(2,1)} %pad_maximum_fusion.5), channel_id=1, source_target_pairs={{0,1},{1,2},{2,3},{3,0},{4,5},{5,6},{6,7},{7,4},{8,9},{9,10},{10,1... | collective-permute-start | bytes 1327112 | tf_op jit(solution)/shard_map/ppermute | solution.py:183
  40.1 68.4 %collective-permute-start = (bf16[128,1536]{1,0:T(8,128)(2,1)S(1)}, bf16[128,1536]{1,0:T(8,128)(2,1)}, u32[]{:S(2)}, u32[]{:S(2)}) collective-permute-start(bf16[128,1536]{1,0:T(8,128)(2,1)S(1)} %copy-done.13), channel_id=1, source_target_pairs={{0,4},{4,0},{8,12},{12,8},{16,20},{20,16},{24,28},{28,24},{1,5},{5... | collective-permute-start | bytes 1179656 | tf_op jit(solution)/shard_map/ppermute | solution.py:158
  42.6 65.1 %collective-permute-start.15 = (s32[1,128]{1,0:T(1,128)S(1)}, s32[1,128]{1,0:T(1,128)S(1)}, u32[]{:S(2)}, u32[]{:S(2)}) collective-permute-start(s32[1,128]{1,0:T(1,128)S(1)} %copy-done.74), channel_id=1, source_target_pairs={{0,4},{4,0},{8,12},{12,8},{16,20},{20,16},{24,28},{28,24},{1,5},{5... | collective-permute-start | bytes 1544 | tf_op jit(solution)/shard_map/ppermute | solution.py:158
  68.8 54.4 %collective-permute-start.3 = (bf16[288,1536]{1,0:T(8,128)(2,1)}, bf16[288,1536]{1,0:T(8,128)(2,1)}, u32[]{:S(2)}, u32[]{:S(2)}) collective-permute-start(bf16[288,1536]{1,0:T(8,128)(2,1)} %pad_maximum_fusion.1.refs_0_), channel_id=1, source_target_pairs={{0,8},{4,20},{8,0},{12,28},{16,24},{20,4},{24,16},{28,12},{1,9},{5... | collective-permute-start | bytes 2654216 | tf_op jit(solution)/shard_map/ppermute | solution.py:158
  87.2 36.0 %collective-permute-start.11 = (bf16[288,1536]{1,0:T(8,128)(2,1)}, bf16[288,1536]{1,0:T(8,128)(2,1)}, u32[]{:S(2)}, u32[]{:S(2)}) collective-permute-start(bf16[288,1536]{1,0:T(8,128)(2,1)} %constant_dynamic-update-slice_fusion.10.refs_4_), channel_id=1, source_target_pairs={{0,8},{4,20},{8,0},{12,28},{16,24},{20,4},{24,16},{28,12},{1,9},{5... | collective-permute-start | bytes 2654216 | tf_op jit(solution)/shard_map/ppermute | solution.py:158
  107.7 23.7 %collective-permute-start.14 = (bf16[288,1536]{1,0:T(8,128)(2,1)}, bf16[288,1536]{1,0:T(8,128)(2,1)}, u32[]{:S(2)}, u32[]{:S(2)}) collective-permute-start(bf16[288,1536]{1,0:T(8,128)(2,1)} %constant_dynamic-update-slice_fusion.12.refs_6_), channel_id=1, source_target_pairs={{0,8},{4,20},{8,0},{12,28},{16,24},{20,4},{24,16},{28,12},{1,9},{5... | collective-permute-start | bytes 2654216 | tf_op jit(solution)/shard_map/ppermute | solution.py:158
  110.1 66.5 %collective-permute-start.23 = (bf16[10,64,1536]{2,1,0:T(8,128)(2,1)S(1)}, bf16[10,64,1536]{2,1,0:T(8,128)(2,1)}, u32[]{:S(2)}, u32[]{:S(2)}) collective-permute-start(bf16[10,64,1536]{2,1,0:T(8,128)(2,1)S(1)} %convert_element_type.302), channel_id=1, source_target_pairs={{0,4},{4,0},{8,12},{12,8},{16,20},{20,16},{24,28},{28,24},{1,5},{5... | collective-permute-start | bytes 5898248 | tf_op jit(solution)/shard_map/ppermute | solution.py:158
  118.1 51.7 %all-to-all-start = ((bf16[4,2,192,1280]{3,2,1,0:T(8,128)(2,1)}), bf16[4,2,192,1280]{3,2,1,0:T(8,128)(2,1)}, u32[]{:S(2)}, u32[]{:S(2)}) async-start(bf16[4,2,192,1280]{3,2,1,0:T(8,128)(2,1)} %shard_map.381), calls=%async_computation | async-start | bytes 7864320 | tf_op jit(solution)/shard_map/all_to_all | solution.py:851
  122.9 462.9 %reduce-scatter.2.cloned.1.call-start = ((), (), s32[]{:S(2)}) async-start(), calls=%async_computation.4 | async-start | bytes 7864320 | tf_op jit(solution)/shard_map/reduce_scatter | solution.py:939
  155.3 18.4 %collective-permute-start.16 = (f32[128,1536]{1,0:T(8,128)S(1)}, f32[128,1536]{1,0:T(8,128)}, u32[]{:S(2)}, u32[]{:S(2)}) collective-permute-start(f32[128,1536]{1,0:T(8,128)S(1)} %slice.362), channel_id=1, source_target_pairs={{0,4},{4,0},{8,12},{12,8},{16,20},{20,16},{24,28},{28,24},{1,5},{5... | collective-permute-start | bytes 2359304 | tf_op jit(solution)/shard_map/ppermute | solution.py:158
  169.8 64.3 %collective-permute-start.22 = (bf16[4,2,192,1280]{3,2,1,0:T(8,128)(2,1)}, bf16[4,2,192,1280]{3,2,1,0:T(8,128)(2,1)}, u32[]{:S(2)}, u32[]{:S(2)}) collective-permute-start(bf16[4,2,192,1280]{3,2,1,0:T(8,128)(2,1)} %all-to-all-done.mine_ref), channel_id=1, source_target_pairs={{0,4},{4,0},{8,12},{12,8},{16,20},{20,16},{24,28},{28,24},{1,5},{5... | collective-permute-start | bytes 11796488 | tf_op jit(solution)/shard_map/ppermute | solution.py:158
  181.1 27.6 %collective-permute-start.30 = (bf16[128,1536]{1,0:T(8,128)(2,1)S(1)}, bf16[128,1536]{1,0:T(8,128)(2,1)S(1)}, u32[]{:S(2)}, u32[]{:S(2)}) collective-permute-start(bf16[128,1536]{1,0:T(8,128)(2,1)S(1)} %multiply_convert_fusion.1), channel_id=1, source_target_pairs={{0,3},{1,0},{2,1},{3,2},{4,7},{5,4},{6,5},{7,6},{8,11},{9,8},{10,9... | collective-permute-start | bytes 1179656 | tf_op jit(solution)/shard_map/ppermute | solution.py:183
  181.1 25.7 %collective-permute-start.17 = (bf16[128,1536]{1,0:T(8,128)(2,1)S(1)}, bf16[128,1536]{1,0:T(8,128)(2,1)S(1)}, u32[]{:S(2)}, u32[]{:S(2)}) collective-permute-start(bf16[128,1536]{1,0:T(8,128)(2,1)S(1)} %multiply_convert_fusion.1), channel_id=1, source_target_pairs={{0,1},{1,2},{2,3},{3,0},{4,5},{5,6},{6,7},{7,4},{8,9},{9,10},{10,1... | collective-permute-start | bytes 1179656 | tf_op jit(solution)/shard_map/ppermute | solution.py:183
  184.7 55.9 %collective-permute-start.25 = (bf16[256,1536]{1,0:T(8,128)(2,1)}, bf16[256,1536]{1,0:T(8,128)(2,1)}, u32[]{:S(2)}, u32[]{:S(2)}) collective-permute-start(bf16[256,1536]{1,0:T(8,128)(2,1)} %constant_dynamic-update-slice_fusion.18.near_ref), channel_id=1, source_target_pairs={{0,8},{4,20},{8,0},{12,28},{16,24},{20,4},{24,16},{28,12},{1,9},{5... | collective-permute-start | bytes 2359304 | tf_op jit(solution)/shard_map/ppermute | solution.py:158
  214.6 49.2 %collective-permute-start.21 = (bf16[256,1536]{1,0:T(8,128)(2,1)S(1)}, bf16[256,1536]{1,0:T(8,128)(2,1)}, u32[]{:S(2)}, u32[]{:S(2)}) collective-permute-start(bf16[256,1536]{1,0:T(8,128)(2,1)S(1)} %constant_dynamic-update-slice_fusion.16.near_ref), channel_id=1, source_target_pairs={{0,8},{4,20},{8,0},{12,28},{16,24},{20,4},{24,16},{28,12},{1,9},{5... | collective-permute-start | bytes 2359304 | tf_op jit(solution)/shard_map/ppermute | solution.py:158
  222.7 65.8 %collective-permute-start.32 = (bf16[256,1536]{1,0:T(8,128)(2,1)S(1)}, bf16[256,1536]{1,0:T(8,128)(2,1)}, u32[]{:S(2)}, u32[]{:S(2)}) collective-permute-start(bf16[256,1536]{1,0:T(8,128)(2,1)S(1)} %constant_dynamic-update-slice_fusion.20.near_ref), channel_id=1, source_target_pairs={{0,8},{4,20},{8,0},{12,28},{16,24},{20,4},{24,16},{28,12},{1,9},{5... | collective-permute-start | bytes 2359304 | tf_op jit(solution)/shard_map/ppermute | solution.py:158
  232.9 79.5 %collective-permute-start.29 = (bf16[256,1536]{1,0:T(8,128)(2,1)S(1)}, bf16[256,1536]{1,0:T(8,128)(2,1)S(1)}, u32[]{:S(2)}, u32[]{:S(2)}) collective-permute-start(bf16[256,1536]{1,0:T(8,128)(2,1)S(1)} %constant_dynamic-update-slice_fusion.14.near_ref), channel_id=1, source_target_pairs={{0,8},{4,20},{8,0},{12,28},{16,24},{20,4},{24,16},{28,12},{1,9},{5... | collective-permute-start | bytes 2359304 | tf_op jit(solution)/shard_map/ppermute | solution.py:158
  262.7 23.9 %collective-permute-start.27 = (bf16[256,1536]{1,0:T(8,128)(2,1)S(1)}, bf16[256,1536]{1,0:T(8,128)(2,1)S(1)}, u32[]{:S(2)}, u32[]{:S(2)}) collective-permute-start(bf16[256,1536]{1,0:T(8,128)(2,1)S(1)} %get-tuple-element.127), channel_id=1, source_target_pairs={{0,8},{4,20},{8,0},{12,28},{16,24},{20,4},{24,16},{28,12},{1,9},{5... | collective-permute-start | bytes 2359304 | tf_op jit(solution)/shard_map/ppermute | solution.py:158
  285.6 26.2 %collective-permute-start.26 = (bf16[256,1536]{1,0:T(8,128)(2,1)S(1)}, bf16[256,1536]{1,0:T(8,128)(2,1)S(1)}, u32[]{:S(2)}, u32[]{:S(2)}) collective-permute-start(bf16[256,1536]{1,0:T(8,128)(2,1)S(1)} %get-tuple-element.125), channel_id=1, source_target_pairs={{0,8},{4,20},{8,0},{12,28},{16,24},{20,4},{24,16},{28,12},{1,9},{5... | collective-permute-start | bytes 2359304 | tf_op jit(solution)/shard_map/ppermute | solution.py:158
  286.9 25.4 %collective-permute-start.28 = (bf16[128,1536]{1,0:T(8,128)(2,1)S(1)}, bf16[128,1536]{1,0:T(8,128)(2,1)S(1)}, u32[]{:S(2)}, u32[]{:S(2)}) collective-permute-start(bf16[128,1536]{1,0:T(8,128)(2,1)S(1)} %slice.523), channel_id=1, source_target_pairs={{0,16},{4,12},{8,24},{12,4},{16,0},{20,28},{24,8},{28,20},{1,17},{... | collective-permute-start | bytes 1179656 | tf_op jit(solution)/shard_map/ppermute | solution.py:158
  310.4 38.4 %collective-permute-start.35 = (bf16[256,1536]{1,0:T(8,128)(2,1)S(1)}, bf16[256,1536]{1,0:T(8,128)(2,1)S(1)}, u32[]{:S(2)}, u32[]{:S(2)}) collective-permute-start(bf16[256,1536]{1,0:T(8,128)(2,1)S(1)} %get-tuple-element.144), channel_id=1, source_target_pairs={{0,8},{4,20},{8,0},{12,28},{16,24},{20,4},{24,16},{28,12},{1,9},{5... | collective-permute-start | bytes 2359304 | tf_op jit(solution)/shard_map/ppermute | solution.py:158
  312.1 23.0 %collective-permute-start.33 = (bf16[128,1536]{1,0:T(8,128)(2,1)S(1)}, bf16[128,1536]{1,0:T(8,128)(2,1)S(1)}, u32[]{:S(2)}, u32[]{:S(2)}) collective-permute-start(bf16[128,1536]{1,0:T(8,128)(2,1)S(1)} %slice.522), channel_id=1, source_target_pairs={{0,16},{4,12},{8,24},{12,4},{16,0},{20,28},{24,8},{28,20},{1,17},{... | collective-permute-start | bytes 1179656 | tf_op jit(solution)/shard_map/ppermute | solution.py:158
  334.0 16.4 %collective-permute-start.38 = (bf16[256,1536]{1,0:T(8,128)(2,1)S(1)}, bf16[256,1536]{1,0:T(8,128)(2,1)S(1)}, u32[]{:S(2)}, u32[]{:S(2)}) collective-permute-start(bf16[256,1536]{1,0:T(8,128)(2,1)S(1)} %get-tuple-element.146), channel_id=1, source_target_pairs={{0,8},{4,20},{8,0},{12,28},{16,24},{20,4},{24,16},{28,12},{1,9},{5... | collective-permute-start | bytes 2359304 | tf_op jit(solution)/shard_map/ppermute | solution.py:158
  335.2 41.2 %collective-permute-start.34 = (bf16[128,1536]{1,0:T(8,128)(2,1)S(1)}, bf16[128,1536]{1,0:T(8,128)(2,1)S(1)}, u32[]{:S(2)}, u32[]{:S(2)}) collective-permute-start(bf16[128,1536]{1,0:T(8,128)(2,1)S(1)} %fusion.55), channel_id=1, source_target_pairs={{0,3},{1,0},{2,1},{3,2},{4,7},{5,4},{6,5},{7,6},{8,11},{9,8},{10,9... | collective-permute-start | bytes 1179656 | tf_op jit(solution)/shard_map/ppermute | solution.py:183
  350.7 17.0 %collective-permute-start.39 = (bf16[128,1536]{1,0:T(8,128)(2,1)S(1)}, bf16[128,1536]{1,0:T(8,128)(2,1)S(1)}, u32[]{:S(2)}, u32[]{:S(2)}) collective-permute-start(bf16[128,1536]{1,0:T(8,128)(2,1)S(1)} %slice.520), channel_id=1, source_target_pairs={{0,16},{4,12},{8,24},{12,4},{16,0},{20,28},{24,8},{28,20},{1,17},{... | collective-permute-start | bytes 1179656 | tf_op jit(solution)/shard_map/ppermute | solution.py:158
  357.0 19.3 %collective-permute-start.37 = (bf16[128,1536]{1,0:T(8,128)(2,1)S(1)}, bf16[128,1536]{1,0:T(8,128)(2,1)S(1)}, u32[]{:S(2)}, u32[]{:S(2)}) collective-permute-start(bf16[128,1536]{1,0:T(8,128)(2,1)S(1)} %fusion.54), channel_id=1, source_target_pairs={{0,1},{1,2},{2,3},{3,0},{4,5},{5,6},{6,7},{7,4},{8,9},{9,10},{10,1... | collective-permute-start | bytes 1179656 | tf_op jit(solution)/shard_map/ppermute | solution.py:183
  367.8 16.6 %collective-permute-start.40 = (bf16[128,1536]{1,0:T(8,128)(2,1)S(1)}, bf16[128,1536]{1,0:T(8,128)(2,1)S(1)}, u32[]{:S(2)}, u32[]{:S(2)}) collective-permute-start(bf16[128,1536]{1,0:T(8,128)(2,1)S(1)} %fusion.53), channel_id=1, source_target_pairs={{0,2},{1,3},{2,0},{3,1},{4,6},{5,7},{6,4},{7,5},{8,10},{9,11},{10,... | collective-permute-start | bytes 1179656 | tf_op jit(solution)/shard_map/ppermute | solution.py:183
  402.3 33.5 %collective-permute-start.42 = (bf16[4,2,192,1280]{3,2,1,0:T(8,128)(2,1)}, bf16[4,2,192,1280]{3,2,1,0:T(8,128)(2,1)}, u32[]{:S(2)}, u32[]{:S(2)}) collective-permute-start(bf16[4,2,192,1280]{3,2,1,0:T(8,128)(2,1)} %get-tuple-element.166), channel_id=1, source_target_pairs={{0,4},{4,0},{8,12},{12,8},{16,20},{20,16},{24,28},{28,24},{1,5},{5... | collective-permute-start | bytes 11796488 | tf_op jit(solution)/shard_map/ppermute | solution.py:158
  443.0 88.3 %all-to-all-start.1 = ((bf16[4,2,192,1280]{3,2,1,0:T(8,128)(2,1)}), bf16[4,2,192,1280]{3,2,1,0:T(8,128)(2,1)}, u32[]{:S(2)}, u32[]{:S(2)}) async-start(bf16[4,2,192,1280]{3,2,1,0:T(8,128)(2,1)} %add_convert_fusion), calls=%async_computation.2 | async-start | bytes 7864320 | tf_op jit(solution)/shard_map/all_to_all | solution.py:936
  465.2 21.3 %collective-permute-start.57 = (f32[128,1536]{1,0:T(8,128)S(1)}, f32[128,1536]{1,0:T(8,128)S(1)}, u32[]{:S(2)}, u32[]{:S(2)}) collective-permute-start(f32[128,1536]{1,0:T(8,128)S(1)} %slice.393), channel_id=1, source_target_pairs={{0,4},{4,0},{8,12},{12,8},{16,20},{20,16},{24,28},{28,24},{1,5},{5... | collective-permute-start | bytes 2359304 | tf_op jit(solution)/shard_map/ppermute | solution.py:158
  479.7 108.5 %collective-permute-start.56 = (f32[10,64,1536]{2,1,0:T(8,128)}, f32[10,64,1536]{2,1,0:T(8,128)}, u32[]{:S(2)}, u32[]{:S(2)}) collective-permute-start(f32[10,64,1536]{2,1,0:T(8,128)} %get-tuple-element.179), channel_id=1, source_target_pairs={{0,4},{4,0},{8,12},{12,8},{16,20},{20,16},{24,28},{28,24},{1,5},{5... | collective-permute-start | bytes 11796488 | tf_op jit(solution)/shard_map/ppermute | solution.py:158
  482.7 73.0 %collective-permute-start.47 = (bf16[288,1536]{1,0:T(8,128)(2,1)}, bf16[288,1536]{1,0:T(8,128)(2,1)}, u32[]{:S(2)}, u32[]{:S(2)}) collective-permute-start(bf16[288,1536]{1,0:T(8,128)(2,1)} %get-tuple-element.311), channel_id=1, source_target_pairs={{0,8},{4,20},{8,0},{12,28},{16,24},{20,4},{24,16},{28,12},{1,9},{5... | collective-permute-start | bytes 2654216 | tf_op jit(solution)/shard_map/ppermute | solution.py:158
  484.5 71.3 %collective-permute-start.49 = (bf16[288,1536]{1,0:T(8,128)(2,1)}, bf16[288,1536]{1,0:T(8,128)(2,1)}, u32[]{:S(2)}, u32[]{:S(2)}) collective-permute-start(bf16[288,1536]{1,0:T(8,128)(2,1)} %get-tuple-element.310), channel_id=1, source_target_pairs={{0,8},{4,20},{8,0},{12,28},{16,24},{20,4},{24,16},{28,12},{1,9},{5... | collective-permute-start | bytes 2654216 | tf_op jit(solution)/shard_map/ppermute | solution.py:158
  484.7 37.1 %collective-permute-start.43 = (bf16[288,1536]{1,0:T(8,128)(2,1)}, bf16[288,1536]{1,0:T(8,128)(2,1)}, u32[]{:S(2)}, u32[]{:S(2)}) collective-permute-start(bf16[288,1536]{1,0:T(8,128)(2,1)} %get-tuple-element.312), channel_id=1, source_target_pairs={{0,8},{4,20},{8,0},{12,28},{16,24},{20,4},{24,16},{28,12},{1,9},{5... | collective-permute-start | bytes 2654216 | tf_op jit(solution)/shard_map/ppermute | solution.py:158
  486.5 44.7 %collective-permute-start.52 = (bf16[288,1536]{1,0:T(8,128)(2,1)}, bf16[288,1536]{1,0:T(8,128)(2,1)}, u32[]{:S(2)}, u32[]{:S(2)}) collective-permute-start(bf16[288,1536]{1,0:T(8,128)(2,1)} %get-tuple-element.309), channel_id=1, source_target_pairs={{0,8},{4,20},{8,0},{12,28},{16,24},{20,4},{24,16},{28,12},{1,9},{5... | collective-permute-start | bytes 2654216 | tf_op jit(solution)/shard_map/ppermute | solution.py:158
  563.9 15.1 %collective-permute-start.53 = (bf16[144,1536]{1,0:T(8,128)(2,1)S(1)}, bf16[144,1536]{1,0:T(8,128)(2,1)S(1)}, u32[]{:S(2)}, u32[]{:S(2)}) collective-permute-start(bf16[144,1536]{1,0:T(8,128)(2,1)S(1)} %slice.515), channel_id=1, source_target_pairs={{0,16},{4,12},{8,24},{12,4},{16,0},{20,28},{24,8},{28,20},{1,17},{... | collective-permute-start | bytes 1327112 | tf_op jit(solution)/shard_map/ppermute | solution.py:158
  564.6 14.2 %collective-permute-start.50 = (bf16[144,1536]{1,0:T(8,128)(2,1)S(1)}, bf16[144,1536]{1,0:T(8,128)(2,1)S(1)}, u32[]{:S(2)}, u32[]{:S(2)}) collective-permute-start(bf16[144,1536]{1,0:T(8,128)(2,1)S(1)} %slice.516), channel_id=1, source_target_pairs={{0,16},{4,12},{8,24},{12,4},{16,0},{20,28},{24,8},{28,20},{1,17},{... | collective-permute-start | bytes 1327112 | tf_op jit(solution)/shard_map/ppermute | solution.py:158
  566.2 17.4 %collective-permute-start.48 = (bf16[144,1536]{1,0:T(8,128)(2,1)S(1)}, bf16[144,1536]{1,0:T(8,128)(2,1)S(1)}, u32[]{:S(2)}, u32[]{:S(2)}) collective-permute-start(bf16[144,1536]{1,0:T(8,128)(2,1)S(1)} %slice.517), channel_id=1, source_target_pairs={{0,16},{4,12},{8,24},{12,4},{16,0},{20,28},{24,8},{28,20},{1,17},{... | collective-permute-start | bytes 1327112 | tf_op jit(solution)/shard_map/ppermute | solution.py:158
  569.4 14.1 %collective-permute-start.54 = (bf16[144,1536]{1,0:T(8,128)(2,1)S(1)}, bf16[144,1536]{1,0:T(8,128)(2,1)S(1)}, u32[]{:S(2)}, u32[]{:S(2)}) collective-permute-start(bf16[144,1536]{1,0:T(8,128)(2,1)S(1)} %slice_add_fusion.5), channel_id=1, source_target_pairs={{0,3},{1,0},{2,1},{3,2},{4,7},{5,4},{6,5},{7,6},{8,11},{9,8},{10,9... | collective-permute-start | bytes 1327112 | tf_op jit(solution)/shard_map/ppermute | solution.py:183
  578.9 23.4 %collective-permute-start.51 = (bf16[144,1536]{1,0:T(8,128)(2,1)S(1)}, bf16[144,1536]{1,0:T(8,128)(2,1)}, u32[]{:S(2)}, u32[]{:S(2)}) collective-permute-start(bf16[144,1536]{1,0:T(8,128)(2,1)S(1)} %fusion.42), channel_id=1, source_target_pairs={{0,1},{1,2},{2,3},{3,0},{4,5},{5,6},{6,7},{7,4},{8,9},{9,10},{10,1... | collective-permute-start | bytes 1327112 | tf_op jit(solution)/shard_map/ppermute | solution.py:183
  584.5 17.8 %collective-permute-start.55 = (bf16[144,1536]{1,0:T(8,128)(2,1)}, bf16[144,1536]{1,0:T(8,128)(2,1)}, u32[]{:S(2)}, u32[]{:S(2)}) collective-permute-start(bf16[144,1536]{1,0:T(8,128)(2,1)} %fusion.41), channel_id=1, source_target_pairs={{0,3},{1,0},{2,1},{3,2},{4,7},{5,4},{6,5},{7,6},{8,11},{9,8},{10,9... | collective-permute-start | bytes 1327112 | tf_op jit(solution)/shard_map/ppermute | solution.py:183
  587.1 14.2 %collective-permute-start.45 = (bf16[256,1536]{1,0:T(8,128)(2,1)S(1)}, bf16[256,1536]{1,0:T(8,128)(2,1)S(1)}, u32[]{:S(2)}, u32[]{:S(2)}) collective-permute-start(bf16[256,1536]{1,0:T(8,128)(2,1)S(1)} %slice.310), channel_id=1, source_target_pairs={{0,8},{4,20},{8,0},{12,28},{16,24},{20,4},{24,16},{28,12},{1,9},{5... | collective-permute-start | bytes 2359304 | tf_op jit(solution)/shard_map/ppermute | solution.py:158
  604.5 18.0 %collective-permute-start.46 = (bf16[128,1536]{1,0:T(8,128)(2,1)}, bf16[128,1536]{1,0:T(8,128)(2,1)}, u32[]{:S(2)}, u32[]{:S(2)}) collective-permute-start(bf16[128,1536]{1,0:T(8,128)(2,1)} %slice.519), channel_id=1, source_target_pairs={{0,16},{4,12},{8,24},{12,4},{16,0},{20,28},{24,8},{28,20},{1,17},{... | collective-permute-start | bytes 1179656 | tf_op jit(solution)/shard_map/ppermute | solution.py:158
  (93 other events, 694.0 us)
Sparse Core Ops, SparseCore 0:
  67.9 126.7 all-gather.1
  402.5 108.3 reduce-scatter.1

commit v4 on v3

--- a/solution.py
+++ b/solution.py
@@ -185,6 +185,11 @@
 
 def after(values, *others):
     return lax.optimization_barrier((values, others))[0]
+
+
+def start_ring(block):
+    ahead, behind = turn(block, 1), turn(block, -1)
+    return [block, ahead, behind, turn(ahead, 1)]
 
 
 def along_first(part):
@@ -496,18 +501,19 @@
     )(normed, joined, attended, grads, gain)
 
 
-def expert_kernel(place_ref, near_ref, away_ref, *refs, per_step, spot):
-    given_ref, gate_ref, upper_ref, down_ref = refs[:4]
-    near_back_ref, away_back_ref = refs[-11:-9]
+def expert_kernel(place_ref, *refs, per_step, count):
+    source_refs = refs[:count]
+    given_ref, gate_ref, upper_ref, down_ref = refs[count : count + 4]
+    back_refs = refs[-9 - count : -9]
     hidden_ref, grad_gate_ref, grad_upper_ref, rows_ref, grads_ref, narrow_ref = refs[-9:-3]
     route_ref, out_ref, back_ref = refs[-3:]
     step = pl.program_id(0)
-    half, width = near_ref.shape
+    half, width = source_refs[0].shape
 
     @pl.when(step == 0)
     def _():
-        rows_ref[:half, :] = near_ref[...]
-        rows_ref[half:, :] = away_ref[...]
+        for i, ref in enumerate(source_refs):
+            rows_ref[half * i : half * (i + 1), :] = ref[...]
         grads_ref[...] = given_ref[:, :width]
         lanes = lax.broadcasted_iota(jnp.int32, route_ref.shape, 1)
         expert = (lanes + place_ref[2]).astype(jnp.float32)
@@ -559,60 +565,56 @@
     @pl.when(step == pl.num_programs(0) - 1)
     def _():
         narrow_ref[...] = out_ref[...].astype(jnp.bfloat16)
-        near_back_ref[...] = back_ref[:half, :]
-        away_back_ref[...] = back_ref[half:, :].astype(jnp.bfloat16)
-
-
-def expert_block(place, spot, near, away, given, weights, experts, filled):
+        for i, ref in enumerate(back_refs):
+            ref[...] = back_ref[half * i : half * (i + 1), :].astype(ref.dtype)
+
+
+def expert_block(place, spot, second, sources, given, weights, experts, filled):
     gate_w, upper_w, down_w = weights
-    half, width = near.shape
-    block = half // 2
+    half, width = sources[0].shape
+    wide = given.shape[1]
     total = gate_w.shape[1]
     per_step = 2
     steps = experts // per_step
     columns = total // steps
-    whole = lambda a: pl.BlockSpec(a.shape, lambda i, p: (0, 0))
-    rows = 2 * half
-    every = rows * len(DISTANCE)
+    count = len(sources)
+    rows = half * count
+    every = 2 * half * len(DISTANCE)
+    at = (2 * spot + second) // count
+    of = lambda p: p[3 + spot] * (2 // count) + second
+    dtypes = (jnp.float32, jnp.bfloat16)[second : second + count]
     b16 = lambda r, c: jax.ShapeDtypeStruct((r, c), jnp.bfloat16)
     fixed = pl.BlockSpec((half, width), lambda i, p: (0, 0))
-    part = pl.BlockSpec((rows, columns), lambda i, p: (spot, i))
-    kept = pl.BlockSpec((rows, width), lambda i, p: (spot, 0))
-    wide = given.shape[1]
-    inputs = (place, near, away, given, gate_w, upper_w, down_w)
+    part = pl.BlockSpec((rows, columns), lambda i, p: (at, i))
+    kept = pl.BlockSpec((rows, width), lambda i, p: (at, 0))
+    inputs = (place, *sources, given, gate_w, upper_w, down_w)
     return pl.pallas_call(
-        functools.partial(expert_kernel, per_step=per_step, spot=spot),
+        functools.partial(expert_kernel, per_step=per_step, count=count),
         grid_spec=pltpu.PrefetchScalarGridSpec(
             num_scalar_prefetch=1,
             grid=(steps,),
-            in_specs=[
-                whole(near),
-                whole(away),
-                pl.BlockSpec((rows, wide), lambda i, p: (p[3 + spot], 0)),
-            ]
+            in_specs=[fixed] * count
             + [
+                pl.BlockSpec((rows, wide), lambda i, p: (of(p), 0)),
                 pl.BlockSpec((width, columns), lambda i, p: (0, i)),
                 pl.BlockSpec((width, columns), lambda i, p: (0, i)),
                 pl.BlockSpec((columns, width), lambda i, p: (i, 0)),
             ]
             + [pl.BlockSpec(memory_space=pl.ANY)] * len(filled),
-            out_specs=[fixed] * 2
+            out_specs=[fixed] * count
             + [part] * 3
             + [kept] * 2
-            + [pl.BlockSpec((rows, width), lambda i, p: (p[3 + spot], 0))],
+            + [pl.BlockSpec((rows, width), lambda i, p: (of(p), 0))],
             scratch_shapes=[
                 pltpu.VMEM((rows, wide - width), jnp.float32),
                 pltpu.VMEM((rows, width), jnp.float32),
                 pltpu.VMEM((rows, width), jnp.float32),
             ],
         ),
-        out_shape=[
-            jax.ShapeDtypeStruct((half, width), jnp.float32),
-            b16(half, width),
-        ]
+        out_shape=[jax.ShapeDtypeStruct((half, width), dtype) for dtype in dtypes]
         + [b16(every, total)] * 3
         + [b16(every, width)] * 3,
-        input_output_aliases={len(inputs) + i: 2 + i for i in range(len(filled))},
+        input_output_aliases={len(inputs) + i: count + i for i in range(len(filled))},
         compiler_params=pltpu.CompilerParams(vmem_limit_bytes=48 * 1024 * 1024),
         cost_estimate=pl.CostEstimate(
             flops=2 * rows * width * total * 6,
@@ -805,9 +807,9 @@
         0,
     )
     share = local_experts * (FF // chips)
-    attention_ring = [block] + [turn(block, distance) for distance in DISTANCE[1:]]
+    attention_ring = start_ring(block)
     attention_pairs = [along_first(part) for part in attention_ring[:2]]
-    pieces = spread_columns(after(w_gate_up, attention_pairs[0]), chips)
+    pieces = spread_columns(after(w_gate_up, taken), chips)
     routes = jnp.concatenate([expert_ids.astype(NARROW)] + split_three(route_weights), 1)
     cotangent_rows = jnp.concatenate(
         [
@@ -821,9 +823,8 @@
     cotangent_all = lax.all_gather(
         after(cotangent_here, attention_ring), "expert", axis=0, tiled=True
     )
-    attention_ring = attention_ring[:2] + after(attention_ring[2:], (pieces, cotangent_pair))
     attention_pairs.append(along_first(attention_ring[2]))
-    attention_pairs.append(along_first(after(attention_ring[3], cotangent_here)))
+    attention_pairs.append(along_first(after(attention_ring[3], (pieces, cotangent_here))))
     attention_blocks = [(pair, swap_second(pair)) for pair in attention_pairs]
 
     sources = jnp.asarray(gathered_sources(count_dp, count_expert))[place_dp, place_expert]
@@ -849,7 +850,7 @@
     )
     parities = [list(range(i, count_dp, 2)) for i in range(2)]
     pieces = lax.all_to_all(
-        after(pieces, attention_blocks[1][1]), "dp", 0, 0, axis_index_groups=parities, tiled=True
+        after(pieces, attention_blocks[2][1]), "dp", 0, 0, axis_index_groups=parities, tiled=True
     )
     down_mine = after(w_down, attention_pairs[0]).astype(NARROW)
     down_theirs = swap_core(down_mine)
@@ -858,6 +859,7 @@
         jnp.concatenate([down_mine, down_theirs], 1),
         jnp.concatenate([down_theirs, down_mine], 1),
     ).reshape(share, MODEL_WIDTH)
+    attention_blocks = after(attention_blocks, down_w)
 
     cosine_table, sine_table = rotary_tables(sequence_length, HEAD_SIZE // 2)
     inputs = tokens.astype(WIDE)
@@ -888,26 +890,32 @@
     normed_two = (resid * scale_two * gain_moe).astype(NARROW)
     normed_two = after(normed_two, pieces)
 
-    normed_blocks, _ = gather_plane_last(normed_two)
+    normed_ring = [normed_two] + [turn(normed_two, distance) for distance in DISTANCE[1:]]
     gate_w, upper_w = stack_rows(place, pieces, after(swap_core(pieces), normed_two))
     back_parts, filled = [], []
-    second_parts = []
-    for spot, (near, away) in enumerate(normed_blocks):
+    second_parts, begun = [], ()
+    for spot, part in enumerate(normed_ring):
+        near = along_first(after(part, begun))
+        away = swap_second(near)
         if spot >= 2:
             near = after(near, (second_parts[spot - 2], back_parts[: spot - 2]))
-        done = expert_block(
-            place,
-            spot,
-            near,
-            away,
-            cotangent_all,
-            (gate_w, upper_w, down_w),
-            local_experts,
-            filled,
-        )
-        filled = done[2:]
+        back = []
+        for second, sources in ((0, [near]), (1, [away])) if spot < 2 else ((0, [near, away]),):
+            done = expert_block(
+                place,
+                spot,
+                second,
+                sources,
+                cotangent_all,
+                (gate_w, upper_w, down_w),
+                local_experts,
+                filled,
+            )
+            back += done[: len(sources)]
+            filled = done[len(sources) :]
+            begun = begun or (back[0],)
         if spot < len(DISTANCE) - 1:
-            second_parts.append(add_second(done[0], done[1]))
+            second_parts.append(add_second(*back))
             back_parts.append(add_first(second_parts[-1]))
     hidden, grad_gate, grad_upper, rows_all, grads_all, out_all = filled
     steps = local_experts // 2
@@ -917,7 +925,7 @@
             place, step, steps, rows_all, grad_gate, grad_upper, chips, kept_grads
         )
         if step == 0:
-            last = add_second(done[0], done[1], kept_grads)
+            last = add_second(*back, kept_grads)
         elif step == 1:
             back_parts.append(add_first(last, kept_grads))
         elif step == 2:
@@ -989,7 +997,7 @@
     )
     in_plane = [None] * len(DISTANCE)
     for i in (3, 1, 2, 0):
-        in_plane[i] = add_second(near_parts[i], away_parts[i], new_gate_up if i in (2, 0) else ())
+        in_plane[i] = add_second(near_parts[i], away_parts[i], new_gate_up)
     for i in (3, 1, 2, 0):
         in_plane[i] = add_first(in_plane[i])
     out_sums = after(out_sums, in_plane[3]).astype(WIDE)

time: 639 us -> 612 us (0.958)
  waiting for transfers between devices: 193 us -> 155 us
  starting transfers between devices: 67.7 us -> 82.3 us
  local copies, waits for them, and re-layouts: 60.1 us -> 49.8 us
  Pallas kernels: 194 us -> 203 us
    ppermute x12, waiting for transfers between devices: 56.5 us -> 39.5 us  [turn(): lax.ppermute(rows, 'expert', [(i, (i + step) % count) for i in range(coun...]
    all_to_all x1, waiting for transfers between devices: 14.4 us -> 0.01 us  [shards_moved(): lax.all_to_all(after(pieces, attention_blocks[2][1]), 'dp', 0, 0, axis_in...]
    ppermute x12, starting transfers between devices: 12.5 us -> 25.9 us  [turn(): lax.ppermute(rows, 'expert', [(i, (i + step) % count) for i in range(coun...]
    ppermute x47, waiting for transfers between devices: 122 us -> 111 us  [swap(): return lax.ppermute(rows, 'dp', [(i, i ^ pick(i)) for i in range(count)])]
    pallas_call x4 -> x6, Pallas kernels: 87.3 us -> 95.7 us  [expert_block(): pl.pallas_call(functools.partial(expert_kernel, per_step=per_step, count=...]
    unnamed x176 -> x161, local copies, waits for them, and re-layouts: 24.7 us -> 25 us
  transfers between devices with their start and end apart: 63 -> 63, of which waited for: 21 -> 23; matrix products, arithmetic and copies ran while one was open for 22% -> 21% of each run, Pallas kernels for 28% -> 32%
where the time goes in v4:
time: 612 us; the launch traced here: 604 us
  Pallas kernels  203 us (33%)
  waiting for transfers between devices  155 us (25%)
  starting transfers between devices  82.3 us (13%)
  other arithmetic  63.2 us (10%)
  local copies, waits for them, and re-layouts  49.8 us (8%)
  matrix products  34 us (6%)
  between operations  16.3 us (3%)
    ppermute x47, waiting for transfers between devices, swap(): return lax.ppermute(rows, 'dp', [(i, i ^ pick(i)) for i in range(count)])  111 us
    pallas_call x6, Pallas kernels, expert_block(): pl.pallas_call(functools.partial(expert_kernel, per_step=per_step, count=...  95.7 us
    ppermute x47, starting transfers between devices, swap(): return lax.ppermute(rows, 'dp', [(i, i ^ pick(i)) for i in range(count)])  46.3 us
    pallas_call x5, Pallas kernels, column_grads(): pl.pallas_call(column_grads_kernel, grid_spec=pltpu.PrefetchScalarGridSpe...  42.8 us
    ppermute x12, waiting for transfers between devices, turn(): lax.ppermute(rows, 'expert', [(i, (i + step) % count) for i in range(coun...  39.5 us
    ppermute x12, starting transfers between devices, turn(): lax.ppermute(rows, 'expert', [(i, (i + step) % count) for i in range(coun...  25.9 us
    unnamed x161, local copies, waits for them, and re-layouts  25 us
    pallas_call x1, Pallas kernels, adam_columns(): pl.pallas_call(adam_columns_kernel, grid=(experts,), in_specs=[block] * 3...  24.5 us
  transfers between devices with their start and end apart: 63, of which 23 were waited for; matrix products, arithmetic and copies ran while one was open for 21% of the time, Pallas kernels for 32%

profile of v4, /device:TPU:0, one launch (start us, length us, event | category | flops | bytes accessed | tf_op | source)
XLA Modules:
  0.0 604.3 jit_solution(13258793886840822401)
XLA Ops:
  10.1 3.0 collective-permute-start.11
  27.3 10.1 %collective-permute-done.4 = bf16[144,1536]{1,0:T(8,128)(2,1)S(1)} collective-permute-done((bf16[144,1536]{1,0:T(8,128)(2,1)}, bf16[144,1536]{1,0:T(8,128)(2,1)S(1)}, u32[]{:S(2)}, u32[]{:S(2)}) %collective-permute-start.4) | collective-permute-done | bytes 442400 | tf_op jit(solution)/shard_map/ppermute | solution.py:183
  37.3 5.0 collective-permute-start.10
  46.8 7.3 %collective-permute-done.10 = bf16[144,1536]{1,0:T(8,128)(2,1)} collective-permute-done((bf16[144,1536]{1,0:T(8,128)(2,1)S(1)}, bf16[144,1536]{1,0:T(8,128)(2,1)}, u32[]{:S(2)}, u32[]{:S(2)}) %collective-permute-start.10) | collective-permute-done | bytes 442400 | tf_op jit(solution)/shard_map/ppermute | solution.py:183
  56.8 8.6 %shard_map.381 = bf16[4,2,192,1280]{3,2,1,0:T(8,128)(2,1)} custom-call(f32[10,192,1024]{2,1,0:T(8,128)} %w_ref.1), custom_call_target="tpu_custom_call" | custom-call | bytes 11796480 | tf_op jit(solution)/shard_map/pallas_call | solution.py:338
  87.0 4.9 collective-permute-done.9.refs_5_
  91.9 4.8 all-to-all-start
  102.1 4.5 maximum_select_fusion
  106.7 14.4 %collective-permute-done.6.refs_3_ = bf16[288,1536]{1,0:T(8,128)(2,1)} collective-permute-done((bf16[288,1536]{1,0:T(8,128)(2,1)}, bf16[288,1536]{1,0:T(8,128)(2,1)}, u32[]{:S(2)}, u32[]{:S(2)}) %collective-permute-start.6) | collective-permute-done | bytes 884768 | tf_op jit(solution)/shard_map/ppermute | solution.py:158
  121.1 41.3 %collective-permute-done.14.refs_7_ = bf16[288,1536]{1,0:T(8,128)(2,1)S(1)} collective-permute-done((bf16[288,1536]{1,0:T(8,128)(2,1)}, bf16[288,1536]{1,0:T(8,128)(2,1)S(1)}, u32[]{:S(2)}, u32[]{:S(2)}) %collective-permute-start.14) | collective-permute-done | bytes 884768 | tf_op jit(solution)/shard_map/ppermute | solution.py:158
  163.4 6.3 %shard_map.382 = (bf16[1536,1280]{1,0:T(8,128)(2,1)}, bf16[1536,128]{1,0:T(8,128)(2,1)}, bf16[768,1536]{1,0:T(8,128)(2,1)}) custom-call(bf16[288,1536]{1,0:T(8,128)(2,1)} %copy-done.21, bf16[288,1536]{1,0:T(8,128)(2,1)} %collective-permute-done.3.refs_1_, bf16[288,1536]{1,0:T(8,128)(2,1)} %constant_dynamic-update-slice_fusion.8.refs_2_, ...), custom_call_target="tpu_custom_call" | custom-call | bytes 14155776 | tf_op jit(solution)/shard_map/pallas_call | solution.py:421
  170.9 3.3 multiply_convert_fusion
  195.4 6.6 %shard_map.383 = (bf16[1536,1280]{1,0:T(8,128)(2,1)}, bf16[1536,1280]{1,0:T(8,128)(2,1)}) custom-call(s32[7]{0:T(128)} %pad_add_fusion.1.place_ref, bf16[4,2,192,1280]{3,2,1,0:T(8,128)(2,1)} %all-to-all-done.mine_ref, bf16[4,2,192,1280]{3,2,1,0:T(8,128)(2,1)} %collective-permute-done.20.theirs_ref), custom_call_target="tpu_custom_call" | custom-call | bytes 15728640 | tf_op jit(solution)/shard_map/pallas_call | solution.py:374
  202.0 13.7 %shard_map.384 = (f32[256,1536]{1,0:T(8,128)S(1)}, bf16[2048,1280]{1,0:T(8,128)(2,1)}, bf16[2048,1280]{1,0:T(8,128)(2,1)}, bf16[2048,1280]{1,0:T(8,128)(2,1)}, b...) custom-call(s32[7]{0:T(128)S(1)} %copy-done.9, ...), custom_call_target="tpu_custom_call" | custom-call | flops 6039797760 | bytes 23199744 | tf_op jit(solution)/shard_map/pallas_call | solution.py:591
  215.7 7.9 %collective-permute-done.18 = bf16[128,1536]{1,0:T(8,128)(2,1)S(1)} collective-permute-done((bf16[128,1536]{1,0:T(8,128)(2,1)S(1)}, bf16[128,1536]{1,0:T(8,128)(2,1)S(1)}, u32[]{:S(2)}, u32[]{:S(2)}) %collective-permute-start.18) | collective-permute-done | bytes 393248 | tf_op jit(solution)/shard_map/ppermute | solution.py:183
  227.1 12.7 %shard_map.385 = (bf16[256,1536]{1,0:T(8,128)(2,1)S(1)}, bf16[2048,1280]{1,0:T(8,128)(2,1)}, bf16[2048,1280]{1,0:T(8,128)(2,1)}, bf16[2048,1280]{1,0:T(8,128)(2,...) custom-call(s32[7]{0:T(128)S(1)} %copy-done.9, ...), custom_call_target="tpu_custom_call", output_to_operand_aliasing={{1}: (6, {}), {2}: (7, {}), {3}: (8, {}), {4}: (9, {}), {5}... | custom-call | flops 6039797760 | bytes 23199744 | tf_op jit(solution)/shard_map/pallas_call | solution.py:591
  246.3 13.4 %shard_map.386 = (f32[256,1536]{1,0:T(8,128)S(1)}, bf16[2048,1280]{1,0:T(8,128)(2,1)}, bf16[2048,1280]{1,0:T(8,128)(2,1)}, bf16[2048,1280]{1,0:T(8,128)(2,1)}, b...) custom-call(s32[7]{0:T(128)S(1)} %copy-done.9, ...), custom_call_target="tpu_custom_call", output_to_operand_aliasing={{1}: (6, {}), {2}: (7, {}), {3}: (8, {}), {4}: (9, {}), {5}... | custom-call | flops 6039797760 | bytes 23199744 | tf_op jit(solution)/shard_map/pallas_call | solution.py:591
  260.7 12.3 %collective-permute-done.25.refs_0_ = bf16[256,1536]{1,0:T(8,128)(2,1)S(1)} collective-permute-done((bf16[256,1536]{1,0:T(8,128)(2,1)S(1)}, bf16[256,1536]{1,0:T(8,128)(2,1)S(1)}, u32[]{:S(2)}, u32[]{:S(2)}) %collective-permute-start.25) | collective-permute-done | bytes 786464 | tf_op jit(solution)/shard_map/ppermute | solution.py:158
  272.9 12.7 %shard_map.387 = (bf16[256,1536]{1,0:T(8,128)(2,1)S(1)}, bf16[2048,1280]{1,0:T(8,128)(2,1)}, bf16[2048,1280]{1,0:T(8,128)(2,1)}, bf16[2048,1280]{1,0:T(8,128)(2,...) custom-call(s32[7]{0:T(128)S(1)} %copy-done.9, ...), custom_call_target="tpu_custom_call", output_to_operand_aliasing={{1}: (6, {}), {2}: (7, {}), {3}: (8, {}), {4}: (9, {}), {5}... | custom-call | flops 6039797760 | bytes 23199744 | tf_op jit(solution)/shard_map/pallas_call | solution.py:591
  286.4 21.7 %shard_map.388 = (f32[256,1536]{1,0:T(8,128)S(1)}, bf16[256,1536]{1,0:T(8,128)(2,1)S(1)}, bf16[2048,1280]{1,0:T(8,128)(2,1)}, bf16[2048,1280]{1,0:T(8,128)(2,1)}...) custom-call(s32[7]{0:T(128)S(1)} %copy-done.9, ...), custom_call_target="tpu_custom_call", output_to_operand_aliasing={{2}: (7, {}), {3}: (8, {}), {4}: (9, {}), {5}: (10, {}), {6... | custom-call | flops 12079595520 | bytes 34603008 | tf_op jit(solution)/shard_map/pallas_call | solution.py:591
  310.6 21.5 %shard_map.389 = (f32[256,1536]{1,0:T(8,128)S(1)}, bf16[256,1536]{1,0:T(8,128)(2,1)S(1)}, bf16[2048,1280]{1,0:T(8,128)(2,1)}, bf16[2048,1280]{1,0:T(8,128)(2,1)}...) custom-call(s32[7]{0:T(128)S(1)} %copy-done.9, ...), custom_call_target="tpu_custom_call", output_to_operand_aliasing={{2}: (7, {}), {3}: (8, {}), {4}: (9, {}), {5}: (10, {}), {6... | custom-call | flops 12079595520 | bytes 34603008 | tf_op jit(solution)/shard_map/pallas_call | solution.py:591
  339.5 8.4 %shard_map.390 = (f32[4,2,192,1280]{3,2,1,0:T(8,128)}, bf16[4,2,192,1280]{3,2,1,0:T(8,128)(2,1)}) custom-call(s32[7]{0:T(128)S(1)} %copy-done.9, bf16[2048,1536]{1,0:T(8,128)(2,1)} %get-tuple-element.206.rows_ref, bf16[2048,1280]{1,0:T(8,128)(2,1)S(1)} %copy-done, bf16[2048,1280]{1,0:T(8,128)(2,1)S(1)} %copy-done.2), custom_call_target="tpu_custom_call" | custom-call | flops 3221225472 | bytes 13107200 | tf_op jit(solution)/shard_map/pallas_call | solution.py:653
  348.1 3.6 collective-permute-start.34
  353.1 8.4 %shard_map.391 = (f32[4,2,192,1280]{3,2,1,0:T(8,128)}, bf16[4,2,192,1280]{3,2,1,0:T(8,128)(2,1)}) custom-call(s32[7]{0:T(128)S(1)} %copy-done.9, bf16[2048,1536]{1,0:T(8,128)(2,1)} %get-tuple-element.206.rows_ref, bf16[2048,1280]{1,0:T(8,128)(2,1)S(1)} %copy-done, bf16[2048,1280]{1,0:T(8,128)(2,1)S(1)} %copy-done.2, ...), custom_call_target="tpu_custom_call", output_to_operand_aliasing={{0}: (4, {}), {1}: (5, {})} | custom-call | flops 3221225472 | bytes 13107200 | tf_op jit(solution)/shard_map/pallas_call | solution.py:653
  362.3 8.4 %shard_map.392 = (f32[4,2,192,1280]{3,2,1,0:T(8,128)}, bf16[4,2,192,1280]{3,2,1,0:T(8,128)(2,1)}) custom-call(s32[7]{0:T(128)S(1)} %copy-done.9, bf16[2048,1536]{1,0:T(8,128)(2,1)} %get-tuple-element.206.rows_ref, bf16[2048,1280]{1,0:T(8,128)(2,1)S(1)} %copy-done, bf16[2048,1280]{1,0:T(8,128)(2,1)S(1)} %copy-done.2, ...), custom_call_target="tpu_custom_call", output_to_operand_aliasing={{0}: (4, {}), {1}: (5, {})} | custom-call | flops 3221225472 | bytes 13107200 | tf_op jit(solution)/shard_map/pallas_call | solution.py:653
  370.7 12.1 %collective-permute-done.40 = bf16[128,1536]{1,0:T(8,128)(2,1)S(1)} collective-permute-done((bf16[128,1536]{1,0:T(8,128)(2,1)S(1)}, bf16[128,1536]{1,0:T(8,128)(2,1)S(1)}, u32[]{:S(2)}, u32[]{:S(2)}) %collective-permute-start.40) | collective-permute-done | bytes 393248 | tf_op jit(solution)/shard_map/ppermute | solution.py:183
  383.2 8.4 %shard_map.393 = (f32[4,2,192,1280]{3,2,1,0:T(8,128)}, bf16[4,2,192,1280]{3,2,1,0:T(8,128)(2,1)}) custom-call(s32[7]{0:T(128)S(1)} %copy-done.9, bf16[2048,1536]{1,0:T(8,128)(2,1)} %get-tuple-element.206.rows_ref, bf16[2048,1280]{1,0:T(8,128)(2,1)S(1)} %copy-done, bf16[2048,1280]{1,0:T(8,128)(2,1)S(1)} %copy-done.2, ...), custom_call_target="tpu_custom_call", output_to_operand_aliasing={{0}: (4, {}), {1}: (5, {})} | custom-call | flops 3221225472 | bytes 13107200 | tf_op jit(solution)/shard_map/pallas_call | solution.py:653
  396.7 9.0 %shard_map.394 = (f32[4,2,192,1280]{3,2,1,0:T(8,128)}, bf16[4,2,192,1280]{3,2,1,0:T(8,128)(2,1)}) custom-call(s32[7]{0:T(128)S(1)} %copy-done.9, bf16[2048,1536]{1,0:T(8,128)(2,1)} %get-tuple-element.206.rows_ref, bf16[2048,1280]{1,0:T(8,128)(2,1)S(1)} %copy-done.1, bf16[2048,1280]{1,0:T(8,128)(2,1)S(1)} %copy-done.3, ...), custom_call_target="tpu_custom_call", output_to_operand_aliasing={{0}: (4, {}), {1}: (5, {})} | custom-call | flops 3221225472 | bytes 13107200 | tf_op jit(solution)/shard_map/pallas_call | solution.py:653
  409.2 3.9 collective-permute-done.41
  413.8 3.1 fusion.25
  422.6 2.8 convolution_bitcast_fusion
  426.9 3.7 fusion.36
  433.2 7.4 %add_convert_fusion = bf16[4,2,192,1280]{3,2,1,0:T(8,128)(2,1)} fusion(f32[4,2,192,1280]{3,2,1,0:T(8,128)} %get-tuple-element.209, bf16[4,2,192,1280]{3,2,1,0:T(8,128)(2,1)} %collective-permute-done.42), kind=kLoop, calls=%fused_computation.7 | loop fusion | flops 5898240 | bytes 15728640 | tf_op jit(solution)/shard_map/convert_element_type | solution.py:942
  440.6 5.0 all-to-all-start.1
  445.6 5.3 fusion.103
  451.2 5.7 fusion.1
  458.6 4.7 shard_map.395
  469.2 14.2 %shard_map.397 = (f32[10,64,1536]{2,1,0:T(8,128)S(1)}, f32[10,64,1536]{2,1,0:T(8,128)}) custom-call(s32[7]{0:T(128)S(1)} %copy-done.9, bf16[2048,1536]{1,0:T(8,128)(2,1)} %get-tuple-element.222.grads_ref, bf16[2048,1280]{1,0:T(8,128)(2,1)S(1)} %bitcast.123), custom_call_target="tpu_custom_call" | custom-call | flops 8053063680 | bytes 19398656 | tf_op jit(solution)/shard_map/pallas_call | solution.py:700
  487.1 4.4 all-to-all-done.1.grad_ref
  491.5 24.5 %shard_map.396 = (f32[10,192,1024]{2,1,0:T(8,128)}, f32[10,192,1024]{2,1,0:T(8,128)}, f32[10,192,1024]{2,1,0:T(8,128)}, f32[10,192,1024]{2,1,0:T(8,128)}) custom-call(f32[10,192,1024]{2,1,0:T(8,128)} %w_ref.1, f32[10,192,1024]{2,1,0:T(8,128)} %first_ref.1, f32[10,192,1024]{2,1,0:T(8,128)} %second_ref.1, bf16[4,2,192,1280]{3,2,1,0:T(8,128)(2,1)} %all-to-all-done.1.grad_ref), custom_call_target="tpu_custom_call" | custom-call | flops 39321600 | bytes 58982400 | tf_op jit(solution)/shard_map/pallas_call | solution.py:745
  516.0 3.2 collective-permute-done.47
  519.2 9.5 %collective-permute-done.43 = bf16[288,1536]{1,0:T(8,128)(2,1)} collective-permute-done((bf16[288,1536]{1,0:T(8,128)(2,1)}, bf16[288,1536]{1,0:T(8,128)(2,1)}, u32[]{:S(2)}, u32[]{:S(2)}) %collective-permute-start.43) | collective-permute-done | bytes 884768 | tf_op jit(solution)/shard_map/ppermute | solution.py:158
  528.7 5.1 bitcast_add_fusion
  542.3 3.6 collective-permute-start.54
  545.9 5.8 collective-permute-done.50
  553.1 3.3 collective-permute-done.53
  557.5 4.3 collective-permute-start.55
  563.3 13.1 %multiply_subtract_fusion = (f32[10,64,1536]{2,1,0:T(8,128)}, f32[10,64,1536]{2,1,0:T(8,128)}, f32[10,64,1536]{2,1,0:T(8,128)}, f32[10,64,1536]{2,1,0:T(8,128)}) fusion(f32[10,64,1536]{2,1,0:T(8,128)} %param.31, f32[10,64,1536]{2,1,0:T(8,128)} %param.36, f32[10,64,1536]{2,1,0:T(8,128)} %param.41, f32[10,64,1536]{2,1,0:T(8,128)} %copy-done.6, ...), kind=kLoop, calls=%fused_computation.15 | loop fusion | flops 15728640 | bytes 35389440 | tf_op jit(solution)/shard_map/sub | solution.py:147
  (447 shorter events, 161.1 us)
Async XLA Ops:
  7.2 194.8 %all-gather.2.cloned.1.call-start = ((), (), s32[]{:S(2)}) async-start(), calls=%async_computation.3 | async-start | bytes 8519680 | tf_op jit(solution)/shard_map/all_gather | solution.py:823
  19.3 23.1 %collective-permute-start.12 = (bf16[256,1664]{1,0:T(8,128)(2,1)S(1)}, bf16[256,1664]{1,0:T(8,128)(2,1)}, u32[]{:S(2)}, u32[]{:S(2)}) collective-permute-start(bf16[256,1664]{1,0:T(8,128)(2,1)S(1)} %pad_maximum_fusion.2), channel_id=1, source_target_pairs={{0,8},{4,20},{8,0},{12,28},{16,24},{20,4},{24,16},{28,12},{1,9},{5... | collective-permute-start | bytes 2555912 | tf_op jit(solution)/shard_map/ppermute | solution.py:158
  22.2 15.2 %collective-permute-start.4 = (bf16[144,1536]{1,0:T(8,128)(2,1)}, bf16[144,1536]{1,0:T(8,128)(2,1)S(1)}, u32[]{:S(2)}, u32[]{:S(2)}) collective-permute-start(bf16[144,1536]{1,0:T(8,128)(2,1)} %pad_maximum_fusion.6), channel_id=1, source_target_pairs={{0,1},{1,2},{2,3},{3,0},{4,5},{5,6},{6,7},{7,4},{8,9},{9,10},{10,1... | collective-permute-start | bytes 1327112 | tf_op jit(solution)/shard_map/ppermute | solution.py:183
  23.8 32.9 %collective-permute-start.16 = (s32[1,128]{1,0:T(1,128)S(1)}, s32[1,128]{1,0:T(1,128)S(1)}, u32[]{:S(2)}, u32[]{:S(2)}) collective-permute-start(s32[1,128]{1,0:T(1,128)S(1)} %copy-done.67), channel_id=1, source_target_pairs={{0,4},{4,0},{8,12},{12,8},{16,20},{20,16},{24,28},{28,24},{1,5},{5... | collective-permute-start | bytes 1544 | tf_op jit(solution)/shard_map/ppermute | solution.py:158
  23.8 51.7 %collective-permute-start = (bf16[128,1536]{1,0:T(8,128)(2,1)S(1)}, bf16[128,1536]{1,0:T(8,128)(2,1)}, u32[]{:S(2)}, u32[]{:S(2)}) collective-permute-start(bf16[128,1536]{1,0:T(8,128)(2,1)S(1)} %copy-done.16), channel_id=1, source_target_pairs={{0,4},{4,0},{8,12},{12,8},{16,20},{20,16},{24,28},{28,24},{1,5},{5... | collective-permute-start | bytes 1179656 | tf_op jit(solution)/shard_map/ppermute | solution.py:158
  25.0 21.9 %collective-permute-start.7 = (bf16[144,1536]{1,0:T(8,128)(2,1)}, bf16[144,1536]{1,0:T(8,128)(2,1)}, u32[]{:S(2)}, u32[]{:S(2)}) collective-permute-start(bf16[144,1536]{1,0:T(8,128)(2,1)} %pad_maximum_fusion.6), channel_id=1, source_target_pairs={{0,3},{1,0},{2,1},{3,2},{4,7},{5,4},{6,5},{7,6},{8,11},{9,8},{10,9... | collective-permute-start | bytes 1327112 | tf_op jit(solution)/shard_map/ppermute | solution.py:183
  37.3 16.8 %collective-permute-start.10 = (bf16[144,1536]{1,0:T(8,128)(2,1)S(1)}, bf16[144,1536]{1,0:T(8,128)(2,1)}, u32[]{:S(2)}, u32[]{:S(2)}) collective-permute-start(bf16[144,1536]{1,0:T(8,128)(2,1)S(1)} %collective-permute-done.4), channel_id=1, source_target_pairs={{0,1},{1,2},{2,3},{3,0},{4,5},{5,6},{6,7},{7,4},{8,9},{9,10},{10,1... | collective-permute-start | bytes 1327112 | tf_op jit(solution)/shard_map/ppermute | solution.py:183
  69.7 32.5 %collective-permute-start.15 = (bf16[10,64,1536]{2,1,0:T(8,128)(2,1)S(1)}, bf16[10,64,1536]{2,1,0:T(8,128)(2,1)}, u32[]{:S(2)}, u32[]{:S(2)}) collective-permute-start(bf16[10,64,1536]{2,1,0:T(8,128)(2,1)S(1)} %convert_element_type.295), channel_id=1, source_target_pairs={{0,4},{4,0},{8,12},{12,8},{16,20},{20,16},{24,28},{28,24},{1,5},{5... | collective-permute-start | bytes 5898248 | tf_op jit(solution)/shard_map/ppermute | solution.py:158
  73.9 18.0 %collective-permute-start.9 = (bf16[288,1536]{1,0:T(8,128)(2,1)S(1)}, bf16[288,1536]{1,0:T(8,128)(2,1)}, u32[]{:S(2)}, u32[]{:S(2)}) collective-permute-start(bf16[288,1536]{1,0:T(8,128)(2,1)S(1)} %constant_dynamic-update-slice_fusion.10.refs_4_), channel_id=1, source_target_pairs={{0,8},{4,20},{8,0},{12,28},{16,24},{20,4},{24,16},{28,12},{1,9},{5... | collective-permute-start | bytes 2654216 | tf_op jit(solution)/shard_map/ppermute | solution.py:158
  76.5 30.2 %collective-permute-start.3 = (bf16[288,1536]{1,0:T(8,128)(2,1)S(1)}, bf16[288,1536]{1,0:T(8,128)(2,1)}, u32[]{:S(2)}, u32[]{:S(2)}) collective-permute-start(bf16[288,1536]{1,0:T(8,128)(2,1)S(1)} %pad_maximum_fusion.1.refs_0_), channel_id=1, source_target_pairs={{0,8},{4,20},{8,0},{12,28},{16,24},{20,4},{24,16},{28,12},{1,9},{5... | collective-permute-start | bytes 2654216 | tf_op jit(solution)/shard_map/ppermute | solution.py:158
  78.0 19.0 %collective-permute-start.13 = (bf16[144,1536]{1,0:T(8,128)(2,1)}, bf16[144,1536]{1,0:T(8,128)(2,1)}, u32[]{:S(2)}, u32[]{:S(2)}) collective-permute-start(bf16[144,1536]{1,0:T(8,128)(2,1)} %collective-permute-done.10), channel_id=1, source_target_pairs={{0,16},{4,12},{8,24},{12,4},{16,0},{20,28},{24,8},{28,20},{1,17},{... | collective-permute-start | bytes 1327112 | tf_op jit(solution)/shard_map/ppermute | solution.py:158
  82.8 38.4 %collective-permute-start.6 = (bf16[288,1536]{1,0:T(8,128)(2,1)}, bf16[288,1536]{1,0:T(8,128)(2,1)}, u32[]{:S(2)}, u32[]{:S(2)}) collective-permute-start(bf16[288,1536]{1,0:T(8,128)(2,1)} %constant_dynamic-update-slice_fusion.8.refs_2_), channel_id=1, source_target_pairs={{0,8},{4,20},{8,0},{12,28},{16,24},{20,4},{24,16},{28,12},{1,9},{5... | collective-permute-start | bytes 2654216 | tf_op jit(solution)/shard_map/ppermute | solution.py:158
  91.9 84.3 %all-to-all-start = ((bf16[4,2,192,1280]{3,2,1,0:T(8,128)(2,1)}), bf16[4,2,192,1280]{3,2,1,0:T(8,128)(2,1)}, u32[]{:S(2)}, u32[]{:S(2)}) async-start(bf16[4,2,192,1280]{3,2,1,0:T(8,128)(2,1)} %shard_map.381), calls=%async_computation | async-start | bytes 7864320 | tf_op jit(solution)/shard_map/all_to_all | solution.py:852
  96.7 465.0 %reduce-scatter.2.cloned.1.call-start = ((), (), s32[]{:S(2)}) async-start(), calls=%async_computation.4 | async-start | bytes 7864320 | tf_op jit(solution)/shard_map/reduce_scatter | solution.py:947
  98.8 63.6 %collective-permute-start.14 = (bf16[288,1536]{1,0:T(8,128)(2,1)}, bf16[288,1536]{1,0:T(8,128)(2,1)S(1)}, u32[]{:S(2)}, u32[]{:S(2)}) collective-permute-start(bf16[288,1536]{1,0:T(8,128)(2,1)} %constant_dynamic-update-slice_fusion.12.refs_6_), channel_id=1, source_target_pairs={{0,8},{4,20},{8,0},{12,28},{16,24},{20,4},{24,16},{28,12},{1,9},{5... | collective-permute-start | bytes 2654216 | tf_op jit(solution)/shard_map/ppermute | solution.py:158
  176.2 19.2 %collective-permute-start.20 = (bf16[4,2,192,1280]{3,2,1,0:T(8,128)(2,1)}, bf16[4,2,192,1280]{3,2,1,0:T(8,128)(2,1)}, u32[]{:S(2)}, u32[]{:S(2)}) collective-permute-start(bf16[4,2,192,1280]{3,2,1,0:T(8,128)(2,1)} %all-to-all-done.mine_ref), channel_id=1, source_target_pairs={{0,4},{4,0},{8,12},{12,8},{16,20},{20,16},{24,28},{28,24},{1,5},{5... | collective-permute-start | bytes 11796488 | tf_op jit(solution)/shard_map/ppermute | solution.py:158
  188.1 27.6 %collective-permute-start.30 = (bf16[128,1536]{1,0:T(8,128)(2,1)S(1)}, bf16[128,1536]{1,0:T(8,128)(2,1)}, u32[]{:S(2)}, u32[]{:S(2)}) collective-permute-start(bf16[128,1536]{1,0:T(8,128)(2,1)S(1)} %multiply_convert_fusion.1), channel_id=1, source_target_pairs={{0,3},{1,0},{2,1},{3,2},{4,7},{5,4},{6,5},{7,6},{8,11},{9,8},{10,9... | collective-permute-start | bytes 1179656 | tf_op jit(solution)/shard_map/ppermute | solution.py:183
  189.8 25.9 %collective-permute-start.22 = (bf16[128,1536]{1,0:T(8,128)(2,1)S(1)}, bf16[128,1536]{1,0:T(8,128)(2,1)}, u32[]{:S(2)}, u32[]{:S(2)}) collective-permute-start(bf16[128,1536]{1,0:T(8,128)(2,1)S(1)} %multiply_convert_fusion.1), channel_id=1, source_target_pairs={{0,1},{1,2},{2,3},{3,0},{4,5},{5,6},{6,7},{7,4},{8,9},{9,10},{10,1... | collective-permute-start | bytes 1179656 | tf_op jit(solution)/shard_map/ppermute | solution.py:183
  190.5 33.1 %collective-permute-start.18 = (bf16[128,1536]{1,0:T(8,128)(2,1)S(1)}, bf16[128,1536]{1,0:T(8,128)(2,1)S(1)}, u32[]{:S(2)}, u32[]{:S(2)}) collective-permute-start(bf16[128,1536]{1,0:T(8,128)(2,1)S(1)} %multiply_convert_fusion.1), channel_id=1, source_target_pairs={{0,2},{1,3},{2,0},{3,1},{4,6},{5,7},{6,4},{7,5},{8,10},{9,11},{10,... | collective-permute-start | bytes 1179656 | tf_op jit(solution)/shard_map/ppermute | solution.py:183
  193.9 33.1 %collective-permute-start.24 = (bf16[256,1536]{1,0:T(8,128)(2,1)S(1)}, bf16[256,1536]{1,0:T(8,128)(2,1)S(1)}, u32[]{:S(2)}, u32[]{:S(2)}) collective-permute-start(bf16[256,1536]{1,0:T(8,128)(2,1)S(1)} %pad_maximum_fusion.3.refs_0_), channel_id=1, source_target_pairs={{0,8},{4,20},{8,0},{12,28},{16,24},{20,4},{24,16},{28,12},{1,9},{5... | collective-permute-start | bytes 2359304 | tf_op jit(solution)/shard_map/ppermute | solution.py:158
  223.6 21.2 %collective-permute-start.21 = (bf16[128,1536]{1,0:T(8,128)(2,1)S(1)}, bf16[128,1536]{1,0:T(8,128)(2,1)S(1)}, u32[]{:S(2)}, u32[]{:S(2)}) collective-permute-start(bf16[128,1536]{1,0:T(8,128)(2,1)S(1)} %collective-permute-done.18), channel_id=1, source_target_pairs={{0,16},{4,12},{8,24},{12,4},{16,0},{20,28},{24,8},{28,20},{1,17},{... | collective-permute-start | bytes 1179656 | tf_op jit(solution)/shard_map/ppermute | solution.py:158
  225.0 19.1 %collective-permute-start.23 = (bf16[128,1536]{1,0:T(8,128)(2,1)}, bf16[128,1536]{1,0:T(8,128)(2,1)S(1)}, u32[]{:S(2)}, u32[]{:S(2)}) collective-permute-start(bf16[128,1536]{1,0:T(8,128)(2,1)} %collective-permute-done.22), channel_id=1, source_target_pairs={{0,16},{4,12},{8,24},{12,4},{16,0},{20,28},{24,8},{28,20},{1,17},{... | collective-permute-start | bytes 1179656 | tf_op jit(solution)/shard_map/ppermute | solution.py:158
  225.7 17.0 %collective-permute-start.31 = (bf16[128,1536]{1,0:T(8,128)(2,1)}, bf16[128,1536]{1,0:T(8,128)(2,1)S(1)}, u32[]{:S(2)}, u32[]{:S(2)}) collective-permute-start(bf16[128,1536]{1,0:T(8,128)(2,1)} %collective-permute-done.30), channel_id=1, source_target_pairs={{0,16},{4,12},{8,24},{12,4},{16,0},{20,28},{24,8},{28,20},{1,17},{... | collective-permute-start | bytes 1179656 | tf_op jit(solution)/shard_map/ppermute | solution.py:158
  239.8 19.9 %collective-permute-start.27 = (bf16[256,1536]{1,0:T(8,128)(2,1)S(1)}, bf16[256,1536]{1,0:T(8,128)(2,1)S(1)}, u32[]{:S(2)}, u32[]{:S(2)}) collective-permute-start(bf16[256,1536]{1,0:T(8,128)(2,1)S(1)} %get-tuple-element.170), channel_id=1, source_target_pairs={{0,8},{4,20},{8,0},{12,28},{16,24},{20,4},{24,16},{28,12},{1,9},{5... | collective-permute-start | bytes 2359304 | tf_op jit(solution)/shard_map/ppermute | solution.py:158
  242.7 43.8 %collective-permute-start.32 = (bf16[256,1536]{1,0:T(8,128)(2,1)S(1)}, bf16[256,1536]{1,0:T(8,128)(2,1)S(1)}, u32[]{:S(2)}, u32[]{:S(2)}) collective-permute-start(bf16[256,1536]{1,0:T(8,128)(2,1)S(1)} %constant_dynamic-update-slice_fusion.18.refs_0_), channel_id=1, source_target_pairs={{0,8},{4,20},{8,0},{12,28},{16,24},{20,4},{24,16},{28,12},{1,9},{5... | collective-permute-start | bytes 2359304 | tf_op jit(solution)/shard_map/ppermute | solution.py:158
  244.1 28.8 %collective-permute-start.25 = (bf16[256,1536]{1,0:T(8,128)(2,1)S(1)}, bf16[256,1536]{1,0:T(8,128)(2,1)S(1)}, u32[]{:S(2)}, u32[]{:S(2)}) collective-permute-start(bf16[256,1536]{1,0:T(8,128)(2,1)S(1)} %constant_dynamic-update-slice_fusion.16.refs_0_), channel_id=1, source_target_pairs={{0,8},{4,20},{8,0},{12,28},{16,24},{20,4},{24,16},{28,12},{1,9},{5... | collective-permute-start | bytes 2359304 | tf_op jit(solution)/shard_map/ppermute | solution.py:158
  244.9 65.7 %collective-permute-start.29 = (bf16[256,1536]{1,0:T(8,128)(2,1)S(1)}, bf16[256,1536]{1,0:T(8,128)(2,1)S(1)}, u32[]{:S(2)}, u32[]{:S(2)}) collective-permute-start(bf16[256,1536]{1,0:T(8,128)(2,1)S(1)} %constant_dynamic-update-slice_fusion.14.refs_0_), channel_id=1, source_target_pairs={{0,8},{4,20},{8,0},{12,28},{16,24},{20,4},{24,16},{28,12},{1,9},{5... | collective-permute-start | bytes 2359304 | tf_op jit(solution)/shard_map/ppermute | solution.py:158
  259.9 48.2 %collective-permute-start.28 = (bf16[128,1536]{1,0:T(8,128)(2,1)S(1)}, bf16[128,1536]{1,0:T(8,128)(2,1)S(1)}, u32[]{:S(2)}, u32[]{:S(2)}) collective-permute-start(bf16[128,1536]{1,0:T(8,128)(2,1)S(1)} %slice.523), channel_id=1, source_target_pairs={{0,16},{4,12},{8,24},{12,4},{16,0},{20,28},{24,8},{28,20},{1,17},{... | collective-permute-start | bytes 1179656 | tf_op jit(solution)/shard_map/ppermute | solution.py:158
  285.7 23.9 %collective-permute-start.26 = (bf16[256,1536]{1,0:T(8,128)(2,1)S(1)}, bf16[256,1536]{1,0:T(8,128)(2,1)S(1)}, u32[]{:S(2)}, u32[]{:S(2)}) collective-permute-start(bf16[256,1536]{1,0:T(8,128)(2,1)S(1)} %get-tuple-element.169), channel_id=1, source_target_pairs={{0,8},{4,20},{8,0},{12,28},{16,24},{20,4},{24,16},{28,12},{1,9},{5... | collective-permute-start | bytes 2359304 | tf_op jit(solution)/shard_map/ppermute | solution.py:158
  308.2 24.5 %collective-permute-start.35 = (bf16[256,1536]{1,0:T(8,128)(2,1)S(1)}, bf16[256,1536]{1,0:T(8,128)(2,1)S(1)}, u32[]{:S(2)}, u32[]{:S(2)}) collective-permute-start(bf16[256,1536]{1,0:T(8,128)(2,1)S(1)} %get-tuple-element.188), channel_id=1, source_target_pairs={{0,8},{4,20},{8,0},{12,28},{16,24},{20,4},{24,16},{28,12},{1,9},{5... | collective-permute-start | bytes 2359304 | tf_op jit(solution)/shard_map/ppermute | solution.py:158
  309.8 38.1 %collective-permute-start.33 = (bf16[128,1536]{1,0:T(8,128)(2,1)S(1)}, bf16[128,1536]{1,0:T(8,128)(2,1)S(1)}, u32[]{:S(2)}, u32[]{:S(2)}) collective-permute-start(bf16[128,1536]{1,0:T(8,128)(2,1)S(1)} %slice.522), channel_id=1, source_target_pairs={{0,16},{4,12},{8,24},{12,4},{16,0},{20,28},{24,8},{28,20},{1,17},{... | collective-permute-start | bytes 1179656 | tf_op jit(solution)/shard_map/ppermute | solution.py:158
  332.1 19.6 %collective-permute-start.38 = (bf16[256,1536]{1,0:T(8,128)(2,1)S(1)}, bf16[256,1536]{1,0:T(8,128)(2,1)S(1)}, u32[]{:S(2)}, u32[]{:S(2)}) collective-permute-start(bf16[256,1536]{1,0:T(8,128)(2,1)S(1)} %get-tuple-element.190), channel_id=1, source_target_pairs={{0,8},{4,20},{8,0},{12,28},{16,24},{20,4},{24,16},{28,12},{1,9},{5... | collective-permute-start | bytes 2359304 | tf_op jit(solution)/shard_map/ppermute | solution.py:158
  333.0 18.7 %collective-permute-start.36 = (bf16[128,1536]{1,0:T(8,128)(2,1)S(1)}, bf16[128,1536]{1,0:T(8,128)(2,1)S(1)}, u32[]{:S(2)}, u32[]{:S(2)}) collective-permute-start(bf16[128,1536]{1,0:T(8,128)(2,1)S(1)} %slice.521), channel_id=1, source_target_pairs={{0,16},{4,12},{8,24},{12,4},{16,0},{20,28},{24,8},{28,20},{1,17},{... | collective-permute-start | bytes 1179656 | tf_op jit(solution)/shard_map/ppermute | solution.py:158
  348.1 22.6 %collective-permute-start.34 = (bf16[128,1536]{1,0:T(8,128)(2,1)S(1)}, bf16[128,1536]{1,0:T(8,128)(2,1)S(1)}, u32[]{:S(2)}, u32[]{:S(2)}) collective-permute-start(bf16[128,1536]{1,0:T(8,128)(2,1)S(1)} %fusion.55), channel_id=1, source_target_pairs={{0,3},{1,0},{2,1},{3,2},{4,7},{5,4},{6,5},{7,6},{8,11},{9,8},{10,9... | collective-permute-start | bytes 1179656 | tf_op jit(solution)/shard_map/ppermute | solution.py:183
  352.6 18.1 %collective-permute-start.37 = (bf16[128,1536]{1,0:T(8,128)(2,1)S(1)}, bf16[128,1536]{1,0:T(8,128)(2,1)S(1)}, u32[]{:S(2)}, u32[]{:S(2)}) collective-permute-start(bf16[128,1536]{1,0:T(8,128)(2,1)S(1)} %fusion.54), channel_id=1, source_target_pairs={{0,1},{1,2},{2,3},{3,0},{4,5},{5,6},{6,7},{7,4},{8,9},{9,10},{10,1... | collective-permute-start | bytes 1179656 | tf_op jit(solution)/shard_map/ppermute | solution.py:183
  361.6 21.2 %collective-permute-start.40 = (bf16[128,1536]{1,0:T(8,128)(2,1)S(1)}, bf16[128,1536]{1,0:T(8,128)(2,1)S(1)}, u32[]{:S(2)}, u32[]{:S(2)}) collective-permute-start(bf16[128,1536]{1,0:T(8,128)(2,1)S(1)} %fusion.53), channel_id=1, source_target_pairs={{0,2},{1,3},{2,0},{3,1},{4,6},{5,7},{6,4},{7,5},{8,10},{9,11},{10,... | collective-permute-start | bytes 1179656 | tf_op jit(solution)/shard_map/ppermute | solution.py:183
  405.7 27.5 %collective-permute-start.42 = (bf16[4,2,192,1280]{3,2,1,0:T(8,128)(2,1)}, bf16[4,2,192,1280]{3,2,1,0:T(8,128)(2,1)}, u32[]{:S(2)}, u32[]{:S(2)}) collective-permute-start(bf16[4,2,192,1280]{3,2,1,0:T(8,128)(2,1)} %get-tuple-element.210), channel_id=1, source_target_pairs={{0,4},{4,0},{8,12},{12,8},{16,20},{20,16},{24,28},{28,24},{1,5},{5... | collective-permute-start | bytes 11796488 | tf_op jit(solution)/shard_map/ppermute | solution.py:158
  440.6 50.9 %all-to-all-start.1 = ((bf16[4,2,192,1280]{3,2,1,0:T(8,128)(2,1)}), bf16[4,2,192,1280]{3,2,1,0:T(8,128)(2,1)}, u32[]{:S(2)}, u32[]{:S(2)}) async-start(bf16[4,2,192,1280]{3,2,1,0:T(8,128)(2,1)} %add_convert_fusion), calls=%async_computation.2 | async-start | bytes 7864320 | tf_op jit(solution)/shard_map/all_to_all | solution.py:944
  457.4 27.9 %collective-permute-start.57 = (f32[128,1536]{1,0:T(8,128)S(1)}, f32[128,1536]{1,0:T(8,128)}, u32[]{:S(2)}, u32[]{:S(2)}) collective-permute-start(f32[128,1536]{1,0:T(8,128)S(1)} %slice.393), channel_id=1, source_target_pairs={{0,4},{4,0},{8,12},{12,8},{16,20},{20,16},{24,28},{28,24},{1,5},{5... | collective-permute-start | bytes 2359304 | tf_op jit(solution)/shard_map/ppermute | solution.py:158
  465.1 50.9 %collective-permute-start.52 = (bf16[288,1536]{1,0:T(8,128)(2,1)}, bf16[288,1536]{1,0:T(8,128)(2,1)}, u32[]{:S(2)}, u32[]{:S(2)}) collective-permute-start(bf16[288,1536]{1,0:T(8,128)(2,1)} %get-tuple-element.355), channel_id=1, source_target_pairs={{0,8},{4,20},{8,0},{12,28},{16,24},{20,4},{24,16},{28,12},{1,9},{5... | collective-permute-start | bytes 2654216 | tf_op jit(solution)/shard_map/ppermute | solution.py:158
  467.1 48.9 %collective-permute-start.49 = (bf16[288,1536]{1,0:T(8,128)(2,1)}, bf16[288,1536]{1,0:T(8,128)(2,1)}, u32[]{:S(2)}, u32[]{:S(2)}) collective-permute-start(bf16[288,1536]{1,0:T(8,128)(2,1)} %get-tuple-element.356), channel_id=1, source_target_pairs={{0,8},{4,20},{8,0},{12,28},{16,24},{20,4},{24,16},{28,12},{1,9},{5... | collective-permute-start | bytes 2654216 | tf_op jit(solution)/shard_map/ppermute | solution.py:158
  467.1 52.1 %collective-permute-start.47 = (bf16[288,1536]{1,0:T(8,128)(2,1)}, bf16[288,1536]{1,0:T(8,128)(2,1)}, u32[]{:S(2)}, u32[]{:S(2)}) collective-permute-start(bf16[288,1536]{1,0:T(8,128)(2,1)} %get-tuple-element.357), channel_id=1, source_target_pairs={{0,8},{4,20},{8,0},{12,28},{16,24},{20,4},{24,16},{28,12},{1,9},{5... | collective-permute-start | bytes 2654216 | tf_op jit(solution)/shard_map/ppermute | solution.py:158
  469.1 59.6 %collective-permute-start.43 = (bf16[288,1536]{1,0:T(8,128)(2,1)}, bf16[288,1536]{1,0:T(8,128)(2,1)}, u32[]{:S(2)}, u32[]{:S(2)}) collective-permute-start(bf16[288,1536]{1,0:T(8,128)(2,1)} %get-tuple-element.358), channel_id=1, source_target_pairs={{0,8},{4,20},{8,0},{12,28},{16,24},{20,4},{24,16},{28,12},{1,9},{5... | collective-permute-start | bytes 2654216 | tf_op jit(solution)/shard_map/ppermute | solution.py:158
  485.3 77.9 %collective-permute-start.56 = (f32[10,64,1536]{2,1,0:T(8,128)}, f32[10,64,1536]{2,1,0:T(8,128)}, u32[]{:S(2)}, u32[]{:S(2)}) collective-permute-start(f32[10,64,1536]{2,1,0:T(8,128)} %get-tuple-element.225), channel_id=1, source_target_pairs={{0,4},{4,0},{8,12},{12,8},{16,20},{20,16},{24,28},{28,24},{1,5},{5... | collective-permute-start | bytes 11796488 | tf_op jit(solution)/shard_map/ppermute | solution.py:158
  540.2 16.3 %collective-permute-start.53 = (bf16[144,1536]{1,0:T(8,128)(2,1)S(1)}, bf16[144,1536]{1,0:T(8,128)(2,1)S(1)}, u32[]{:S(2)}, u32[]{:S(2)}) collective-permute-start(bf16[144,1536]{1,0:T(8,128)(2,1)S(1)} %slice.515), channel_id=1, source_target_pairs={{0,16},{4,12},{8,24},{12,4},{16,0},{20,28},{24,8},{28,20},{1,17},{... | collective-permute-start | bytes 1327112 | tf_op jit(solution)/shard_map/ppermute | solution.py:158
  551.8 25.6 %collective-permute-start.51 = (bf16[144,1536]{1,0:T(8,128)(2,1)S(1)}, bf16[144,1536]{1,0:T(8,128)(2,1)}, u32[]{:S(2)}, u32[]{:S(2)}) collective-permute-start(bf16[144,1536]{1,0:T(8,128)(2,1)S(1)} %fusion.42), channel_id=1, source_target_pairs={{0,1},{1,2},{2,3},{3,0},{4,5},{5,6},{6,7},{7,4},{8,9},{9,10},{10,1... | collective-permute-start | bytes 1327112 | tf_op jit(solution)/shard_map/ppermute | solution.py:183
  557.5 19.9 %collective-permute-start.55 = (bf16[144,1536]{1,0:T(8,128)(2,1)}, bf16[144,1536]{1,0:T(8,128)(2,1)}, u32[]{:S(2)}, u32[]{:S(2)}) collective-permute-start(bf16[144,1536]{1,0:T(8,128)(2,1)} %fusion.41), channel_id=1, source_target_pairs={{0,3},{1,0},{2,1},{3,2},{4,7},{5,4},{6,5},{7,6},{8,11},{9,8},{10,9... | collective-permute-start | bytes 1327112 | tf_op jit(solution)/shard_map/ppermute | solution.py:183
  579.4 15.6 %collective-permute-start.46 = (bf16[128,1536]{1,0:T(8,128)(2,1)}, bf16[128,1536]{1,0:T(8,128)(2,1)}, u32[]{:S(2)}, u32[]{:S(2)}) collective-permute-start(bf16[128,1536]{1,0:T(8,128)(2,1)} %slice.519), channel_id=1, source_target_pairs={{0,16},{4,12},{8,24},{12,4},{16,0},{20,28},{24,8},{28,20},{1,17},{... | collective-permute-start | bytes 1179656 | tf_op jit(solution)/shard_map/ppermute | solution.py:158
  (86 other events, 1100.7 us)
Sparse Core Ops, SparseCore 0:
  54.3 122.3 all-gather.1
  391.8 110.0 reduce-scatter.1

commit v5 on v4

--- a/solution.py
+++ b/solution.py
@@ -185,11 +185,6 @@
 
 def after(values, *others):
     return lax.optimization_barrier((values, others))[0]
-
-
-def start_ring(block):
-    ahead, behind = turn(block, 1), turn(block, -1)
-    return [block, ahead, behind, turn(ahead, 1)]
 
 
 def along_first(part):
@@ -665,7 +660,7 @@
             jax.ShapeDtypeStruct(shape, jnp.bfloat16),
         ],
         input_output_aliases={4 + i: i for i in range(len(filled))},
-        compiler_params=pltpu.CompilerParams(vmem_limit_bytes=36 * 1024 * 1024),
+        compiler_params=pltpu.CompilerParams(vmem_limit_bytes=56 * 1024 * 1024),
         cost_estimate=pl.CostEstimate(
             flops=4 * tokens * width * columns,
             bytes_accessed=2 * tokens * (width + 2 * columns) + 6 * 2 * width * columns,
@@ -807,9 +802,10 @@
         0,
     )
     share = local_experts * (FF // chips)
-    attention_ring = start_ring(block)
+    ahead, behind = turn(block, 1), turn(block, -1)
+    pieces = spread_columns(after(w_gate_up, taken), chips)
+    attention_ring = [block, ahead, behind, turn(after(ahead, pieces), 1)]
     attention_pairs = [along_first(part) for part in attention_ring[:2]]
-    pieces = spread_columns(after(w_gate_up, taken), chips)
     routes = jnp.concatenate([expert_ids.astype(NARROW)] + split_three(route_weights), 1)
     cotangent_rows = jnp.concatenate(
         [
@@ -824,7 +820,7 @@
         after(cotangent_here, attention_ring), "expert", axis=0, tiled=True
     )
     attention_pairs.append(along_first(attention_ring[2]))
-    attention_pairs.append(along_first(after(attention_ring[3], (pieces, cotangent_here))))
+    attention_pairs.append(along_first(after(attention_ring[3], cotangent_here)))
     attention_blocks = [(pair, swap_second(pair)) for pair in attention_pairs]
 
     sources = jnp.asarray(gathered_sources(count_dp, count_expert))[place_dp, place_expert]
@@ -850,7 +846,7 @@
     )
     parities = [list(range(i, count_dp, 2)) for i in range(2)]
     pieces = lax.all_to_all(
-        after(pieces, attention_blocks[2][1]), "dp", 0, 0, axis_index_groups=parities, tiled=True
+        pieces, "dp", 0, 0, axis_index_groups=parities, tiled=True
     )
     down_mine = after(w_down, attention_pairs[0]).astype(NARROW)
     down_theirs = swap_core(down_mine)
@@ -859,7 +855,7 @@
         jnp.concatenate([down_mine, down_theirs], 1),
         jnp.concatenate([down_theirs, down_mine], 1),
     ).reshape(share, MODEL_WIDTH)
-    attention_blocks = after(attention_blocks, down_w)
+    attention_blocks = after(attention_blocks, (down_w, pieces))
 
     cosine_table, sine_table = rotary_tables(sequence_length, HEAD_SIZE // 2)
     inputs = tokens.astype(WIDE)

time: 612 us -> 598 us (0.977)
  local copies, waits for them, and re-layouts: 49.8 us -> 38.5 us
    ppermute x47, waiting for transfers between devices: 111 us -> 123 us  [swap(): return lax.ppermute(rows, 'dp', [(i, i ^ pick(i)) for i in range(count)])]
    unnamed x161 -> x155, local copies, waits for them, and re-layouts: 25 us -> 15.4 us
    ppermute x12, waiting for transfers between devices: 39.5 us -> 30.1 us  [turn(): lax.ppermute(rows, 'expert', [(i, (i + step) % count) for i in range(coun...]
  transfers between devices with their start and end apart: 63 -> 63, of which waited for: 23 -> 23; matrix products, arithmetic and copies ran while one was open for 21% -> 20% of each run, Pallas kernels for 32% -> 33%
where the time goes in v5:
time: 598 us; the launch traced here: 592 us
  Pallas kernels  206 us (34%)
  waiting for transfers between devices  158 us (26%)
  starting transfers between devices  76.3 us (13%)
  other arithmetic  63.1 us (11%)
  local copies, waits for them, and re-layouts  38.5 us (6%)
  matrix products  33.6 us (6%)
  between operations  16.3 us (3%)
    ppermute x47, waiting for transfers between devices, swap(): return lax.ppermute(rows, 'dp', [(i, i ^ pick(i)) for i in range(count)])  123 us
    pallas_call x6, Pallas kernels, expert_block(): pl.pallas_call(functools.partial(expert_kernel, per_step=per_step, count=...  95.7 us
    pallas_call x5, Pallas kernels, column_grads(): pl.pallas_call(column_grads_kernel, grid_spec=pltpu.PrefetchScalarGridSpe...  45.9 us
    ppermute x47, starting transfers between devices, swap(): return lax.ppermute(rows, 'dp', [(i, i ^ pick(i)) for i in range(count)])  44.3 us
    ppermute x12, waiting for transfers between devices, turn(): lax.ppermute(rows, 'expert', [(i, (i + step) % count) for i in range(coun...  30.1 us
    pallas_call x1, Pallas kernels, adam_columns(): pl.pallas_call(adam_columns_kernel, grid=(experts,), in_specs=[block] * 3...  24.5 us
    ppermute x12, starting transfers between devices, turn(): lax.ppermute(rows, 'expert', [(i, (i + step) % count) for i in range(coun...  21.6 us
    sub x4, other arithmetic, adam_step(): return (weight - step_rate * (update + shrink * weight), first, second)  16.9 us
  transfers between devices with their start and end apart: 63, of which 23 were waited for; matrix products, arithmetic and copies ran while one was open for 20% of the time, Pallas kernels for 33%

profile of v5, /device:TPU:0, one launch (start us, length us, event | category | flops | bytes accessed | tf_op | source)
XLA Modules:
  0.0 591.6 jit_solution(1186449527585744242)
XLA Ops:
  27.3 8.2 %shard_map.381 = bf16[4,2,192,1280]{3,2,1,0:T(8,128)(2,1)} custom-call(f32[10,192,1024]{2,1,0:T(8,128)} %w_ref.1), custom_call_target="tpu_custom_call" | custom-call | bytes 11796480 | tf_op jit(solution)/shard_map/pallas_call | solution.py:333
  40.0 6.9 %collective-permute-done.7 = bf16[144,1536]{1,0:T(8,128)(2,1)} collective-permute-done((bf16[144,1536]{1,0:T(8,128)(2,1)}, bf16[144,1536]{1,0:T(8,128)(2,1)}, u32[]{:S(2)}, u32[]{:S(2)}) %collective-permute-start.7) | collective-permute-done | bytes 442400 | tf_op jit(solution)/shard_map/ppermute | solution.py:183
  46.8 7.3 %collective-permute-done.10 = bf16[144,1536]{1,0:T(8,128)(2,1)} collective-permute-done((bf16[144,1536]{1,0:T(8,128)(2,1)}, bf16[144,1536]{1,0:T(8,128)(2,1)}, u32[]{:S(2)}, u32[]{:S(2)}) %collective-permute-start.10) | collective-permute-done | bytes 442400 | tf_op jit(solution)/shard_map/ppermute | solution.py:183
  56.0 4.9 all-to-all-start
  61.3 25.3 %collective-permute-done.2 = bf16[144,1536]{1,0:T(8,128)(2,1)S(1)} collective-permute-done((bf16[144,1536]{1,0:T(8,128)(2,1)}, bf16[144,1536]{1,0:T(8,128)(2,1)S(1)}, u32[]{:S(2)}, u32[]{:S(2)}) %collective-permute-start.2) | collective-permute-done | bytes 442400 | tf_op jit(solution)/shard_map/ppermute | solution.py:158
  94.8 22.4 %collective-permute-done.8 = bf16[144,1536]{1,0:T(8,128)(2,1)S(1)} collective-permute-done((bf16[144,1536]{1,0:T(8,128)(2,1)}, bf16[144,1536]{1,0:T(8,128)(2,1)S(1)}, u32[]{:S(2)}, u32[]{:S(2)}) %collective-permute-start.8) | collective-permute-done | bytes 442400 | tf_op jit(solution)/shard_map/ppermute | solution.py:158
  119.2 7.4 %collective-permute-done.5 = bf16[144,1536]{1,0:T(8,128)(2,1)S(1)} collective-permute-done((bf16[144,1536]{1,0:T(8,128)(2,1)}, bf16[144,1536]{1,0:T(8,128)(2,1)S(1)}, u32[]{:S(2)}, u32[]{:S(2)}) %collective-permute-start.5) | collective-permute-done | bytes 442400 | tf_op jit(solution)/shard_map/ppermute | solution.py:158
  129.3 6.8 %collective-permute-done.13 = bf16[144,1536]{1,0:T(8,128)(2,1)S(1)} collective-permute-done((bf16[144,1536]{1,0:T(8,128)(2,1)}, bf16[144,1536]{1,0:T(8,128)(2,1)S(1)}, u32[]{:S(2)}, u32[]{:S(2)}) %collective-permute-start.13) | collective-permute-done | bytes 442400 | tf_op jit(solution)/shard_map/ppermute | solution.py:158
  140.6 6.2 %collective-permute-done.6.refs_3_ = bf16[288,1536]{1,0:T(8,128)(2,1)S(1)} collective-permute-done((bf16[288,1536]{1,0:T(8,128)(2,1)S(1)}, bf16[288,1536]{1,0:T(8,128)(2,1)S(1)}, u32[]{:S(2)}, u32[]{:S(2)}) %collective-permute-start.6) | collective-permute-done | bytes 884768 | tf_op jit(solution)/shard_map/ppermute | solution.py:158
  147.7 8.7 %collective-permute-done.14.refs_7_ = bf16[288,1536]{1,0:T(8,128)(2,1)} collective-permute-done((bf16[288,1536]{1,0:T(8,128)(2,1)S(1)}, bf16[288,1536]{1,0:T(8,128)(2,1)}, u32[]{:S(2)}, u32[]{:S(2)}) %collective-permute-start.14) | collective-permute-done | bytes 884768 | tf_op jit(solution)/shard_map/ppermute | solution.py:158
  156.4 6.3 %shard_map.382 = (bf16[1536,1280]{1,0:T(8,128)(2,1)}, bf16[1536,128]{1,0:T(8,128)(2,1)}, bf16[768,1536]{1,0:T(8,128)(2,1)}) custom-call(bf16[288,1536]{1,0:T(8,128)(2,1)} %copy-done.18, bf16[288,1536]{1,0:T(8,128)(2,1)} %copy-done.33, bf16[288,1536]{1,0:T(8,128)(2,1)} %copy-done.22, bf16[288,1536]{1,0:T(8,128)(2,1)} %copy-done.35, ...), custom_call_target="tpu_custom_call" | custom-call | bytes 14155776 | tf_op jit(solution)/shard_map/pallas_call | solution.py:416
  163.9 3.3 multiply_convert_fusion
  184.3 3.6 collective-permute-done.19
  189.5 6.6 %shard_map.383 = (bf16[1536,1280]{1,0:T(8,128)(2,1)}, bf16[1536,1280]{1,0:T(8,128)(2,1)}) custom-call(s32[7]{0:T(128)} %pad_add_fusion.1.place_ref, bf16[4,2,192,1280]{3,2,1,0:T(8,128)(2,1)} %all-to-all-done.mine_ref, bf16[4,2,192,1280]{3,2,1,0:T(8,128)(2,1)} %collective-permute-done.20.theirs_ref), custom_call_target="tpu_custom_call" | custom-call | bytes 15728640 | tf_op jit(solution)/shard_map/pallas_call | solution.py:369
  196.1 13.7 %shard_map.384 = (f32[256,1536]{1,0:T(8,128)S(1)}, bf16[2048,1280]{1,0:T(8,128)(2,1)}, bf16[2048,1280]{1,0:T(8,128)(2,1)}, bf16[2048,1280]{1,0:T(8,128)(2,1)}, b...) custom-call(s32[7]{0:T(128)S(1)} %copy-done.5, ...), custom_call_target="tpu_custom_call" | custom-call | flops 6039797760 | bytes 23199744 | tf_op jit(solution)/shard_map/pallas_call | solution.py:586
  209.8 7.9 %collective-permute-done.18 = bf16[128,1536]{1,0:T(8,128)(2,1)} collective-permute-done((bf16[128,1536]{1,0:T(8,128)(2,1)S(1)}, bf16[128,1536]{1,0:T(8,128)(2,1)}, u32[]{:S(2)}, u32[]{:S(2)}) %collective-permute-start.18) | collective-permute-done | bytes 393248 | tf_op jit(solution)/shard_map/ppermute | solution.py:183
  221.4 12.8 %shard_map.385 = (bf16[256,1536]{1,0:T(8,128)(2,1)S(1)}, bf16[2048,1280]{1,0:T(8,128)(2,1)}, bf16[2048,1280]{1,0:T(8,128)(2,1)}, bf16[2048,1280]{1,0:T(8,128)(2,...) custom-call(s32[7]{0:T(128)S(1)} %copy-done.5, ...), custom_call_target="tpu_custom_call", output_to_operand_aliasing={{1}: (6, {}), {2}: (7, {}), {3}: (8, {}), {4}: (9, {}), {5}... | custom-call | flops 6039797760 | bytes 23199744 | tf_op jit(solution)/shard_map/pallas_call | solution.py:586
  240.7 13.4 %shard_map.386 = (f32[256,1536]{1,0:T(8,128)S(1)}, bf16[2048,1280]{1,0:T(8,128)(2,1)}, bf16[2048,1280]{1,0:T(8,128)(2,1)}, bf16[2048,1280]{1,0:T(8,128)(2,1)}, b...) custom-call(s32[7]{0:T(128)S(1)} %copy-done.5, ...), custom_call_target="tpu_custom_call", output_to_operand_aliasing={{1}: (6, {}), {2}: (7, {}), {3}: (8, {}), {4}: (9, {}), {5}... | custom-call | flops 6039797760 | bytes 23199744 | tf_op jit(solution)/shard_map/pallas_call | solution.py:586
  255.7 11.6 %collective-permute-done.25.refs_0_ = bf16[256,1536]{1,0:T(8,128)(2,1)S(1)} collective-permute-done((bf16[256,1536]{1,0:T(8,128)(2,1)S(1)}, bf16[256,1536]{1,0:T(8,128)(2,1)S(1)}, u32[]{:S(2)}, u32[]{:S(2)}) %collective-permute-start.25) | collective-permute-done | bytes 786464 | tf_op jit(solution)/shard_map/ppermute | solution.py:158
  267.3 12.7 %shard_map.387 = (bf16[256,1536]{1,0:T(8,128)(2,1)S(1)}, bf16[2048,1280]{1,0:T(8,128)(2,1)}, bf16[2048,1280]{1,0:T(8,128)(2,1)}, bf16[2048,1280]{1,0:T(8,128)(2,...) custom-call(s32[7]{0:T(128)S(1)} %copy-done.5, ...), custom_call_target="tpu_custom_call", output_to_operand_aliasing={{1}: (6, {}), {2}: (7, {}), {3}: (8, {}), {4}: (9, {}), {5}... | custom-call | flops 6039797760 | bytes 23199744 | tf_op jit(solution)/shard_map/pallas_call | solution.py:586
  281.0 21.7 %shard_map.388 = (f32[256,1536]{1,0:T(8,128)S(1)}, bf16[256,1536]{1,0:T(8,128)(2,1)S(1)}, bf16[2048,1280]{1,0:T(8,128)(2,1)}, bf16[2048,1280]{1,0:T(8,128)(2,1)}...) custom-call(s32[7]{0:T(128)S(1)} %copy-done.5, ...), custom_call_target="tpu_custom_call", output_to_operand_aliasing={{2}: (7, {}), {3}: (8, {}), {4}: (9, {}), {5}: (10, {}), {6... | custom-call | flops 12079595520 | bytes 34603008 | tf_op jit(solution)/shard_map/pallas_call | solution.py:586
  305.6 21.6 %shard_map.389 = (f32[256,1536]{1,0:T(8,128)S(1)}, bf16[256,1536]{1,0:T(8,128)(2,1)S(1)}, bf16[2048,1280]{1,0:T(8,128)(2,1)}, bf16[2048,1280]{1,0:T(8,128)(2,1)}...) custom-call(s32[7]{0:T(128)S(1)} %copy-done.5, ...), custom_call_target="tpu_custom_call", output_to_operand_aliasing={{2}: (7, {}), {3}: (8, {}), {4}: (9, {}), {5}: (10, {}), {6... | custom-call | flops 12079595520 | bytes 34603008 | tf_op jit(solution)/shard_map/pallas_call | solution.py:586
  329.8 9.1 %shard_map.390 = (f32[4,2,192,1280]{3,2,1,0:T(8,128)}, bf16[4,2,192,1280]{3,2,1,0:T(8,128)(2,1)}) custom-call(s32[7]{0:T(128)} %pad_add_fusion.1.place_ref, bf16[2048,1536]{1,0:T(8,128)(2,1)} %get-tuple-element.206.rows_ref, bf16[2048,1280]{1,0:T(8,128)(2,1)} %get-tuple-element.192.grad_gate_ref, bf16[2048,1280]{1,0:T(8,128)(2,1)} %get-tuple-element.193.grad_upper_ref), custom_call_target="tpu_custom_call" | custom-call | flops 3221225472 | bytes 13107200 | tf_op jit(solution)/shard_map/pallas_call | solution.py:648
  340.0 3.2 collective-permute-start.34
  346.6 9.1 %shard_map.391 = (f32[4,2,192,1280]{3,2,1,0:T(8,128)}, bf16[4,2,192,1280]{3,2,1,0:T(8,128)(2,1)}) custom-call(s32[7]{0:T(128)} %pad_add_fusion.1.place_ref, bf16[2048,1536]{1,0:T(8,128)(2,1)} %get-tuple-element.206.rows_ref, bf16[2048,1280]{1,0:T(8,128)(2,1)} %get-tuple-element.192.grad_gate_ref, ...), custom_call_target="tpu_custom_call", output_to_operand_aliasing={{0}: (4, {}), {1}: (5, {})} | custom-call | flops 3221225472 | bytes 13107200 | tf_op jit(solution)/shard_map/pallas_call | solution.py:648
  355.8 3.2 collective-permute-start.40
  359.0 9.1 %shard_map.392 = (f32[4,2,192,1280]{3,2,1,0:T(8,128)}, bf16[4,2,192,1280]{3,2,1,0:T(8,128)(2,1)}) custom-call(s32[7]{0:T(128)} %pad_add_fusion.1.place_ref, bf16[2048,1536]{1,0:T(8,128)(2,1)} %get-tuple-element.206.rows_ref, bf16[2048,1280]{1,0:T(8,128)(2,1)} %get-tuple-element.192.grad_gate_ref, ...), custom_call_target="tpu_custom_call", output_to_operand_aliasing={{0}: (4, {}), {1}: (5, {})} | custom-call | flops 3221225472 | bytes 13107200 | tf_op jit(solution)/shard_map/pallas_call | solution.py:648
  368.1 6.1 %collective-permute-done.40 = bf16[128,1536]{1,0:T(8,128)(2,1)S(1)} collective-permute-done((bf16[128,1536]{1,0:T(8,128)(2,1)S(1)}, bf16[128,1536]{1,0:T(8,128)(2,1)S(1)}, u32[]{:S(2)}, u32[]{:S(2)}) %collective-permute-start.40) | collective-permute-done | bytes 393248 | tf_op jit(solution)/shard_map/ppermute | solution.py:183
  375.7 9.1 %shard_map.393 = (f32[4,2,192,1280]{3,2,1,0:T(8,128)}, bf16[4,2,192,1280]{3,2,1,0:T(8,128)(2,1)}) custom-call(s32[7]{0:T(128)} %pad_add_fusion.1.place_ref, bf16[2048,1536]{1,0:T(8,128)(2,1)} %get-tuple-element.206.rows_ref, bf16[2048,1280]{1,0:T(8,128)(2,1)} %get-tuple-element.192.grad_gate_ref, ...), custom_call_target="tpu_custom_call", output_to_operand_aliasing={{0}: (4, {}), {1}: (5, {})} | custom-call | flops 3221225472 | bytes 13107200 | tf_op jit(solution)/shard_map/pallas_call | solution.py:648
  384.9 9.4 %shard_map.394 = (f32[4,2,192,1280]{3,2,1,0:T(8,128)}, bf16[4,2,192,1280]{3,2,1,0:T(8,128)(2,1)}) custom-call(s32[7]{0:T(128)} %pad_add_fusion.1.place_ref, bf16[2048,1536]{1,0:T(8,128)(2,1)} %get-tuple-element.206.rows_ref, bf16[2048,1280]{1,0:T(8,128)(2,1)} %get-tuple-element.192.grad_gate_ref, ...), custom_call_target="tpu_custom_call", output_to_operand_aliasing={{0}: (4, {}), {1}: (5, {})} | custom-call | flops 3221225472 | bytes 13107200 | tf_op jit(solution)/shard_map/pallas_call | solution.py:648
  398.4 3.3 collective-permute-done.41
  402.4 3.1 fusion.25
  420.9 7.2 %add_convert_fusion = bf16[4,2,192,1280]{3,2,1,0:T(8,128)(2,1)} fusion(f32[4,2,192,1280]{3,2,1,0:T(8,128)} %get-tuple-element.209, bf16[4,2,192,1280]{3,2,1,0:T(8,128)(2,1)} %collective-permute-done.42), kind=kLoop, calls=%fused_computation.7 | loop fusion | flops 5898240 | bytes 15728640 | tf_op jit(solution)/shard_map/convert_element_type | solution.py:938
  428.1 5.2 all-to-all-start.1
  433.3 5.4 fusion.103
  439.1 5.7 fusion.1
  446.4 4.8 shard_map.395
  457.3 14.2 %shard_map.397 = (f32[10,64,1536]{2,1,0:T(8,128)S(1)}, f32[10,64,1536]{2,1,0:T(8,128)}) custom-call(s32[7]{0:T(128)S(1)} %copy-done.6, bf16[2048,1536]{1,0:T(8,128)(2,1)} %get-tuple-element.222.grads_ref, bf16[2048,1280]{1,0:T(8,128)(2,1)S(1)} %bitcast.123), custom_call_target="tpu_custom_call" | custom-call | flops 8053063680 | bytes 19398656 | tf_op jit(solution)/shard_map/pallas_call | solution.py:695
  475.1 4.1 all-to-all-done.1.grad_ref
  479.2 24.5 %shard_map.396 = (f32[10,192,1024]{2,1,0:T(8,128)}, f32[10,192,1024]{2,1,0:T(8,128)}, f32[10,192,1024]{2,1,0:T(8,128)}, f32[10,192,1024]{2,1,0:T(8,128)}) custom-call(f32[10,192,1024]{2,1,0:T(8,128)} %w_ref.1, f32[10,192,1024]{2,1,0:T(8,128)} %first_ref.1, f32[10,192,1024]{2,1,0:T(8,128)} %second_ref.1, bf16[4,2,192,1280]{3,2,1,0:T(8,128)(2,1)} %all-to-all-done.1.grad_ref), custom_call_target="tpu_custom_call" | custom-call | flops 39321600 | bytes 58982400 | tf_op jit(solution)/shard_map/pallas_call | solution.py:740
  503.8 3.1 collective-permute-done.47
  506.9 9.5 %collective-permute-done.43 = bf16[288,1536]{1,0:T(8,128)(2,1)} collective-permute-done((bf16[288,1536]{1,0:T(8,128)(2,1)}, bf16[288,1536]{1,0:T(8,128)(2,1)}, u32[]{:S(2)}, u32[]{:S(2)}) %collective-permute-start.43) | collective-permute-done | bytes 884768 | tf_op jit(solution)/shard_map/ppermute | solution.py:158
  516.4 5.1 bitcast_add_fusion
  530.0 3.2 collective-permute-start.54
  533.2 6.2 %collective-permute-done.50 = bf16[144,1536]{1,0:T(8,128)(2,1)S(1)} collective-permute-done((bf16[144,1536]{1,0:T(8,128)(2,1)S(1)}, bf16[144,1536]{1,0:T(8,128)(2,1)S(1)}, u32[]{:S(2)}, u32[]{:S(2)}) %collective-permute-start.50) | collective-permute-done | bytes 442400 | tf_op jit(solution)/shard_map/ppermute | solution.py:158
  540.0 4.1 collective-permute-done.53
  545.1 4.0 collective-permute-start.55
  550.6 13.1 %multiply_subtract_fusion = (f32[10,64,1536]{2,1,0:T(8,128)}, f32[10,64,1536]{2,1,0:T(8,128)}, f32[10,64,1536]{2,1,0:T(8,128)}, f32[10,64,1536]{2,1,0:T(8,128)}) fusion(f32[10,64,1536]{2,1,0:T(8,128)} %param.31, f32[10,64,1536]{2,1,0:T(8,128)} %param.36, f32[10,64,1536]{2,1,0:T(8,128)} %param.41, f32[10,64,1536]{2,1,0:T(8,128)} %copy-done.2, ...), kind=kLoop, calls=%fused_computation.15 | loop fusion | flops 15728640 | bytes 35389440 | tf_op jit(solution)/shard_map/sub | solution.py:147
  (441 shorter events, 152.0 us)
Async XLA Ops:
  7.2 188.9 %all-gather.2.cloned.1.call-start = ((), (), s32[]{:S(2)}) async-start(), calls=%async_computation.3 | async-start | bytes 8519680 | tf_op jit(solution)/shard_map/all_gather | solution.py:819
  19.3 18.2 %collective-permute-start.12 = (bf16[256,1664]{1,0:T(8,128)(2,1)S(1)}, bf16[256,1664]{1,0:T(8,128)(2,1)}, u32[]{:S(2)}, u32[]{:S(2)}) collective-permute-start(bf16[256,1664]{1,0:T(8,128)(2,1)S(1)} %pad_maximum_fusion.2), channel_id=1, source_target_pairs={{0,8},{4,20},{8,0},{12,28},{16,24},{20,4},{24,16},{28,12},{1,9},{5... | collective-permute-start | bytes 2555912 | tf_op jit(solution)/shard_map/ppermute | solution.py:158
  23.8 32.2 %collective-permute-start.16 = (s32[1,128]{1,0:T(1,128)S(1)}, s32[1,128]{1,0:T(1,128)S(1)}, u32[]{:S(2)}, u32[]{:S(2)}) collective-permute-start(s32[1,128]{1,0:T(1,128)S(1)} %copy-done.64), channel_id=1, source_target_pairs={{0,4},{4,0},{8,12},{12,8},{16,20},{20,16},{24,28},{28,24},{1,5},{5... | collective-permute-start | bytes 1544 | tf_op jit(solution)/shard_map/ppermute | solution.py:158
  23.8 65.7 %collective-permute-start = (bf16[128,1536]{1,0:T(8,128)(2,1)S(1)}, bf16[128,1536]{1,0:T(8,128)(2,1)}, u32[]{:S(2)}, u32[]{:S(2)}) collective-permute-start(bf16[128,1536]{1,0:T(8,128)(2,1)S(1)} %copy-done.13), channel_id=1, source_target_pairs={{0,4},{4,0},{8,12},{12,8},{16,20},{20,16},{24,28},{28,24},{1,5},{5... | collective-permute-start | bytes 1179656 | tf_op jit(solution)/shard_map/ppermute | solution.py:158
  25.0 21.9 %collective-permute-start.7 = (bf16[144,1536]{1,0:T(8,128)(2,1)}, bf16[144,1536]{1,0:T(8,128)(2,1)}, u32[]{:S(2)}, u32[]{:S(2)}) collective-permute-start(bf16[144,1536]{1,0:T(8,128)(2,1)} %pad_maximum_fusion.6), channel_id=1, source_target_pairs={{0,3},{1,0},{2,1},{3,2},{4,7},{5,4},{6,5},{7,6},{8,11},{9,8},{10,9... | collective-permute-start | bytes 1327112 | tf_op jit(solution)/shard_map/ppermute | solution.py:183
  37.5 16.7 %collective-permute-start.10 = (bf16[144,1536]{1,0:T(8,128)(2,1)}, bf16[144,1536]{1,0:T(8,128)(2,1)}, u32[]{:S(2)}, u32[]{:S(2)}) collective-permute-start(bf16[144,1536]{1,0:T(8,128)(2,1)} %collective-permute-done.4), channel_id=1, source_target_pairs={{0,1},{1,2},{2,3},{3,0},{4,5},{5,6},{6,7},{7,4},{8,9},{9,10},{10,1... | collective-permute-start | bytes 1327112 | tf_op jit(solution)/shard_map/ppermute | solution.py:183
  55.2 31.4 %collective-permute-start.2 = (bf16[144,1536]{1,0:T(8,128)(2,1)}, bf16[144,1536]{1,0:T(8,128)(2,1)S(1)}, u32[]{:S(2)}, u32[]{:S(2)}) collective-permute-start(bf16[144,1536]{1,0:T(8,128)(2,1)} %pad_maximum_fusion.6), channel_id=1, source_target_pairs={{0,16},{4,12},{8,24},{12,4},{16,0},{20,28},{24,8},{28,20},{1,17},{... | collective-permute-start | bytes 1327112 | tf_op jit(solution)/shard_map/ppermute | solution.py:158
  56.0 100.4 %all-to-all-start = ((bf16[4,2,192,1280]{3,2,1,0:T(8,128)(2,1)}), bf16[4,2,192,1280]{3,2,1,0:T(8,128)(2,1)}, u32[]{:S(2)}, u32[]{:S(2)}) async-start(bf16[4,2,192,1280]{3,2,1,0:T(8,128)(2,1)} %shard_map.381), calls=%async_computation | async-start | bytes 7864320 | tf_op jit(solution)/shard_map/all_to_all | solution.py:848
  60.9 488.2 %reduce-scatter.2.cloned.1.call-start = ((), (), s32[]{:S(2)}) async-start(), calls=%async_computation.4 | async-start | bytes 7864320 | tf_op jit(solution)/shard_map/reduce_scatter | solution.py:943
  89.4 48.6 %collective-permute-start.15 = (bf16[10,64,1536]{2,1,0:T(8,128)(2,1)S(1)}, bf16[10,64,1536]{2,1,0:T(8,128)(2,1)S(1)}, u32[]{:S(2)}, u32[]{:S(2)}) collective-permute-start(bf16[10,64,1536]{2,1,0:T(8,128)(2,1)S(1)} %convert_element_type.295), channel_id=1, source_target_pairs={{0,4},{4,0},{8,12},{12,8},{16,20},{20,16},{24,28},{28,24},{1,5},{5... | collective-permute-start | bytes 5898248 | tf_op jit(solution)/shard_map/ppermute | solution.py:158
  90.5 50.0 %collective-permute-start.3 = (bf16[288,1536]{1,0:T(8,128)(2,1)S(1)}, bf16[288,1536]{1,0:T(8,128)(2,1)S(1)}, u32[]{:S(2)}, u32[]{:S(2)}) collective-permute-start(bf16[288,1536]{1,0:T(8,128)(2,1)S(1)} %pad_maximum_fusion.1.refs_0_), channel_id=1, source_target_pairs={{0,8},{4,20},{8,0},{12,28},{16,24},{20,4},{24,16},{28,12},{1,9},{5... | collective-permute-start | bytes 2654216 | tf_op jit(solution)/shard_map/ppermute | solution.py:158
  90.6 26.6 %collective-permute-start.8 = (bf16[144,1536]{1,0:T(8,128)(2,1)}, bf16[144,1536]{1,0:T(8,128)(2,1)S(1)}, u32[]{:S(2)}, u32[]{:S(2)}) collective-permute-start(bf16[144,1536]{1,0:T(8,128)(2,1)} %collective-permute-done.7), channel_id=1, source_target_pairs={{0,16},{4,12},{8,24},{12,4},{16,0},{20,28},{24,8},{28,20},{1,17},{... | collective-permute-start | bytes 1327112 | tf_op jit(solution)/shard_map/ppermute | solution.py:158
  91.4 35.3 %collective-permute-start.5 = (bf16[144,1536]{1,0:T(8,128)(2,1)}, bf16[144,1536]{1,0:T(8,128)(2,1)S(1)}, u32[]{:S(2)}, u32[]{:S(2)}) collective-permute-start(bf16[144,1536]{1,0:T(8,128)(2,1)} %collective-permute-done.4), channel_id=1, source_target_pairs={{0,16},{4,12},{8,24},{12,4},{16,0},{20,28},{24,8},{28,20},{1,17},{... | collective-permute-start | bytes 1327112 | tf_op jit(solution)/shard_map/ppermute | solution.py:158
  117.2 23.3 %collective-permute-start.9 = (bf16[288,1536]{1,0:T(8,128)(2,1)S(1)}, bf16[288,1536]{1,0:T(8,128)(2,1)S(1)}, u32[]{:S(2)}, u32[]{:S(2)}) collective-permute-start(bf16[288,1536]{1,0:T(8,128)(2,1)S(1)} %constant_dynamic-update-slice_fusion.10.refs_4_), channel_id=1, source_target_pairs={{0,8},{4,20},{8,0},{12,28},{16,24},{20,4},{24,16},{28,12},{1,9},{5... | collective-permute-start | bytes 2654216 | tf_op jit(solution)/shard_map/ppermute | solution.py:158
  118.8 17.3 %collective-permute-start.13 = (bf16[144,1536]{1,0:T(8,128)(2,1)}, bf16[144,1536]{1,0:T(8,128)(2,1)S(1)}, u32[]{:S(2)}, u32[]{:S(2)}) collective-permute-start(bf16[144,1536]{1,0:T(8,128)(2,1)} %collective-permute-done.10), channel_id=1, source_target_pairs={{0,16},{4,12},{8,24},{12,4},{16,0},{20,28},{24,8},{28,20},{1,17},{... | collective-permute-start | bytes 1327112 | tf_op jit(solution)/shard_map/ppermute | solution.py:158
  126.7 20.1 %collective-permute-start.6 = (bf16[288,1536]{1,0:T(8,128)(2,1)S(1)}, bf16[288,1536]{1,0:T(8,128)(2,1)S(1)}, u32[]{:S(2)}, u32[]{:S(2)}) collective-permute-start(bf16[288,1536]{1,0:T(8,128)(2,1)S(1)} %constant_dynamic-update-slice_fusion.8.refs_2_), channel_id=1, source_target_pairs={{0,8},{4,20},{8,0},{12,28},{16,24},{20,4},{24,16},{28,12},{1,9},{5... | collective-permute-start | bytes 2654216 | tf_op jit(solution)/shard_map/ppermute | solution.py:158
  136.2 20.2 %collective-permute-start.14 = (bf16[288,1536]{1,0:T(8,128)(2,1)S(1)}, bf16[288,1536]{1,0:T(8,128)(2,1)}, u32[]{:S(2)}, u32[]{:S(2)}) collective-permute-start(bf16[288,1536]{1,0:T(8,128)(2,1)S(1)} %constant_dynamic-update-slice_fusion.12.refs_6_), channel_id=1, source_target_pairs={{0,8},{4,20},{8,0},{12,28},{16,24},{20,4},{24,16},{28,12},{1,9},{5... | collective-permute-start | bytes 2654216 | tf_op jit(solution)/shard_map/ppermute | solution.py:158
  169.1 20.4 %collective-permute-start.20 = (bf16[4,2,192,1280]{3,2,1,0:T(8,128)(2,1)}, bf16[4,2,192,1280]{3,2,1,0:T(8,128)(2,1)}, u32[]{:S(2)}, u32[]{:S(2)}) collective-permute-start(bf16[4,2,192,1280]{3,2,1,0:T(8,128)(2,1)} %all-to-all-done.mine_ref), channel_id=1, source_target_pairs={{0,4},{4,0},{8,12},{12,8},{16,20},{20,16},{24,28},{28,24},{1,5},{5... | collective-permute-start | bytes 11796488 | tf_op jit(solution)/shard_map/ppermute | solution.py:158
  181.2 28.6 %collective-permute-start.30 = (bf16[128,1536]{1,0:T(8,128)(2,1)S(1)}, bf16[128,1536]{1,0:T(8,128)(2,1)}, u32[]{:S(2)}, u32[]{:S(2)}) collective-permute-start(bf16[128,1536]{1,0:T(8,128)(2,1)S(1)} %multiply_convert_fusion.1), channel_id=1, source_target_pairs={{0,3},{1,0},{2,1},{3,2},{4,7},{5,4},{6,5},{7,6},{8,11},{9,8},{10,9... | collective-permute-start | bytes 1179656 | tf_op jit(solution)/shard_map/ppermute | solution.py:183
  182.9 26.9 %collective-permute-start.22 = (bf16[128,1536]{1,0:T(8,128)(2,1)S(1)}, bf16[128,1536]{1,0:T(8,128)(2,1)}, u32[]{:S(2)}, u32[]{:S(2)}) collective-permute-start(bf16[128,1536]{1,0:T(8,128)(2,1)S(1)} %multiply_convert_fusion.1), channel_id=1, source_target_pairs={{0,1},{1,2},{2,3},{3,0},{4,5},{5,6},{6,7},{7,4},{8,9},{9,10},{10,1... | collective-permute-start | bytes 1179656 | tf_op jit(solution)/shard_map/ppermute | solution.py:183
  183.6 34.1 %collective-permute-start.18 = (bf16[128,1536]{1,0:T(8,128)(2,1)S(1)}, bf16[128,1536]{1,0:T(8,128)(2,1)}, u32[]{:S(2)}, u32[]{:S(2)}) collective-permute-start(bf16[128,1536]{1,0:T(8,128)(2,1)S(1)} %multiply_convert_fusion.1), channel_id=1, source_target_pairs={{0,2},{1,3},{2,0},{3,1},{4,6},{5,7},{6,4},{7,5},{8,10},{9,11},{10,... | collective-permute-start | bytes 1179656 | tf_op jit(solution)/shard_map/ppermute | solution.py:183
  187.9 33.5 %collective-permute-start.24 = (bf16[256,1536]{1,0:T(8,128)(2,1)S(1)}, bf16[256,1536]{1,0:T(8,128)(2,1)S(1)}, u32[]{:S(2)}, u32[]{:S(2)}) collective-permute-start(bf16[256,1536]{1,0:T(8,128)(2,1)S(1)} %pad_maximum_fusion.3.refs_0_), channel_id=1, source_target_pairs={{0,8},{4,20},{8,0},{12,28},{16,24},{20,4},{24,16},{28,12},{1,9},{5... | collective-permute-start | bytes 2359304 | tf_op jit(solution)/shard_map/ppermute | solution.py:158
  217.7 21.8 %collective-permute-start.21 = (bf16[128,1536]{1,0:T(8,128)(2,1)}, bf16[128,1536]{1,0:T(8,128)(2,1)S(1)}, u32[]{:S(2)}, u32[]{:S(2)}) collective-permute-start(bf16[128,1536]{1,0:T(8,128)(2,1)} %collective-permute-done.18), channel_id=1, source_target_pairs={{0,16},{4,12},{8,24},{12,4},{16,0},{20,28},{24,8},{28,20},{1,17},{... | collective-permute-start | bytes 1179656 | tf_op jit(solution)/shard_map/ppermute | solution.py:158
  218.3 20.1 %collective-permute-start.23 = (bf16[128,1536]{1,0:T(8,128)(2,1)}, bf16[128,1536]{1,0:T(8,128)(2,1)S(1)}, u32[]{:S(2)}, u32[]{:S(2)}) collective-permute-start(bf16[128,1536]{1,0:T(8,128)(2,1)} %collective-permute-done.22), channel_id=1, source_target_pairs={{0,16},{4,12},{8,24},{12,4},{16,0},{20,28},{24,8},{28,20},{1,17},{... | collective-permute-start | bytes 1179656 | tf_op jit(solution)/shard_map/ppermute | solution.py:158
  219.7 17.5 %collective-permute-start.31 = (bf16[128,1536]{1,0:T(8,128)(2,1)}, bf16[128,1536]{1,0:T(8,128)(2,1)S(1)}, u32[]{:S(2)}, u32[]{:S(2)}) collective-permute-start(bf16[128,1536]{1,0:T(8,128)(2,1)} %collective-permute-done.30), channel_id=1, source_target_pairs={{0,16},{4,12},{8,24},{12,4},{16,0},{20,28},{24,8},{28,20},{1,17},{... | collective-permute-start | bytes 1179656 | tf_op jit(solution)/shard_map/ppermute | solution.py:158
  234.2 19.9 %collective-permute-start.27 = (bf16[256,1536]{1,0:T(8,128)(2,1)S(1)}, bf16[256,1536]{1,0:T(8,128)(2,1)S(1)}, u32[]{:S(2)}, u32[]{:S(2)}) collective-permute-start(bf16[256,1536]{1,0:T(8,128)(2,1)S(1)} %get-tuple-element.170), channel_id=1, source_target_pairs={{0,8},{4,20},{8,0},{12,28},{16,24},{20,4},{24,16},{28,12},{1,9},{5... | collective-permute-start | bytes 2359304 | tf_op jit(solution)/shard_map/ppermute | solution.py:158
  237.2 43.8 %collective-permute-start.32 = (bf16[256,1536]{1,0:T(8,128)(2,1)S(1)}, bf16[256,1536]{1,0:T(8,128)(2,1)S(1)}, u32[]{:S(2)}, u32[]{:S(2)}) collective-permute-start(bf16[256,1536]{1,0:T(8,128)(2,1)S(1)} %constant_dynamic-update-slice_fusion.18.refs_0_), channel_id=1, source_target_pairs={{0,8},{4,20},{8,0},{12,28},{16,24},{20,4},{24,16},{28,12},{1,9},{5... | collective-permute-start | bytes 2359304 | tf_op jit(solution)/shard_map/ppermute | solution.py:158
  238.5 28.8 %collective-permute-start.25 = (bf16[256,1536]{1,0:T(8,128)(2,1)S(1)}, bf16[256,1536]{1,0:T(8,128)(2,1)S(1)}, u32[]{:S(2)}, u32[]{:S(2)}) collective-permute-start(bf16[256,1536]{1,0:T(8,128)(2,1)S(1)} %constant_dynamic-update-slice_fusion.16.refs_0_), channel_id=1, source_target_pairs={{0,8},{4,20},{8,0},{12,28},{16,24},{20,4},{24,16},{28,12},{1,9},{5... | collective-permute-start | bytes 2359304 | tf_op jit(solution)/shard_map/ppermute | solution.py:158
  239.5 66.2 %collective-permute-start.29 = (bf16[256,1536]{1,0:T(8,128)(2,1)S(1)}, bf16[256,1536]{1,0:T(8,128)(2,1)S(1)}, u32[]{:S(2)}, u32[]{:S(2)}) collective-permute-start(bf16[256,1536]{1,0:T(8,128)(2,1)S(1)} %constant_dynamic-update-slice_fusion.14.refs_0_), channel_id=1, source_target_pairs={{0,8},{4,20},{8,0},{12,28},{16,24},{20,4},{24,16},{28,12},{1,9},{5... | collective-permute-start | bytes 2359304 | tf_op jit(solution)/shard_map/ppermute | solution.py:158
  254.3 48.3 %collective-permute-start.28 = (bf16[128,1536]{1,0:T(8,128)(2,1)S(1)}, bf16[128,1536]{1,0:T(8,128)(2,1)S(1)}, u32[]{:S(2)}, u32[]{:S(2)}) collective-permute-start(bf16[128,1536]{1,0:T(8,128)(2,1)S(1)} %slice.523), channel_id=1, source_target_pairs={{0,16},{4,12},{8,24},{12,4},{16,0},{20,28},{24,8},{28,20},{1,17},{... | collective-permute-start | bytes 1179656 | tf_op jit(solution)/shard_map/ppermute | solution.py:158
  280.0 23.9 %collective-permute-start.26 = (bf16[256,1536]{1,0:T(8,128)(2,1)S(1)}, bf16[256,1536]{1,0:T(8,128)(2,1)S(1)}, u32[]{:S(2)}, u32[]{:S(2)}) collective-permute-start(bf16[256,1536]{1,0:T(8,128)(2,1)S(1)} %get-tuple-element.169), channel_id=1, source_target_pairs={{0,8},{4,20},{8,0},{12,28},{16,24},{20,4},{24,16},{28,12},{1,9},{5... | collective-permute-start | bytes 2359304 | tf_op jit(solution)/shard_map/ppermute | solution.py:158
  302.7 25.0 %collective-permute-start.35 = (bf16[256,1536]{1,0:T(8,128)(2,1)S(1)}, bf16[256,1536]{1,0:T(8,128)(2,1)S(1)}, u32[]{:S(2)}, u32[]{:S(2)}) collective-permute-start(bf16[256,1536]{1,0:T(8,128)(2,1)S(1)} %get-tuple-element.188), channel_id=1, source_target_pairs={{0,8},{4,20},{8,0},{12,28},{16,24},{20,4},{24,16},{28,12},{1,9},{5... | collective-permute-start | bytes 2359304 | tf_op jit(solution)/shard_map/ppermute | solution.py:158
  304.2 34.7 %collective-permute-start.33 = (bf16[128,1536]{1,0:T(8,128)(2,1)S(1)}, bf16[128,1536]{1,0:T(8,128)(2,1)}, u32[]{:S(2)}, u32[]{:S(2)}) collective-permute-start(bf16[128,1536]{1,0:T(8,128)(2,1)S(1)} %slice.522), channel_id=1, source_target_pairs={{0,16},{4,12},{8,24},{12,4},{16,0},{20,28},{24,8},{28,20},{1,17},{... | collective-permute-start | bytes 1179656 | tf_op jit(solution)/shard_map/ppermute | solution.py:158
  327.2 16.0 %collective-permute-start.38 = (bf16[256,1536]{1,0:T(8,128)(2,1)S(1)}, bf16[256,1536]{1,0:T(8,128)(2,1)S(1)}, u32[]{:S(2)}, u32[]{:S(2)}) collective-permute-start(bf16[256,1536]{1,0:T(8,128)(2,1)S(1)} %get-tuple-element.190), channel_id=1, source_target_pairs={{0,8},{4,20},{8,0},{12,28},{16,24},{20,4},{24,16},{28,12},{1,9},{5... | collective-permute-start | bytes 2359304 | tf_op jit(solution)/shard_map/ppermute | solution.py:158
  340.0 28.1 %collective-permute-start.34 = (bf16[128,1536]{1,0:T(8,128)(2,1)S(1)}, bf16[128,1536]{1,0:T(8,128)(2,1)}, u32[]{:S(2)}, u32[]{:S(2)}) collective-permute-start(bf16[128,1536]{1,0:T(8,128)(2,1)S(1)} %fusion.55), channel_id=1, source_target_pairs={{0,3},{1,0},{2,1},{3,2},{4,7},{5,4},{6,5},{7,6},{8,11},{9,8},{10,9... | collective-permute-start | bytes 1179656 | tf_op jit(solution)/shard_map/ppermute | solution.py:183
  346.1 22.0 %collective-permute-start.37 = (bf16[128,1536]{1,0:T(8,128)(2,1)S(1)}, bf16[128,1536]{1,0:T(8,128)(2,1)S(1)}, u32[]{:S(2)}, u32[]{:S(2)}) collective-permute-start(bf16[128,1536]{1,0:T(8,128)(2,1)S(1)} %fusion.54), channel_id=1, source_target_pairs={{0,1},{1,2},{2,3},{3,0},{4,5},{5,6},{6,7},{7,4},{8,9},{9,10},{10,1... | collective-permute-start | bytes 1179656 | tf_op jit(solution)/shard_map/ppermute | solution.py:183
  355.8 18.5 %collective-permute-start.40 = (bf16[128,1536]{1,0:T(8,128)(2,1)S(1)}, bf16[128,1536]{1,0:T(8,128)(2,1)S(1)}, u32[]{:S(2)}, u32[]{:S(2)}) collective-permute-start(bf16[128,1536]{1,0:T(8,128)(2,1)S(1)} %fusion.53), channel_id=1, source_target_pairs={{0,2},{1,3},{2,0},{3,1},{4,6},{5,7},{6,4},{7,5},{8,10},{9,11},{10,... | collective-permute-start | bytes 1179656 | tf_op jit(solution)/shard_map/ppermute | solution.py:183
  394.3 26.6 %collective-permute-start.42 = (bf16[4,2,192,1280]{3,2,1,0:T(8,128)(2,1)}, bf16[4,2,192,1280]{3,2,1,0:T(8,128)(2,1)}, u32[]{:S(2)}, u32[]{:S(2)}) collective-permute-start(bf16[4,2,192,1280]{3,2,1,0:T(8,128)(2,1)} %get-tuple-element.210), channel_id=1, source_target_pairs={{0,4},{4,0},{8,12},{12,8},{16,20},{20,16},{24,28},{28,24},{1,5},{5... | collective-permute-start | bytes 11796488 | tf_op jit(solution)/shard_map/ppermute | solution.py:158
  428.1 51.1 %all-to-all-start.1 = ((bf16[4,2,192,1280]{3,2,1,0:T(8,128)(2,1)}), bf16[4,2,192,1280]{3,2,1,0:T(8,128)(2,1)}, u32[]{:S(2)}, u32[]{:S(2)}) async-start(bf16[4,2,192,1280]{3,2,1,0:T(8,128)(2,1)} %add_convert_fusion), calls=%async_computation.2 | async-start | bytes 7864320 | tf_op jit(solution)/shard_map/all_to_all | solution.py:940
  445.3 28.2 %collective-permute-start.57 = (f32[128,1536]{1,0:T(8,128)S(1)}, f32[128,1536]{1,0:T(8,128)}, u32[]{:S(2)}, u32[]{:S(2)}) collective-permute-start(f32[128,1536]{1,0:T(8,128)S(1)} %slice.393), channel_id=1, source_target_pairs={{0,4},{4,0},{8,12},{12,8},{16,20},{20,16},{24,28},{28,24},{1,5},{5... | collective-permute-start | bytes 2359304 | tf_op jit(solution)/shard_map/ppermute | solution.py:158
  453.1 50.6 %collective-permute-start.52 = (bf16[288,1536]{1,0:T(8,128)(2,1)}, bf16[288,1536]{1,0:T(8,128)(2,1)}, u32[]{:S(2)}, u32[]{:S(2)}) collective-permute-start(bf16[288,1536]{1,0:T(8,128)(2,1)} %get-tuple-element.355), channel_id=1, source_target_pairs={{0,8},{4,20},{8,0},{12,28},{16,24},{20,4},{24,16},{28,12},{1,9},{5... | collective-permute-start | bytes 2654216 | tf_op jit(solution)/shard_map/ppermute | solution.py:158
  455.1 48.7 %collective-permute-start.49 = (bf16[288,1536]{1,0:T(8,128)(2,1)}, bf16[288,1536]{1,0:T(8,128)(2,1)}, u32[]{:S(2)}, u32[]{:S(2)}) collective-permute-start(bf16[288,1536]{1,0:T(8,128)(2,1)} %get-tuple-element.356), channel_id=1, source_target_pairs={{0,8},{4,20},{8,0},{12,28},{16,24},{20,4},{24,16},{28,12},{1,9},{5... | collective-permute-start | bytes 2654216 | tf_op jit(solution)/shard_map/ppermute | solution.py:158
  455.2 51.7 %collective-permute-start.47 = (bf16[288,1536]{1,0:T(8,128)(2,1)}, bf16[288,1536]{1,0:T(8,128)(2,1)}, u32[]{:S(2)}, u32[]{:S(2)}) collective-permute-start(bf16[288,1536]{1,0:T(8,128)(2,1)} %get-tuple-element.357), channel_id=1, source_target_pairs={{0,8},{4,20},{8,0},{12,28},{16,24},{20,4},{24,16},{28,12},{1,9},{5... | collective-permute-start | bytes 2654216 | tf_op jit(solution)/shard_map/ppermute | solution.py:158
  457.2 59.2 %collective-permute-start.43 = (bf16[288,1536]{1,0:T(8,128)(2,1)}, bf16[288,1536]{1,0:T(8,128)(2,1)}, u32[]{:S(2)}, u32[]{:S(2)}) collective-permute-start(bf16[288,1536]{1,0:T(8,128)(2,1)} %get-tuple-element.358), channel_id=1, source_target_pairs={{0,8},{4,20},{8,0},{12,28},{16,24},{20,4},{24,16},{28,12},{1,9},{5... | collective-permute-start | bytes 2654216 | tf_op jit(solution)/shard_map/ppermute | solution.py:158
  473.4 77.1 %collective-permute-start.56 = (f32[10,64,1536]{2,1,0:T(8,128)}, f32[10,64,1536]{2,1,0:T(8,128)}, u32[]{:S(2)}, u32[]{:S(2)}) collective-permute-start(f32[10,64,1536]{2,1,0:T(8,128)} %get-tuple-element.225), channel_id=1, source_target_pairs={{0,4},{4,0},{8,12},{12,8},{16,20},{20,16},{24,28},{28,24},{1,5},{5... | collective-permute-start | bytes 11796488 | tf_op jit(solution)/shard_map/ppermute | solution.py:158
  527.8 16.3 %collective-permute-start.53 = (bf16[144,1536]{1,0:T(8,128)(2,1)S(1)}, bf16[144,1536]{1,0:T(8,128)(2,1)S(1)}, u32[]{:S(2)}, u32[]{:S(2)}) collective-permute-start(bf16[144,1536]{1,0:T(8,128)(2,1)S(1)} %slice.515), channel_id=1, source_target_pairs={{0,16},{4,12},{8,24},{12,4},{16,0},{20,28},{24,8},{28,20},{1,17},{... | collective-permute-start | bytes 1327112 | tf_op jit(solution)/shard_map/ppermute | solution.py:158
  539.5 25.2 %collective-permute-start.51 = (bf16[144,1536]{1,0:T(8,128)(2,1)S(1)}, bf16[144,1536]{1,0:T(8,128)(2,1)}, u32[]{:S(2)}, u32[]{:S(2)}) collective-permute-start(bf16[144,1536]{1,0:T(8,128)(2,1)S(1)} %fusion.42), channel_id=1, source_target_pairs={{0,1},{1,2},{2,3},{3,0},{4,5},{5,6},{6,7},{7,4},{8,9},{9,10},{10,1... | collective-permute-start | bytes 1327112 | tf_op jit(solution)/shard_map/ppermute | solution.py:183
  545.1 19.6 %collective-permute-start.55 = (bf16[144,1536]{1,0:T(8,128)(2,1)}, bf16[144,1536]{1,0:T(8,128)(2,1)}, u32[]{:S(2)}, u32[]{:S(2)}) collective-permute-start(bf16[144,1536]{1,0:T(8,128)(2,1)} %fusion.41), channel_id=1, source_target_pairs={{0,3},{1,0},{2,1},{3,2},{4,7},{5,4},{6,5},{7,6},{8,11},{9,8},{10,9... | collective-permute-start | bytes 1327112 | tf_op jit(solution)/shard_map/ppermute | solution.py:183
  (83 other events, 966.2 us)
Sparse Core Ops, SparseCore 0:
  54.3 122.5 all-gather.1
  384.9 111.4 reduce-scatter.1

commit v6 on v5

--- a/solution.py
+++ b/solution.py
@@ -889,30 +889,32 @@
     normed_ring = [normed_two] + [turn(normed_two, distance) for distance in DISTANCE[1:]]
     gate_w, upper_w = stack_rows(place, pieces, after(swap_core(pieces), normed_two))
     back_parts, filled = [], []
-    second_parts, begun = [], ()
-    for spot, part in enumerate(normed_ring):
-        near = along_first(after(part, begun))
-        away = swap_second(near)
-        if spot >= 2:
-            near = after(near, (second_parts[spot - 2], back_parts[: spot - 2]))
-        back = []
-        for second, sources in ((0, [near]), (1, [away])) if spot < 2 else ((0, [near, away]),):
-            done = expert_block(
-                place,
-                spot,
-                second,
-                sources,
-                cotangent_all,
-                (gate_w, upper_w, down_w),
-                local_experts,
-                filled,
-            )
-            back += done[: len(sources)]
-            filled = done[len(sources) :]
-            begun = begun or (back[0],)
-        if spot < len(DISTANCE) - 1:
-            second_parts.append(add_second(*back))
+    second_parts, begun, halves, backs = [], (), [], {}
+    for spot, second in ((0, 0), (0, 1), (1, 0), (2, 0), (1, 1), (2, 1), (3, 0)):
+        if second == 0:
+            near = along_first(after(normed_ring[spot], begun))
+            halves.append((near, swap_second(near)))
+        sources = halves[spot] if spot == 3 else halves[spot][second : second + 1]
+        if spot >= 2 and (spot, second) != (2, 0):
+            gate = (second_parts[spot - 2], back_parts[: spot - 2])
+            sources = after(sources, gate)
+        done = expert_block(
+            place,
+            spot,
+            second,
+            sources,
+            cotangent_all,
+            (gate_w, upper_w, down_w),
+            local_experts,
+            filled,
+        )
+        backs.setdefault(spot, []).extend(done[: len(sources)])
+        filled = done[len(sources) :]
+        begun = begun or (done[0],)
+        if second == 1:
+            second_parts.append(add_second(*backs[spot]))
             back_parts.append(add_first(second_parts[-1]))
+    back = backs[3]
     hidden, grad_gate, grad_upper, rows_all, grads_all, out_all = filled
     steps = local_experts // 2
     kept_grads = []

time: 598 us -> 592 us (0.990)
  waiting for transfers between devices: 158 us -> 146 us
    ppermute x47, waiting for transfers between devices: 123 us -> 113 us  [swap(): return lax.ppermute(rows, 'dp', [(i, i ^ pick(i)) for i in range(count)])]
    pallas_call x6 -> x7, Pallas kernels: 95.7 us -> 100 us  [expert_block(): pl.pallas_call(functools.partial(expert_kernel, per_step=per_step, count=...]
    unnamed x155 -> x173, local copies, waits for them, and re-layouts: 15.4 us -> 17.9 us
  transfers between devices with their start and end apart: 63 -> 63, of which waited for: 23 -> 22; matrix products, arithmetic and copies ran while one was open for 20% -> 21% of each run, Pallas kernels for 33% -> 34%
where the time goes in v6:
time: 592 us; the launch traced here: 586 us
  Pallas kernels  211 us (36%)
  waiting for transfers between devices  146 us (25%)
  starting transfers between devices  75.2 us (13%)
  other arithmetic  63.3 us (11%)
  local copies, waits for them, and re-layouts  40.4 us (7%)
  matrix products  33 us (6%)
  between operations  16.4 us (3%)
    ppermute x47, waiting for transfers between devices, swap(): return lax.ppermute(rows, 'dp', [(i, i ^ pick(i)) for i in range(count)])  113 us
    pallas_call x7, Pallas kernels, expert_block(): pl.pallas_call(functools.partial(expert_kernel, per_step=per_step, count=...  100 us
    pallas_call x5, Pallas kernels, column_grads(): pl.pallas_call(column_grads_kernel, grid_spec=pltpu.PrefetchScalarGridSpe...  45.9 us
    ppermute x47, starting transfers between devices, swap(): return lax.ppermute(rows, 'dp', [(i, i ^ pick(i)) for i in range(count)])  43.9 us
    ppermute x12, waiting for transfers between devices, turn(): lax.ppermute(rows, 'expert', [(i, (i + step) % count) for i in range(coun...  30.1 us
    pallas_call x1, Pallas kernels, adam_columns(): pl.pallas_call(adam_columns_kernel, grid=(experts,), in_specs=[block] * 3...  24.5 us
    ppermute x12, starting transfers between devices, turn(): lax.ppermute(rows, 'expert', [(i, (i + step) % count) for i in range(coun...  21 us
    unnamed x173, local copies, waits for them, and re-layouts  17.9 us
  transfers between devices with their start and end apart: 63, of which 22 were waited for; matrix products, arithmetic and copies ran while one was open for 21% of the time, Pallas kernels for 34%

profile of v6, /device:TPU:0, one launch (start us, length us, event | category | flops | bytes accessed | tf_op | source)
XLA Modules:
  0.0 585.6 jit_solution(14830962261405102684)
XLA Ops:
  10.1 3.0 collective-permute-start.11
  27.3 8.2 %shard_map.381 = bf16[4,2,192,1280]{3,2,1,0:T(8,128)(2,1)} custom-call(f32[10,192,1024]{2,1,0:T(8,128)} %w_ref.1), custom_call_target="tpu_custom_call" | custom-call | bytes 11796480 | tf_op jit(solution)/shard_map/pallas_call | solution.py:333
  40.0 6.9 %collective-permute-done.7 = bf16[144,1536]{1,0:T(8,128)(2,1)} collective-permute-done((bf16[144,1536]{1,0:T(8,128)(2,1)}, bf16[144,1536]{1,0:T(8,128)(2,1)}, u32[]{:S(2)}, u32[]{:S(2)}) %collective-permute-start.7) | collective-permute-done | bytes 442400 | tf_op jit(solution)/shard_map/ppermute | solution.py:183
  46.8 7.3 %collective-permute-done.10 = bf16[144,1536]{1,0:T(8,128)(2,1)} collective-permute-done((bf16[144,1536]{1,0:T(8,128)(2,1)S(1)}, bf16[144,1536]{1,0:T(8,128)(2,1)}, u32[]{:S(2)}, u32[]{:S(2)}) %collective-permute-start.10) | collective-permute-done | bytes 442400 | tf_op jit(solution)/shard_map/ppermute | solution.py:183
  56.0 4.9 all-to-all-start
  61.2 24.9 %collective-permute-done.2 = bf16[144,1536]{1,0:T(8,128)(2,1)S(1)} collective-permute-done((bf16[144,1536]{1,0:T(8,128)(2,1)}, bf16[144,1536]{1,0:T(8,128)(2,1)S(1)}, u32[]{:S(2)}, u32[]{:S(2)}) %collective-permute-start.2) | collective-permute-done | bytes 442400 | tf_op jit(solution)/shard_map/ppermute | solution.py:158
  93.4 23.5 %collective-permute-done.8 = bf16[144,1536]{1,0:T(8,128)(2,1)S(1)} collective-permute-done((bf16[144,1536]{1,0:T(8,128)(2,1)}, bf16[144,1536]{1,0:T(8,128)(2,1)S(1)}, u32[]{:S(2)}, u32[]{:S(2)}) %collective-permute-start.8) | collective-permute-done | bytes 442400 | tf_op jit(solution)/shard_map/ppermute | solution.py:158
  119.0 7.4 %collective-permute-done.5 = bf16[144,1536]{1,0:T(8,128)(2,1)S(1)} collective-permute-done((bf16[144,1536]{1,0:T(8,128)(2,1)S(1)}, bf16[144,1536]{1,0:T(8,128)(2,1)S(1)}, u32[]{:S(2)}, u32[]{:S(2)}) %collective-permute-start.5) | collective-permute-done | bytes 442400 | tf_op jit(solution)/shard_map/ppermute | solution.py:158
  129.1 6.8 %collective-permute-done.13 = bf16[144,1536]{1,0:T(8,128)(2,1)S(1)} collective-permute-done((bf16[144,1536]{1,0:T(8,128)(2,1)}, bf16[144,1536]{1,0:T(8,128)(2,1)S(1)}, u32[]{:S(2)}, u32[]{:S(2)}) %collective-permute-start.13) | collective-permute-done | bytes 442400 | tf_op jit(solution)/shard_map/ppermute | solution.py:158
  140.3 6.7 %collective-permute-done.6.refs_3_ = bf16[288,1536]{1,0:T(8,128)(2,1)S(1)} collective-permute-done((bf16[288,1536]{1,0:T(8,128)(2,1)S(1)}, bf16[288,1536]{1,0:T(8,128)(2,1)S(1)}, u32[]{:S(2)}, u32[]{:S(2)}) %collective-permute-start.6) | collective-permute-done | bytes 884768 | tf_op jit(solution)/shard_map/ppermute | solution.py:158
  148.0 8.7 %collective-permute-done.14.refs_7_ = bf16[288,1536]{1,0:T(8,128)(2,1)} collective-permute-done((bf16[288,1536]{1,0:T(8,128)(2,1)S(1)}, bf16[288,1536]{1,0:T(8,128)(2,1)}, u32[]{:S(2)}, u32[]{:S(2)}) %collective-permute-start.14) | collective-permute-done | bytes 884768 | tf_op jit(solution)/shard_map/ppermute | solution.py:158
  156.7 6.3 %shard_map.382 = (bf16[1536,1280]{1,0:T(8,128)(2,1)}, bf16[1536,128]{1,0:T(8,128)(2,1)}, bf16[768,1536]{1,0:T(8,128)(2,1)}) custom-call(bf16[288,1536]{1,0:T(8,128)(2,1)} %copy-done.20, bf16[288,1536]{1,0:T(8,128)(2,1)} %copy-done.40, bf16[288,1536]{1,0:T(8,128)(2,1)} %copy-done.24, bf16[288,1536]{1,0:T(8,128)(2,1)} %copy-done.42, ...), custom_call_target="tpu_custom_call" | custom-call | bytes 14155776 | tf_op jit(solution)/shard_map/pallas_call | solution.py:416
  164.2 3.3 multiply_convert_fusion
  183.3 3.6 collective-permute-done.19
  188.5 6.6 %shard_map.383 = (bf16[1536,1280]{1,0:T(8,128)(2,1)}, bf16[1536,1280]{1,0:T(8,128)(2,1)}) custom-call(s32[7]{0:T(128)} %pad_add_fusion.1.place_ref, bf16[4,2,192,1280]{3,2,1,0:T(8,128)(2,1)} %all-to-all-done.mine_ref, bf16[4,2,192,1280]{3,2,1,0:T(8,128)(2,1)} %collective-permute-done.20.theirs_ref), custom_call_target="tpu_custom_call" | custom-call | bytes 15728640 | tf_op jit(solution)/shard_map/pallas_call | solution.py:369
  195.1 13.7 %shard_map.384 = (f32[256,1536]{1,0:T(8,128)S(1)}, bf16[2048,1280]{1,0:T(8,128)(2,1)}, bf16[2048,1280]{1,0:T(8,128)(2,1)}, bf16[2048,1280]{1,0:T(8,128)(2,1)}, b...) custom-call(s32[7]{0:T(128)S(1)} %copy-done.5, ...), custom_call_target="tpu_custom_call" | custom-call | flops 6039797760 | bytes 23199744 | tf_op jit(solution)/shard_map/pallas_call | solution.py:586
  208.8 7.9 %collective-permute-done.18 = bf16[128,1536]{1,0:T(8,128)(2,1)} collective-permute-done((bf16[128,1536]{1,0:T(8,128)(2,1)S(1)}, bf16[128,1536]{1,0:T(8,128)(2,1)}, u32[]{:S(2)}, u32[]{:S(2)}) %collective-permute-start.18) | collective-permute-done | bytes 393248 | tf_op jit(solution)/shard_map/ppermute | solution.py:183
  220.4 12.8 %shard_map.385 = (bf16[256,1536]{1,0:T(8,128)(2,1)S(1)}, bf16[2048,1280]{1,0:T(8,128)(2,1)}, bf16[2048,1280]{1,0:T(8,128)(2,1)}, bf16[2048,1280]{1,0:T(8,128)(2,...) custom-call(s32[7]{0:T(128)S(1)} %copy-done.5, ...), custom_call_target="tpu_custom_call", output_to_operand_aliasing={{1}: (6, {}), {2}: (7, {}), {3}: (8, {}), {4}: (9, {}), {5}... | custom-call | flops 6039797760 | bytes 23199744 | tf_op jit(solution)/shard_map/pallas_call | solution.py:586
  239.7 13.4 %shard_map.386 = (f32[256,1536]{1,0:T(8,128)S(1)}, bf16[2048,1280]{1,0:T(8,128)(2,1)}, bf16[2048,1280]{1,0:T(8,128)(2,1)}, bf16[2048,1280]{1,0:T(8,128)(2,1)}, b...) custom-call(s32[7]{0:T(128)S(1)} %copy-done.5, ...), custom_call_target="tpu_custom_call", output_to_operand_aliasing={{1}: (6, {}), {2}: (7, {}), {3}: (8, {}), {4}: (9, {}), {5}... | custom-call | flops 6039797760 | bytes 23199744 | tf_op jit(solution)/shard_map/pallas_call | solution.py:586
  253.1 13.4 %shard_map.387 = (f32[256,1536]{1,0:T(8,128)S(1)}, bf16[2048,1280]{1,0:T(8,128)(2,1)}, bf16[2048,1280]{1,0:T(8,128)(2,1)}, bf16[2048,1280]{1,0:T(8,128)(2,1)}, b...) custom-call(s32[7]{0:T(128)S(1)} %copy-done.5, ...), custom_call_target="tpu_custom_call", output_to_operand_aliasing={{1}: (6, {}), {2}: (7, {}), {3}: (8, {}), {4}: (9, {}), {5}... | custom-call | flops 6039797760 | bytes 23199744 | tf_op jit(solution)/shard_map/pallas_call | solution.py:586
  268.6 12.9 %shard_map.388 = (bf16[256,1536]{1,0:T(8,128)(2,1)S(1)}, bf16[2048,1280]{1,0:T(8,128)(2,1)}, bf16[2048,1280]{1,0:T(8,128)(2,1)}, bf16[2048,1280]{1,0:T(8,128)(2,...) custom-call(s32[7]{0:T(128)S(1)} %copy-done.5, ...), custom_call_target="tpu_custom_call", output_to_operand_aliasing={{1}: (6, {}), {2}: (7, {}), {3}: (8, {}), {4}: (9, {}), {5}... | custom-call | flops 6039797760 | bytes 23199744 | tf_op jit(solution)/shard_map/pallas_call | solution.py:586
  282.4 12.7 %shard_map.389 = (bf16[256,1536]{1,0:T(8,128)(2,1)S(1)}, bf16[2048,1280]{1,0:T(8,128)(2,1)}, bf16[2048,1280]{1,0:T(8,128)(2,1)}, bf16[2048,1280]{1,0:T(8,128)(2,...) custom-call(s32[7]{0:T(128)S(1)} %copy-done.5, ...), custom_call_target="tpu_custom_call", output_to_operand_aliasing={{1}: (6, {}), {2}: (7, {}), {3}: (8, {}), {4}: (9, {}), {5}... | custom-call | flops 6039797760 | bytes 23199744 | tf_op jit(solution)/shard_map/pallas_call | solution.py:586
  299.8 21.6 %shard_map.390 = (f32[256,1536]{1,0:T(8,128)S(1)}, bf16[256,1536]{1,0:T(8,128)(2,1)S(1)}, bf16[2048,1280]{1,0:T(8,128)(2,1)}, bf16[2048,1280]{1,0:T(8,128)(2,1)}...) custom-call(s32[7]{0:T(128)S(1)} %copy-done.5, ...), custom_call_target="tpu_custom_call", output_to_operand_aliasing={{2}: (7, {}), {3}: (8, {}), {4}: (9, {}), {5}: (10, {}), {6... | custom-call | flops 12079595520 | bytes 34603008 | tf_op jit(solution)/shard_map/pallas_call | solution.py:586
  324.4 9.1 %shard_map.391 = (f32[4,2,192,1280]{3,2,1,0:T(8,128)}, bf16[4,2,192,1280]{3,2,1,0:T(8,128)(2,1)}) custom-call(s32[7]{0:T(128)} %pad_add_fusion.1.place_ref, bf16[2048,1536]{1,0:T(8,128)(2,1)} %get-tuple-element.220.rows_ref, bf16[2048,1280]{1,0:T(8,128)(2,1)} %get-tuple-element.206.grad_gate_ref, bf16[2048,1280]{1,0:T(8,128)(2,1)} %get-tuple-element.207.grad_upper_ref), custom_call_target="tpu_custom_call" | custom-call | flops 3221225472 | bytes 13107200 | tf_op jit(solution)/shard_map/pallas_call | solution.py:648
  334.6 3.3 collective-permute-start.34
  342.5 9.1 %shard_map.392 = (f32[4,2,192,1280]{3,2,1,0:T(8,128)}, bf16[4,2,192,1280]{3,2,1,0:T(8,128)(2,1)}) custom-call(s32[7]{0:T(128)} %pad_add_fusion.1.place_ref, bf16[2048,1536]{1,0:T(8,128)(2,1)} %get-tuple-element.220.rows_ref, bf16[2048,1280]{1,0:T(8,128)(2,1)} %get-tuple-element.206.grad_gate_ref, ...), custom_call_target="tpu_custom_call", output_to_operand_aliasing={{0}: (4, {}), {1}: (5, {})} | custom-call | flops 3221225472 | bytes 13107200 | tf_op jit(solution)/shard_map/pallas_call | solution.py:648
  353.6 9.1 %shard_map.393 = (f32[4,2,192,1280]{3,2,1,0:T(8,128)}, bf16[4,2,192,1280]{3,2,1,0:T(8,128)(2,1)}) custom-call(s32[7]{0:T(128)} %pad_add_fusion.1.place_ref, bf16[2048,1536]{1,0:T(8,128)(2,1)} %get-tuple-element.220.rows_ref, bf16[2048,1280]{1,0:T(8,128)(2,1)} %get-tuple-element.206.grad_gate_ref, ...), custom_call_target="tpu_custom_call", output_to_operand_aliasing={{0}: (4, {}), {1}: (5, {})} | custom-call | flops 3221225472 | bytes 13107200 | tf_op jit(solution)/shard_map/pallas_call | solution.py:648
  362.8 6.2 %collective-permute-done.40 = bf16[128,1536]{1,0:T(8,128)(2,1)S(1)} collective-permute-done((bf16[128,1536]{1,0:T(8,128)(2,1)S(1)}, bf16[128,1536]{1,0:T(8,128)(2,1)S(1)}, u32[]{:S(2)}, u32[]{:S(2)}) %collective-permute-start.40) | collective-permute-done | bytes 393248 | tf_op jit(solution)/shard_map/ppermute | solution.py:183
  370.4 9.1 %shard_map.394 = (f32[4,2,192,1280]{3,2,1,0:T(8,128)}, bf16[4,2,192,1280]{3,2,1,0:T(8,128)(2,1)}) custom-call(s32[7]{0:T(128)} %pad_add_fusion.1.place_ref, bf16[2048,1536]{1,0:T(8,128)(2,1)} %get-tuple-element.220.rows_ref, bf16[2048,1280]{1,0:T(8,128)(2,1)} %get-tuple-element.206.grad_gate_ref, ...), custom_call_target="tpu_custom_call", output_to_operand_aliasing={{0}: (4, {}), {1}: (5, {})} | custom-call | flops 3221225472 | bytes 13107200 | tf_op jit(solution)/shard_map/pallas_call | solution.py:648
  379.6 9.4 %shard_map.395 = (f32[4,2,192,1280]{3,2,1,0:T(8,128)}, bf16[4,2,192,1280]{3,2,1,0:T(8,128)(2,1)}) custom-call(s32[7]{0:T(128)} %pad_add_fusion.1.place_ref, bf16[2048,1536]{1,0:T(8,128)(2,1)} %get-tuple-element.220.rows_ref, bf16[2048,1280]{1,0:T(8,128)(2,1)} %get-tuple-element.206.grad_gate_ref, ...), custom_call_target="tpu_custom_call", output_to_operand_aliasing={{0}: (4, {}), {1}: (5, {})} | custom-call | flops 3221225472 | bytes 13107200 | tf_op jit(solution)/shard_map/pallas_call | solution.py:648
  392.5 3.9 collective-permute-done.41
  397.1 3.7 fusion.25
  408.1 3.6 fusion.36
  414.2 7.3 %add_convert_fusion = bf16[4,2,192,1280]{3,2,1,0:T(8,128)(2,1)} fusion(f32[4,2,192,1280]{3,2,1,0:T(8,128)} %get-tuple-element.223, bf16[4,2,192,1280]{3,2,1,0:T(8,128)(2,1)} %collective-permute-done.42), kind=kLoop, calls=%fused_computation.7 | loop fusion | flops 5898240 | bytes 15728640 | tf_op jit(solution)/shard_map/convert_element_type | solution.py:940
  421.5 5.1 all-to-all-start.1
  426.7 5.3 fusion.103
  432.3 5.7 fusion.1
  439.8 4.8 shard_map.396
  450.6 14.2 %shard_map.398 = (f32[10,64,1536]{2,1,0:T(8,128)S(1)}, f32[10,64,1536]{2,1,0:T(8,128)}) custom-call(s32[7]{0:T(128)S(1)} %copy-done.6, bf16[2048,1536]{1,0:T(8,128)(2,1)} %get-tuple-element.236.grads_ref, bf16[2048,1280]{1,0:T(8,128)(2,1)S(1)} %bitcast.123), custom_call_target="tpu_custom_call" | custom-call | flops 8053063680 | bytes 19398656 | tf_op jit(solution)/shard_map/pallas_call | solution.py:695
  472.6 24.5 %shard_map.397 = (f32[10,192,1024]{2,1,0:T(8,128)}, f32[10,192,1024]{2,1,0:T(8,128)}, f32[10,192,1024]{2,1,0:T(8,128)}, f32[10,192,1024]{2,1,0:T(8,128)}) custom-call(f32[10,192,1024]{2,1,0:T(8,128)} %w_ref.1, f32[10,192,1024]{2,1,0:T(8,128)} %first_ref.1, f32[10,192,1024]{2,1,0:T(8,128)} %second_ref.1, bf16[4,2,192,1280]{3,2,1,0:T(8,128)(2,1)} %all-to-all-done.1.grad_ref), custom_call_target="tpu_custom_call" | custom-call | flops 39321600 | bytes 58982400 | tf_op jit(solution)/shard_map/pallas_call | solution.py:740
  497.2 3.1 collective-permute-done.47
  500.3 9.5 %collective-permute-done.43 = bf16[288,1536]{1,0:T(8,128)(2,1)} collective-permute-done((bf16[288,1536]{1,0:T(8,128)(2,1)}, bf16[288,1536]{1,0:T(8,128)(2,1)}, u32[]{:S(2)}, u32[]{:S(2)}) %collective-permute-start.43) | collective-permute-done | bytes 884768 | tf_op jit(solution)/shard_map/ppermute | solution.py:158
  509.8 5.2 bitcast_add_fusion
  523.5 3.4 collective-permute-start.54
  526.9 6.0 %collective-permute-done.50 = bf16[144,1536]{1,0:T(8,128)(2,1)S(1)} collective-permute-done((bf16[144,1536]{1,0:T(8,128)(2,1)S(1)}, bf16[144,1536]{1,0:T(8,128)(2,1)S(1)}, u32[]{:S(2)}, u32[]{:S(2)}) %collective-permute-start.50) | collective-permute-done | bytes 442400 | tf_op jit(solution)/shard_map/ppermute | solution.py:158
  533.7 4.0 collective-permute-done.53
  538.5 4.2 collective-permute-start.55
  544.2 13.1 %multiply_subtract_fusion = (f32[10,64,1536]{2,1,0:T(8,128)}, f32[10,64,1536]{2,1,0:T(8,128)}, f32[10,64,1536]{2,1,0:T(8,128)}, f32[10,64,1536]{2,1,0:T(8,128)}) fusion(f32[10,64,1536]{2,1,0:T(8,128)} %param.31, f32[10,64,1536]{2,1,0:T(8,128)} %param.36, f32[10,64,1536]{2,1,0:T(8,128)} %param.41, f32[10,64,1536]{2,1,0:T(8,128)} %copy-done.2, ...), kind=kLoop, calls=%fused_computation.15 | loop fusion | flops 15728640 | bytes 35389440 | tf_op jit(solution)/shard_map/sub | solution.py:147
  (460 shorter events, 151.1 us)
Async XLA Ops:
  7.2 187.9 %all-gather.2.cloned.1.call-start = ((), (), s32[]{:S(2)}) async-start(), calls=%async_computation.3 | async-start | bytes 8519680 | tf_op jit(solution)/shard_map/all_gather | solution.py:819
  19.3 18.1 %collective-permute-start.12 = (bf16[256,1664]{1,0:T(8,128)(2,1)S(1)}, bf16[256,1664]{1,0:T(8,128)(2,1)}, u32[]{:S(2)}, u32[]{:S(2)}) collective-permute-start(bf16[256,1664]{1,0:T(8,128)(2,1)S(1)} %pad_maximum_fusion.2), channel_id=1, source_target_pairs={{0,8},{4,20},{8,0},{12,28},{16,24},{20,4},{24,16},{28,12},{1,9},{5... | collective-permute-start | bytes 2555912 | tf_op jit(solution)/shard_map/ppermute | solution.py:158
  23.8 32.2 %collective-permute-start.16 = (s32[1,128]{1,0:T(1,128)S(1)}, s32[1,128]{1,0:T(1,128)S(1)}, u32[]{:S(2)}, u32[]{:S(2)}) collective-permute-start(s32[1,128]{1,0:T(1,128)S(1)} %copy-done.73), channel_id=1, source_target_pairs={{0,4},{4,0},{8,12},{12,8},{16,20},{20,16},{24,28},{28,24},{1,5},{5... | collective-permute-start | bytes 1544 | tf_op jit(solution)/shard_map/ppermute | solution.py:158
  23.8 65.2 %collective-permute-start = (bf16[128,1536]{1,0:T(8,128)(2,1)S(1)}, bf16[128,1536]{1,0:T(8,128)(2,1)}, u32[]{:S(2)}, u32[]{:S(2)}) collective-permute-start(bf16[128,1536]{1,0:T(8,128)(2,1)S(1)} %copy-done.13), channel_id=1, source_target_pairs={{0,4},{4,0},{8,12},{12,8},{16,20},{20,16},{24,28},{28,24},{1,5},{5... | collective-permute-start | bytes 1179656 | tf_op jit(solution)/shard_map/ppermute | solution.py:158
  25.0 21.9 %collective-permute-start.7 = (bf16[144,1536]{1,0:T(8,128)(2,1)}, bf16[144,1536]{1,0:T(8,128)(2,1)}, u32[]{:S(2)}, u32[]{:S(2)}) collective-permute-start(bf16[144,1536]{1,0:T(8,128)(2,1)} %pad_maximum_fusion.6), channel_id=1, source_target_pairs={{0,3},{1,0},{2,1},{3,2},{4,7},{5,4},{6,5},{7,6},{8,11},{9,8},{10,9... | collective-permute-start | bytes 1327112 | tf_op jit(solution)/shard_map/ppermute | solution.py:183
  37.3 16.8 %collective-permute-start.10 = (bf16[144,1536]{1,0:T(8,128)(2,1)S(1)}, bf16[144,1536]{1,0:T(8,128)(2,1)}, u32[]{:S(2)}, u32[]{:S(2)}) collective-permute-start(bf16[144,1536]{1,0:T(8,128)(2,1)S(1)} %collective-permute-done.4), channel_id=1, source_target_pairs={{0,1},{1,2},{2,3},{3,0},{4,5},{5,6},{6,7},{7,4},{8,9},{9,10},{10,1... | collective-permute-start | bytes 1327112 | tf_op jit(solution)/shard_map/ppermute | solution.py:183
  55.2 30.9 %collective-permute-start.2 = (bf16[144,1536]{1,0:T(8,128)(2,1)}, bf16[144,1536]{1,0:T(8,128)(2,1)S(1)}, u32[]{:S(2)}, u32[]{:S(2)}) collective-permute-start(bf16[144,1536]{1,0:T(8,128)(2,1)} %pad_maximum_fusion.6), channel_id=1, source_target_pairs={{0,16},{4,12},{8,24},{12,4},{16,0},{20,28},{24,8},{28,20},{1,17},{... | collective-permute-start | bytes 1327112 | tf_op jit(solution)/shard_map/ppermute | solution.py:158
  56.0 100.7 %all-to-all-start = ((bf16[4,2,192,1280]{3,2,1,0:T(8,128)(2,1)}), bf16[4,2,192,1280]{3,2,1,0:T(8,128)(2,1)}, u32[]{:S(2)}, u32[]{:S(2)}) async-start(bf16[4,2,192,1280]{3,2,1,0:T(8,128)(2,1)} %shard_map.381), calls=%async_computation | async-start | bytes 7864320 | tf_op jit(solution)/shard_map/all_to_all | solution.py:848
  60.9 481.9 %reduce-scatter.2.cloned.1.call-start = ((), (), s32[]{:S(2)}) async-start(), calls=%async_computation.4 | async-start | bytes 7864320 | tf_op jit(solution)/shard_map/reduce_scatter | solution.py:945
  88.9 48.8 %collective-permute-start.15 = (bf16[10,64,1536]{2,1,0:T(8,128)(2,1)S(1)}, bf16[10,64,1536]{2,1,0:T(8,128)(2,1)S(1)}, u32[]{:S(2)}, u32[]{:S(2)}) collective-permute-start(bf16[10,64,1536]{2,1,0:T(8,128)(2,1)S(1)} %convert_element_type.295), channel_id=1, source_target_pairs={{0,4},{4,0},{8,12},{12,8},{16,20},{20,16},{24,28},{28,24},{1,5},{5... | collective-permute-start | bytes 5898248 | tf_op jit(solution)/shard_map/ppermute | solution.py:158
  90.1 50.2 %collective-permute-start.3 = (bf16[288,1536]{1,0:T(8,128)(2,1)S(1)}, bf16[288,1536]{1,0:T(8,128)(2,1)S(1)}, u32[]{:S(2)}, u32[]{:S(2)}) collective-permute-start(bf16[288,1536]{1,0:T(8,128)(2,1)S(1)} %pad_maximum_fusion.1.refs_0_), channel_id=1, source_target_pairs={{0,8},{4,20},{8,0},{12,28},{16,24},{20,4},{24,16},{28,12},{1,9},{5... | collective-permute-start | bytes 2654216 | tf_op jit(solution)/shard_map/ppermute | solution.py:158
  90.2 26.8 %collective-permute-start.8 = (bf16[144,1536]{1,0:T(8,128)(2,1)}, bf16[144,1536]{1,0:T(8,128)(2,1)S(1)}, u32[]{:S(2)}, u32[]{:S(2)}) collective-permute-start(bf16[144,1536]{1,0:T(8,128)(2,1)} %collective-permute-done.7), channel_id=1, source_target_pairs={{0,16},{4,12},{8,24},{12,4},{16,0},{20,28},{24,8},{28,20},{1,17},{... | collective-permute-start | bytes 1327112 | tf_op jit(solution)/shard_map/ppermute | solution.py:158
  91.1 35.3 %collective-permute-start.5 = (bf16[144,1536]{1,0:T(8,128)(2,1)S(1)}, bf16[144,1536]{1,0:T(8,128)(2,1)S(1)}, u32[]{:S(2)}, u32[]{:S(2)}) collective-permute-start(bf16[144,1536]{1,0:T(8,128)(2,1)S(1)} %copy-done.45), channel_id=1, source_target_pairs={{0,16},{4,12},{8,24},{12,4},{16,0},{20,28},{24,8},{28,20},{1,17},{... | collective-permute-start | bytes 1327112 | tf_op jit(solution)/shard_map/ppermute | solution.py:158
  117.0 23.3 %collective-permute-start.9 = (bf16[288,1536]{1,0:T(8,128)(2,1)S(1)}, bf16[288,1536]{1,0:T(8,128)(2,1)S(1)}, u32[]{:S(2)}, u32[]{:S(2)}) collective-permute-start(bf16[288,1536]{1,0:T(8,128)(2,1)S(1)} %constant_dynamic-update-slice_fusion.10.refs_4_), channel_id=1, source_target_pairs={{0,8},{4,20},{8,0},{12,28},{16,24},{20,4},{24,16},{28,12},{1,9},{5... | collective-permute-start | bytes 2654216 | tf_op jit(solution)/shard_map/ppermute | solution.py:158
  118.5 17.3 %collective-permute-start.13 = (bf16[144,1536]{1,0:T(8,128)(2,1)}, bf16[144,1536]{1,0:T(8,128)(2,1)S(1)}, u32[]{:S(2)}, u32[]{:S(2)}) collective-permute-start(bf16[144,1536]{1,0:T(8,128)(2,1)} %collective-permute-done.10), channel_id=1, source_target_pairs={{0,16},{4,12},{8,24},{12,4},{16,0},{20,28},{24,8},{28,20},{1,17},{... | collective-permute-start | bytes 1327112 | tf_op jit(solution)/shard_map/ppermute | solution.py:158
  126.4 20.6 %collective-permute-start.6 = (bf16[288,1536]{1,0:T(8,128)(2,1)S(1)}, bf16[288,1536]{1,0:T(8,128)(2,1)S(1)}, u32[]{:S(2)}, u32[]{:S(2)}) collective-permute-start(bf16[288,1536]{1,0:T(8,128)(2,1)S(1)} %constant_dynamic-update-slice_fusion.8.refs_2_), channel_id=1, source_target_pairs={{0,8},{4,20},{8,0},{12,28},{16,24},{20,4},{24,16},{28,12},{1,9},{5... | collective-permute-start | bytes 2654216 | tf_op jit(solution)/shard_map/ppermute | solution.py:158
  135.9 20.7 %collective-permute-start.14 = (bf16[288,1536]{1,0:T(8,128)(2,1)S(1)}, bf16[288,1536]{1,0:T(8,128)(2,1)}, u32[]{:S(2)}, u32[]{:S(2)}) collective-permute-start(bf16[288,1536]{1,0:T(8,128)(2,1)S(1)} %constant_dynamic-update-slice_fusion.12.refs_6_), channel_id=1, source_target_pairs={{0,8},{4,20},{8,0},{12,28},{16,24},{20,4},{24,16},{28,12},{1,9},{5... | collective-permute-start | bytes 2654216 | tf_op jit(solution)/shard_map/ppermute | solution.py:158
  169.4 19.1 %collective-permute-start.20 = (bf16[4,2,192,1280]{3,2,1,0:T(8,128)(2,1)}, bf16[4,2,192,1280]{3,2,1,0:T(8,128)(2,1)}, u32[]{:S(2)}, u32[]{:S(2)}) collective-permute-start(bf16[4,2,192,1280]{3,2,1,0:T(8,128)(2,1)} %all-to-all-done.mine_ref), channel_id=1, source_target_pairs={{0,4},{4,0},{8,12},{12,8},{16,20},{20,16},{24,28},{28,24},{1,5},{5... | collective-permute-start | bytes 11796488 | tf_op jit(solution)/shard_map/ppermute | solution.py:158
  180.2 28.6 %collective-permute-start.27 = (bf16[128,1536]{1,0:T(8,128)(2,1)S(1)}, bf16[128,1536]{1,0:T(8,128)(2,1)}, u32[]{:S(2)}, u32[]{:S(2)}) collective-permute-start(bf16[128,1536]{1,0:T(8,128)(2,1)S(1)} %multiply_convert_fusion.1), channel_id=1, source_target_pairs={{0,3},{1,0},{2,1},{3,2},{4,7},{5,4},{6,5},{7,6},{8,11},{9,8},{10,9... | collective-permute-start | bytes 1179656 | tf_op jit(solution)/shard_map/ppermute | solution.py:183
  181.9 26.9 %collective-permute-start.23 = (bf16[128,1536]{1,0:T(8,128)(2,1)S(1)}, bf16[128,1536]{1,0:T(8,128)(2,1)}, u32[]{:S(2)}, u32[]{:S(2)}) collective-permute-start(bf16[128,1536]{1,0:T(8,128)(2,1)S(1)} %multiply_convert_fusion.1), channel_id=1, source_target_pairs={{0,1},{1,2},{2,3},{3,0},{4,5},{5,6},{6,7},{7,4},{8,9},{9,10},{10,1... | collective-permute-start | bytes 1179656 | tf_op jit(solution)/shard_map/ppermute | solution.py:183
  182.6 34.1 %collective-permute-start.18 = (bf16[128,1536]{1,0:T(8,128)(2,1)S(1)}, bf16[128,1536]{1,0:T(8,128)(2,1)}, u32[]{:S(2)}, u32[]{:S(2)}) collective-permute-start(bf16[128,1536]{1,0:T(8,128)(2,1)S(1)} %multiply_convert_fusion.1), channel_id=1, source_target_pairs={{0,2},{1,3},{2,0},{3,1},{4,6},{5,7},{6,4},{7,5},{8,10},{9,11},{10,... | collective-permute-start | bytes 1179656 | tf_op jit(solution)/shard_map/ppermute | solution.py:183
  187.0 33.5 %collective-permute-start.25 = (bf16[256,1536]{1,0:T(8,128)(2,1)S(1)}, bf16[256,1536]{1,0:T(8,128)(2,1)S(1)}, u32[]{:S(2)}, u32[]{:S(2)}) collective-permute-start(bf16[256,1536]{1,0:T(8,128)(2,1)S(1)} %pad_maximum_fusion.3.refs_0_), channel_id=1, source_target_pairs={{0,8},{4,20},{8,0},{12,28},{16,24},{20,4},{24,16},{28,12},{1,9},{5... | collective-permute-start | bytes 2359304 | tf_op jit(solution)/shard_map/ppermute | solution.py:158
  216.7 21.7 %collective-permute-start.21 = (bf16[128,1536]{1,0:T(8,128)(2,1)}, bf16[128,1536]{1,0:T(8,128)(2,1)S(1)}, u32[]{:S(2)}, u32[]{:S(2)}) collective-permute-start(bf16[128,1536]{1,0:T(8,128)(2,1)} %collective-permute-done.18), channel_id=1, source_target_pairs={{0,16},{4,12},{8,24},{12,4},{16,0},{20,28},{24,8},{28,20},{1,17},{... | collective-permute-start | bytes 1179656 | tf_op jit(solution)/shard_map/ppermute | solution.py:158
  217.4 20.1 %collective-permute-start.24 = (bf16[128,1536]{1,0:T(8,128)(2,1)}, bf16[128,1536]{1,0:T(8,128)(2,1)S(1)}, u32[]{:S(2)}, u32[]{:S(2)}) collective-permute-start(bf16[128,1536]{1,0:T(8,128)(2,1)} %collective-permute-done.23), channel_id=1, source_target_pairs={{0,16},{4,12},{8,24},{12,4},{16,0},{20,28},{24,8},{28,20},{1,17},{... | collective-permute-start | bytes 1179656 | tf_op jit(solution)/shard_map/ppermute | solution.py:158
  218.7 17.4 %collective-permute-start.28 = (bf16[128,1536]{1,0:T(8,128)(2,1)}, bf16[128,1536]{1,0:T(8,128)(2,1)S(1)}, u32[]{:S(2)}, u32[]{:S(2)}) collective-permute-start(bf16[128,1536]{1,0:T(8,128)(2,1)} %collective-permute-done.27), channel_id=1, source_target_pairs={{0,16},{4,12},{8,24},{12,4},{16,0},{20,28},{24,8},{28,20},{1,17},{... | collective-permute-start | bytes 1179656 | tf_op jit(solution)/shard_map/ppermute | solution.py:158
  233.2 33.3 %collective-permute-start.30 = (bf16[256,1536]{1,0:T(8,128)(2,1)S(1)}, bf16[256,1536]{1,0:T(8,128)(2,1)S(1)}, u32[]{:S(2)}, u32[]{:S(2)}) collective-permute-start(bf16[256,1536]{1,0:T(8,128)(2,1)S(1)} %get-tuple-element.184), channel_id=1, source_target_pairs={{0,8},{4,20},{8,0},{12,28},{16,24},{20,4},{24,16},{28,12},{1,9},{5... | collective-permute-start | bytes 2359304 | tf_op jit(solution)/shard_map/ppermute | solution.py:158
  236.2 32.0 %collective-permute-start.32 = (bf16[256,1536]{1,0:T(8,128)(2,1)S(1)}, bf16[256,1536]{1,0:T(8,128)(2,1)S(1)}, u32[]{:S(2)}, u32[]{:S(2)}) collective-permute-start(bf16[256,1536]{1,0:T(8,128)(2,1)S(1)} %constant_dynamic-update-slice_fusion.18.refs_0_), channel_id=1, source_target_pairs={{0,8},{4,20},{8,0},{12,28},{16,24},{20,4},{24,16},{28,12},{1,9},{5... | collective-permute-start | bytes 2359304 | tf_op jit(solution)/shard_map/ppermute | solution.py:158
  237.5 30.7 %collective-permute-start.26 = (bf16[256,1536]{1,0:T(8,128)(2,1)S(1)}, bf16[256,1536]{1,0:T(8,128)(2,1)S(1)}, u32[]{:S(2)}, u32[]{:S(2)}) collective-permute-start(bf16[256,1536]{1,0:T(8,128)(2,1)S(1)} %constant_dynamic-update-slice_fusion.16.refs_0_), channel_id=1, source_target_pairs={{0,8},{4,20},{8,0},{12,28},{16,24},{20,4},{24,16},{28,12},{1,9},{5... | collective-permute-start | bytes 2359304 | tf_op jit(solution)/shard_map/ppermute | solution.py:158
  238.4 60.1 %collective-permute-start.22 = (bf16[256,1536]{1,0:T(8,128)(2,1)S(1)}, bf16[256,1536]{1,0:T(8,128)(2,1)S(1)}, u32[]{:S(2)}, u32[]{:S(2)}) collective-permute-start(bf16[256,1536]{1,0:T(8,128)(2,1)S(1)} %constant_dynamic-update-slice_fusion.14.refs_0_), channel_id=1, source_target_pairs={{0,8},{4,20},{8,0},{12,28},{16,24},{20,4},{24,16},{28,12},{1,9},{5... | collective-permute-start | bytes 2359304 | tf_op jit(solution)/shard_map/ppermute | solution.py:158
  266.8 28.3 %collective-permute-start.31 = (bf16[128,1536]{1,0:T(8,128)(2,1)S(1)}, bf16[128,1536]{1,0:T(8,128)(2,1)}, u32[]{:S(2)}, u32[]{:S(2)}) collective-permute-start(bf16[128,1536]{1,0:T(8,128)(2,1)S(1)} %slice.523), channel_id=1, source_target_pairs={{0,16},{4,12},{8,24},{12,4},{16,0},{20,28},{24,8},{28,20},{1,17},{... | collective-permute-start | bytes 1179656 | tf_op jit(solution)/shard_map/ppermute | solution.py:158
  281.5 16.0 %collective-permute-start.29 = (bf16[256,1536]{1,0:T(8,128)(2,1)S(1)}, bf16[256,1536]{1,0:T(8,128)(2,1)S(1)}, u32[]{:S(2)}, u32[]{:S(2)}) collective-permute-start(bf16[256,1536]{1,0:T(8,128)(2,1)S(1)} %get-tuple-element.183), channel_id=1, source_target_pairs={{0,8},{4,20},{8,0},{12,28},{16,24},{20,4},{24,16},{28,12},{1,9},{5... | collective-permute-start | bytes 2359304 | tf_op jit(solution)/shard_map/ppermute | solution.py:158
  296.2 25.8 %collective-permute-start.35 = (bf16[256,1536]{1,0:T(8,128)(2,1)S(1)}, bf16[256,1536]{1,0:T(8,128)(2,1)S(1)}, u32[]{:S(2)}, u32[]{:S(2)}) collective-permute-start(bf16[256,1536]{1,0:T(8,128)(2,1)S(1)} %get-tuple-element.202), channel_id=1, source_target_pairs={{0,8},{4,20},{8,0},{12,28},{16,24},{20,4},{24,16},{28,12},{1,9},{5... | collective-permute-start | bytes 2359304 | tf_op jit(solution)/shard_map/ppermute | solution.py:158
  298.5 35.1 %collective-permute-start.33 = (bf16[128,1536]{1,0:T(8,128)(2,1)}, bf16[128,1536]{1,0:T(8,128)(2,1)}, u32[]{:S(2)}, u32[]{:S(2)}) collective-permute-start(bf16[128,1536]{1,0:T(8,128)(2,1)} %slice.522), channel_id=1, source_target_pairs={{0,16},{4,12},{8,24},{12,4},{16,0},{20,28},{24,8},{28,20},{1,17},{... | collective-permute-start | bytes 1179656 | tf_op jit(solution)/shard_map/ppermute | solution.py:158
  321.4 16.5 %collective-permute-start.38 = (bf16[256,1536]{1,0:T(8,128)(2,1)S(1)}, bf16[256,1536]{1,0:T(8,128)(2,1)S(1)}, u32[]{:S(2)}, u32[]{:S(2)}) collective-permute-start(bf16[256,1536]{1,0:T(8,128)(2,1)S(1)} %get-tuple-element.204), channel_id=1, source_target_pairs={{0,8},{4,20},{8,0},{12,28},{16,24},{20,4},{24,16},{28,12},{1,9},{5... | collective-permute-start | bytes 2359304 | tf_op jit(solution)/shard_map/ppermute | solution.py:158
  334.6 28.1 %collective-permute-start.34 = (bf16[128,1536]{1,0:T(8,128)(2,1)S(1)}, bf16[128,1536]{1,0:T(8,128)(2,1)}, u32[]{:S(2)}, u32[]{:S(2)}) collective-permute-start(bf16[128,1536]{1,0:T(8,128)(2,1)S(1)} %fusion.55), channel_id=1, source_target_pairs={{0,3},{1,0},{2,1},{3,2},{4,7},{5,4},{6,5},{7,6},{8,11},{9,8},{10,9... | collective-permute-start | bytes 1179656 | tf_op jit(solution)/shard_map/ppermute | solution.py:183
  342.0 20.7 %collective-permute-start.37 = (bf16[128,1536]{1,0:T(8,128)(2,1)S(1)}, bf16[128,1536]{1,0:T(8,128)(2,1)S(1)}, u32[]{:S(2)}, u32[]{:S(2)}) collective-permute-start(bf16[128,1536]{1,0:T(8,128)(2,1)S(1)} %fusion.54), channel_id=1, source_target_pairs={{0,1},{1,2},{2,3},{3,0},{4,5},{5,6},{6,7},{7,4},{8,9},{9,10},{10,1... | collective-permute-start | bytes 1179656 | tf_op jit(solution)/shard_map/ppermute | solution.py:183
  351.7 17.3 %collective-permute-start.40 = (bf16[128,1536]{1,0:T(8,128)(2,1)S(1)}, bf16[128,1536]{1,0:T(8,128)(2,1)S(1)}, u32[]{:S(2)}, u32[]{:S(2)}) collective-permute-start(bf16[128,1536]{1,0:T(8,128)(2,1)S(1)} %fusion.53), channel_id=1, source_target_pairs={{0,2},{1,3},{2,0},{3,1},{4,6},{5,7},{6,4},{7,5},{8,10},{9,11},{10,... | collective-permute-start | bytes 1179656 | tf_op jit(solution)/shard_map/ppermute | solution.py:183
  389.0 25.2 %collective-permute-start.42 = (bf16[4,2,192,1280]{3,2,1,0:T(8,128)(2,1)}, bf16[4,2,192,1280]{3,2,1,0:T(8,128)(2,1)}, u32[]{:S(2)}, u32[]{:S(2)}) collective-permute-start(bf16[4,2,192,1280]{3,2,1,0:T(8,128)(2,1)} %get-tuple-element.224), channel_id=1, source_target_pairs={{0,4},{4,0},{8,12},{12,8},{16,20},{20,16},{24,28},{28,24},{1,5},{5... | collective-permute-start | bytes 11796488 | tf_op jit(solution)/shard_map/ppermute | solution.py:158
  421.5 51.1 %all-to-all-start.1 = ((bf16[4,2,192,1280]{3,2,1,0:T(8,128)(2,1)}), bf16[4,2,192,1280]{3,2,1,0:T(8,128)(2,1)}, u32[]{:S(2)}, u32[]{:S(2)}) async-start(bf16[4,2,192,1280]{3,2,1,0:T(8,128)(2,1)} %add_convert_fusion), calls=%async_computation.2 | async-start | bytes 7864320 | tf_op jit(solution)/shard_map/all_to_all | solution.py:942
  439.6 27.2 %collective-permute-start.57 = (f32[128,1536]{1,0:T(8,128)S(1)}, f32[128,1536]{1,0:T(8,128)}, u32[]{:S(2)}, u32[]{:S(2)}) collective-permute-start(f32[128,1536]{1,0:T(8,128)S(1)} %slice.393), channel_id=1, source_target_pairs={{0,4},{4,0},{8,12},{12,8},{16,20},{20,16},{24,28},{28,24},{1,5},{5... | collective-permute-start | bytes 2359304 | tf_op jit(solution)/shard_map/ppermute | solution.py:158
  446.5 50.7 %collective-permute-start.52 = (bf16[288,1536]{1,0:T(8,128)(2,1)}, bf16[288,1536]{1,0:T(8,128)(2,1)}, u32[]{:S(2)}, u32[]{:S(2)}) collective-permute-start(bf16[288,1536]{1,0:T(8,128)(2,1)} %get-tuple-element.369), channel_id=1, source_target_pairs={{0,8},{4,20},{8,0},{12,28},{16,24},{20,4},{24,16},{28,12},{1,9},{5... | collective-permute-start | bytes 2654216 | tf_op jit(solution)/shard_map/ppermute | solution.py:158
  448.4 48.8 %collective-permute-start.49 = (bf16[288,1536]{1,0:T(8,128)(2,1)}, bf16[288,1536]{1,0:T(8,128)(2,1)}, u32[]{:S(2)}, u32[]{:S(2)}) collective-permute-start(bf16[288,1536]{1,0:T(8,128)(2,1)} %get-tuple-element.370), channel_id=1, source_target_pairs={{0,8},{4,20},{8,0},{12,28},{16,24},{20,4},{24,16},{28,12},{1,9},{5... | collective-permute-start | bytes 2654216 | tf_op jit(solution)/shard_map/ppermute | solution.py:158
  448.5 51.8 %collective-permute-start.47 = (bf16[288,1536]{1,0:T(8,128)(2,1)}, bf16[288,1536]{1,0:T(8,128)(2,1)}, u32[]{:S(2)}, u32[]{:S(2)}) collective-permute-start(bf16[288,1536]{1,0:T(8,128)(2,1)} %get-tuple-element.371), channel_id=1, source_target_pairs={{0,8},{4,20},{8,0},{12,28},{16,24},{20,4},{24,16},{28,12},{1,9},{5... | collective-permute-start | bytes 2654216 | tf_op jit(solution)/shard_map/ppermute | solution.py:158
  450.4 59.4 %collective-permute-start.43 = (bf16[288,1536]{1,0:T(8,128)(2,1)}, bf16[288,1536]{1,0:T(8,128)(2,1)}, u32[]{:S(2)}, u32[]{:S(2)}) collective-permute-start(bf16[288,1536]{1,0:T(8,128)(2,1)} %get-tuple-element.372), channel_id=1, source_target_pairs={{0,8},{4,20},{8,0},{12,28},{16,24},{20,4},{24,16},{28,12},{1,9},{5... | collective-permute-start | bytes 2654216 | tf_op jit(solution)/shard_map/ppermute | solution.py:158
  466.7 77.5 %collective-permute-start.56 = (f32[10,64,1536]{2,1,0:T(8,128)}, f32[10,64,1536]{2,1,0:T(8,128)}, u32[]{:S(2)}, u32[]{:S(2)}) collective-permute-start(f32[10,64,1536]{2,1,0:T(8,128)} %get-tuple-element.239), channel_id=1, source_target_pairs={{0,4},{4,0},{8,12},{12,8},{16,20},{20,16},{24,28},{28,24},{1,5},{5... | collective-permute-start | bytes 11796488 | tf_op jit(solution)/shard_map/ppermute | solution.py:158
  521.3 16.3 %collective-permute-start.53 = (bf16[144,1536]{1,0:T(8,128)(2,1)S(1)}, bf16[144,1536]{1,0:T(8,128)(2,1)S(1)}, u32[]{:S(2)}, u32[]{:S(2)}) collective-permute-start(bf16[144,1536]{1,0:T(8,128)(2,1)S(1)} %slice.515), channel_id=1, source_target_pairs={{0,16},{4,12},{8,24},{12,4},{16,0},{20,28},{24,8},{28,20},{1,17},{... | collective-permute-start | bytes 1327112 | tf_op jit(solution)/shard_map/ppermute | solution.py:158
  533.0 25.4 %collective-permute-start.51 = (bf16[144,1536]{1,0:T(8,128)(2,1)S(1)}, bf16[144,1536]{1,0:T(8,128)(2,1)}, u32[]{:S(2)}, u32[]{:S(2)}) collective-permute-start(bf16[144,1536]{1,0:T(8,128)(2,1)S(1)} %fusion.42), channel_id=1, source_target_pairs={{0,1},{1,2},{2,3},{3,0},{4,5},{5,6},{6,7},{7,4},{8,9},{9,10},{10,1... | collective-permute-start | bytes 1327112 | tf_op jit(solution)/shard_map/ppermute | solution.py:183
  538.5 19.8 %collective-permute-start.55 = (bf16[144,1536]{1,0:T(8,128)(2,1)}, bf16[144,1536]{1,0:T(8,128)(2,1)}, u32[]{:S(2)}, u32[]{:S(2)}) collective-permute-start(bf16[144,1536]{1,0:T(8,128)(2,1)} %fusion.41), channel_id=1, source_target_pairs={{0,3},{1,0},{2,1},{3,2},{4,7},{5,4},{6,5},{7,6},{8,11},{9,8},{10,9... | collective-permute-start | bytes 1327112 | tf_op jit(solution)/shard_map/ppermute | solution.py:183
  (92 other events, 1044.6 us)
Sparse Core Ops, SparseCore 0:
  54.3 122.3 all-gather.1
  379.7 112.0 reduce-scatter.1

commit v7 on v6

--- a/solution.py
+++ b/solution.py
@@ -264,31 +264,6 @@
         [
             rows[:, low:high].reshape(count, KEY_VALUE_HEADS // 2, 2, -1)[:, :, parity]
             .reshape(count, -1)
-            for low, high in bounds
-        ],
-        1,
-    )
-
-
-def join_parities(even, odd):
-    count = even.shape[0]
-    query_half = QUERY_HEADS * HEAD_SIZE // 2
-    key_half = KEY_VALUE_HEADS * HEAD_SIZE // 2
-    bounds = (
-        (0, query_half),
-        (query_half, query_half + key_half),
-        (query_half + key_half, query_half + 2 * key_half),
-    )
-    heads = KEY_VALUE_HEADS // 2
-    return jnp.concatenate(
-        [
-            jnp.stack(
-                [
-                    even[:, low:high].reshape(count, heads, -1),
-                    odd[:, low:high].reshape(count, heads, -1),
-                ],
-                2,
-            ).reshape(count, -1)
             for low, high in bounds
         ],
         1,
@@ -750,6 +725,42 @@
             transcendentals=experts * rows * both,
         ),
     )(weight, first, second, grads)
+
+
+def adam_heads_kernel(
+    place_ref, here_ref, there_ref, w_ref, first_ref, second_ref, grad_ref, *new_refs
+):
+    mine_even = place_ref[1] == 0
+    rows = w_ref.shape[0]
+    heads = KEY_VALUE_HEADS // 2
+    start = 0
+    for total in (QUERY_HEADS, KEY_VALUE_HEADS, KEY_VALUE_HEADS):
+        width = total * HEAD_SIZE // KEY_VALUE_HEADS
+        for i in range(heads):
+            columns = slice(start // 2 + width * i, start // 2 + width * (i + 1))
+            mine, theirs = here_ref[:rows, columns], there_ref[:rows, columns]
+            at = start + 2 * width * i
+            grad_ref[:, at : at + 2 * width] = jnp.concatenate(
+                [jnp.where(mine_even, mine, theirs), jnp.where(mine_even, theirs, mine)], 1
+            )
+        start += 2 * width * heads
+    found = adam_step(
+        w_ref[...], grad_ref[...], first_ref[...], second_ref[...], learn_rate, weight_decay
+    )
+    for ref, value in zip(new_refs, found):
+        ref[...] = value
+
+
+def adam_heads(place, here, there, weight, first, second):
+    return pl.pallas_call(
+        adam_heads_kernel,
+        in_specs=[pl.BlockSpec(memory_space=pltpu.SMEM)]
+        + [pl.BlockSpec(memory_space=pltpu.VMEM)] * 5,
+        out_shape=[jax.ShapeDtypeStruct(weight.shape, jnp.float32)] * 4,
+        cost_estimate=pl.CostEstimate(
+            flops=20 * weight.size, bytes_accessed=40 * weight.size, transcendentals=weight.size
+        ),
+    )(place, here, there, weight, first, second)
 
 
 def shards_moved(
@@ -1008,9 +1019,8 @@
     part_gains = (
         here[:, half_columns : half_columns + 2] + there[:, half_columns : half_columns + 2]
     ).T
-    here, there = here[:, :half_columns], there[:, :half_columns]
-    part_qkv = join_parities(
-        jnp.where(core == 0, here, there), jnp.where(core == 0, there, here)
+    part_qkv, new_qkv, new_first_qkv, new_second_qkv = adam_heads(
+        place, summed, there, w_qkv, first_moment_projection, second_moment_projection
     )
 
     grad_normed_parts = select_columns(grad_normed_parts, from_gathered)
@@ -1022,9 +1032,6 @@
         hat_one - inputs * scale_one**2 * jnp.mean(hat_one * inputs, -1, keepdims=True)
     )
 
-    new_qkv, new_first_qkv, new_second_qkv = adam_step(
-        w_qkv, part_qkv, first_moment_projection, second_moment_projection, learn_rate, weight_decay
-    )
     new_out, new_first_out, new_second_out = adam_step(
         w_out, part_out, first_out, second_out, out_rate, weight_decay
     )

time: 592 us -> 585 us (0.988)
  local copies, waits for them, and re-layouts: 40.4 us -> 33.6 us
    sub x4 -> x3, other arithmetic: 16.9 us -> 14.1 us  [adam_step(): return (weight - step_rate * (update + shrink * weight), first, second)]
    unnamed x173 -> x171, local copies, waits for them, and re-layouts: 17.9 us -> 16.9 us
  transfers between devices with their start and end apart: 63 -> 63, of which waited for: 22 -> 22; matrix products, arithmetic and copies ran while one was open for 21% -> 19% of each run, Pallas kernels for 34% -> 35%
where the time goes in v7:
time: 585 us; the launch traced here: 579 us
  Pallas kernels  214 us (37%)
  waiting for transfers between devices  148 us (25%)
  starting transfers between devices  75.3 us (13%)
  other arithmetic  58.7 us (10%)
  local copies, waits for them, and re-layouts  33.6 us (6%)
  matrix products  33 us (6%)
  between operations  16.1 us (3%)
    ppermute x47, waiting for transfers between devices, swap(): return lax.ppermute(rows, 'dp', [(i, i ^ pick(i)) for i in range(count)])  113 us
    pallas_call x7, Pallas kernels, expert_block(): pl.pallas_call(functools.partial(expert_kernel, per_step=per_step, count=...  100 us
    pallas_call x5, Pallas kernels, column_grads(): pl.pallas_call(column_grads_kernel, grid_spec=pltpu.PrefetchScalarGridSpe...  45.9 us
    ppermute x47, starting transfers between devices, swap(): return lax.ppermute(rows, 'dp', [(i, i ^ pick(i)) for i in range(count)])  43.9 us
    ppermute x12, waiting for transfers between devices, turn(): lax.ppermute(rows, 'expert', [(i, (i + step) % count) for i in range(coun...  30.2 us
    pallas_call x1, Pallas kernels, adam_columns(): pl.pallas_call(adam_columns_kernel, grid=(experts,), in_specs=[block] * 3...  24.5 us
    ppermute x12, starting transfers between devices, turn(): lax.ppermute(rows, 'expert', [(i, (i + step) % count) for i in range(coun...  21 us
    unnamed x171, local copies, waits for them, and re-layouts  16.9 us
  transfers between devices with their start and end apart: 63, of which 22 were waited for; matrix products, arithmetic and copies ran while one was open for 19% of the time, Pallas kernels for 35%

profile of v7, /device:TPU:0, one launch (start us, length us, event | category | flops | bytes accessed | tf_op | source)
XLA Modules:
  0.0 578.5 jit_solution(9336747681484305010)
XLA Ops:
  27.3 8.2 %shard_map.381 = bf16[4,2,192,1280]{3,2,1,0:T(8,128)(2,1)} custom-call(f32[10,192,1024]{2,1,0:T(8,128)} %w_ref.2), custom_call_target="tpu_custom_call" | custom-call | bytes 11796480 | tf_op jit(solution)/shard_map/pallas_call | solution.py:308
  40.0 6.9 %collective-permute-done.7 = bf16[144,1536]{1,0:T(8,128)(2,1)} collective-permute-done((bf16[144,1536]{1,0:T(8,128)(2,1)}, bf16[144,1536]{1,0:T(8,128)(2,1)}, u32[]{:S(2)}, u32[]{:S(2)}) %collective-permute-start.7) | collective-permute-done | bytes 442400 | tf_op jit(solution)/shard_map/ppermute | solution.py:183
  46.8 7.3 %collective-permute-done.10 = bf16[144,1536]{1,0:T(8,128)(2,1)} collective-permute-done((bf16[144,1536]{1,0:T(8,128)(2,1)S(1)}, bf16[144,1536]{1,0:T(8,128)(2,1)}, u32[]{:S(2)}, u32[]{:S(2)}) %collective-permute-start.10) | collective-permute-done | bytes 442400 | tf_op jit(solution)/shard_map/ppermute | solution.py:183
  56.0 4.9 all-to-all-start
  61.3 24.8 %collective-permute-done.2 = bf16[144,1536]{1,0:T(8,128)(2,1)S(1)} collective-permute-done((bf16[144,1536]{1,0:T(8,128)(2,1)}, bf16[144,1536]{1,0:T(8,128)(2,1)S(1)}, u32[]{:S(2)}, u32[]{:S(2)}) %collective-permute-start.2) | collective-permute-done | bytes 442400 | tf_op jit(solution)/shard_map/ppermute | solution.py:158
  93.4 23.5 %collective-permute-done.8 = bf16[144,1536]{1,0:T(8,128)(2,1)S(1)} collective-permute-done((bf16[144,1536]{1,0:T(8,128)(2,1)}, bf16[144,1536]{1,0:T(8,128)(2,1)S(1)}, u32[]{:S(2)}, u32[]{:S(2)}) %collective-permute-start.8) | collective-permute-done | bytes 442400 | tf_op jit(solution)/shard_map/ppermute | solution.py:158
  119.0 7.4 %collective-permute-done.5 = bf16[144,1536]{1,0:T(8,128)(2,1)S(1)} collective-permute-done((bf16[144,1536]{1,0:T(8,128)(2,1)S(1)}, bf16[144,1536]{1,0:T(8,128)(2,1)S(1)}, u32[]{:S(2)}, u32[]{:S(2)}) %collective-permute-start.5) | collective-permute-done | bytes 442400 | tf_op jit(solution)/shard_map/ppermute | solution.py:158
  129.0 6.8 %collective-permute-done.13 = bf16[144,1536]{1,0:T(8,128)(2,1)S(1)} collective-permute-done((bf16[144,1536]{1,0:T(8,128)(2,1)}, bf16[144,1536]{1,0:T(8,128)(2,1)S(1)}, u32[]{:S(2)}, u32[]{:S(2)}) %collective-permute-start.13) | collective-permute-done | bytes 442400 | tf_op jit(solution)/shard_map/ppermute | solution.py:158
  140.3 6.8 %collective-permute-done.6.refs_3_ = bf16[288,1536]{1,0:T(8,128)(2,1)S(1)} collective-permute-done((bf16[288,1536]{1,0:T(8,128)(2,1)S(1)}, bf16[288,1536]{1,0:T(8,128)(2,1)S(1)}, u32[]{:S(2)}, u32[]{:S(2)}) %collective-permute-start.6) | collective-permute-done | bytes 884768 | tf_op jit(solution)/shard_map/ppermute | solution.py:158
  148.0 8.7 %collective-permute-done.14.refs_7_ = bf16[288,1536]{1,0:T(8,128)(2,1)} collective-permute-done((bf16[288,1536]{1,0:T(8,128)(2,1)S(1)}, bf16[288,1536]{1,0:T(8,128)(2,1)}, u32[]{:S(2)}, u32[]{:S(2)}) %collective-permute-start.14) | collective-permute-done | bytes 884768 | tf_op jit(solution)/shard_map/ppermute | solution.py:158
  156.7 6.3 %shard_map.382 = (bf16[1536,1280]{1,0:T(8,128)(2,1)}, bf16[1536,128]{1,0:T(8,128)(2,1)}, bf16[768,1536]{1,0:T(8,128)(2,1)}) custom-call(bf16[288,1536]{1,0:T(8,128)(2,1)} %copy-done.22, bf16[288,1536]{1,0:T(8,128)(2,1)} %copy-done.40, bf16[288,1536]{1,0:T(8,128)(2,1)} %copy-done.26, bf16[288,1536]{1,0:T(8,128)(2,1)} %copy-done.42, ...), custom_call_target="tpu_custom_call" | custom-call | bytes 14155776 | tf_op jit(solution)/shard_map/pallas_call | solution.py:391
  164.2 3.3 multiply_convert_fusion
  183.4 3.4 collective-permute-done.19
  188.5 6.6 %shard_map.383 = (bf16[1536,1280]{1,0:T(8,128)(2,1)}, bf16[1536,1280]{1,0:T(8,128)(2,1)}) custom-call(s32[7]{0:T(128)} %pad_add_fusion.1.place_ref, bf16[4,2,192,1280]{3,2,1,0:T(8,128)(2,1)} %all-to-all-done.mine_ref, bf16[4,2,192,1280]{3,2,1,0:T(8,128)(2,1)} %collective-permute-done.20.theirs_ref), custom_call_target="tpu_custom_call" | custom-call | bytes 15728640 | tf_op jit(solution)/shard_map/pallas_call | solution.py:344
  195.1 13.6 %shard_map.384 = (f32[256,1536]{1,0:T(8,128)S(1)}, bf16[2048,1280]{1,0:T(8,128)(2,1)}, bf16[2048,1280]{1,0:T(8,128)(2,1)}, bf16[2048,1280]{1,0:T(8,128)(2,1)}, b...) custom-call(s32[7]{0:T(128)S(1)} %copy-done.5, ...), custom_call_target="tpu_custom_call" | custom-call | flops 6039797760 | bytes 23199744 | tf_op jit(solution)/shard_map/pallas_call | solution.py:561
  208.8 7.9 %collective-permute-done.18 = bf16[128,1536]{1,0:T(8,128)(2,1)} collective-permute-done((bf16[128,1536]{1,0:T(8,128)(2,1)S(1)}, bf16[128,1536]{1,0:T(8,128)(2,1)}, u32[]{:S(2)}, u32[]{:S(2)}) %collective-permute-start.18) | collective-permute-done | bytes 393248 | tf_op jit(solution)/shard_map/ppermute | solution.py:183
  220.4 12.8 %shard_map.385 = (bf16[256,1536]{1,0:T(8,128)(2,1)S(1)}, bf16[2048,1280]{1,0:T(8,128)(2,1)}, bf16[2048,1280]{1,0:T(8,128)(2,1)}, bf16[2048,1280]{1,0:T(8,128)(2,...) custom-call(s32[7]{0:T(128)S(1)} %copy-done.5, ...), custom_call_target="tpu_custom_call", output_to_operand_aliasing={{1}: (6, {}), {2}: (7, {}), {3}: (8, {}), {4}: (9, {}), {5}... | custom-call | flops 6039797760 | bytes 23199744 | tf_op jit(solution)/shard_map/pallas_call | solution.py:561
  239.7 13.4 %shard_map.386 = (f32[256,1536]{1,0:T(8,128)S(1)}, bf16[2048,1280]{1,0:T(8,128)(2,1)}, bf16[2048,1280]{1,0:T(8,128)(2,1)}, bf16[2048,1280]{1,0:T(8,128)(2,1)}, b...) custom-call(s32[7]{0:T(128)S(1)} %copy-done.5, ...), custom_call_target="tpu_custom_call", output_to_operand_aliasing={{1}: (6, {}), {2}: (7, {}), {3}: (8, {}), {4}: (9, {}), {5}... | custom-call | flops 6039797760 | bytes 23199744 | tf_op jit(solution)/shard_map/pallas_call | solution.py:561
  253.1 13.4 %shard_map.387 = (f32[256,1536]{1,0:T(8,128)S(1)}, bf16[2048,1280]{1,0:T(8,128)(2,1)}, bf16[2048,1280]{1,0:T(8,128)(2,1)}, bf16[2048,1280]{1,0:T(8,128)(2,1)}, b...) custom-call(s32[7]{0:T(128)S(1)} %copy-done.5, ...), custom_call_target="tpu_custom_call", output_to_operand_aliasing={{1}: (6, {}), {2}: (7, {}), {3}: (8, {}), {4}: (9, {}), {5}... | custom-call | flops 6039797760 | bytes 23199744 | tf_op jit(solution)/shard_map/pallas_call | solution.py:561
  268.6 12.9 %shard_map.388 = (bf16[256,1536]{1,0:T(8,128)(2,1)S(1)}, bf16[2048,1280]{1,0:T(8,128)(2,1)}, bf16[2048,1280]{1,0:T(8,128)(2,1)}, bf16[2048,1280]{1,0:T(8,128)(2,...) custom-call(s32[7]{0:T(128)S(1)} %copy-done.5, ...), custom_call_target="tpu_custom_call", output_to_operand_aliasing={{1}: (6, {}), {2}: (7, {}), {3}: (8, {}), {4}: (9, {}), {5}... | custom-call | flops 6039797760 | bytes 23199744 | tf_op jit(solution)/shard_map/pallas_call | solution.py:561
  282.4 12.7 %shard_map.389 = (bf16[256,1536]{1,0:T(8,128)(2,1)S(1)}, bf16[2048,1280]{1,0:T(8,128)(2,1)}, bf16[2048,1280]{1,0:T(8,128)(2,1)}, bf16[2048,1280]{1,0:T(8,128)(2,...) custom-call(s32[7]{0:T(128)S(1)} %copy-done.5, ...), custom_call_target="tpu_custom_call", output_to_operand_aliasing={{1}: (6, {}), {2}: (7, {}), {3}: (8, {}), {4}: (9, {}), {5}... | custom-call | flops 6039797760 | bytes 23199744 | tf_op jit(solution)/shard_map/pallas_call | solution.py:561
  299.8 21.6 %shard_map.390 = (f32[256,1536]{1,0:T(8,128)S(1)}, bf16[256,1536]{1,0:T(8,128)(2,1)S(1)}, bf16[2048,1280]{1,0:T(8,128)(2,1)}, bf16[2048,1280]{1,0:T(8,128)(2,1)}...) custom-call(s32[7]{0:T(128)S(1)} %copy-done.5, ...), custom_call_target="tpu_custom_call", output_to_operand_aliasing={{2}: (7, {}), {3}: (8, {}), {4}: (9, {}), {5}: (10, {}), {6... | custom-call | flops 12079595520 | bytes 34603008 | tf_op jit(solution)/shard_map/pallas_call | solution.py:561
  324.4 9.1 %shard_map.391 = (f32[4,2,192,1280]{3,2,1,0:T(8,128)}, bf16[4,2,192,1280]{3,2,1,0:T(8,128)(2,1)}) custom-call(s32[7]{0:T(128)} %pad_add_fusion.1.place_ref, bf16[2048,1536]{1,0:T(8,128)(2,1)} %get-tuple-element.224.rows_ref, bf16[2048,1280]{1,0:T(8,128)(2,1)} %get-tuple-element.210.grad_gate_ref, bf16[2048,1280]{1,0:T(8,128)(2,1)} %get-tuple-element.211.grad_upper_ref), custom_call_target="tpu_custom_call" | custom-call | flops 3221225472 | bytes 13107200 | tf_op jit(solution)/shard_map/pallas_call | solution.py:623
  334.6 3.4 collective-permute-start.34
  342.5 9.1 %shard_map.392 = (f32[4,2,192,1280]{3,2,1,0:T(8,128)}, bf16[4,2,192,1280]{3,2,1,0:T(8,128)(2,1)}) custom-call(s32[7]{0:T(128)} %pad_add_fusion.1.place_ref, bf16[2048,1536]{1,0:T(8,128)(2,1)} %get-tuple-element.224.rows_ref, bf16[2048,1280]{1,0:T(8,128)(2,1)} %get-tuple-element.210.grad_gate_ref, ...), custom_call_target="tpu_custom_call", output_to_operand_aliasing={{0}: (4, {}), {1}: (5, {})} | custom-call | flops 3221225472 | bytes 13107200 | tf_op jit(solution)/shard_map/pallas_call | solution.py:623
  353.7 9.1 %shard_map.393 = (f32[4,2,192,1280]{3,2,1,0:T(8,128)}, bf16[4,2,192,1280]{3,2,1,0:T(8,128)(2,1)}) custom-call(s32[7]{0:T(128)} %pad_add_fusion.1.place_ref, bf16[2048,1536]{1,0:T(8,128)(2,1)} %get-tuple-element.224.rows_ref, bf16[2048,1280]{1,0:T(8,128)(2,1)} %get-tuple-element.210.grad_gate_ref, ...), custom_call_target="tpu_custom_call", output_to_operand_aliasing={{0}: (4, {}), {1}: (5, {})} | custom-call | flops 3221225472 | bytes 13107200 | tf_op jit(solution)/shard_map/pallas_call | solution.py:623
  362.8 6.3 %collective-permute-done.40 = bf16[128,1536]{1,0:T(8,128)(2,1)S(1)} collective-permute-done((bf16[128,1536]{1,0:T(8,128)(2,1)S(1)}, bf16[128,1536]{1,0:T(8,128)(2,1)S(1)}, u32[]{:S(2)}, u32[]{:S(2)}) %collective-permute-start.40) | collective-permute-done | bytes 393248 | tf_op jit(solution)/shard_map/ppermute | solution.py:183
  370.5 9.1 %shard_map.394 = (f32[4,2,192,1280]{3,2,1,0:T(8,128)}, bf16[4,2,192,1280]{3,2,1,0:T(8,128)(2,1)}) custom-call(s32[7]{0:T(128)} %pad_add_fusion.1.place_ref, bf16[2048,1536]{1,0:T(8,128)(2,1)} %get-tuple-element.224.rows_ref, bf16[2048,1280]{1,0:T(8,128)(2,1)} %get-tuple-element.210.grad_gate_ref, ...), custom_call_target="tpu_custom_call", output_to_operand_aliasing={{0}: (4, {}), {1}: (5, {})} | custom-call | flops 3221225472 | bytes 13107200 | tf_op jit(solution)/shard_map/pallas_call | solution.py:623
  379.6 9.4 %shard_map.395 = (f32[4,2,192,1280]{3,2,1,0:T(8,128)}, bf16[4,2,192,1280]{3,2,1,0:T(8,128)(2,1)}) custom-call(s32[7]{0:T(128)} %pad_add_fusion.1.place_ref, bf16[2048,1536]{1,0:T(8,128)(2,1)} %get-tuple-element.224.rows_ref, bf16[2048,1280]{1,0:T(8,128)(2,1)} %get-tuple-element.210.grad_gate_ref, ...), custom_call_target="tpu_custom_call", output_to_operand_aliasing={{0}: (4, {}), {1}: (5, {})} | custom-call | flops 3221225472 | bytes 13107200 | tf_op jit(solution)/shard_map/pallas_call | solution.py:623
  392.6 3.9 collective-permute-done.41
  397.2 3.7 fusion.25
  408.2 3.6 fusion.36
  414.3 7.3 %add_convert_fusion = bf16[4,2,192,1280]{3,2,1,0:T(8,128)(2,1)} fusion(f32[4,2,192,1280]{3,2,1,0:T(8,128)} %get-tuple-element.227, bf16[4,2,192,1280]{3,2,1,0:T(8,128)(2,1)} %collective-permute-done.42), kind=kLoop, calls=%fused_computation.7 | loop fusion | flops 5898240 | bytes 15728640 | tf_op jit(solution)/shard_map/convert_element_type | solution.py:951
  421.6 5.2 all-to-all-start.1
  426.8 5.3 fusion.101
  432.4 5.7 fusion.1
  439.9 4.8 shard_map.396
  450.7 14.1 %shard_map.398 = (f32[10,64,1536]{2,1,0:T(8,128)S(1)}, f32[10,64,1536]{2,1,0:T(8,128)}) custom-call(s32[7]{0:T(128)S(1)} %copy-done.6, bf16[2048,1536]{1,0:T(8,128)(2,1)} %get-tuple-element.240.grads_ref, bf16[2048,1280]{1,0:T(8,128)(2,1)S(1)} %bitcast.123), custom_call_target="tpu_custom_call" | custom-call | flops 8053063680 | bytes 19398656 | tf_op jit(solution)/shard_map/pallas_call | solution.py:670
  468.5 4.2 all-to-all-done.1.grad_ref
  472.7 24.5 %shard_map.397 = (f32[10,192,1024]{2,1,0:T(8,128)}, f32[10,192,1024]{2,1,0:T(8,128)}, f32[10,192,1024]{2,1,0:T(8,128)}, f32[10,192,1024]{2,1,0:T(8,128)}) custom-call(f32[10,192,1024]{2,1,0:T(8,128)} %w_ref.2, f32[10,192,1024]{2,1,0:T(8,128)} %first_ref.2, f32[10,192,1024]{2,1,0:T(8,128)} %second_ref.2, bf16[4,2,192,1280]{3,2,1,0:T(8,128)(2,1)} %all-to-all-done.1.grad_ref), custom_call_target="tpu_custom_call" | custom-call | flops 39321600 | bytes 58982400 | tf_op jit(solution)/shard_map/pallas_call | solution.py:715
  500.4 9.5 %collective-permute-done.43 = bf16[288,1536]{1,0:T(8,128)(2,1)} collective-permute-done((bf16[288,1536]{1,0:T(8,128)(2,1)}, bf16[288,1536]{1,0:T(8,128)(2,1)}, u32[]{:S(2)}, u32[]{:S(2)}) %collective-permute-start.43) | collective-permute-done | bytes 884768 | tf_op jit(solution)/shard_map/ppermute | solution.py:158
  509.8 5.1 bitcast_add_fusion
  523.5 3.4 collective-permute-start.54
  526.9 6.0 %collective-permute-done.50 = bf16[144,1536]{1,0:T(8,128)(2,1)S(1)} collective-permute-done((bf16[144,1536]{1,0:T(8,128)(2,1)S(1)}, bf16[144,1536]{1,0:T(8,128)(2,1)S(1)}, u32[]{:S(2)}, u32[]{:S(2)}) %collective-permute-start.50) | collective-permute-done | bytes 442400 | tf_op jit(solution)/shard_map/ppermute | solution.py:158
  533.7 4.0 collective-permute-done.53
  537.8 4.2 collective-permute-start.55
  543.5 13.1 %multiply_subtract_fusion = (f32[10,64,1536]{2,1,0:T(8,128)}, f32[10,64,1536]{2,1,0:T(8,128)}, f32[10,64,1536]{2,1,0:T(8,128)}, f32[10,64,1536]{2,1,0:T(8,128)}) fusion(f32[10,64,1536]{2,1,0:T(8,128)} %param.31, f32[10,64,1536]{2,1,0:T(8,128)} %param.36, f32[10,64,1536]{2,1,0:T(8,128)} %param.41, f32[10,64,1536]{2,1,0:T(8,128)} %copy-done.2, ...), kind=kLoop, calls=%fused_computation.15 | loop fusion | flops 15728640 | bytes 35389440 | tf_op jit(solution)/shard_map/sub | solution.py:147
  565.9 3.4 shard_map.399
  (437 shorter events, 143.0 us)
Async XLA Ops:
  7.2 187.9 %all-gather.2.cloned.1.call-start = ((), (), s32[]{:S(2)}) async-start(), calls=%async_computation.3 | async-start | bytes 8519680 | tf_op jit(solution)/shard_map/all_gather | solution.py:830
  19.3 18.1 %collective-permute-start.12 = (bf16[256,1664]{1,0:T(8,128)(2,1)S(1)}, bf16[256,1664]{1,0:T(8,128)(2,1)}, u32[]{:S(2)}, u32[]{:S(2)}) collective-permute-start(bf16[256,1664]{1,0:T(8,128)(2,1)S(1)} %pad_maximum_fusion.2), channel_id=1, source_target_pairs={{0,8},{4,20},{8,0},{12,28},{16,24},{20,4},{24,16},{28,12},{1,9},{5... | collective-permute-start | bytes 2555912 | tf_op jit(solution)/shard_map/ppermute | solution.py:158
  23.8 32.2 %collective-permute-start.16 = (s32[1,128]{1,0:T(1,128)S(1)}, s32[1,128]{1,0:T(1,128)S(1)}, u32[]{:S(2)}, u32[]{:S(2)}) collective-permute-start(s32[1,128]{1,0:T(1,128)S(1)} %copy-done.73), channel_id=1, source_target_pairs={{0,4},{4,0},{8,12},{12,8},{16,20},{20,16},{24,28},{28,24},{1,5},{5... | collective-permute-start | bytes 1544 | tf_op jit(solution)/shard_map/ppermute | solution.py:158
  23.8 65.2 %collective-permute-start = (bf16[128,1536]{1,0:T(8,128)(2,1)S(1)}, bf16[128,1536]{1,0:T(8,128)(2,1)}, u32[]{:S(2)}, u32[]{:S(2)}) collective-permute-start(bf16[128,1536]{1,0:T(8,128)(2,1)S(1)} %copy-done.14), channel_id=1, source_target_pairs={{0,4},{4,0},{8,12},{12,8},{16,20},{20,16},{24,28},{28,24},{1,5},{5... | collective-permute-start | bytes 1179656 | tf_op jit(solution)/shard_map/ppermute | solution.py:158
  25.0 21.9 %collective-permute-start.7 = (bf16[144,1536]{1,0:T(8,128)(2,1)}, bf16[144,1536]{1,0:T(8,128)(2,1)}, u32[]{:S(2)}, u32[]{:S(2)}) collective-permute-start(bf16[144,1536]{1,0:T(8,128)(2,1)} %pad_maximum_fusion.6), channel_id=1, source_target_pairs={{0,3},{1,0},{2,1},{3,2},{4,7},{5,4},{6,5},{7,6},{8,11},{9,8},{10,9... | collective-permute-start | bytes 1327112 | tf_op jit(solution)/shard_map/ppermute | solution.py:183
  37.3 16.8 %collective-permute-start.10 = (bf16[144,1536]{1,0:T(8,128)(2,1)S(1)}, bf16[144,1536]{1,0:T(8,128)(2,1)}, u32[]{:S(2)}, u32[]{:S(2)}) collective-permute-start(bf16[144,1536]{1,0:T(8,128)(2,1)S(1)} %collective-permute-done.4), channel_id=1, source_target_pairs={{0,1},{1,2},{2,3},{3,0},{4,5},{5,6},{6,7},{7,4},{8,9},{9,10},{10,1... | collective-permute-start | bytes 1327112 | tf_op jit(solution)/shard_map/ppermute | solution.py:183
  55.2 30.9 %collective-permute-start.2 = (bf16[144,1536]{1,0:T(8,128)(2,1)}, bf16[144,1536]{1,0:T(8,128)(2,1)S(1)}, u32[]{:S(2)}, u32[]{:S(2)}) collective-permute-start(bf16[144,1536]{1,0:T(8,128)(2,1)} %pad_maximum_fusion.6), channel_id=1, source_target_pairs={{0,16},{4,12},{8,24},{12,4},{16,0},{20,28},{24,8},{28,20},{1,17},{... | collective-permute-start | bytes 1327112 | tf_op jit(solution)/shard_map/ppermute | solution.py:158
  56.0 100.7 %all-to-all-start = ((bf16[4,2,192,1280]{3,2,1,0:T(8,128)(2,1)}), bf16[4,2,192,1280]{3,2,1,0:T(8,128)(2,1)}, u32[]{:S(2)}, u32[]{:S(2)}) async-start(bf16[4,2,192,1280]{3,2,1,0:T(8,128)(2,1)} %shard_map.381), calls=%async_computation | async-start | bytes 7864320 | tf_op jit(solution)/shard_map/all_to_all | solution.py:859
  60.9 481.2 %reduce-scatter.2.cloned.1.call-start = ((), (), s32[]{:S(2)}) async-start(), calls=%async_computation.4 | async-start | bytes 7864320 | tf_op jit(solution)/shard_map/reduce_scatter | solution.py:956
  88.9 48.9 %collective-permute-start.15 = (bf16[10,64,1536]{2,1,0:T(8,128)(2,1)S(1)}, bf16[10,64,1536]{2,1,0:T(8,128)(2,1)S(1)}, u32[]{:S(2)}, u32[]{:S(2)}) collective-permute-start(bf16[10,64,1536]{2,1,0:T(8,128)(2,1)S(1)} %convert_element_type.295), channel_id=1, source_target_pairs={{0,4},{4,0},{8,12},{12,8},{16,20},{20,16},{24,28},{28,24},{1,5},{5... | collective-permute-start | bytes 5898248 | tf_op jit(solution)/shard_map/ppermute | solution.py:158
  90.0 50.2 %collective-permute-start.3 = (bf16[288,1536]{1,0:T(8,128)(2,1)S(1)}, bf16[288,1536]{1,0:T(8,128)(2,1)S(1)}, u32[]{:S(2)}, u32[]{:S(2)}) collective-permute-start(bf16[288,1536]{1,0:T(8,128)(2,1)S(1)} %pad_maximum_fusion.1.refs_0_), channel_id=1, source_target_pairs={{0,8},{4,20},{8,0},{12,28},{16,24},{20,4},{24,16},{28,12},{1,9},{5... | collective-permute-start | bytes 2654216 | tf_op jit(solution)/shard_map/ppermute | solution.py:158
  90.1 26.8 %collective-permute-start.8 = (bf16[144,1536]{1,0:T(8,128)(2,1)}, bf16[144,1536]{1,0:T(8,128)(2,1)S(1)}, u32[]{:S(2)}, u32[]{:S(2)}) collective-permute-start(bf16[144,1536]{1,0:T(8,128)(2,1)} %collective-permute-done.7), channel_id=1, source_target_pairs={{0,16},{4,12},{8,24},{12,4},{16,0},{20,28},{24,8},{28,20},{1,17},{... | collective-permute-start | bytes 1327112 | tf_op jit(solution)/shard_map/ppermute | solution.py:158
  91.0 35.4 %collective-permute-start.5 = (bf16[144,1536]{1,0:T(8,128)(2,1)S(1)}, bf16[144,1536]{1,0:T(8,128)(2,1)S(1)}, u32[]{:S(2)}, u32[]{:S(2)}) collective-permute-start(bf16[144,1536]{1,0:T(8,128)(2,1)S(1)} %copy-done.45), channel_id=1, source_target_pairs={{0,16},{4,12},{8,24},{12,4},{16,0},{20,28},{24,8},{28,20},{1,17},{... | collective-permute-start | bytes 1327112 | tf_op jit(solution)/shard_map/ppermute | solution.py:158
  116.9 23.3 %collective-permute-start.9 = (bf16[288,1536]{1,0:T(8,128)(2,1)S(1)}, bf16[288,1536]{1,0:T(8,128)(2,1)S(1)}, u32[]{:S(2)}, u32[]{:S(2)}) collective-permute-start(bf16[288,1536]{1,0:T(8,128)(2,1)S(1)} %constant_dynamic-update-slice_fusion.10.refs_4_), channel_id=1, source_target_pairs={{0,8},{4,20},{8,0},{12,28},{16,24},{20,4},{24,16},{28,12},{1,9},{5... | collective-permute-start | bytes 2654216 | tf_op jit(solution)/shard_map/ppermute | solution.py:158
  118.5 17.3 %collective-permute-start.13 = (bf16[144,1536]{1,0:T(8,128)(2,1)}, bf16[144,1536]{1,0:T(8,128)(2,1)S(1)}, u32[]{:S(2)}, u32[]{:S(2)}) collective-permute-start(bf16[144,1536]{1,0:T(8,128)(2,1)} %collective-permute-done.10), channel_id=1, source_target_pairs={{0,16},{4,12},{8,24},{12,4},{16,0},{20,28},{24,8},{28,20},{1,17},{... | collective-permute-start | bytes 1327112 | tf_op jit(solution)/shard_map/ppermute | solution.py:158
  126.4 20.7 %collective-permute-start.6 = (bf16[288,1536]{1,0:T(8,128)(2,1)S(1)}, bf16[288,1536]{1,0:T(8,128)(2,1)S(1)}, u32[]{:S(2)}, u32[]{:S(2)}) collective-permute-start(bf16[288,1536]{1,0:T(8,128)(2,1)S(1)} %constant_dynamic-update-slice_fusion.8.refs_2_), channel_id=1, source_target_pairs={{0,8},{4,20},{8,0},{12,28},{16,24},{20,4},{24,16},{28,12},{1,9},{5... | collective-permute-start | bytes 2654216 | tf_op jit(solution)/shard_map/ppermute | solution.py:158
  135.9 20.8 %collective-permute-start.14 = (bf16[288,1536]{1,0:T(8,128)(2,1)S(1)}, bf16[288,1536]{1,0:T(8,128)(2,1)}, u32[]{:S(2)}, u32[]{:S(2)}) collective-permute-start(bf16[288,1536]{1,0:T(8,128)(2,1)S(1)} %constant_dynamic-update-slice_fusion.12.refs_6_), channel_id=1, source_target_pairs={{0,8},{4,20},{8,0},{12,28},{16,24},{20,4},{24,16},{28,12},{1,9},{5... | collective-permute-start | bytes 2654216 | tf_op jit(solution)/shard_map/ppermute | solution.py:158
  169.4 19.1 %collective-permute-start.20 = (bf16[4,2,192,1280]{3,2,1,0:T(8,128)(2,1)}, bf16[4,2,192,1280]{3,2,1,0:T(8,128)(2,1)}, u32[]{:S(2)}, u32[]{:S(2)}) collective-permute-start(bf16[4,2,192,1280]{3,2,1,0:T(8,128)(2,1)} %all-to-all-done.mine_ref), channel_id=1, source_target_pairs={{0,4},{4,0},{8,12},{12,8},{16,20},{20,16},{24,28},{28,24},{1,5},{5... | collective-permute-start | bytes 11796488 | tf_op jit(solution)/shard_map/ppermute | solution.py:158
  180.2 28.6 %collective-permute-start.27 = (bf16[128,1536]{1,0:T(8,128)(2,1)S(1)}, bf16[128,1536]{1,0:T(8,128)(2,1)}, u32[]{:S(2)}, u32[]{:S(2)}) collective-permute-start(bf16[128,1536]{1,0:T(8,128)(2,1)S(1)} %multiply_convert_fusion.1), channel_id=1, source_target_pairs={{0,3},{1,0},{2,1},{3,2},{4,7},{5,4},{6,5},{7,6},{8,11},{9,8},{10,9... | collective-permute-start | bytes 1179656 | tf_op jit(solution)/shard_map/ppermute | solution.py:183
  181.9 26.9 %collective-permute-start.23 = (bf16[128,1536]{1,0:T(8,128)(2,1)S(1)}, bf16[128,1536]{1,0:T(8,128)(2,1)}, u32[]{:S(2)}, u32[]{:S(2)}) collective-permute-start(bf16[128,1536]{1,0:T(8,128)(2,1)S(1)} %multiply_convert_fusion.1), channel_id=1, source_target_pairs={{0,1},{1,2},{2,3},{3,0},{4,5},{5,6},{6,7},{7,4},{8,9},{9,10},{10,1... | collective-permute-start | bytes 1179656 | tf_op jit(solution)/shard_map/ppermute | solution.py:183
  182.7 33.9 %collective-permute-start.18 = (bf16[128,1536]{1,0:T(8,128)(2,1)S(1)}, bf16[128,1536]{1,0:T(8,128)(2,1)}, u32[]{:S(2)}, u32[]{:S(2)}) collective-permute-start(bf16[128,1536]{1,0:T(8,128)(2,1)S(1)} %multiply_convert_fusion.1), channel_id=1, source_target_pairs={{0,2},{1,3},{2,0},{3,1},{4,6},{5,7},{6,4},{7,5},{8,10},{9,11},{10,... | collective-permute-start | bytes 1179656 | tf_op jit(solution)/shard_map/ppermute | solution.py:183
  186.9 33.5 %collective-permute-start.25 = (bf16[256,1536]{1,0:T(8,128)(2,1)S(1)}, bf16[256,1536]{1,0:T(8,128)(2,1)S(1)}, u32[]{:S(2)}, u32[]{:S(2)}) collective-permute-start(bf16[256,1536]{1,0:T(8,128)(2,1)S(1)} %pad_maximum_fusion.3.refs_0_), channel_id=1, source_target_pairs={{0,8},{4,20},{8,0},{12,28},{16,24},{20,4},{24,16},{28,12},{1,9},{5... | collective-permute-start | bytes 2359304 | tf_op jit(solution)/shard_map/ppermute | solution.py:158
  216.7 21.7 %collective-permute-start.21 = (bf16[128,1536]{1,0:T(8,128)(2,1)}, bf16[128,1536]{1,0:T(8,128)(2,1)S(1)}, u32[]{:S(2)}, u32[]{:S(2)}) collective-permute-start(bf16[128,1536]{1,0:T(8,128)(2,1)} %collective-permute-done.18), channel_id=1, source_target_pairs={{0,16},{4,12},{8,24},{12,4},{16,0},{20,28},{24,8},{28,20},{1,17},{... | collective-permute-start | bytes 1179656 | tf_op jit(solution)/shard_map/ppermute | solution.py:158
  217.3 20.1 %collective-permute-start.24 = (bf16[128,1536]{1,0:T(8,128)(2,1)}, bf16[128,1536]{1,0:T(8,128)(2,1)S(1)}, u32[]{:S(2)}, u32[]{:S(2)}) collective-permute-start(bf16[128,1536]{1,0:T(8,128)(2,1)} %collective-permute-done.23), channel_id=1, source_target_pairs={{0,16},{4,12},{8,24},{12,4},{16,0},{20,28},{24,8},{28,20},{1,17},{... | collective-permute-start | bytes 1179656 | tf_op jit(solution)/shard_map/ppermute | solution.py:158
  218.7 17.5 %collective-permute-start.28 = (bf16[128,1536]{1,0:T(8,128)(2,1)}, bf16[128,1536]{1,0:T(8,128)(2,1)S(1)}, u32[]{:S(2)}, u32[]{:S(2)}) collective-permute-start(bf16[128,1536]{1,0:T(8,128)(2,1)} %collective-permute-done.27), channel_id=1, source_target_pairs={{0,16},{4,12},{8,24},{12,4},{16,0},{20,28},{24,8},{28,20},{1,17},{... | collective-permute-start | bytes 1179656 | tf_op jit(solution)/shard_map/ppermute | solution.py:158
  233.2 33.3 %collective-permute-start.30 = (bf16[256,1536]{1,0:T(8,128)(2,1)S(1)}, bf16[256,1536]{1,0:T(8,128)(2,1)S(1)}, u32[]{:S(2)}, u32[]{:S(2)}) collective-permute-start(bf16[256,1536]{1,0:T(8,128)(2,1)S(1)} %get-tuple-element.188), channel_id=1, source_target_pairs={{0,8},{4,20},{8,0},{12,28},{16,24},{20,4},{24,16},{28,12},{1,9},{5... | collective-permute-start | bytes 2359304 | tf_op jit(solution)/shard_map/ppermute | solution.py:158
  236.2 32.0 %collective-permute-start.32 = (bf16[256,1536]{1,0:T(8,128)(2,1)S(1)}, bf16[256,1536]{1,0:T(8,128)(2,1)S(1)}, u32[]{:S(2)}, u32[]{:S(2)}) collective-permute-start(bf16[256,1536]{1,0:T(8,128)(2,1)S(1)} %constant_dynamic-update-slice_fusion.18.refs_0_), channel_id=1, source_target_pairs={{0,8},{4,20},{8,0},{12,28},{16,24},{20,4},{24,16},{28,12},{1,9},{5... | collective-permute-start | bytes 2359304 | tf_op jit(solution)/shard_map/ppermute | solution.py:158
  237.5 30.7 %collective-permute-start.26 = (bf16[256,1536]{1,0:T(8,128)(2,1)S(1)}, bf16[256,1536]{1,0:T(8,128)(2,1)S(1)}, u32[]{:S(2)}, u32[]{:S(2)}) collective-permute-start(bf16[256,1536]{1,0:T(8,128)(2,1)S(1)} %constant_dynamic-update-slice_fusion.16.refs_0_), channel_id=1, source_target_pairs={{0,8},{4,20},{8,0},{12,28},{16,24},{20,4},{24,16},{28,12},{1,9},{5... | collective-permute-start | bytes 2359304 | tf_op jit(solution)/shard_map/ppermute | solution.py:158
  238.4 60.0 %collective-permute-start.22 = (bf16[256,1536]{1,0:T(8,128)(2,1)S(1)}, bf16[256,1536]{1,0:T(8,128)(2,1)S(1)}, u32[]{:S(2)}, u32[]{:S(2)}) collective-permute-start(bf16[256,1536]{1,0:T(8,128)(2,1)S(1)} %constant_dynamic-update-slice_fusion.14.refs_0_), channel_id=1, source_target_pairs={{0,8},{4,20},{8,0},{12,28},{16,24},{20,4},{24,16},{28,12},{1,9},{5... | collective-permute-start | bytes 2359304 | tf_op jit(solution)/shard_map/ppermute | solution.py:158
  266.8 28.3 %collective-permute-start.31 = (bf16[128,1536]{1,0:T(8,128)(2,1)S(1)}, bf16[128,1536]{1,0:T(8,128)(2,1)}, u32[]{:S(2)}, u32[]{:S(2)}) collective-permute-start(bf16[128,1536]{1,0:T(8,128)(2,1)S(1)} %slice.478), channel_id=1, source_target_pairs={{0,16},{4,12},{8,24},{12,4},{16,0},{20,28},{24,8},{28,20},{1,17},{... | collective-permute-start | bytes 1179656 | tf_op jit(solution)/shard_map/ppermute | solution.py:158
  281.5 16.0 %collective-permute-start.29 = (bf16[256,1536]{1,0:T(8,128)(2,1)S(1)}, bf16[256,1536]{1,0:T(8,128)(2,1)S(1)}, u32[]{:S(2)}, u32[]{:S(2)}) collective-permute-start(bf16[256,1536]{1,0:T(8,128)(2,1)S(1)} %get-tuple-element.187), channel_id=1, source_target_pairs={{0,8},{4,20},{8,0},{12,28},{16,24},{20,4},{24,16},{28,12},{1,9},{5... | collective-permute-start | bytes 2359304 | tf_op jit(solution)/shard_map/ppermute | solution.py:158
  296.2 25.7 %collective-permute-start.35 = (bf16[256,1536]{1,0:T(8,128)(2,1)S(1)}, bf16[256,1536]{1,0:T(8,128)(2,1)S(1)}, u32[]{:S(2)}, u32[]{:S(2)}) collective-permute-start(bf16[256,1536]{1,0:T(8,128)(2,1)S(1)} %get-tuple-element.206), channel_id=1, source_target_pairs={{0,8},{4,20},{8,0},{12,28},{16,24},{20,4},{24,16},{28,12},{1,9},{5... | collective-permute-start | bytes 2359304 | tf_op jit(solution)/shard_map/ppermute | solution.py:158
  298.4 35.1 %collective-permute-start.33 = (bf16[128,1536]{1,0:T(8,128)(2,1)}, bf16[128,1536]{1,0:T(8,128)(2,1)}, u32[]{:S(2)}, u32[]{:S(2)}) collective-permute-start(bf16[128,1536]{1,0:T(8,128)(2,1)} %slice.477), channel_id=1, source_target_pairs={{0,16},{4,12},{8,24},{12,4},{16,0},{20,28},{24,8},{28,20},{1,17},{... | collective-permute-start | bytes 1179656 | tf_op jit(solution)/shard_map/ppermute | solution.py:158
  321.4 16.6 %collective-permute-start.38 = (bf16[256,1536]{1,0:T(8,128)(2,1)S(1)}, bf16[256,1536]{1,0:T(8,128)(2,1)S(1)}, u32[]{:S(2)}, u32[]{:S(2)}) collective-permute-start(bf16[256,1536]{1,0:T(8,128)(2,1)S(1)} %get-tuple-element.208), channel_id=1, source_target_pairs={{0,8},{4,20},{8,0},{12,28},{16,24},{20,4},{24,16},{28,12},{1,9},{5... | collective-permute-start | bytes 2359304 | tf_op jit(solution)/shard_map/ppermute | solution.py:158
  334.6 28.2 %collective-permute-start.34 = (bf16[128,1536]{1,0:T(8,128)(2,1)S(1)}, bf16[128,1536]{1,0:T(8,128)(2,1)}, u32[]{:S(2)}, u32[]{:S(2)}) collective-permute-start(bf16[128,1536]{1,0:T(8,128)(2,1)S(1)} %fusion.55), channel_id=1, source_target_pairs={{0,3},{1,0},{2,1},{3,2},{4,7},{5,4},{6,5},{7,6},{8,11},{9,8},{10,9... | collective-permute-start | bytes 1179656 | tf_op jit(solution)/shard_map/ppermute | solution.py:183
  342.1 20.7 %collective-permute-start.37 = (bf16[128,1536]{1,0:T(8,128)(2,1)S(1)}, bf16[128,1536]{1,0:T(8,128)(2,1)S(1)}, u32[]{:S(2)}, u32[]{:S(2)}) collective-permute-start(bf16[128,1536]{1,0:T(8,128)(2,1)S(1)} %fusion.54), channel_id=1, source_target_pairs={{0,1},{1,2},{2,3},{3,0},{4,5},{5,6},{6,7},{7,4},{8,9},{9,10},{10,1... | collective-permute-start | bytes 1179656 | tf_op jit(solution)/shard_map/ppermute | solution.py:183
  351.7 17.3 %collective-permute-start.40 = (bf16[128,1536]{1,0:T(8,128)(2,1)S(1)}, bf16[128,1536]{1,0:T(8,128)(2,1)S(1)}, u32[]{:S(2)}, u32[]{:S(2)}) collective-permute-start(bf16[128,1536]{1,0:T(8,128)(2,1)S(1)} %fusion.53), channel_id=1, source_target_pairs={{0,2},{1,3},{2,0},{3,1},{4,6},{5,7},{6,4},{7,5},{8,10},{9,11},{10,... | collective-permute-start | bytes 1179656 | tf_op jit(solution)/shard_map/ppermute | solution.py:183
  389.1 25.2 %collective-permute-start.42 = (bf16[4,2,192,1280]{3,2,1,0:T(8,128)(2,1)}, bf16[4,2,192,1280]{3,2,1,0:T(8,128)(2,1)}, u32[]{:S(2)}, u32[]{:S(2)}) collective-permute-start(bf16[4,2,192,1280]{3,2,1,0:T(8,128)(2,1)} %get-tuple-element.228), channel_id=1, source_target_pairs={{0,4},{4,0},{8,12},{12,8},{16,20},{20,16},{24,28},{28,24},{1,5},{5... | collective-permute-start | bytes 11796488 | tf_op jit(solution)/shard_map/ppermute | solution.py:158
  421.6 51.1 %all-to-all-start.1 = ((bf16[4,2,192,1280]{3,2,1,0:T(8,128)(2,1)}), bf16[4,2,192,1280]{3,2,1,0:T(8,128)(2,1)}, u32[]{:S(2)}, u32[]{:S(2)}) async-start(bf16[4,2,192,1280]{3,2,1,0:T(8,128)(2,1)} %add_convert_fusion), calls=%async_computation.2 | async-start | bytes 7864320 | tf_op jit(solution)/shard_map/all_to_all | solution.py:953
  439.6 27.2 %collective-permute-start.57 = (f32[128,1536]{1,0:T(8,128)S(1)}, f32[128,1536]{1,0:T(8,128)}, u32[]{:S(2)}, u32[]{:S(2)}) collective-permute-start(f32[128,1536]{1,0:T(8,128)S(1)} %slice.360), channel_id=1, source_target_pairs={{0,4},{4,0},{8,12},{12,8},{16,20},{20,16},{24,28},{28,24},{1,5},{5... | collective-permute-start | bytes 2359304 | tf_op jit(solution)/shard_map/ppermute | solution.py:158
  446.6 50.6 %collective-permute-start.52 = (bf16[288,1536]{1,0:T(8,128)(2,1)}, bf16[288,1536]{1,0:T(8,128)(2,1)}, u32[]{:S(2)}, u32[]{:S(2)}) collective-permute-start(bf16[288,1536]{1,0:T(8,128)(2,1)} %get-tuple-element.374), channel_id=1, source_target_pairs={{0,8},{4,20},{8,0},{12,28},{16,24},{20,4},{24,16},{28,12},{1,9},{5... | collective-permute-start | bytes 2654216 | tf_op jit(solution)/shard_map/ppermute | solution.py:158
  448.4 48.8 %collective-permute-start.49 = (bf16[288,1536]{1,0:T(8,128)(2,1)}, bf16[288,1536]{1,0:T(8,128)(2,1)}, u32[]{:S(2)}, u32[]{:S(2)}) collective-permute-start(bf16[288,1536]{1,0:T(8,128)(2,1)} %get-tuple-element.375), channel_id=1, source_target_pairs={{0,8},{4,20},{8,0},{12,28},{16,24},{20,4},{24,16},{28,12},{1,9},{5... | collective-permute-start | bytes 2654216 | tf_op jit(solution)/shard_map/ppermute | solution.py:158
  448.6 51.8 %collective-permute-start.47 = (bf16[288,1536]{1,0:T(8,128)(2,1)}, bf16[288,1536]{1,0:T(8,128)(2,1)}, u32[]{:S(2)}, u32[]{:S(2)}) collective-permute-start(bf16[288,1536]{1,0:T(8,128)(2,1)} %get-tuple-element.376), channel_id=1, source_target_pairs={{0,8},{4,20},{8,0},{12,28},{16,24},{20,4},{24,16},{28,12},{1,9},{5... | collective-permute-start | bytes 2654216 | tf_op jit(solution)/shard_map/ppermute | solution.py:158
  450.4 59.4 %collective-permute-start.43 = (bf16[288,1536]{1,0:T(8,128)(2,1)}, bf16[288,1536]{1,0:T(8,128)(2,1)}, u32[]{:S(2)}, u32[]{:S(2)}) collective-permute-start(bf16[288,1536]{1,0:T(8,128)(2,1)} %get-tuple-element.377), channel_id=1, source_target_pairs={{0,8},{4,20},{8,0},{12,28},{16,24},{20,4},{24,16},{28,12},{1,9},{5... | collective-permute-start | bytes 2654216 | tf_op jit(solution)/shard_map/ppermute | solution.py:158
  466.8 76.7 %collective-permute-start.56 = (f32[10,64,1536]{2,1,0:T(8,128)}, f32[10,64,1536]{2,1,0:T(8,128)}, u32[]{:S(2)}, u32[]{:S(2)}) collective-permute-start(f32[10,64,1536]{2,1,0:T(8,128)} %get-tuple-element.243), channel_id=1, source_target_pairs={{0,4},{4,0},{8,12},{12,8},{16,20},{20,16},{24,28},{28,24},{1,5},{5... | collective-permute-start | bytes 11796488 | tf_op jit(solution)/shard_map/ppermute | solution.py:158
  521.4 16.3 %collective-permute-start.53 = (bf16[144,1536]{1,0:T(8,128)(2,1)S(1)}, bf16[144,1536]{1,0:T(8,128)(2,1)S(1)}, u32[]{:S(2)}, u32[]{:S(2)}) collective-permute-start(bf16[144,1536]{1,0:T(8,128)(2,1)S(1)} %slice.470), channel_id=1, source_target_pairs={{0,16},{4,12},{8,24},{12,4},{16,0},{20,28},{24,8},{28,20},{1,17},{... | collective-permute-start | bytes 1327112 | tf_op jit(solution)/shard_map/ppermute | solution.py:158
  533.0 24.6 %collective-permute-start.51 = (bf16[144,1536]{1,0:T(8,128)(2,1)S(1)}, bf16[144,1536]{1,0:T(8,128)(2,1)S(1)}, u32[]{:S(2)}, u32[]{:S(2)}) collective-permute-start(bf16[144,1536]{1,0:T(8,128)(2,1)S(1)} %fusion.42), channel_id=1, source_target_pairs={{0,1},{1,2},{2,3},{3,0},{4,5},{5,6},{6,7},{7,4},{8,9},{9,10},{10,1... | collective-permute-start | bytes 1327112 | tf_op jit(solution)/shard_map/ppermute | solution.py:183
  537.8 19.8 %collective-permute-start.55 = (bf16[144,1536]{1,0:T(8,128)(2,1)S(1)}, bf16[144,1536]{1,0:T(8,128)(2,1)S(1)}, u32[]{:S(2)}, u32[]{:S(2)}) collective-permute-start(bf16[144,1536]{1,0:T(8,128)(2,1)S(1)} %fusion.41), channel_id=1, source_target_pairs={{0,3},{1,0},{2,1},{3,2},{4,7},{5,4},{6,5},{7,6},{8,11},{9,8},{10,9... | collective-permute-start | bytes 1327112 | tf_op jit(solution)/shard_map/ppermute | solution.py:183
  (92 other events, 1031.1 us)
Sparse Core Ops, SparseCore 0:
  54.3 122.3 all-gather.1
  379.7 112.0 reduce-scatter.1
